TPU v7x, 32 devices: a whole 2x2x4 slice. The times are simulated.
32 devices in a mesh: space: 16 (over z, y, x), sig: 2 (over core).
Axes of the slice: x: 2, y: 2, z: 4, core: 2. Of those that a mesh axis runs over, the one named last changes fastest.
Arguments:
- positions: float32 [3, 32768], P(None, 'space'), may hold values from 0 to 8, as said below
- density: bfloat16 [34, 32768], P('sig', 'space'), may hold values from -4.2 to 13.2
- leaf_count: int32 [128], P('space'), may hold values from 1 to 256, as said below
- sigma_weights: float32 [34], P('sig'), may hold values from 0.1 to 2
Outputs:
- potential: float32 [34, 32768], P('sig', 'space')
- ensemble_mean: float32 [32768], P('space')
Inputs may be any that keep to these rules, and one draw needn't show every extreme that they name: `positions`: each point lies in the unit cell of its leaf: g_l <= x_p < g_l + 1 in each component. `leaf_count`: in every draw some box has all 8 of its leaves at 256 points.
All inputs are finite; a program needn't handle non-finite values.
Results may differ from a plain program's by a relative error of at most 0.0003.
Values may be sent and summed in bfloat16 or wider, within the bound.
No kernel may reach another device: no remote copies, remote signals or barrier semaphores. Data moves between devices by JAX's collectives and lax.ppermute only.
A program may use at most 64 MiB of HBM per device.

v0:
```python
import jax
import jax.numpy as jnp
import numpy as np
from jax import lax
from jax.sharding import PartitionSpec as P

ORDER = 5


softening = 0.1
across = 4
highest = lax.Precision.HIGHEST


def passed_along(block, axis, distance):
    devices = range(lax.axis_size(axis))
    route = [(i - distance, i) for i in devices if i - distance in devices]
    return lax.ppermute(block, axis, route)


def exponent_table(order_max):
    entries_list = []
    for degree in range(order_max + 1):
        for first_power in range(degree, -1, -1):
            for second_power in range(degree - first_power, -1, -1):
                entries_list.append(
                    (first_power, second_power, degree - first_power - second_power)
                )
    return np.array(entries_list, dtype=np.int32)


def node_table(count_nodes, offset_value):
    counter = np.arange(1, count_nodes + 1, dtype=np.float32)[:, None]
    stride_set = np.array(
        [0.7548776662466927, 0.5698402909980532, 0.4142135623730951], dtype=np.float32
    )[None, :]
    unit_points = np.mod(counter * stride_set + np.float32(offset_value), np.float32(1.0))
    return (np.float32(2.0) * unit_points - np.float32(1.0)).astype(np.float32)


def monomials(scaled, power_table):
    highest_power = int(power_table.max())
    power_lists = []
    for axis_number in range(3):
        current = jnp.ones_like(scaled[axis_number])
        column_list = [current]
        for repeat_count in range(highest_power):
            current = current * scaled[axis_number]
            column_list.append(current)
        power_lists.append(column_list)
    return jnp.stack(
        [
            power_lists[0][int(exponents[0])]
            * power_lists[1][int(exponents[1])]
            * power_lists[2][int(exponents[2])]
            for exponents in power_table
        ]
    )


def kernel_value(first_part, second_part, third_part, coupling):
    return coupling / jnp.sqrt(
        first_part * first_part
        + second_part * second_part
        + third_part * third_part
        + softening * softening
    )


def translation(separation, half_width, check_nodes, equiv_nodes, coupling):
    shifted = [
        separation[..., axis_number, None, None]
        + half_width * (check_nodes[:, axis_number][:, None] - equiv_nodes[:, axis_number][None, :])
        for axis_number in range(3)
    ]
    return kernel_value(shifted[0], shifted[1], shifted[2], coupling) / check_nodes.shape[0]


def directions():
    return [
        (step_x, step_z)
        for step_z in (-1, 0, 1)
        for step_x in (-1, 0, 1)
        if step_x != 0 or step_z != 0
    ]


def facing_octants(step_x, step_z):
    chosen = []
    for octant in range(8):
        keep_x = step_x == 0 or octant % 2 == (0 if step_x > 0 else 1)
        keep_z = step_z == 0 or octant // 4 == (0 if step_z > 0 else 1)
        if keep_x and keep_z:
            chosen.append(octant)
    return chosen


def halo_cell(step_x, step_z, octant):
    cell_x = (3 if step_x > 0 else 0) if step_x != 0 else 1 + octant % 2
    cell_z = (3 if step_z > 0 else 0) if step_z != 0 else 1 + octant // 4
    return cell_x + 4 * (octant // 2 % 2) + 8 * cell_z


def own_cell(octant):
    return 1 + octant % 2 + 4 * (octant // 2 % 2) + 8 * (1 + octant // 4)


def octant_table():
    return np.array(
        [[octant % 2, octant // 2 % 2, octant // 4] for octant in range(8)], dtype=np.float32
    )


def near_cells():
    cell_table = np.zeros((8, 18), np.int32)
    for octant in range(8):
        column_index = 0
        for step_z in (-1, 0, 1):
            for step_x in (-1, 0, 1):
                for layer_y in (0, 1):
                    cell_table[octant, column_index] = (
                        1 + octant % 2 + step_x + 4 * layer_y + 8 * (1 + octant // 4 + step_z)
                    )
                    column_index += 1
    return cell_table


def far_entries():
    far_rows = np.zeros((8, 54), np.int32)
    far_offsets = np.zeros((8, 54, 3), np.float32)
    for octant in range(8):
        column_index = 0
        for direction_index, (step_x, step_z) in enumerate(directions()):
            for source_octant in range(8):
                gap_x = 2 * step_x + source_octant % 2 - octant % 2
                gap_y = source_octant // 2 % 2 - octant // 2 % 2
                gap_z = 2 * step_z + source_octant // 4 - octant // 4
                if max(abs(gap_x), abs(gap_z)) >= 2:
                    far_rows[octant, column_index] = 8 * direction_index + source_octant
                    far_offsets[octant, column_index] = (-gap_x, -gap_y, -gap_z)
                    column_index += 1
    return (far_rows, far_offsets)


def per_device(positions, density, leaf_count, sigma_weights):
    leaf_pts = positions.shape[1] // 8
    sig_cols = density.shape[0]
    power_table = exponent_table(ORDER)
    coeffs = power_table.shape[0]
    coupling = 1.0 / (128.0 * leaf_pts)
    check_nodes = jnp.asarray(node_table(coeffs, 0.5))
    equiv_nodes = jnp.asarray(node_table(coeffs, 0.0))
    space_count = lax.axis_size("space")
    depth_z = space_count // across
    device_label = lax.axis_index("space")
    box_x = device_label % across
    box_z = device_label // across
    box_xf = box_x.astype(jnp.float32)
    box_zf = box_z.astype(jnp.float32)
    bit_table = octant_table()
    slot_mask = (jnp.arange(leaf_pts)[None, :] < leaf_count[:, None]).astype(jnp.float32)
    own_points = positions.reshape(3, 8, leaf_pts)
    leaf_points = jnp.transpose(own_points, (1, 0, 2))
    mass_low = jnp.transpose(
        density.reshape(sig_cols, 8, leaf_pts) * slot_mask.astype(jnp.bfloat16)[None], (1, 0, 2)
    )
    own_mass = mass_low.astype(jnp.float32)
    leaf_centre = jnp.stack(
        [
            2.0 * box_xf + bit_table[:, 0] + 0.5,
            jnp.asarray(bit_table[:, 1] + np.float32(0.5)),
            2.0 * box_zf + bit_table[:, 2] + 0.5,
        ]
    )
    leaf_basis = monomials(2.0 * (own_points - leaf_centre[:, :, None]), power_table)
    leaf_moment = jnp.einsum("klp,lsp->lks", leaf_basis, own_mass, precision=highest)
    moment_rows = leaf_moment.reshape(8, coeffs * sig_cols)
    box_centre = jnp.stack([2.0 * box_xf + 1.0, jnp.float32(1.0), 2.0 * box_zf + 1.0])
    box_basis = monomials(own_points - box_centre[:, None, None], power_table)
    box_moment = jnp.einsum("klp,lsp->ks", box_basis, own_mass, precision=highest)
    step_list = directions()
    received = []
    for step_x, step_z in step_list:
        chosen_rows = np.array(facing_octants(step_x, step_z), dtype=np.int32)
        distance = -(step_x + across * step_z)
        points_in = passed_along(leaf_points[chosen_rows], "space", distance)
        moment_in = passed_along(moment_rows, "space", distance)
        mass_in = passed_along(mass_low[chosen_rows], "space", distance)
        received.append((points_in, mass_in, moment_in))
    ext_points = [None] * 32
    ext_mass = [None] * 32
    for octant in range(8):
        ext_points[own_cell(octant)] = leaf_points[octant]
        ext_mass[own_cell(octant)] = own_mass[octant]
    moment_blocks = []
    for direction_index, (step_x, step_z) in enumerate(step_list):
        points_in, mass_in, moment_in = received[direction_index]
        inside = (
            (box_x + step_x >= 0)
            & (box_x + step_x < across)
            & (box_z + step_z >= 0)
            & (box_z + step_z < depth_z)
        ).astype(jnp.float32)
        for slot_number, octant in enumerate(facing_octants(step_x, step_z)):
            cell_label = halo_cell(step_x, step_z, octant)
            ext_points[cell_label] = points_in[slot_number]
            ext_mass[cell_label] = mass_in[slot_number].astype(jnp.float32) * inside
        moment_blocks.append(moment_in.reshape(8, coeffs, sig_cols) * inside)
    ext_point_array = jnp.stack(ext_points)
    ext_mass_array = jnp.stack(ext_mass)
    near_table = near_cells()
    source_points = jnp.transpose(ext_point_array[near_table], (0, 2, 1, 3)).reshape(
        8, 3, 18 * leaf_pts
    )
    source_mass = jnp.transpose(ext_mass_array[near_table], (0, 2, 1, 3)).reshape(
        8, sig_cols, 18 * leaf_pts
    )
    kernel_block = kernel_value(
        leaf_points[:, 0, :, None] - source_points[:, 0, None, :],
        leaf_points[:, 1, :, None] - source_points[:, 1, None, :],
        leaf_points[:, 2, :, None] - source_points[:, 2, None, :],
        coupling,
    )
    near_part = jnp.einsum("tpq,tsq->tsp", kernel_block, source_mass, precision=highest)
    far_rows, far_offsets = far_entries()
    neighbour_stack = jnp.stack(moment_blocks).reshape(64, coeffs, sig_cols)
    far_sources = neighbour_stack[far_rows]
    far_operator = translation(jnp.asarray(far_offsets), 0.5, check_nodes, equiv_nodes, coupling)
    leaf_local = jnp.einsum("tejk,teks->tjs", far_operator, far_sources, precision=highest)
    far_part = jnp.einsum("klp,lks->lsp", leaf_basis, leaf_local, precision=highest)
    all_boxes = lax.all_gather(
        box_moment.reshape(1, coeffs * sig_cols), "space", axis=0, tiled=True
    ).reshape(space_count, coeffs, sig_cols)
    source_label = jnp.arange(space_count)
    separation = jnp.stack(
        [
            box_centre[0] - (2.0 * (source_label % across).astype(jnp.float32) + 1.0),
            jnp.zeros((space_count,), jnp.float32),
            box_centre[2] - (2.0 * (source_label // across).astype(jnp.float32) + 1.0),
        ],
        1,
    )
    far_flag = (jnp.maximum(jnp.abs(separation[:, 0]), jnp.abs(separation[:, 2])) >= 3.5).astype(
        jnp.float32
    )
    operator = (
        translation(separation, 1.0, check_nodes, equiv_nodes, coupling) * far_flag[:, None, None]
    )
    box_local = jnp.einsum("njk,nks->js", operator, all_boxes, precision=highest)
    coarse_part = jnp.einsum("klp,ks->lsp", box_basis, box_local, precision=highest)
    total_leaf = (near_part + far_part + coarse_part) * slot_mask[:, None, :]
    potential = jnp.transpose(total_leaf, (1, 0, 2)).reshape(sig_cols, 8 * leaf_pts)
    weighted = jnp.sum(sigma_weights[:, None] * potential, 0)
    weight_total = jnp.sum(sigma_weights)
    weighted_all, weight_all = lax.psum((weighted, weight_total), "sig")
    return (potential, weighted_all / weight_all)


def solution(mesh):
    in_specs = (P(None, "space"), P("sig", "space"), P("space"), P("sig"))
    out_specs = (P("sig", "space"), P("space"))
    return jax.shard_map(
        per_device, mesh=mesh, in_specs=in_specs, out_specs=out_specs, check_vma=False
    )
```

profile of v0, /device:TPU:25, one launch (start us, length us, event | category | flops | bytes accessed | tf_op | source)
XLA Modules:
  0.0 267.0 jit_solution(12758449612166294555)
XLA Ops:
  9.2 4.1 %collective-permute-start.18 = (f32[8,952]{1,0:T(8,128)}, f32[8,952]{1,0:T(8,128)S(1)}, u32[]{:S(2)}, u32[]{:S(2)}) collective-permute-start(f32[8,952]{1,0:T(8,128)} %reshape.420), channel_id=1, source_target_pairs={{0,6},{2,8},{4,10},{6,12},{8,14},{10,16},{12,18},{14,20},{16,22},{... | collective-permute-start | bytes 91400 | tf_op jit(solution)/shard_map/ppermute | solution.py:18
  21.9 29.9 %all-gather = f32[16,1,952]{2,1,0:T(1,128)S(1)} all-gather(f32[1,1,952]{2,1,0:T(1,128)S(1)} %reshape.584), channel_id=1, replica_groups=mesh['space'=16,'sig'=2] {'space'}, dimensions={0}, use_global_device_ids=true | all-gather | bytes 64736 | tf_op jit(solution)/shard_map/all_gather | solution.py:231
  68.7 7.1 %collective-permute-start.10 = (f32[2,3,256]{2,0,1:T(2,128)S(1)}, f32[2,3,256]{2,0,1:T(2,128)S(1)}, u32[]{:S(2)}, u32[]{:S(2)}) collective-permute-start(f32[2,3,256]{2,0,1:T(2,128)S(1)} %copy.146), channel_id=1, source_target_pairs={{0,6},{2,8},{4,10},{6,12},{8,14},{10,16},{12,18},{14,20},{16,22},{... | collective-permute-start | bytes 18440 | tf_op jit(solution)/shard_map/ppermute | solution.py:18
  78.5 3.3 %collective-permute-done.13 = f32[2,3,256]{2,0,1:T(2,128)S(1)} collective-permute-done((f32[2,3,256]{2,0,1:T(2,128)S(1)}, f32[2,3,256]{2,0,1:T(2,128)S(1)}, u32[]{:S(2)}, u32[]{:S(2)}) %collective-permute-start.13) | collective-permute-done | bytes 6176 | tf_op jit(solution)/shard_map/ppermute | solution.py:18
  81.8 4.0 %collective-permute-start.15 = (f32[2,3,256]{2,0,1:T(2,128)S(1)}, f32[2,3,256]{2,0,1:T(2,128)S(1)}, u32[]{:S(2)}, u32[]{:S(2)}) collective-permute-start(f32[2,3,256]{2,0,1:T(2,128)S(1)} %copy.156), channel_id=1, source_target_pairs={{10,0},{12,2},{14,4},{16,6},{18,8},{20,10},{22,12},{24,14},{26,16}... | collective-permute-start | bytes 18440 | tf_op jit(solution)/shard_map/ppermute | solution.py:18
  87.8 3.1 %collective-permute-done.9 = f32[4,3,256]{2,0,1:T(4,128)S(1)} collective-permute-done((f32[4,3,256]{2,0,1:T(4,128)S(1)}, f32[4,3,256]{2,0,1:T(4,128)S(1)}, u32[]{:S(2)}, u32[]{:S(2)}) %collective-permute-start.9) | collective-permute-done | bytes 12320 | tf_op jit(solution)/shard_map/ppermute | solution.py:18
  91.0 2.4 collective-permute-start.11
  93.4 3.8 %collective-permute-done.11 = f32[4,3,256]{2,0,1:T(4,128)S(1)} collective-permute-done((f32[4,3,256]{2,0,1:T(4,128)S(1)}, f32[4,3,256]{2,0,1:T(4,128)S(1)}, u32[]{:S(2)}, u32[]{:S(2)}) %collective-permute-start.11) | collective-permute-done | bytes 12320 | tf_op jit(solution)/shard_map/ppermute | solution.py:18
  97.2 3.3 %collective-permute-start.12 = (f32[4,3,256]{2,0,1:T(4,128)S(1)}, f32[4,3,256]{2,0,1:T(4,128)S(1)}, u32[]{:S(2)}, u32[]{:S(2)}) collective-permute-start(f32[4,3,256]{2,0,1:T(4,128)S(1)} %copy.150), channel_id=1, source_target_pairs={{2,0},{4,2},{6,4},{8,6},{10,8},{12,10},{14,12},{16,14},{18,16},{20... | collective-permute-start | bytes 36872 | tf_op jit(solution)/shard_map/ppermute | solution.py:18
  101.6 3.9 %collective-permute-start.14 = (f32[4,3,256]{2,0,1:T(4,128)S(1)}, f32[4,3,256]{2,0,1:T(4,128)S(1)}, u32[]{:S(2)}, u32[]{:S(2)}) collective-permute-start(f32[4,3,256]{2,0,1:T(4,128)S(1)} %copy.154), channel_id=1, source_target_pairs={{8,0},{10,2},{12,4},{14,6},{16,8},{18,10},{20,12},{22,14},{24,16},... | collective-permute-start | bytes 36872 | tf_op jit(solution)/shard_map/ppermute | solution.py:18
  109.8 3.8 %collective-permute-done = bf16[2,17,256]{2,1,0:T(8,128)(2,1)S(1)} collective-permute-done((bf16[2,17,256]{2,1,0:T(8,128)(2,1)S(1)}, bf16[2,17,256]{2,1,0:T(8,128)(2,1)S(1)}, u32[]{:S(2)}, u32[]{:S(2)}) %collective-permute-start) | collective-permute-done | bytes 17440 | tf_op jit(solution)/shard_map/ppermute | solution.py:18
  113.6 3.1 %collective-permute-start.20 = (f32[8,952]{1,0:T(8,128)}, f32[8,952]{1,0:T(8,128)S(1)}, u32[]{:S(2)}, u32[]{:S(2)}) collective-permute-start(f32[8,952]{1,0:T(8,128)} %reshape.420), channel_id=1, source_target_pairs={{2,0},{4,2},{6,4},{8,6},{10,8},{12,10},{14,12},{16,14},{18,16},{20... | collective-permute-start | bytes 91400 | tf_op jit(solution)/shard_map/ppermute | solution.py:18
  116.7 3.6 %collective-permute-start.21 = (f32[8,952]{1,0:T(8,128)}, f32[8,952]{1,0:T(8,128)S(1)}, u32[]{:S(2)}, u32[]{:S(2)}) collective-permute-start(f32[8,952]{1,0:T(8,128)} %reshape.420), channel_id=1, source_target_pairs={{6,0},{8,2},{10,4},{12,6},{14,8},{16,10},{18,12},{20,14},{22,16},{... | collective-permute-start | bytes 91400 | tf_op jit(solution)/shard_map/ppermute | solution.py:18
  122.0 4.7 %collective-permute-start.23 = (f32[8,952]{1,0:T(8,128)}, f32[8,952]{1,0:T(8,128)}, u32[]{:S(2)}, u32[]{:S(2)}) collective-permute-start(f32[8,952]{1,0:T(8,128)} %reshape.420), channel_id=1, source_target_pairs={{10,0},{12,2},{14,4},{16,6},{18,8},{20,10},{22,12},{24,14},{26,16}... | collective-permute-start | bytes 91400 | tf_op jit(solution)/shard_map/ppermute | solution.py:18
  132.9 5.2 %collective-permute-start.4 = (bf16[4,17,256]{2,1,0:T(8,128)(2,1)}, bf16[4,17,256]{2,1,0:T(8,128)(2,1)}, u32[]{:S(2)}, u32[]{:S(2)}) collective-permute-start(bf16[4,17,256]{2,1,0:T(8,128)(2,1)} %gather_fusion.4), channel_id=1, source_target_pairs={{2,0},{4,2},{6,4},{8,6},{10,8},{12,10},{14,12},{16,14},{18,16},{20... | collective-permute-start | bytes 104456 | tf_op jit(solution)/shard_map/ppermute | solution.py:18
  142.4 2.4 collective-permute-start.5
  151.5 3.5 %gather_fusion.18 = f32[432,56,17]{1,2,0:T(8,128)} fusion(f32[64,56,17]{1,2,0:T(8,128)S(1)} %copy.163, s32[1024]{0:T(1024)S(1)} %pad_clamp_fusion), kind=kCustom, calls=%fused_computation.18 | custom fusion | bytes 3291840 | tf_op jit(solution)/shard_map/gather | solution.py:227
  155.0 18.9 %fusion.45 = f32[8,56,17]{1,2,0:T(8,128)} fusion(f32[8,54,56,17]{2,3,1,0:T(8,128)} %bitcast.71, f32[56,56]{1,0:T(8,128)S(1)} %copy-done.10, f32[8,54]{1,0:T(8,128)S(1)} %copy-done.30, f32[56,56]{1,0:T(8,128)S(1)} %copy-done.9, f32[8,54]{1,0:T(8,128)S(1)} %copy-done.31, f32[56,56]{1,0:T(8,128)S(1)} %copy-done.8, f32[8,54]{1,0:T(8,128)S(1)} %copy-done.32), kind=kOutput, calls=%fused_computation.67 | convolution fusion | flops 291271680 | bytes 1718336 | tf_op jit(solution)/shard_map/tejk,teks->tjs/dot_general | solution.py:229
  173.9 4.0 %collective-permute-start.6 = (bf16[4,17,256]{2,1,0:T(8,128)(2,1)S(1)}, bf16[4,17,256]{2,1,0:T(8,128)(2,1)S(1)}, u32[]{:S(2)}, u32[]{:S(2)}) collective-permute-start(bf16[4,17,256]{2,1,0:T(8,128)(2,1)S(1)} %copy-done.7), channel_id=1, source_target_pairs={{8,0},{10,2},{12,4},{14,6},{16,8},{18,10},{20,12},{22,14},{24,16},... | collective-permute-start | bytes 104456 | tf_op jit(solution)/shard_map/ppermute | solution.py:18
  179.3 3.7 %collective-permute-start.7 = (bf16[2,17,256]{2,1,0:T(8,128)(2,1)S(1)}, bf16[2,17,256]{2,1,0:T(8,128)(2,1)S(1)}, u32[]{:S(2)}, u32[]{:S(2)}) collective-permute-start(bf16[2,17,256]{2,1,0:T(8,128)(2,1)S(1)} %copy-done.11), channel_id=1, source_target_pairs={{10,0},{12,2},{14,4},{16,6},{18,8},{20,10},{22,12},{24,14},{26,16}... | collective-permute-start | bytes 52232 | tf_op jit(solution)/shard_map/ppermute | solution.py:18
  193.1 2.7 %gather_fusion.8 = f32[144,17,256]{2,1,0:T(8,128)} fusion(f32[32,17,256]{2,1,0:T(8,128)S(1)} %constant_dynamic-update-slice_fusion, s32[1024]{0:T(1024)S(1)} %pad_clamp_fusion.1), kind=kCustom, calls=%fused_computation.8 | custom fusion | bytes 5014080 | tf_op jit(solution)/shard_map/gather | solution.py:215
  195.8 2.9 %copy.209 = f32[8,18,17,256]{3,1,0,2:T(8,128)S(1)} copy(f32[8,18,17,256]{3,2,1,0:T(8,128)} %bitcast.72) | data formatting | bytes 5013504 | tf_op jit(solution)/shard_map/gather | solution.py:215
  200.7 41.5 %fusion = f32[8,17,256]{2,1,0:T(8,128)S(1)} fusion(f32[8,4608]{1,0:T(8,128)} %get-tuple-element.13, f32[8,256]{1,0:T(8,128)S(1)} %copy-done.17, f32[8,4608]{1,0:T(8,128)} %get-tuple-element.14, f32[8,256]{1,0:T(8,128)S(1)} %copy-done.16, f32[8,4608]{1,0:T(8,128)S(1)} %copy-done.5, f32[8,256]{1,0:T(8,128)S(1)} %copy-done.15, f32[8,17,4608]{2,0,1:T(8,128)} %reshape.417), kind=kOutput, calls=%fused_computation.19 | convolution fusion | flops 2019557376 | bytes 3112960 | tf_op jit(solution)/shard_map/tpq,tsq->tsp/dot_general | solution.py:224
  244.0 21.7 %all-reduce = (f32[2048]{0:T(1024)S(1)}, f32[]{:T(128)}) all-reduce(f32[2048]{0:T(1024)S(1)} %bitcast.87, f32[]{:T(128)} %reduce_sum.22), channel_id=1, replica_groups=mesh['space'=16,'sig'=2] {'sig'}, use_global_device_ids=true, to_apply=%region_1.2 | all-reduce | flops 2049 | bytes 16392 | tf_op jit(solution)/shard_map/psum | solution.py:255
  (334 shorter events, 78.0 us)
Async XLA Ops:
  6.6 110.1 %collective-permute-start.16 = (f32[8,952]{1,0:T(8,128)}, f32[8,952]{1,0:T(8,128)S(1)}, u32[]{:S(2)}, u32[]{:S(2)}) collective-permute-start(f32[8,952]{1,0:T(8,128)} %reshape.420), channel_id=1, source_target_pairs={{0,10},{2,12},{4,14},{6,16},{8,18},{10,20},{12,22},{14,24},{16,26}... | collective-permute-start | bytes 91400 | tf_op jit(solution)/shard_map/ppermute | solution.py:18
  7.9 112.5 %collective-permute-start.17 = (f32[8,952]{1,0:T(8,128)}, f32[8,952]{1,0:T(8,128)S(1)}, u32[]{:S(2)}, u32[]{:S(2)}) collective-permute-start(f32[8,952]{1,0:T(8,128)} %reshape.420), channel_id=1, source_target_pairs={{0,8},{2,10},{4,12},{6,14},{8,16},{10,18},{12,20},{14,22},{16,24},... | collective-permute-start | bytes 91400 | tf_op jit(solution)/shard_map/ppermute | solution.py:18
  9.2 112.8 %collective-permute-start.18 = (f32[8,952]{1,0:T(8,128)}, f32[8,952]{1,0:T(8,128)S(1)}, u32[]{:S(2)}, u32[]{:S(2)}) collective-permute-start(f32[8,952]{1,0:T(8,128)} %reshape.420), channel_id=1, source_target_pairs={{0,6},{2,8},{4,10},{6,12},{8,14},{10,16},{12,18},{14,20},{16,22},{... | collective-permute-start | bytes 91400 | tf_op jit(solution)/shard_map/ppermute | solution.py:18
  13.3 113.4 %collective-permute-start.19 = (f32[8,952]{1,0:T(8,128)}, f32[8,952]{1,0:T(8,128)S(1)}, u32[]{:S(2)}, u32[]{:S(2)}) collective-permute-start(f32[8,952]{1,0:T(8,128)} %reshape.420), channel_id=1, source_target_pairs={{0,2},{2,4},{4,6},{6,8},{8,10},{10,12},{12,14},{14,16},{16,18},{18... | collective-permute-start | bytes 91400 | tf_op jit(solution)/shard_map/ppermute | solution.py:18
  17.2 51.5 %collective-permute-start.8 = (f32[2,3,256]{2,0,1:T(2,128)S(1)}, f32[2,3,256]{2,0,1:T(2,128)S(1)}, u32[]{:S(2)}, u32[]{:S(2)}) collective-permute-start(f32[2,3,256]{2,0,1:T(2,128)S(1)} %copy.142), channel_id=1, source_target_pairs={{0,10},{2,12},{4,14},{6,16},{8,18},{10,20},{12,22},{14,24},{16,26}... | collective-permute-start | bytes 18440 | tf_op jit(solution)/shard_map/ppermute | solution.py:18
  68.7 7.8 %collective-permute-start.10 = (f32[2,3,256]{2,0,1:T(2,128)S(1)}, f32[2,3,256]{2,0,1:T(2,128)S(1)}, u32[]{:S(2)}, u32[]{:S(2)}) collective-permute-start(f32[2,3,256]{2,0,1:T(2,128)S(1)} %copy.146), channel_id=1, source_target_pairs={{0,6},{2,8},{4,10},{6,12},{8,14},{10,16},{12,18},{14,20},{16,22},{... | collective-permute-start | bytes 18440 | tf_op jit(solution)/shard_map/ppermute | solution.py:18
  76.5 5.3 %collective-permute-start.13 = (f32[2,3,256]{2,0,1:T(2,128)S(1)}, f32[2,3,256]{2,0,1:T(2,128)S(1)}, u32[]{:S(2)}, u32[]{:S(2)}) collective-permute-start(f32[2,3,256]{2,0,1:T(2,128)S(1)} %copy.152), channel_id=1, source_target_pairs={{6,0},{8,2},{10,4},{12,6},{14,8},{16,10},{18,12},{20,14},{22,16},{... | collective-permute-start | bytes 18440 | tf_op jit(solution)/shard_map/ppermute | solution.py:18
  81.8 4.7 %collective-permute-start.15 = (f32[2,3,256]{2,0,1:T(2,128)S(1)}, f32[2,3,256]{2,0,1:T(2,128)S(1)}, u32[]{:S(2)}, u32[]{:S(2)}) collective-permute-start(f32[2,3,256]{2,0,1:T(2,128)S(1)} %copy.156), channel_id=1, source_target_pairs={{10,0},{12,2},{14,4},{16,6},{18,8},{20,10},{22,12},{24,14},{26,16}... | collective-permute-start | bytes 18440 | tf_op jit(solution)/shard_map/ppermute | solution.py:18
  86.5 4.4 %collective-permute-start.9 = (f32[4,3,256]{2,0,1:T(4,128)S(1)}, f32[4,3,256]{2,0,1:T(4,128)S(1)}, u32[]{:S(2)}, u32[]{:S(2)}) collective-permute-start(f32[4,3,256]{2,0,1:T(4,128)S(1)} %copy.144), channel_id=1, source_target_pairs={{0,8},{2,10},{4,12},{6,14},{8,16},{10,18},{12,20},{14,22},{16,24},... | collective-permute-start | bytes 36872 | tf_op jit(solution)/shard_map/ppermute | solution.py:18
  91.0 6.2 %collective-permute-start.11 = (f32[4,3,256]{2,0,1:T(4,128)S(1)}, f32[4,3,256]{2,0,1:T(4,128)S(1)}, u32[]{:S(2)}, u32[]{:S(2)}) collective-permute-start(f32[4,3,256]{2,0,1:T(4,128)S(1)} %copy.148), channel_id=1, source_target_pairs={{0,2},{2,4},{4,6},{6,8},{8,10},{10,12},{12,14},{14,16},{16,18},{18... | collective-permute-start | bytes 36872 | tf_op jit(solution)/shard_map/ppermute | solution.py:18
  97.2 4.4 %collective-permute-start.12 = (f32[4,3,256]{2,0,1:T(4,128)S(1)}, f32[4,3,256]{2,0,1:T(4,128)S(1)}, u32[]{:S(2)}, u32[]{:S(2)}) collective-permute-start(f32[4,3,256]{2,0,1:T(4,128)S(1)} %copy.150), channel_id=1, source_target_pairs={{2,0},{4,2},{6,4},{8,6},{10,8},{12,10},{14,12},{16,14},{18,16},{20... | collective-permute-start | bytes 36872 | tf_op jit(solution)/shard_map/ppermute | solution.py:18
  101.6 4.7 %collective-permute-start.14 = (f32[4,3,256]{2,0,1:T(4,128)S(1)}, f32[4,3,256]{2,0,1:T(4,128)S(1)}, u32[]{:S(2)}, u32[]{:S(2)}) collective-permute-start(f32[4,3,256]{2,0,1:T(4,128)S(1)} %copy.154), channel_id=1, source_target_pairs={{8,0},{10,2},{12,4},{14,6},{16,8},{18,10},{20,12},{22,14},{24,16},... | collective-permute-start | bytes 36872 | tf_op jit(solution)/shard_map/ppermute | solution.py:18
  106.3 7.3 %collective-permute-start = (bf16[2,17,256]{2,1,0:T(8,128)(2,1)S(1)}, bf16[2,17,256]{2,1,0:T(8,128)(2,1)S(1)}, u32[]{:S(2)}, u32[]{:S(2)}) collective-permute-start(bf16[2,17,256]{2,1,0:T(8,128)(2,1)S(1)} %gather_fusion), channel_id=1, source_target_pairs={{0,10},{2,12},{4,14},{6,16},{8,18},{10,20},{12,22},{14,24},{16,26}... | collective-permute-start | bytes 52232 | tf_op jit(solution)/shard_map/ppermute | solution.py:18
  113.6 14.5 %collective-permute-start.20 = (f32[8,952]{1,0:T(8,128)}, f32[8,952]{1,0:T(8,128)S(1)}, u32[]{:S(2)}, u32[]{:S(2)}) collective-permute-start(f32[8,952]{1,0:T(8,128)} %reshape.420), channel_id=1, source_target_pairs={{2,0},{4,2},{6,4},{8,6},{10,8},{12,10},{14,12},{16,14},{18,16},{20... | collective-permute-start | bytes 91400 | tf_op jit(solution)/shard_map/ppermute | solution.py:18
  116.7 13.6 %collective-permute-start.21 = (f32[8,952]{1,0:T(8,128)}, f32[8,952]{1,0:T(8,128)S(1)}, u32[]{:S(2)}, u32[]{:S(2)}) collective-permute-start(f32[8,952]{1,0:T(8,128)} %reshape.420), channel_id=1, source_target_pairs={{6,0},{8,2},{10,4},{12,6},{14,8},{16,10},{18,12},{20,14},{22,16},{... | collective-permute-start | bytes 91400 | tf_op jit(solution)/shard_map/ppermute | solution.py:18
  120.4 12.6 %collective-permute-start.22 = (f32[8,952]{1,0:T(8,128)}, f32[8,952]{1,0:T(8,128)S(1)}, u32[]{:S(2)}, u32[]{:S(2)}) collective-permute-start(f32[8,952]{1,0:T(8,128)} %reshape.420), channel_id=1, source_target_pairs={{8,0},{10,2},{12,4},{14,6},{16,8},{18,10},{20,12},{22,14},{24,16},... | collective-permute-start | bytes 91400 | tf_op jit(solution)/shard_map/ppermute | solution.py:18
  122.0 20.4 %collective-permute-start.23 = (f32[8,952]{1,0:T(8,128)}, f32[8,952]{1,0:T(8,128)}, u32[]{:S(2)}, u32[]{:S(2)}) collective-permute-start(f32[8,952]{1,0:T(8,128)} %reshape.420), channel_id=1, source_target_pairs={{10,0},{12,2},{14,4},{16,6},{18,8},{20,10},{22,12},{24,14},{26,16}... | collective-permute-start | bytes 91400 | tf_op jit(solution)/shard_map/ppermute | solution.py:18
  126.7 47.2 %collective-permute-start.1 = (bf16[4,17,256]{2,1,0:T(8,128)(2,1)}, bf16[4,17,256]{2,1,0:T(8,128)(2,1)}, u32[]{:S(2)}, u32[]{:S(2)}) collective-permute-start(bf16[4,17,256]{2,1,0:T(8,128)(2,1)} %gather_fusion.1), channel_id=1, source_target_pairs={{0,8},{2,10},{4,12},{6,14},{8,16},{10,18},{12,20},{14,22},{16,24},... | collective-permute-start | bytes 104456 | tf_op jit(solution)/shard_map/ppermute | solution.py:18
  128.0 51.3 %collective-permute-start.2 = (bf16[2,17,256]{2,1,0:T(8,128)(2,1)}, bf16[2,17,256]{2,1,0:T(8,128)(2,1)}, u32[]{:S(2)}, u32[]{:S(2)}) collective-permute-start(bf16[2,17,256]{2,1,0:T(8,128)(2,1)} %gather_fusion.2), channel_id=1, source_target_pairs={{0,6},{2,8},{4,10},{6,12},{8,14},{10,16},{12,18},{14,20},{16,22},{... | collective-permute-start | bytes 52232 | tf_op jit(solution)/shard_map/ppermute | solution.py:18
  130.2 55.6 %collective-permute-start.3 = (bf16[4,17,256]{2,1,0:T(8,128)(2,1)}, bf16[4,17,256]{2,1,0:T(8,128)(2,1)}, u32[]{:S(2)}, u32[]{:S(2)}) collective-permute-start(bf16[4,17,256]{2,1,0:T(8,128)(2,1)} %gather_fusion.3), channel_id=1, source_target_pairs={{0,2},{2,4},{4,6},{6,8},{8,10},{10,12},{12,14},{14,16},{16,18},{18... | collective-permute-start | bytes 104456 | tf_op jit(solution)/shard_map/ppermute | solution.py:18
  132.9 53.6 %collective-permute-start.4 = (bf16[4,17,256]{2,1,0:T(8,128)(2,1)}, bf16[4,17,256]{2,1,0:T(8,128)(2,1)}, u32[]{:S(2)}, u32[]{:S(2)}) collective-permute-start(bf16[4,17,256]{2,1,0:T(8,128)(2,1)} %gather_fusion.4), channel_id=1, source_target_pairs={{2,0},{4,2},{6,4},{8,6},{10,8},{12,10},{14,12},{16,14},{18,16},{20... | collective-permute-start | bytes 104456 | tf_op jit(solution)/shard_map/ppermute | solution.py:18
  142.4 49.2 %collective-permute-start.5 = (bf16[2,17,256]{2,1,0:T(8,128)(2,1)}, bf16[2,17,256]{2,1,0:T(8,128)(2,1)}, u32[]{:S(2)}, u32[]{:S(2)}) collective-permute-start(bf16[2,17,256]{2,1,0:T(8,128)(2,1)} %gather_fusion.5), channel_id=1, source_target_pairs={{6,0},{8,2},{10,4},{12,6},{14,8},{16,10},{18,12},{20,14},{22,16},{... | collective-permute-start | bytes 52232 | tf_op jit(solution)/shard_map/ppermute | solution.py:18
  173.9 18.4 %collective-permute-start.6 = (bf16[4,17,256]{2,1,0:T(8,128)(2,1)S(1)}, bf16[4,17,256]{2,1,0:T(8,128)(2,1)S(1)}, u32[]{:S(2)}, u32[]{:S(2)}) collective-permute-start(bf16[4,17,256]{2,1,0:T(8,128)(2,1)S(1)} %copy-done.7), channel_id=1, source_target_pairs={{8,0},{10,2},{12,4},{14,6},{16,8},{18,10},{20,12},{22,14},{24,16},... | collective-permute-start | bytes 104456 | tf_op jit(solution)/shard_map/ppermute | solution.py:18
  179.3 13.0 %collective-permute-start.7 = (bf16[2,17,256]{2,1,0:T(8,128)(2,1)S(1)}, bf16[2,17,256]{2,1,0:T(8,128)(2,1)S(1)}, u32[]{:S(2)}, u32[]{:S(2)}) collective-permute-start(bf16[2,17,256]{2,1,0:T(8,128)(2,1)S(1)} %copy-done.11), channel_id=1, source_target_pairs={{10,0},{12,2},{14,4},{16,6},{18,8},{20,10},{22,12},{24,14},{26,16}... | collective-permute-start | bytes 52232 | tf_op jit(solution)/shard_map/ppermute | solution.py:18
  (33 other events, 1156.8 us)
where the time goes:
time: 269 us; the launch traced here: 267 us
  starting transfers between devices  68.6 us (26%)
  matrix products  63.8 us (24%)
  blocking collectives  51.6 us (19%)
  local copies, waits for them, and re-layouts  39.7 us (15%)
  other arithmetic  23.3 us (9%)
  waiting for transfers between devices  17.4 us (6%)
    ppermute x24, starting transfers between devices, passed_along(): return lax.ppermute(block, axis, route)  68.6 us
    dot_general x1, matrix products, per_device(): jnp.einsum('tpq,tsq->tsp', kernel_block, source_mass, precision=highest)  41.5 us
    all_gather x1, blocking collectives, per_device(): lax.all_gather(box_moment.reshape(1, coeffs * sig_cols), 'space', axis=0,...  29.9 us
    psum x1, blocking collectives, per_device(): weighted_all, weight_all = lax.psum((weighted, weight_total), 'sig')  21.7 us
    dot_general x1, matrix products, per_device(): jnp.einsum('tejk,teks->tjs', far_operator, far_sources, precision=highest)  18.9 us
    ppermute x24, waiting for transfers between devices, passed_along(): return lax.ppermute(block, axis, route)  17.4 us
    unnamed x126, other arithmetic  12.9 us
    gather x8, local copies, waits for them, and re-layouts, per_device(): mass_in = passed_along(mass_low[chosen_rows], 'space', distance)  8.64 us
  transfers between devices with their start and end apart: 24, of which 8 were waited for; matrix products, arithmetic and copies ran while one was open for 26% of the time, Pallas kernels for 0%

commit v1 on v0

v1 whole, which is shorter than its diff:
```python
import functools
import math

import jax
import jax.numpy as jnp
import numpy as np
from jax import lax
from jax.experimental import pallas as pl
from jax.experimental.pallas import tpu as pltpu
from jax.sharding import PartitionSpec as P

ORDER = 5
SOFTENING = 0.1
ACROSS = 4
SLOT = 64
ROWS = 32
FEATURES = 48


def exponent_table(order_max):
    entries_list = []
    for degree in range(order_max + 1):
        for first_power in range(degree, -1, -1):
            for second_power in range(degree - first_power, -1, -1):
                entries_list.append((first_power, second_power, degree - first_power - second_power))
    return entries_list


def node_table(count_nodes, offset_value):
    counter = np.arange(1, count_nodes + 1, dtype=np.float32)[:, None]
    stride_set = np.array([0.7548776662466927, 0.5698402909980532, 0.4142135623730951], dtype=np.float32)[None, :]
    unit_points = np.mod(counter * stride_set + np.float32(offset_value), np.float32(1.0))
    return (np.float32(2.0) * unit_points - np.float32(1.0)).astype(np.float32)


EXPONENTS = exponent_table(ORDER)
COEFFS = len(EXPONENTS)
CHECK = node_table(COEFFS, 0.5).astype(np.float64)
EQUIV = node_table(COEFFS, 0.0).astype(np.float64)
STEPS = [(sx, sz) for sz in (-1, 0, 1) for sx in (-1, 0, 1) if sx != 0 or sz != 0]


def bits(octant):
    return octant % 2, octant // 2 % 2, octant // 4


def facing_octants(step_x, step_z):
    chosen = []
    for octant in range(8):
        bit_x, _, bit_z = bits(octant)
        keep_x = step_x == 0 or bit_x == (0 if step_x > 0 else 1)
        keep_z = step_z == 0 or bit_z == (0 if step_z > 0 else 1)
        if keep_x and keep_z:
            chosen.append(octant)
    return chosen


def leaf_slot(octant):
    bit_x, bit_y, bit_z = bits(octant)
    return (bit_x + 2 * bit_z) * 2 + bit_y


def split_table(table):
    high = table.astype(np.float32).astype(jnp.bfloat16)
    low = (table - high.astype(np.float64)).astype(np.float32).astype(jnp.bfloat16)
    return high, low


@functools.lru_cache(None)
def far_table():
    shape = (len(STEPS), 8, SLOT, 8, SLOT)
    table = np.zeros(shape)
    gap_nodes = 0.5 * (CHECK[None, :, :] - EQUIV[:, None, :])
    for index, (step_x, step_z) in enumerate(STEPS):
        for source in range(8):
            for target in range(8):
                s, t = bits(source), bits(target)
                gap = np.array([2 * step_x + s[0] - t[0], s[1] - t[1], 2 * step_z + s[2] - t[2]], np.float64)
                if max(abs(gap[0]), abs(gap[2])) >= 2:
                    shifted = gap_nodes - gap
                    value = 1.0 / np.sqrt(np.sum(shifted * shifted, -1) + SOFTENING * SOFTENING) / COEFFS
                    table[index, source, :COEFFS, target, :COEFFS] = value
    return split_table(table.reshape(len(STEPS) * 8 * SLOT, 8 * SLOT))


@functools.lru_cache(None)
def shift_table():
    table = np.zeros((8, SLOT, SLOT))
    for leaf in range(8):
        offset = [bit - 0.5 for bit in bits(leaf)]
        for k, target in enumerate(EXPONENTS):
            for i, source in enumerate(EXPONENTS):
                if all(b <= a for a, b in zip(target, source)):
                    value = 1.0
                    for a, b, h in zip(target, source, offset):
                        value *= math.comb(a, b) * 0.5**b * h ** (a - b)
                    table[leaf, i, k] = value
    return table.reshape(8 * SLOT, SLOT)


@functools.lru_cache(None)
def box_nodes():
    gaps = np.zeros((3, SLOT, SLOT))
    gaps[:, :COEFFS, :COEFFS] = np.moveaxis(CHECK[None, :, :] - EQUIV[:, None, :], -1, 0)
    gaps[1] = gaps[1] ** 2 + SOFTENING * SOFTENING
    return gaps.astype(np.float32)


def centre_table(leaf_pts):
    table = np.zeros((3, 8, leaf_pts), np.float32)
    for octant in range(8):
        for axis, bit in enumerate(bits(octant)):
            table[axis, octant] = bit + 0.5
    return table.reshape(3, 8 * leaf_pts)


def high_low(value):
    high = value.astype(jnp.bfloat16)
    low = (value - high.astype(jnp.float32)).astype(jnp.bfloat16)
    return high, low


def dot(left, right):
    return jnp.dot(left, right, preferred_element_type=jnp.float32)


def dot_nt(left, right):
    return lax.dot_general(left, right, (((1,), (1,)), ((), ())), preferred_element_type=jnp.float32)


def by_row(values, shape):
    row = lax.broadcasted_iota(jnp.int32, shape, 0)
    result = jnp.zeros(shape, jnp.float32)
    for index, value in enumerate(values):
        result = jnp.where(row == index, value, result)
    return result


def box_place():
    label = lax.axis_index("space")
    return lax.rem(label, ACROSS), lax.div(label, ACROSS)


def pack_kernel(count, positions, density, centres, shift, own, basis, slots, *rest):
    payloads, mono = rest[:-1], rest[-1]
    fields, points = density.shape
    pts = points // 8
    box_x, box_z = box_place()
    corner = by_row([2.0 * box_x.astype(jnp.float32), 0.0, 2.0 * box_z.astype(jnp.float32)], (3, 1))
    local = positions[...] - (centres[...] + corner)
    high = local.astype(jnp.bfloat16).astype(jnp.float32)
    middle = (local - high).astype(jnp.bfloat16).astype(jnp.float32)
    low = local - high - middle
    lane = lax.broadcasted_iota(jnp.int32, (fields, pts), 1)
    raw = density[...].astype(jnp.float32)
    mass = jnp.concatenate(
        [jnp.where(lane < count[leaf], raw[:, leaf * pts : (leaf + 1) * pts], 0.0) for leaf in range(8)], axis=1
    )
    spare = jnp.zeros((ROWS - fields - 9, points), jnp.float32)
    own[...] = jnp.concatenate([mass, high, middle, low, spare], axis=0).astype(jnp.bfloat16)

    scaled = 2.0 * local
    axes = [
        jnp.concatenate([scaled[a : a + 1, leaf * pts : (leaf + 1) * pts] for leaf in range(8)], axis=0)
        for a in range(3)
    ]
    made = {(0, 0, 0): jnp.ones((8, pts), jnp.float32)}
    for k, powers in enumerate(EXPONENTS):
        if powers not in made:
            a = next(i for i in range(3) if powers[i] > 0)
            before = tuple(p - (i == a) for i, p in enumerate(powers))
            made[powers] = made[before] * axes[a]
        mono[k] = made[powers]
    mono[COEFFS:SLOT] = jnp.zeros((SLOT - COEFFS, 8, pts), jnp.float32)
    moments = []
    for leaf in range(8):
        part = pl.ds(leaf * pts, pts)
        basis_high, basis_low = high_low(mono[:, leaf, :])
        basis[0:SLOT, part] = basis_high
        basis[SLOT : 2 * SLOT, part] = basis_low
        block = own[:, part]
        moments.append(dot_nt(block, basis_high) + dot_nt(block, basis_low))
    moment_high, moment_low = high_low(jnp.concatenate(moments, axis=1))
    box_moment = dot(moment_high, shift[...]) + dot(moment_low, shift[...])
    slot = jnp.concatenate([box_moment, jnp.zeros_like(box_moment)], axis=1)
    slots[...] = jnp.broadcast_to(slot[None], slots.shape)
    for (step_x, step_z), payload in zip(STEPS, payloads):
        chosen = facing_octants(step_x, step_z)
        for place, leaf in enumerate(chosen):
            payload[:, pl.ds(place * pts, pts)] = own[:, pl.ds(leaf * pts, pts)]
        base = len(chosen) * pts
        payload[:, pl.ds(base, 8 * SLOT)] = moment_high
        payload[:, pl.ds(base + 8 * SLOT, 8 * SLOT)] = moment_low


def features(piece, centre, target):
    value = piece.astype(jnp.float32)
    x = value[1:4] + value[4:7] + value[7:10] + by_row(centre, (3, 1))
    norm = jnp.sum(x * x, axis=0, keepdims=True)
    if target:
        norm = norm + SOFTENING * SOFTENING
    parts, norms = [], []
    for source, out in ((x, parts), (norm, norms)):
        left = source
        for _ in range(3):
            high = left.astype(jnp.bfloat16).astype(jnp.float32)
            out.append(high)
            left = left - high
    one = jnp.ones_like(norm)
    zero = jnp.zeros_like(norm)
    blank = jnp.zeros((3, norm.shape[1]), jnp.float32)
    blocks = []
    order = (0, 1, 0, 2, 0, 1) if target else (0, 0, 1, 0, 2, 1)
    for index, which in enumerate(order):
        coords = -2.0 * parts[which] if target else parts[which]
        if index < 3:
            pair = [one, norms[index]] if target else [norms[index], one]
        else:
            pair = [zero, zero]
        blocks += [coords, *pair, blank]
    return jnp.concatenate(blocks, axis=0)


def cell_places(pts):
    places = [None] * 32
    for octant in range(8):
        x, y, z = bits(octant)
        places[1 + x + 4 * y + 8 * (1 + z)] = (-1, octant * pts)
    for index, (step_x, step_z) in enumerate(STEPS):
        for place, octant in enumerate(facing_octants(step_x, step_z)):
            bit_x, bit_y, bit_z = bits(octant)
            x = 1 + bit_x + 2 * step_x
            z = 1 + bit_z + 2 * step_z
            places[x + 4 * bit_y + 8 * z] = (index, place * pts)
    return [
        (array, lane, (cell % 4 - 1.5, cell // 4 % 2 - 0.5, cell // 8 - 1.5))
        for cell, (array, lane) in enumerate(places)
    ]


def field_kernel(count, weights, own, basis, slots, nodes, shift, *rest):
    payloads, rest = rest[: len(STEPS)], rest[len(STEPS) :]
    far_high, far_low, potential, sums, source, masses, target, near, table_high, table_low, sems = rest
    fields, points = potential.shape
    pts = points // 8
    boxes = slots.shape[0]
    loads = [
        pltpu.make_async_copy(far_high, table_high, sems.at[0]),
        pltpu.make_async_copy(far_low, table_low, sems.at[1]),
    ]
    for load in loads:
        load.start()

    for cell, (array, lane, centre) in enumerate(cell_places(pts)):
        held = own if array < 0 else payloads[array]
        place = pl.ds(cell * pts, pts)
        piece = held[16:32, pl.ds(lane, pts)]
        masses[:, place] = held[0:ROWS, pl.ds(lane, pts)]
        source[place, :] = jnp.transpose(features(piece, centre, False)).astype(jnp.bfloat16)
        if array < 0:
            leaf = lane // pts
            target[:, pl.ds(leaf_slot(leaf) * pts, pts)] = features(piece, centre, True).astype(jnp.bfloat16)

    wide = 2 * pts
    for group in range(4):
        first = group % 2 + 8 * (group // 2)
        points_in = target[:, group * wide : (group + 1) * wide]

        def layer(index, total, first=first, points_in=points_in):
            for step_y in range(2):
                start = pl.multiple_of((first + 4 * step_y + 8 * index) * pts, pts)
                for step_x in range(3):
                    place = pl.ds(start + step_x * pts, pts)
                    kernel = lax.rsqrt(dot(source[place, :], points_in))
                    kernel_high, kernel_low = high_low(kernel)
                    mass = masses[:, place]
                    total = total + dot(mass, kernel_high) + dot(mass, kernel_low)
            return total

        near[:, group * wide : (group + 1) * wide] = lax.fori_loop(
            0, 3, layer, jnp.zeros((ROWS, wide), jnp.float32)
        )

    box_x, box_z = box_place()
    lefts, rights = [], []
    for box in range(0, boxes, 2):
        lefts.append(jnp.concatenate([slots[box][:, :SLOT], slots[box + 1][:, :SLOT]], axis=1))
    for box in range(boxes):
        gap_x = 2 * (box_x - box % ACROSS)
        gap_z = 2 * (box_z - box // ACROSS)
        across_x = nodes[0] + gap_x.astype(jnp.float32)
        across_z = nodes[2] + gap_z.astype(jnp.float32)
        value = lax.rsqrt(across_x * across_x + across_z * across_z + nodes[1])
        far = jnp.maximum(jnp.abs(gap_x), jnp.abs(gap_z)) >= 4
        rights.append(value * jnp.where(far, 1.0 / COEFFS, 0.0))
    left_high, left_low = high_low(jnp.concatenate(lefts, axis=1))
    right_high, right_low = high_low(jnp.concatenate(rights, axis=0))
    box_local = dot(left_high, right_high) + dot(left_high, right_low) + dot(left_low, right_high)
    box_high, box_low = high_low(box_local)
    local = dot(box_high, shift[...]) + dot(box_low, shift[...])

    highs, lows = [], []
    for (step_x, step_z), payload in zip(STEPS, payloads):
        base = len(facing_octants(step_x, step_z)) * pts
        highs.append(payload[:, pl.ds(base, 8 * SLOT)])
        lows.append(payload[:, pl.ds(base + 8 * SLOT, 8 * SLOT)])
    for load in loads:
        load.wait()
    for index in range(len(STEPS)):
        rows = pl.ds(index * 8 * SLOT, 8 * SLOT)
        local = local + dot(highs[index], table_high[rows, :]) + dot(lows[index], table_high[rows, :])
        local = local + dot(highs[index], table_low[rows, :])
    local_high, local_low = high_low(local)

    weight_column = by_row([weights[field] for field in range(fields)], (fields, 1))
    lane_index = lax.broadcasted_iota(jnp.int32, (fields, pts), 1)
    coupling = 1.0 / (128.0 * pts)
    for leaf in range(8):
        part = pl.ds(leaf * pts, pts)
        here = slice(leaf * SLOT, (leaf + 1) * SLOT)
        left = jnp.concatenate([local_high[:, here], local_high[:, here]], axis=1)
        far_part = dot(left, basis[:, part]) + dot(local_low[:, here], basis[0:SLOT, part])
        total = (near[:, pl.ds(leaf_slot(leaf) * pts, pts)] + far_part)[:fields]
        total = jnp.where(lane_index < count[leaf], total * coupling, 0.0)
        potential[:, part] = total
        sums[:, part] = jnp.sum(total * weight_column, axis=0, keepdims=True)
    sums[:, points:] = jnp.broadcast_to(jnp.sum(weight_column), (1, sums.shape[1] - points))


def sent_on(block, step_x, step_z):
    boxes = lax.axis_size("space")
    route = []
    for box in range(boxes):
        x, z = box % ACROSS + step_x, box // ACROSS + step_z
        if 0 <= x < ACROSS and 0 <= z < boxes // ACROSS:
            route.append((x + ACROSS * z, box))
    return lax.ppermute(block, "space", route)


def per_device(positions, density, leaf_count, sigma_weights):
    fields, points = density.shape
    pts = points // 8
    boxes = lax.axis_size("space")
    vmem, smem = pl.BlockSpec(memory_space=pltpu.VMEM), pl.BlockSpec(memory_space=pltpu.SMEM)
    anywhere = pl.BlockSpec(memory_space=pl.ANY)
    limit = pltpu.CompilerParams(vmem_limit_bytes=48 * 1024 * 1024)
    shift = shift_table()
    payload_shapes = [
        jax.ShapeDtypeStruct((ROWS, len(facing_octants(*step)) * pts + 16 * SLOT), jnp.bfloat16) for step in STEPS
    ]
    own, basis, slots, *payloads = pl.pallas_call(
        pack_kernel,
        in_specs=[smem, vmem, vmem, vmem, vmem],
        out_specs=[vmem] * (3 + len(STEPS)),
        out_shape=[
            jax.ShapeDtypeStruct((ROWS, points), jnp.bfloat16),
            jax.ShapeDtypeStruct((2 * SLOT, points), jnp.bfloat16),
            jax.ShapeDtypeStruct((boxes, ROWS, 2 * SLOT), jnp.float32),
            *payload_shapes,
        ],
        scratch_shapes=[pltpu.VMEM((SLOT, 8, pts), jnp.float32)],
        compiler_params=limit,
        name="pack",
    )(leaf_count, positions, density, jnp.asarray(centre_table(pts)), jnp.asarray(shift, jnp.bfloat16))
    all_slots = lax.all_to_all(slots, "space", 0, 0, tiled=True)
    received = [sent_on(payload, *step) for step, payload in zip(STEPS, payloads)]
    far_high, far_low = far_table()
    potential, sums = pl.pallas_call(
        field_kernel,
        in_specs=[smem, smem] + [vmem] * (5 + len(STEPS)) + [anywhere, anywhere],
        out_specs=[vmem, vmem],
        out_shape=[
            jax.ShapeDtypeStruct((fields, points), jnp.float32),
            jax.ShapeDtypeStruct((1, points + 128), jnp.float32),
        ],
        scratch_shapes=[
            pltpu.VMEM((32 * pts, FEATURES), jnp.bfloat16),
            pltpu.VMEM((ROWS, 32 * pts), jnp.bfloat16),
            pltpu.VMEM((FEATURES, points), jnp.bfloat16),
            pltpu.VMEM((ROWS, points), jnp.float32),
            pltpu.VMEM(far_high.shape, jnp.bfloat16),
            pltpu.VMEM(far_low.shape, jnp.bfloat16),
            pltpu.SemaphoreType.DMA((2,)),
        ],
        compiler_params=limit,
        name="field",
    )(
        leaf_count,
        sigma_weights,
        own,
        basis,
        all_slots,
        jnp.asarray(box_nodes()),
        jnp.asarray(shift.T.copy(), jnp.bfloat16),
        *received,
        jnp.asarray(far_high),
        jnp.asarray(far_low),
    )
    sums = lax.psum(sums, "sig")
    return potential, sums[0, :points] / sums[0, points]


def solution(mesh):
    in_specs = (P(None, "space"), P("sig", "space"), P("space"), P("sig"))
    out_specs = (P("sig", "space"), P("space"))
    return jax.shard_map(per_device, mesh=mesh, in_specs=in_specs, out_specs=out_specs, check_vma=False)
```

time: 269 us -> 82.8 us (0.31)
  the two profiles are of different devices: /device:TPU:25 before, /device:TPU:0 now
where the time goes in v1:
time: 82.8 us; the launch traced here: 81.9 us
  starting transfers between devices  31.3 us (38%)
  Pallas kernels  28.3 us (34%)
  local copies, waits for them, and re-layouts  9.78 us (12%)
  waiting for transfers between devices  7.94 us (10%)
  blocking collectives  2.52 us (3%)
  other arithmetic  1.3 us (2%)
    pallas_call x1, Pallas kernels, per_device(): pl.pallas_call(field_kernel, in_specs=[smem, smem] + [vmem] * (5 + len(ST...  25 us
    ppermute x8, starting transfers between devices, sent_on(): return lax.ppermute(block, 'space', route)  23 us
    unnamed x20, local copies, waits for them, and re-layouts  9.19 us
    all_to_all x1, starting transfers between devices, per_device(): all_slots = lax.all_to_all(slots, 'space', 0, 0, tiled=True)  8.31 us
    ppermute x8, waiting for transfers between devices, sent_on(): return lax.ppermute(block, 'space', route)  7.94 us
    pallas_call x1, Pallas kernels, per_device(): pl.pallas_call(pack_kernel, in_specs=[smem, vmem, vmem, vmem, vmem], out_...  3.26 us
    psum x1, blocking collectives, per_device(): sums = lax.psum(sums, 'sig')  2.52 us
  transfers between devices with their start and end apart: 9, of which 1 were waited for; matrix products, arithmetic and copies ran while one was open for 0% of the time, Pallas kernels for 0%

profile of v1, /device:TPU:0, one launch (start us, length us, event | category | flops | bytes accessed | tf_op | source)
XLA Modules:
  0.0 81.9 jit_solution(5061015920330481456)
XLA Ops:
  0.6 0.9 %copy-done.1 = bf16[512,64]{1,0:T(8,128)(2,1)S(1)} copy-done((bf16[512,64]{1,0:T(8,128)(2,1)S(1)}, bf16[512,64]{1,0:T(8,128)(2,1)}, u32[]{:S(2)}) %copy-start.1) | copy-done | bytes 65560
  1.5 0.9 %copy-done.3 = bf16[17,2048]{1,0:T(8,128)(2,1)S(1)} copy-done((bf16[17,2048]{1,0:T(8,128)(2,1)S(1)}, bf16[17,2048]{1,0:T(8,128)(2,1)}, u32[]{:S(2)}) %copy-start.3) | copy-done | bytes 69656
  2.4 0.8 copy-done.5
  3.2 0.8 copy-done.6
  3.9 0.7 copy-done.7
  4.6 3.3 %pack.1 = (bf16[32,2048]{1,0:T(8,128)(2,1)S(1)}, bf16[128,2048]{1,0:T(8,128)(2,1)S(1)}, f32[16,32,128]{2,1,0:T(8,128)}, bf16[32,1536]{1,0:T(8,128)(2,1)S(1)}, bf...) custom-call(s32[8]{0:T(128)S(1)} %copy-done.7, ...), custom_call_target="tpu_custom_call" | custom-call | tf_op jit(solution)/shard_map/pack/pallas_call | solution.py:351
  7.9 8.3 %all-to-all-start = ((f32[16,32,128]{2,1,0:T(8,128)}), f32[16,32,128]{2,1,0:T(8,128)S(1)}, u32[]{:S(2)}, u32[]{:S(2)}) async-start(f32[16,32,128]{2,1,0:T(8,128)} %get-tuple-element.17), calls=%async_computation | async-start | bytes 524288 | tf_op jit(solution)/shard_map/all_to_all | solution.py:365
  16.2 4.7 %collective-permute-start = (bf16[32,1536]{1,0:T(8,128)(2,1)S(1)}, bf16[32,1536]{1,0:T(8,128)(2,1)S(1)}, u32[]{:S(2)}, u32[]{:S(2)}) collective-permute-start(bf16[32,1536]{1,0:T(8,128)(2,1)S(1)} %get-tuple-element.18), channel_id=1, source_target_pairs={{0,10},{2,12},{4,14},{8,18},{10,20},{12,22},{16,26},{18,28},{20,30... | collective-permute-start | bytes 294920 | tf_op jit(solution)/shard_map/ppermute | solution.py:337
  20.9 0.7 collective-permute-start.2
  21.6 0.7 collective-permute-start.5
  22.3 8.8 %collective-permute-start.1 = (bf16[32,2048]{1,0:T(8,128)(2,1)S(1)}, bf16[32,2048]{1,0:T(8,128)(2,1)S(1)}, u32[]{:S(2)}, u32[]{:S(2)}) collective-permute-start(bf16[32,2048]{1,0:T(8,128)(2,1)S(1)} %get-tuple-element.19), channel_id=1, source_target_pairs={{0,8},{2,10},{4,12},{6,14},{8,16},{10,18},{12,20},{14,22},{16,24},... | collective-permute-start | bytes 393224 | tf_op jit(solution)/shard_map/ppermute | solution.py:337
  31.1 4.3 %collective-permute-start.3 = (bf16[32,2048]{1,0:T(8,128)(2,1)S(1)}, bf16[32,2048]{1,0:T(8,128)(2,1)S(1)}, u32[]{:S(2)}, u32[]{:S(2)}) collective-permute-start(bf16[32,2048]{1,0:T(8,128)(2,1)S(1)} %get-tuple-element.21), channel_id=1, source_target_pairs={{0,2},{2,4},{4,6},{8,10},{10,12},{12,14},{16,18},{18,20},{20,22},{... | collective-permute-start | bytes 393224 | tf_op jit(solution)/shard_map/ppermute | solution.py:337
  35.3 1.3 %collective-permute-start.4 = (bf16[32,2048]{1,0:T(8,128)(2,1)S(1)}, bf16[32,2048]{1,0:T(8,128)(2,1)S(1)}, u32[]{:S(2)}, u32[]{:S(2)}) collective-permute-start(bf16[32,2048]{1,0:T(8,128)(2,1)S(1)} %get-tuple-element.22), channel_id=1, source_target_pairs={{2,0},{4,2},{6,4},{10,8},{12,10},{14,12},{18,16},{20,18},{22,20},{... | collective-permute-start | bytes 393224 | tf_op jit(solution)/shard_map/ppermute | solution.py:337
  36.7 1.3 %collective-permute-start.6 = (bf16[32,2048]{1,0:T(8,128)(2,1)S(1)}, bf16[32,2048]{1,0:T(8,128)(2,1)S(1)}, u32[]{:S(2)}, u32[]{:S(2)}) collective-permute-start(bf16[32,2048]{1,0:T(8,128)(2,1)S(1)} %get-tuple-element.24), channel_id=1, source_target_pairs={{8,0},{10,2},{12,4},{14,6},{16,8},{18,10},{20,12},{22,14},{24,16},... | collective-permute-start | bytes 393224 | tf_op jit(solution)/shard_map/ppermute | solution.py:337
  38.0 1.3 %collective-permute-start.7 = (bf16[32,1536]{1,0:T(8,128)(2,1)S(1)}, bf16[32,1536]{1,0:T(8,128)(2,1)S(1)}, u32[]{:S(2)}, u32[]{:S(2)}) collective-permute-start(bf16[32,1536]{1,0:T(8,128)(2,1)S(1)} %get-tuple-element.25), channel_id=1, source_target_pairs={{10,0},{12,2},{14,4},{18,8},{20,10},{22,12},{26,16},{28,18},{30,20... | collective-permute-start | bytes 294920 | tf_op jit(solution)/shard_map/ppermute | solution.py:337
  39.3 7.9 %collective-permute-done.7.rest_7_ = bf16[32,1536]{1,0:T(8,128)(2,1)S(1)} collective-permute-done((bf16[32,1536]{1,0:T(8,128)(2,1)S(1)}, bf16[32,1536]{1,0:T(8,128)(2,1)S(1)}, u32[]{:S(2)}, u32[]{:S(2)}) %collective-permute-start.7) | collective-permute-done | bytes 98336 | tf_op jit(solution)/shard_map/ppermute | solution.py:337
  47.2 2.2 %copy-done = bf16[4096,512]{1,0:T(8,128)(2,1)S(1)} copy-done((bf16[4096,512]{1,0:T(8,128)(2,1)S(1)}, bf16[4096,512]{1,0:T(8,128)(2,1)}, u32[]{:S(2)}) %copy-start) | copy-done | bytes 4194328
  49.4 0.9 %copy-done.2 = f32[3,64,64]{2,1,0:T(8,128)S(1)} copy-done((f32[3,64,64]{2,1,0:T(8,128)S(1)}, f32[3,64,64]{2,1,0:T(8,128)}, u32[]{:S(2)}) %copy-start.2) | copy-done | bytes 49176
  50.3 0.8 %copy-done.4 = bf16[64,512]{1,0:T(8,128)(2,1)S(1)} copy-done((bf16[64,512]{1,0:T(8,128)(2,1)S(1)}, bf16[64,512]{1,0:T(8,128)(2,1)}, u32[]{:S(2)}) %copy-start.4) | copy-done | bytes 65560
  51.1 0.7 copy-done.8
  51.8 0.7 copy-done.9
  52.5 25.0 %field.1 = (f32[17,2048]{1,0:T(8,128)}, f32[1,2176]{1,0:T(1,128)S(1)}) custom-call(s32[8]{0:T(128)S(1)} %copy-done.8, f32[17]{0:T(128)S(1)} %copy-done.9, bf16[32,2048]{1,0:T(8,128)(2,1)S(1)} %get-tuple-element.15.own, bf16[128,2048]{1,0:T(8,128)(2,1)S(1)} %get-tuple-element.16.basis, f32[16,32,128]{2,1,0:T(8,128)S(1)} %all-to-all-done.slots, ...), custom_call_target="tpu_custom_call" | custom-call | tf_op jit(solution)/shard_map/field/pallas_call | solution.py:368
  77.5 2.5 %psum.7 = f32[1,2176]{1,0:T(1,128)S(1)} all-reduce(f32[1,2176]{1,0:T(1,128)S(1)} %get-tuple-element.27), channel_id=1, replica_groups=mesh['space'=16,'sig'=2] {'sig'}, use_global_device_ids=true, to_apply=%region_0.0 | all-reduce | flops 2176 | bytes 17408 | tf_op jit(solution)/shard_map/psum | solution.py:399
  80.6 1.3 %slice_divide_fusion = f32[1,2048]{1,0:T(1,128)} fusion(f32[1,2176]{1,0:T(1,128)S(1)} %psum.7, f32[]{:T(128)} %bitcast), kind=kLoop, calls=%fused_computation | loop fusion | flops 2048 | bytes 16388 | tf_op jit(solution)/shard_map/div | solution.py:400
  (19 shorter events, 0.6 us)
Async XLA Ops:
  0.6 0.9 %copy-start.1 = (bf16[512,64]{1,0:T(8,128)(2,1)S(1)}, bf16[512,64]{1,0:T(8,128)(2,1)}, u32[]{:S(2)}) copy-start(bf16[512,64]{1,0:T(8,128)(2,1)} %constant.13.clone.shift) | copy-start | bytes 196612
  1.5 0.9 %copy-start.3 = (bf16[17,2048]{1,0:T(8,128)(2,1)S(1)}, bf16[17,2048]{1,0:T(8,128)(2,1)}, u32[]{:S(2)}) copy-start(bf16[17,2048]{1,0:T(8,128)(2,1)} %density.1) | copy-start | bytes 208900
  2.4 0.8 copy-start.5
  3.2 0.8 copy-start.6
  3.9 0.7 copy-start.7
  7.9 39.4 %all-to-all-start = ((f32[16,32,128]{2,1,0:T(8,128)}), f32[16,32,128]{2,1,0:T(8,128)S(1)}, u32[]{:S(2)}, u32[]{:S(2)}) async-start(f32[16,32,128]{2,1,0:T(8,128)} %get-tuple-element.17), calls=%async_computation | async-start | bytes 524288 | tf_op jit(solution)/shard_map/all_to_all | solution.py:365
  16.2 19.2 %collective-permute-start = (bf16[32,1536]{1,0:T(8,128)(2,1)S(1)}, bf16[32,1536]{1,0:T(8,128)(2,1)S(1)}, u32[]{:S(2)}, u32[]{:S(2)}) collective-permute-start(bf16[32,1536]{1,0:T(8,128)(2,1)S(1)} %get-tuple-element.18), channel_id=1, source_target_pairs={{0,10},{2,12},{4,14},{8,18},{10,20},{12,22},{16,26},{18,28},{20,30... | collective-permute-start | bytes 294920 | tf_op jit(solution)/shard_map/ppermute | solution.py:337
  20.9 15.7 %collective-permute-start.2 = (bf16[32,1536]{1,0:T(8,128)(2,1)S(1)}, bf16[32,1536]{1,0:T(8,128)(2,1)S(1)}, u32[]{:S(2)}, u32[]{:S(2)}) collective-permute-start(bf16[32,1536]{1,0:T(8,128)(2,1)S(1)} %get-tuple-element.20), channel_id=1, source_target_pairs={{2,8},{4,10},{6,12},{10,16},{12,18},{14,20},{18,24},{20,26},{22,28... | collective-permute-start | bytes 294920 | tf_op jit(solution)/shard_map/ppermute | solution.py:337
  21.6 16.4 %collective-permute-start.5 = (bf16[32,1536]{1,0:T(8,128)(2,1)S(1)}, bf16[32,1536]{1,0:T(8,128)(2,1)S(1)}, u32[]{:S(2)}, u32[]{:S(2)}) collective-permute-start(bf16[32,1536]{1,0:T(8,128)(2,1)S(1)} %get-tuple-element.23), channel_id=1, source_target_pairs={{8,2},{10,4},{12,6},{16,10},{18,12},{20,14},{24,18},{26,20},{28,22... | collective-permute-start | bytes 294920 | tf_op jit(solution)/shard_map/ppermute | solution.py:337
  22.3 24.9 %collective-permute-start.1 = (bf16[32,2048]{1,0:T(8,128)(2,1)S(1)}, bf16[32,2048]{1,0:T(8,128)(2,1)S(1)}, u32[]{:S(2)}, u32[]{:S(2)}) collective-permute-start(bf16[32,2048]{1,0:T(8,128)(2,1)S(1)} %get-tuple-element.19), channel_id=1, source_target_pairs={{0,8},{2,10},{4,12},{6,14},{8,16},{10,18},{12,20},{14,22},{16,24},... | collective-permute-start | bytes 393224 | tf_op jit(solution)/shard_map/ppermute | solution.py:337
  31.1 16.1 %collective-permute-start.3 = (bf16[32,2048]{1,0:T(8,128)(2,1)S(1)}, bf16[32,2048]{1,0:T(8,128)(2,1)S(1)}, u32[]{:S(2)}, u32[]{:S(2)}) collective-permute-start(bf16[32,2048]{1,0:T(8,128)(2,1)S(1)} %get-tuple-element.21), channel_id=1, source_target_pairs={{0,2},{2,4},{4,6},{8,10},{10,12},{12,14},{16,18},{18,20},{20,22},{... | collective-permute-start | bytes 393224 | tf_op jit(solution)/shard_map/ppermute | solution.py:337
  35.3 11.8 %collective-permute-start.4 = (bf16[32,2048]{1,0:T(8,128)(2,1)S(1)}, bf16[32,2048]{1,0:T(8,128)(2,1)S(1)}, u32[]{:S(2)}, u32[]{:S(2)}) collective-permute-start(bf16[32,2048]{1,0:T(8,128)(2,1)S(1)} %get-tuple-element.22), channel_id=1, source_target_pairs={{2,0},{4,2},{6,4},{10,8},{12,10},{14,12},{18,16},{20,18},{22,20},{... | collective-permute-start | bytes 393224 | tf_op jit(solution)/shard_map/ppermute | solution.py:337
  36.7 10.5 %collective-permute-start.6 = (bf16[32,2048]{1,0:T(8,128)(2,1)S(1)}, bf16[32,2048]{1,0:T(8,128)(2,1)S(1)}, u32[]{:S(2)}, u32[]{:S(2)}) collective-permute-start(bf16[32,2048]{1,0:T(8,128)(2,1)S(1)} %get-tuple-element.24), channel_id=1, source_target_pairs={{8,0},{10,2},{12,4},{14,6},{16,8},{18,10},{20,12},{22,14},{24,16},... | collective-permute-start | bytes 393224 | tf_op jit(solution)/shard_map/ppermute | solution.py:337
  38.0 9.2 %collective-permute-start.7 = (bf16[32,1536]{1,0:T(8,128)(2,1)S(1)}, bf16[32,1536]{1,0:T(8,128)(2,1)S(1)}, u32[]{:S(2)}, u32[]{:S(2)}) collective-permute-start(bf16[32,1536]{1,0:T(8,128)(2,1)S(1)} %get-tuple-element.25), channel_id=1, source_target_pairs={{10,0},{12,2},{14,4},{18,8},{20,10},{22,12},{26,16},{28,18},{30,20... | collective-permute-start | bytes 294920 | tf_op jit(solution)/shard_map/ppermute | solution.py:337
  47.2 2.2 %copy-start = (bf16[4096,512]{1,0:T(8,128)(2,1)S(1)}, bf16[4096,512]{1,0:T(8,128)(2,1)}, u32[]{:S(2)}) copy-start(bf16[4096,512]{1,0:T(8,128)(2,1)} %constant.16.clone.rest_8_) | copy-start | bytes 12582916
  49.4 0.9 %copy-start.2 = (f32[3,64,64]{2,1,0:T(8,128)S(1)}, f32[3,64,64]{2,1,0:T(8,128)}, u32[]{:S(2)}) copy-start(f32[3,64,64]{2,1,0:T(8,128)} %constant.14.clone.nodes) | copy-start | bytes 147460
  50.3 0.8 %copy-start.4 = (bf16[64,512]{1,0:T(8,128)(2,1)S(1)}, bf16[64,512]{1,0:T(8,128)(2,1)}, u32[]{:S(2)}) copy-start(bf16[64,512]{1,0:T(8,128)(2,1)} %constant.15.clone.shift) | copy-start | bytes 196612
  51.1 0.7 copy-start.8
  51.8 0.7 copy-start.9

commit v2 on v1

v2 whole, which is shorter than its diff:
```python
import functools
import math

import jax
import jax.numpy as jnp
import numpy as np
from jax import lax
from jax.experimental import pallas as pl
from jax.experimental.pallas import tpu as pltpu
from jax.sharding import PartitionSpec as P

ORDER = 5
SOFTENING = 0.1
ACROSS = 4
SLOT = 64
ROWS = 32
LEAVES = 8 * SLOT
MEGA = 1024 * 1024
FEATURES = 48


def exponent_table(order_max):
    entries_list = []
    for degree in range(order_max + 1):
        for first_power in range(degree, -1, -1):
            for second_power in range(degree - first_power, -1, -1):
                entries_list.append((first_power, second_power, degree - first_power - second_power))
    return entries_list


def node_table(count_nodes, offset_value):
    counter = np.arange(1, count_nodes + 1, dtype=np.float32)[:, None]
    stride_set = np.array([0.7548776662466927, 0.5698402909980532, 0.4142135623730951], dtype=np.float32)[None, :]
    unit_points = np.mod(counter * stride_set + np.float32(offset_value), np.float32(1.0))
    return (np.float32(2.0) * unit_points - np.float32(1.0)).astype(np.float32)


EXPONENTS = exponent_table(ORDER)
COEFFS = len(EXPONENTS)
CHECK = node_table(COEFFS, 0.5).astype(np.float64)
EQUIV = node_table(COEFFS, 0.0).astype(np.float64)
STEPS = [(sx, sz) for sz in (-1, 0, 1) for sx in (-1, 0, 1) if sx != 0 or sz != 0]


def bits(octant):
    return octant % 2, octant // 2 % 2, octant // 4


def touching(distance):
    return distance & (distance + 1) == 0


def leaf_slot(octant):
    bit_x, bit_y, bit_z = bits(octant)
    return (bit_x + 2 * bit_z) * 2 + bit_y


@functools.lru_cache(None)
def far_table():
    shape = (len(STEPS), 8, SLOT, 8, SLOT)
    table = np.zeros(shape)
    gap_nodes = 0.5 * (CHECK[None, :, :] - EQUIV[:, None, :])
    for index, (step_x, step_z) in enumerate(STEPS):
        for source in range(8):
            for target in range(8):
                s, t = bits(source), bits(target)
                gap = np.array([2 * step_x + s[0] - t[0], s[1] - t[1], 2 * step_z + s[2] - t[2]], np.float64)
                if max(abs(gap[0]), abs(gap[2])) >= 2:
                    shifted = gap_nodes - gap
                    value = 1.0 / np.sqrt(np.sum(shifted * shifted, -1) + SOFTENING * SOFTENING) / COEFFS
                    table[index, source, :COEFFS, target, :COEFFS] = value
    return table.reshape(len(STEPS) * LEAVES, LEAVES)


@functools.lru_cache(None)
def shift_table():
    table = np.zeros((8, SLOT, SLOT))
    for leaf in range(8):
        offset = [bit - 0.5 for bit in bits(leaf)]
        for k, target in enumerate(EXPONENTS):
            for i, source in enumerate(EXPONENTS):
                if all(b <= a for a, b in zip(target, source)):
                    value = 1.0
                    for a, b, h in zip(target, source, offset):
                        value *= math.comb(a, b) * 0.5**b * h ** (a - b)
                    table[leaf, i, k] = value
    return table.reshape(8 * SLOT, SLOT)


@functools.lru_cache(None)
def box_nodes():
    gaps = np.zeros((3, SLOT, SLOT))
    gaps[:, :COEFFS, :COEFFS] = np.moveaxis(CHECK[None, :, :] - EQUIV[:, None, :], -1, 0)
    gaps[1] = gaps[1] ** 2 + SOFTENING * SOFTENING
    return gaps.astype(np.float32)


def dot(left, right):
    return jnp.dot(left, right, preferred_element_type=jnp.float32)


def dot_nt(left, right):
    return lax.dot_general(left, right, (((1,), (1,)), ((), ())), preferred_element_type=jnp.float32)


def low_bits(value):
    return value.astype(jnp.bfloat16)


def high_low(value):
    high = low_bits(value)
    return high, low_bits(value - high.astype(jnp.float32))


def by_row(values, shape):
    row = lax.broadcasted_iota(jnp.int32, shape, 0)
    result = jnp.zeros(shape, jnp.float32)
    for index, value in enumerate(values):
        result = jnp.where(row == index, value, result)
    return result


def box_place():
    label = lax.axis_index("space")
    return lax.rem(label, ACROSS), lax.div(label, ACROSS)


def lanes(start, size):
    return pl.ds(start if isinstance(start, int) else pl.multiple_of(start, 128), size)


def fetch(pairs, sems):
    copies = [pltpu.make_async_copy(src, dst, sems.at[i]) for i, (src, dst) in enumerate(pairs)]
    for copy in copies:
        copy.start()
    return copies


def pack_kernel(count_in, positions_in, density_in, shift_in, own, basis, moments, totals, *rest):
    payloads, (count, positions, density, shift, mono, sems) = rest[:3], rest[3:]
    copies = fetch(
        [(count_in, count), (positions_in, positions), (density_in, density), (shift_in, shift)], sems
    )
    fields, points = density.shape
    pts = points // 8
    box_x, box_z = box_place()
    for copy in copies:
        copy.wait()
    local = []
    for leaf in range(8):
        bit_x, bit_y, bit_z = bits(leaf)
        centre = by_row(
            [2.0 * box_x.astype(jnp.float32) + (bit_x + 0.5), bit_y + 0.5, 2.0 * box_z.astype(jnp.float32) + (bit_z + 0.5)],
            (3, 1),
        )
        here = slice(leaf * pts, (leaf + 1) * pts)
        offset = positions[:, here] - centre
        local.append(offset)
        high = low_bits(offset).astype(jnp.float32)
        middle = low_bits(offset - high).astype(jnp.float32)
        low = offset - high - middle
        raw = density[:, here].astype(jnp.float32)
        mass = jnp.where(lax.broadcasted_iota(jnp.int32, raw.shape, 1) < count[leaf], raw, 0.0)
        spare = jnp.zeros((ROWS - fields - 9, pts), jnp.float32)
        own[:, here] = low_bits(jnp.concatenate([mass, high, middle, low, spare], axis=0))

    axes = [2.0 * jnp.concatenate([part[a : a + 1] for part in local], axis=0) for a in range(3)]
    made = {(0, 0, 0): jnp.ones((8, pts), jnp.float32)}
    for k, powers in enumerate(EXPONENTS):
        if powers not in made:
            a = next(i for i in range(3) if powers[i] > 0)
            before = tuple(p - (i == a) for i, p in enumerate(powers))
            made[powers] = made[before] * axes[a]
        mono[k] = made[powers]
    mono[COEFFS:SLOT] = jnp.zeros((SLOT - COEFFS, 8, pts), jnp.float32)
    parts = []
    for leaf in range(8):
        here = slice(leaf * pts, (leaf + 1) * pts)
        high, low = high_low(mono[:, leaf, :])
        basis[0:SLOT, here] = high
        basis[SLOT:, here] = low
        parts.append(dot_nt(own[:, here], high))
    moment, rest = high_low(jnp.concatenate(parts, axis=1))
    moments[...] = moment
    total = dot(moment, shift[...]) + dot(rest, shift[...])
    total = jnp.concatenate(high_low(total), axis=1)
    totals[...] = total
    payloads[1][...] = total
    for distance, payload in ((1, payloads[0]), (3, payloads[2])):
        bit = jnp.where((box_x ^ distance) > box_x, 1, 0)
        for place in range(4):
            payload[:, lanes(place * pts, pts)] = own[:, lanes((bit + 2 * place) * pts, pts)]
        payload[:, lanes(4 * pts, LEAVES)] = moment
        payload[:, lanes(4 * pts + LEAVES, 2 * SLOT)] = total


def features(held, start, size, centre, target):
    value = held[16:32, lanes(start, size)].astype(jnp.float32)
    x = value[1:4] + value[4:7] + value[7:10] + by_row(centre, (3, 1))
    norm = jnp.sum(x * x, axis=0, keepdims=True)
    if target:
        norm = norm + SOFTENING * SOFTENING
    parts, norms = [], []
    for source, out in ((x, parts), (norm, norms)):
        left = source
        for _ in range(3):
            high = low_bits(left).astype(jnp.float32)
            out.append(high)
            left = left - high
    one = jnp.ones_like(norm)
    zero = jnp.zeros_like(norm)
    blank = jnp.zeros((3, norm.shape[1]), jnp.float32)
    blocks = []
    order = (0, 1, 0, 2, 0, 1) if target else (0, 0, 1, 0, 2, 1)
    for index, which in enumerate(order):
        coords = -2.0 * parts[which] if target else parts[which]
        if index < 3:
            pair = [one, norms[index]] if target else [norms[index], one]
        else:
            pair = [zero, zero]
        blocks += [coords, *pair, blank]
    return jnp.concatenate(blocks, axis=0)


def source_features(held, start, size, centre):
    return low_bits(jnp.transpose(features(held, start, size, centre, False)))


def pulled(total, wanted, source, masses, starts, pts):
    for start in starts:
        place = lanes(start, pts)
        kernel = lax.rsqrt(dot(source[place, :], wanted))
        high = low_bits(kernel)
        low = low_bits(kernel - high.astype(jnp.float32))
        mass = masses[:, place]
        total = total + dot(mass, high) + dot(mass, low)
    return total


def own_kernel(own, far_in, nodes_in, spread_in, near, source, target, far, nodes, spread, sems):
    copies = fetch([(far_in, far), (nodes_in, nodes), (spread_in, spread)], sems)
    points = own.shape[1]
    pts = points // 8
    for leaf in range(8):
        centre = [bit - 0.5 for bit in bits(leaf)]
        source[lanes(leaf * pts, pts), :] = source_features(own, leaf * pts, pts, centre)
        target[:, lanes(leaf_slot(leaf) * pts, pts)] = low_bits(features(own, leaf * pts, pts, centre, True))

    def group(index, carry):
        here = lanes(index * (2 * pts), 2 * pts)
        zero = jnp.zeros((ROWS, 2 * pts), jnp.float32)
        near[:, here] = pulled(zero, target[:, here], source, own, [leaf * pts for leaf in range(8)], pts)
        return carry

    lax.fori_loop(0, 2, group, 0)
    for copy in copies:
        copy.wait()


def row_kernel(depth, own, moments, totals, from_1, from_2, from_3, far, nodes, spread, *rest):
    left, right, own_local, *payloads = rest
    points = own.shape[1]
    pts = points // 8
    box_x, box_z = box_place()
    wide = 4 * pts + LEAVES
    for side, step in ((left, -1), (right, 1)):
        side[...] = jnp.zeros(side.shape, side.dtype)
        for distance, held in ((1, from_1), (3, from_3)):

            @pl.when((box_x ^ distance) - box_x == step)
            def _(side=side, held=held):
                side[...] = held[:, lanes(0, wide)]

    base = 4 * pts
    row = jnp.concatenate([left[:, lanes(base, LEAVES)], moments[...], right[:, lanes(base, LEAVES)]], axis=1)
    below_rows, same_rows, above_rows = pl.ds(0, 3 * LEAVES), pl.ds(3 * LEAVES, 2 * LEAVES), pl.ds(5 * LEAVES, 3 * LEAVES)
    up = dot(row, far[below_rows, :])
    down = dot(row, far[above_rows, :])
    same = dot(jnp.concatenate([row[:, :LEAVES], row[:, 2 * LEAVES :]], axis=1), far[same_rows, :])

    boxes = [totals[...], from_1[:, lanes(wide, 2 * SLOT)], from_2[...], from_3[:, lanes(wide, 2 * SLOT)]]
    boxes_high = jnp.concatenate([held[:, :SLOT] for held in boxes], axis=1)
    boxes_low = jnp.concatenate([held[:, SLOT:] for held in boxes], axis=1)
    columns = []
    for distance_z in range(depth):
        gap_z = 2 * ((box_z ^ distance_z) - box_z)
        across_z = nodes[2] + gap_z.astype(jnp.float32)
        rest_z = across_z * across_z + nodes[1]
        blocks = []
        for distance_x in range(ACROSS):
            gap_x = 2 * (box_x - (box_x ^ distance_x))
            across_x = nodes[0] + gap_x.astype(jnp.float32)
            distant = jnp.maximum(jnp.abs(gap_x), jnp.abs(gap_z)) >= 4
            blocks.append(lax.rsqrt(across_x * across_x + rest_z) * jnp.where(distant, 1.0 / COEFFS, 0.0))
        columns.append(jnp.concatenate(blocks, axis=0))
    columns = low_bits(jnp.concatenate(columns, axis=1))
    coarse = dot(boxes_high, columns) + dot(boxes_low, columns)
    coarse = jnp.concatenate([coarse[:, d * SLOT : (d + 1) * SLOT] for d in range(depth)], axis=0)
    coarse_high, coarse_low = high_low(coarse)
    coarse = dot(coarse_high, spread[...]) + dot(coarse_low, spread[...])

    own_local[...] = same + coarse[:ROWS]
    for distance in range(1, depth):
        payload = payloads[distance - 1]
        gap = (box_z ^ distance) - box_z
        given = coarse[distance * ROWS : (distance + 1) * ROWS]
        if touching(distance):
            given = given + jnp.where(gap == 1, up, 0.0) + jnp.where(gap == -1, down, 0.0)
            bit = jnp.where(gap > 0, 1, 0)
            for y in range(2):
                for x in range(4):
                    place = lanes((4 * y + x) * pts, pts)
                    if x in (0, 3):
                        side = left if x == 0 else right
                        payload[:, place] = side[:, lanes((y + 2 * bit) * pts, pts)]
                    else:
                        payload[:, place] = own[:, lanes((x - 1 + 2 * y + 4 * bit) * pts, pts)]
        start = payload.shape[1] - 2 * LEAVES
        given_high, given_low = high_low(given)
        payload[:, lanes(start, LEAVES)] = given_high
        payload[:, lanes(start + LEAVES, LEAVES)] = given_low


def side_kernel(own, left, right, half, source, target, near, sides):
    points = own.shape[1]
    pts = points // 8

    def group(index, carry):
        here = lanes(index * (2 * pts), 2 * pts)
        zero = jnp.zeros((ROWS, 2 * pts), jnp.float32)
        near[:, here] = pulled(zero, target[:, here], source, own, [leaf * pts for leaf in range(8)], pts)
        return carry

    near[:, lanes(0, 4 * pts)] = half[...]
    lax.fori_loop(2, 4, group, 0)
    for step, side in ((0, left), (1, right)):
        for place in range(4):
            centre = (1.5 if step else -1.5, place % 2 - 0.5, place // 2 - 0.5)
            sides[lanes(place * pts, pts), :] = source_features(side, place * pts, pts, centre)

        def layer(index, carry, step=step, side=side):
            here = lanes((step + 2 * index) * (2 * pts), 2 * pts)
            near[:, here] = pulled(near[:, here], target[:, here], sides, side, [p * pts for p in range(4)], pts)
            return carry

        lax.fori_loop(0, 2, layer, 0)


def last_kernel(depth, count_in, weights_in, near, target, basis, own_local, *rest):
    received, rest = rest[: depth - 1], rest[depth - 1 :]
    potential, sums, held, sides, total, count, weights, sems = rest
    copies = fetch([(count_in, count), (weights_in, weights)], sems)
    fields, points = potential.shape
    pts = points // 8
    _, box_z = box_place()
    for step in range(2):
        held[...] = jnp.zeros(held.shape, held.dtype)
        for distance in range(1, depth):
            if touching(distance):

                @pl.when((box_z ^ distance) - box_z == 2 * step - 1)
                def _(block=received[distance - 1]):
                    held[...] = block[:, lanes(0, points)]

        for place in range(8):
            centre = (place % 4 - 1.5, place // 4 - 0.5, 1.5 if step else -1.5)
            sides[lanes(place * pts, pts), :] = source_features(held, place * pts, pts, centre)

        def pair(index, carry, step=step):
            here = lanes((index + 2 * step) * (2 * pts), 2 * pts)
            starts = [(4 * y + x + index) * pts for y in range(2) for x in range(3)]
            total[:, here] = pulled(near[:, here], target[:, here], sides, held, starts, pts)
            return carry

        lax.fori_loop(0, 2, pair, 0)

    local = own_local[...]
    for distance in range(1, depth):
        block = received[distance - 1]
        start = block.shape[1] - 2 * LEAVES
        local = local + block[:, lanes(start, LEAVES)].astype(jnp.float32)
        local = local + block[:, lanes(start + LEAVES, LEAVES)].astype(jnp.float32)
    local_high, local_low = high_low(local)
    for copy in copies:
        copy.wait()
    column = by_row([weights[field] for field in range(fields)], (fields, 1))
    lane_index = lax.broadcasted_iota(jnp.int32, (fields, pts), 1)
    coupling = 1.0 / (128.0 * pts)
    for leaf in range(8):
        here = slice(leaf * pts, (leaf + 1) * pts)
        slot = slice(leaf * SLOT, (leaf + 1) * SLOT)
        left = jnp.concatenate([local_high[:, slot], local_high[:, slot]], axis=1)
        far_part = dot(left, basis[:, here]) + dot(local_low[:, slot], basis[0:SLOT, here])
        value = (total[:, lanes(leaf_slot(leaf) * pts, pts)] + far_part)[:fields]
        value = jnp.where(lane_index < count[leaf], value * coupling, 0.0)
        potential[:, here] = value
        sums[:, here] = jnp.sum(value * column, axis=0, keepdims=True)
    sums[:, points:] = jnp.broadcast_to(jnp.sum(column), (1, sums.shape[1] - points))


def mean_kernel(mine, other, mean):
    points = mean.shape[1]
    total = mine[...] + other[...]
    mean[...] = total[:, :points] / total[:, points : points + 1]


def swapped(block, axis, partner):
    return lax.ppermute(block, axis, [(i, partner(i)) for i in range(lax.axis_size(axis))])


def per_device(positions, density, leaf_count, sigma_weights):
    fields, points = density.shape
    pts = points // 8
    depth = lax.axis_size("space") // ACROSS
    vmem, hbm = pl.BlockSpec(memory_space=pltpu.VMEM), pl.BlockSpec(memory_space=pltpu.HBM)

    def call(kernel, name, in_specs, outs, scratch, *args):
        return pl.pallas_call(
            kernel,
            in_specs=in_specs,
            out_specs=[vmem] * len(outs),
            out_shape=[jax.ShapeDtypeStruct(shape, dtype) for shape, dtype in outs],
            scratch_shapes=scratch,
            compiler_params=pltpu.CompilerParams(vmem_limit_bytes=24 * MEGA),
            name=name,
        )(*(pltpu.with_memory_space_constraint(a, pltpu.HBM) if s is hbm else a for s, a in zip(in_specs, args)))

    half, full = jnp.bfloat16, jnp.float32
    shift = shift_table()
    face = 4 * pts + LEAVES + 2 * SLOT
    own, basis, moments, totals, *given = call(
        pack_kernel,
        "pack",
        [hbm] * 4,
        [
            ((ROWS, points), half),
            ((2 * SLOT, points), half),
            ((ROWS, LEAVES), half),
            ((ROWS, 2 * SLOT), half),
            ((ROWS, face), half),
            ((ROWS, 2 * SLOT), half),
            ((ROWS, face), half),
        ],
        [
            pltpu.SMEM((8,), jnp.int32),
            pltpu.VMEM((3, points), full),
            pltpu.VMEM((fields, points), half),
            pltpu.VMEM((LEAVES, SLOT), half),
            pltpu.VMEM((SLOT, 8, pts), full),
            pltpu.SemaphoreType.DMA((4,)),
        ],
        leaf_count,
        positions,
        density,
        jnp.asarray(shift, half),
    )
    from_2 = swapped(given[1], "space", lambda i: i ^ 2)
    from_3 = swapped(given[2], "space", lambda i: i ^ 3)
    from_1 = swapped(given[0], "space", lambda i: i ^ 1)
    near, source, target, far, nodes, spread = call(
        own_kernel,
        "near_own",
        [vmem] + [hbm] * 3,
        [
            ((ROWS, points // 2), full),
            ((points, FEATURES), half),
            ((FEATURES, points), half),
            ((len(STEPS) * LEAVES, LEAVES), half),
            ((3, SLOT, SLOT), full),
            ((SLOT, LEAVES), half),
        ],
        [pltpu.SemaphoreType.DMA((3,))],
        own,
        jnp.asarray(far_table(), half),
        jnp.asarray(box_nodes()),
        jnp.asarray(shift.T.copy(), half),
    )
    widths = [(points if touching(d) else 0) + 2 * LEAVES for d in range(1, depth)]
    left, right, own_local, *given = call(
        functools.partial(row_kernel, depth),
        "row",
        [vmem] * 9,
        [((ROWS, 4 * pts + LEAVES), half)] * 2 + [((ROWS, LEAVES), full)] + [((ROWS, w), half) for w in widths],
        [],
        own,
        moments,
        totals,
        from_1,
        from_2,
        from_3,
        far,
        nodes,
        spread,
    )
    received = [None] * (depth - 1)
    for d in sorted(range(1, depth), key=lambda d: (touching(d), -d)):
        received[d - 1] = swapped(given[d - 1], "space", lambda i: i ^ (ACROSS * d))
    near, = call(
        side_kernel,
        "near_side",
        [vmem] * 6,
        [((ROWS, points), full)],
        [pltpu.VMEM((4 * pts, FEATURES), half)],
        own,
        left,
        right,
        near,
        source,
        target,
    )
    potential, sums = call(
        functools.partial(last_kernel, depth),
        "near_rows",
        [hbm] * 2 + [vmem] * (4 + len(received)),
        [((fields, points), full), ((1, points + 128), full)],
        [
            pltpu.VMEM((ROWS, points), half),
            pltpu.VMEM((8 * pts, FEATURES), half),
            pltpu.VMEM((ROWS, points), full),
            pltpu.SMEM((8,), jnp.int32),
            pltpu.SMEM((fields,), full),
            pltpu.SemaphoreType.DMA((2,)),
        ],
        leaf_count,
        sigma_weights,
        near,
        target,
        basis,
        own_local,
        *received,
    )
    if lax.axis_size("sig") == 2:
        other = swapped(sums, "sig", lambda i: i ^ 1)
    else:
        other = lax.psum(sums, "sig") - sums
    mean, = call(mean_kernel, "mean", [vmem] * 2, [((1, points), full)], [], sums, other)
    return potential, mean.reshape(points)


def solution(mesh):
    in_specs = (P(None, "space"), P("sig", "space"), P("space"), P("sig"))
    out_specs = (P("sig", "space"), P("space"))
    return jax.shard_map(per_device, mesh=mesh, in_specs=in_specs, out_specs=out_specs, check_vma=False)
```

time: 82.8 us -> 40.1 us (0.48)
  starting transfers between devices: 31.3 us -> 9.08 us
  local copies, waits for them, and re-layouts: 9.78 us -> 0 us
  waiting for transfers between devices: 7.94 us -> 2.96 us
  blocking collectives: 2.52 us -> 0 us
  other arithmetic: 1.3 us -> 0 us
  Pallas kernels: 28.3 us -> 27.2 us
    ppermute x8 -> x7, starting transfers between devices: 23 us -> 9.08 us  [swapped(): lax.ppermute(block, axis, [(i, partner(i)) for i in range(lax.axis_size(a...]
    unnamed x20 -> x0, local copies, waits for them, and re-layouts: 9.19 us -> none
    all_to_all x1 -> x0, starting transfers between devices: 8.31 us -> none  [per_device(): all_slots = lax.all_to_all(slots, 'space', 0, 0, tiled=True)]
    ppermute x8 -> x7, waiting for transfers between devices: 7.94 us -> 2.96 us  [swapped(): lax.ppermute(block, axis, [(i, partner(i)) for i in range(lax.axis_size(a...]
    psum x1 -> x0, blocking collectives: 2.52 us -> none  [per_device(): sums = lax.psum(sums, 'sig')]
    div x1 -> x0, other arithmetic: 1.3 us -> none  [per_device(): return (potential, sums[0, :points] / sums[0, points])]
    pallas_call x2 -> x6, Pallas kernels: 28.3 us -> 27.2 us  [call(): pl.pallas_call(kernel, in_specs=in_specs, out_specs=[vmem] * len(outs), o...]
  transfers between devices with their start and end apart: 9 -> 7, of which waited for: 1 -> 3; matrix products, arithmetic and copies ran while one was open for 0% -> 0% of each run, Pallas kernels for 0% -> 35%
where the time goes in v2:
time: 40.1 us; the launch traced here: 39.9 us
  Pallas kernels  27.2 us (68%)
  starting transfers between devices  9.08 us (23%)
  waiting for transfers between devices  2.96 us (7%)
  between operations  0.68 us (2%)
    pallas_call x6, Pallas kernels, call(): pl.pallas_call(kernel, in_specs=in_specs, out_specs=[vmem] * len(outs), o...  27.2 us
    ppermute x7, starting transfers between devices, swapped(): lax.ppermute(block, axis, [(i, partner(i)) for i in range(lax.axis_size(a...  9.08 us
    ppermute x7, waiting for transfers between devices, swapped(): lax.ppermute(block, axis, [(i, partner(i)) for i in range(lax.axis_size(a...  2.96 us
  transfers between devices with their start and end apart: 7, of which 3 were waited for; matrix products, arithmetic and copies ran while one was open for 0% of the time, Pallas kernels for 35%

profile of v2, /device:TPU:0, one launch (start us, length us, event | category | flops | bytes accessed | tf_op | source)
XLA Modules:
  0.0 39.9 jit_solution(6014594146199024227)
XLA Ops:
  0.6 3.0 %pack.1 = (bf16[32,2048]{1,0:T(8,128)(2,1)S(1)}, bf16[128,2048]{1,0:T(8,128)(2,1)S(1)}, bf16[32,512]{1,0:T(8,128)(2,1)S(1)}, bf16[32,128]{1,0:T(8,128)(2,1)S(1)}...) custom-call(s32[8]{0:T(128)} %count_in.3, f32[3,2048]{1,0:T(4,128)} %positions_in.1, ...), custom_call_target="tpu_custom_call" | custom-call | tf_op jit(solution)/shard_map/pack/pallas_call | solution.py:418
  3.7 3.0 %collective-permute-start = (bf16[32,1664]{1,0:T(8,128)(2,1)S(1)}, bf16[32,1664]{1,0:T(8,128)(2,1)S(1)}, u32[]{:S(2)}, u32[]{:S(2)}) collective-permute-start(bf16[32,1664]{1,0:T(8,128)(2,1)S(1)} %get-tuple-element.26), channel_id=1, source_target_pairs={{0,2},{2,0},{4,6},{6,4},{8,10},{10,8},{12,14},{14,12},{16,18},{18,... | collective-permute-start | bytes 319496 | tf_op jit(solution)/shard_map/ppermute | solution.py:408
  6.7 1.5 %collective-permute-start.2 = (bf16[32,1664]{1,0:T(8,128)(2,1)S(1)}, bf16[32,1664]{1,0:T(8,128)(2,1)S(1)}, u32[]{:S(2)}, u32[]{:S(2)}) collective-permute-start(bf16[32,1664]{1,0:T(8,128)(2,1)S(1)} %get-tuple-element.28), channel_id=1, source_target_pairs={{0,6},{2,4},{4,2},{6,0},{8,14},{10,12},{12,10},{14,8},{16,22},{18,... | collective-permute-start | bytes 319496 | tf_op jit(solution)/shard_map/ppermute | solution.py:408
  8.2 0.1 collective-permute-start.1
  8.2 4.7 %near_own.1 = (f32[32,1024]{1,0:T(8,128)S(1)}, bf16[2048,48]{1,0:T(8,128)(2,1)S(1)}, bf16[48,2048]{1,0:T(8,128)(2,1)S(1)}, bf16[4096,512]{1,0:T(8,128)(2,1)S(1)}...) custom-call(bf16[32,2048]{1,0:T(8,128)(2,1)S(1)} %get-tuple-element.23.own, ...), custom_call_target="tpu_custom_call" | custom-call | tf_op jit(solution)/shard_map/near_own/pallas_call | solution.py:418
  13.0 0.0 collective-permute-done.1.from_2
  13.0 0.0 collective-permute-done.from_1
  13.0 0.2 collective-permute-done.2.from_3
  13.2 1.3 %row.1 = (bf16[32,1536]{1,0:T(8,128)(2,1)S(1)}, bf16[32,1536]{1,0:T(8,128)(2,1)S(1)}, f32[32,512]{1,0:T(8,128)S(1)}, bf16[32,3072]{1,0:T(8,128)(2,1)S(1)}, bf16[...) custom-call(bf16[32,2048]{1,0:T(8,128)(2,1)S(1)} %get-tuple-element.23.own, ...), custom_call_target="tpu_custom_call" | custom-call | tf_op jit(solution)/shard_map/row/pallas_call | solution.py:418
  14.5 1.9 %collective-permute-start.3 = (bf16[32,3072]{1,0:T(8,128)(2,1)S(1)}, bf16[32,3072]{1,0:T(8,128)(2,1)S(1)}, u32[]{:S(2)}, u32[]{:S(2)}) collective-permute-start(bf16[32,3072]{1,0:T(8,128)(2,1)S(1)} %get-tuple-element.39), channel_id=1, source_target_pairs={{0,8},{2,10},{4,12},{6,14},{8,0},{10,2},{12,4},{14,6},{16,24},{18,... | collective-permute-start | bytes 589832 | tf_op jit(solution)/shard_map/ppermute | solution.py:408
  16.3 2.5 %collective-permute-start.5 = (bf16[32,3072]{1,0:T(8,128)(2,1)S(1)}, bf16[32,3072]{1,0:T(8,128)(2,1)S(1)}, u32[]{:S(2)}, u32[]{:S(2)}) collective-permute-start(bf16[32,3072]{1,0:T(8,128)(2,1)S(1)} %get-tuple-element.41), channel_id=1, source_target_pairs={{0,24},{2,26},{4,28},{6,30},{8,16},{10,18},{12,20},{14,22},{16,8},... | collective-permute-start | bytes 589832 | tf_op jit(solution)/shard_map/ppermute | solution.py:408
  18.8 0.1 collective-permute-start.4
  18.9 9.2 %near_side.1.near = f32[32,2048]{1,0:T(8,128)S(1)} custom-call(bf16[32,2048]{1,0:T(8,128)(2,1)S(1)} %get-tuple-element.23.own, bf16[32,1536]{1,0:T(8,128)(2,1)S(1)} %get-tuple-element.32.left, bf16[32,1536]{1,0:T(8,128)(2,1)S(1)} %get-tuple-element.33.right, f32[32,1024]{1,0:T(8,128)S(1)} %get-tuple-element.34.half, ...), custom_call_target="tpu_custom_call" | custom-call | tf_op jit(solution)/shard_map/near_side/pallas_call | solution.py:418
  28.1 1.6 %collective-permute-done.4.rest_1_ = bf16[32,1024]{1,0:T(8,128)(2,1)S(1)} collective-permute-done((bf16[32,1024]{1,0:T(8,128)(2,1)S(1)}, bf16[32,1024]{1,0:T(8,128)(2,1)S(1)}, u32[]{:S(2)}, u32[]{:S(2)}) %collective-permute-start.4) | collective-permute-done | bytes 65568 | tf_op jit(solution)/shard_map/ppermute | solution.py:408
  29.8 0.0 collective-permute-done.3.rest_0_
  29.8 0.0 collective-permute-done.5.rest_2_
  29.8 8.2 %near_rows.1 = (f32[17,2048]{1,0:T(8,128)}, f32[1,2176]{1,0:T(1,128)S(1)}) custom-call(s32[8]{0:T(128)} %count_in.3, f32[17]{0:T(128)} %weights_in.1, f32[32,2048]{1,0:T(8,128)S(1)} %near_side.1.near, bf16[48,2048]{1,0:T(8,128)(2,1)S(1)} %get-tuple-element.36.target, bf16[128,2048]{1,0:T(8,128)(2,1)S(1)} %get-tuple-element.37.basis, ...), custom_call_target="tpu_custom_call" | custom-call | tf_op jit(solution)/shard_map/near_rows/pallas_call | solution.py:418
  38.0 0.1 collective-permute-start.6
  38.1 1.2 %collective-permute-done.6.other = f32[1,2176]{1,0:T(1,128)S(1)} collective-permute-done((f32[1,2176]{1,0:T(1,128)S(1)}, f32[1,2176]{1,0:T(1,128)S(1)}, u32[]{:S(2)}, u32[]{:S(2)}) %collective-permute-start.6) | collective-permute-done | bytes 8736 | tf_op jit(solution)/shard_map/ppermute | solution.py:408
  39.2 0.7 %mean.1 = f32[1,2048]{1,0:T(1,128)} custom-call(f32[1,2176]{1,0:T(1,128)S(1)} %get-tuple-element.43.mine, f32[1,2176]{1,0:T(1,128)S(1)} %collective-permute-done.6.other), custom_call_target="tpu_custom_call" | custom-call | tf_op jit(solution)/shard_map/mean/pallas_call | solution.py:418
Async XLA Ops:
  3.7 9.3 %collective-permute-start = (bf16[32,1664]{1,0:T(8,128)(2,1)S(1)}, bf16[32,1664]{1,0:T(8,128)(2,1)S(1)}, u32[]{:S(2)}, u32[]{:S(2)}) collective-permute-start(bf16[32,1664]{1,0:T(8,128)(2,1)S(1)} %get-tuple-element.26), channel_id=1, source_target_pairs={{0,2},{2,0},{4,6},{6,4},{8,10},{10,8},{12,14},{14,12},{16,18},{18,... | collective-permute-start | bytes 319496 | tf_op jit(solution)/shard_map/ppermute | solution.py:408
  6.7 6.4 %collective-permute-start.2 = (bf16[32,1664]{1,0:T(8,128)(2,1)S(1)}, bf16[32,1664]{1,0:T(8,128)(2,1)S(1)}, u32[]{:S(2)}, u32[]{:S(2)}) collective-permute-start(bf16[32,1664]{1,0:T(8,128)(2,1)S(1)} %get-tuple-element.28), channel_id=1, source_target_pairs={{0,6},{2,4},{4,2},{6,0},{8,14},{10,12},{12,10},{14,8},{16,22},{18,... | collective-permute-start | bytes 319496 | tf_op jit(solution)/shard_map/ppermute | solution.py:408
  8.2 4.8 %collective-permute-start.1 = (bf16[32,128]{1,0:T(8,128)(2,1)S(1)}, bf16[32,128]{1,0:T(8,128)(2,1)S(1)}, u32[]{:S(2)}, u32[]{:S(2)}) collective-permute-start(bf16[32,128]{1,0:T(8,128)(2,1)S(1)} %get-tuple-element.27), channel_id=1, source_target_pairs={{0,4},{2,6},{4,0},{6,2},{8,12},{10,14},{12,8},{14,10},{16,20},{18,... | collective-permute-start | bytes 24584 | tf_op jit(solution)/shard_map/ppermute | solution.py:408
  14.5 15.3 %collective-permute-start.3 = (bf16[32,3072]{1,0:T(8,128)(2,1)S(1)}, bf16[32,3072]{1,0:T(8,128)(2,1)S(1)}, u32[]{:S(2)}, u32[]{:S(2)}) collective-permute-start(bf16[32,3072]{1,0:T(8,128)(2,1)S(1)} %get-tuple-element.39), channel_id=1, source_target_pairs={{0,8},{2,10},{4,12},{6,14},{8,0},{10,2},{12,4},{14,6},{16,24},{18,... | collective-permute-start | bytes 589832 | tf_op jit(solution)/shard_map/ppermute | solution.py:408
  16.3 13.4 %collective-permute-start.5 = (bf16[32,3072]{1,0:T(8,128)(2,1)S(1)}, bf16[32,3072]{1,0:T(8,128)(2,1)S(1)}, u32[]{:S(2)}, u32[]{:S(2)}) collective-permute-start(bf16[32,3072]{1,0:T(8,128)(2,1)S(1)} %get-tuple-element.41), channel_id=1, source_target_pairs={{0,24},{2,26},{4,28},{6,30},{8,16},{10,18},{12,20},{14,22},{16,8},... | collective-permute-start | bytes 589832 | tf_op jit(solution)/shard_map/ppermute | solution.py:408
  18.8 11.0 %collective-permute-start.4 = (bf16[32,1024]{1,0:T(8,128)(2,1)S(1)}, bf16[32,1024]{1,0:T(8,128)(2,1)S(1)}, u32[]{:S(2)}, u32[]{:S(2)}) collective-permute-start(bf16[32,1024]{1,0:T(8,128)(2,1)S(1)} %get-tuple-element.40), channel_id=1, source_target_pairs={{0,16},{2,18},{4,20},{6,22},{8,24},{10,26},{12,28},{14,30},{16,0},... | collective-permute-start | bytes 196616 | tf_op jit(solution)/shard_map/ppermute | solution.py:408
  38.0 1.2 %collective-permute-start.6 = (f32[1,2176]{1,0:T(1,128)S(1)}, f32[1,2176]{1,0:T(1,128)S(1)}, u32[]{:S(2)}, u32[]{:S(2)}) collective-permute-start(f32[1,2176]{1,0:T(1,128)S(1)} %get-tuple-element.43.mine), channel_id=1, source_target_pairs={{0,1},{1,0},{2,3},{3,2},{4,5},{5,4},{6,7},{7,6},{8,9},{9,8},{10,11... | collective-permute-start | bytes 26120 | tf_op jit(solution)/shard_map/ppermute | solution.py:408

commit v3 on v2

--- a/solution.py
+++ b/solution.py
@@ -222,34 +222,37 @@
     return jnp.concatenate(blocks, axis=0)
 
 
-def source_features(held, start, size, centre):
-    return low_bits(jnp.transpose(features(held, start, size, centre, False)))
+def columns_of(held, start, size):
+    return low_bits(jnp.transpose(held[0:ROWS, lanes(start, size)].astype(jnp.float32)))
 
 
 def pulled(total, wanted, source, masses, starts, pts):
     for start in starts:
         place = lanes(start, pts)
-        kernel = lax.rsqrt(dot(source[place, :], wanted))
+        kernel = lax.rsqrt(dot(wanted, source[:, place]))
         high = low_bits(kernel)
         low = low_bits(kernel - high.astype(jnp.float32))
-        mass = masses[:, place]
-        total = total + dot(mass, high) + dot(mass, low)
+        mass = masses[place, :]
+        total = total + dot(high, mass) + dot(low, mass)
     return total
 
 
-def own_kernel(own, far_in, nodes_in, spread_in, near, source, target, far, nodes, spread, sems):
+def own_kernel(own, far_in, nodes_in, spread_in, near, source, target, masses, far, nodes, spread, sems):
     copies = fetch([(far_in, far), (nodes_in, nodes), (spread_in, spread)], sems)
     points = own.shape[1]
     pts = points // 8
     for leaf in range(8):
         centre = [bit - 0.5 for bit in bits(leaf)]
-        source[lanes(leaf * pts, pts), :] = source_features(own, leaf * pts, pts, centre)
-        target[:, lanes(leaf_slot(leaf) * pts, pts)] = low_bits(features(own, leaf * pts, pts, centre, True))
+        here = lanes(leaf * pts, pts)
+        source[:, here] = low_bits(features(own, leaf * pts, pts, centre, False))
+        wanted = features(own, leaf * pts, pts, centre, True)
+        target[lanes(leaf_slot(leaf) * pts, pts), :] = low_bits(jnp.transpose(wanted))
+        masses[here, :] = columns_of(own, leaf * pts, pts)
 
     def group(index, carry):
         here = lanes(index * (2 * pts), 2 * pts)
-        zero = jnp.zeros((ROWS, 2 * pts), jnp.float32)
-        near[:, here] = pulled(zero, target[:, here], source, own, [leaf * pts for leaf in range(8)], pts)
+        zero = jnp.zeros((2 * pts, ROWS), jnp.float32)
+        near[here, :] = pulled(zero, target[here, :], source, masses, [leaf * pts for leaf in range(8)], pts)
         return carry
 
     lax.fori_loop(0, 2, group, 0)
@@ -321,26 +324,29 @@
         payload[:, lanes(start + LEAVES, LEAVES)] = given_low
 
 
-def side_kernel(own, left, right, half, source, target, near, sides):
-    points = own.shape[1]
+def side_kernel(left, right, half, source, target, masses, near, sides, side_masses):
+    points = source.shape[1]
     pts = points // 8
 
     def group(index, carry):
         here = lanes(index * (2 * pts), 2 * pts)
-        zero = jnp.zeros((ROWS, 2 * pts), jnp.float32)
-        near[:, here] = pulled(zero, target[:, here], source, own, [leaf * pts for leaf in range(8)], pts)
+        zero = jnp.zeros((2 * pts, ROWS), jnp.float32)
+        near[here, :] = pulled(zero, target[here, :], source, masses, [leaf * pts for leaf in range(8)], pts)
         return carry
 
-    near[:, lanes(0, 4 * pts)] = half[...]
+    near[lanes(0, 4 * pts), :] = half[...]
     lax.fori_loop(2, 4, group, 0)
     for step, side in ((0, left), (1, right)):
         for place in range(4):
             centre = (1.5 if step else -1.5, place % 2 - 0.5, place // 2 - 0.5)
-            sides[lanes(place * pts, pts), :] = source_features(side, place * pts, pts, centre)
-
-        def layer(index, carry, step=step, side=side):
+            here = lanes(place * pts, pts)
+            sides[:, here] = low_bits(features(side, place * pts, pts, centre, False))
+            side_masses[here, :] = columns_of(side, place * pts, pts)
+
+        def layer(index, carry, step=step):
             here = lanes((step + 2 * index) * (2 * pts), 2 * pts)
-            near[:, here] = pulled(near[:, here], target[:, here], sides, side, [p * pts for p in range(4)], pts)
+            starts = [p * pts for p in range(4)]
+            near[here, :] = pulled(near[here, :], target[here, :], sides, side_masses, starts, pts)
             return carry
 
         lax.fori_loop(0, 2, layer, 0)
@@ -348,7 +354,7 @@
 
 def last_kernel(depth, count_in, weights_in, near, target, basis, own_local, *rest):
     received, rest = rest[: depth - 1], rest[depth - 1 :]
-    potential, sums, held, sides, total, count, weights, sems = rest
+    potential, sums, held, sides, side_masses, total, count, weights, sems = rest
     copies = fetch([(count_in, count), (weights_in, weights)], sems)
     fields, points = potential.shape
     pts = points // 8
@@ -364,12 +370,14 @@
 
         for place in range(8):
             centre = (place % 4 - 1.5, place // 4 - 0.5, 1.5 if step else -1.5)
-            sides[lanes(place * pts, pts), :] = source_features(held, place * pts, pts, centre)
+            here = lanes(place * pts, pts)
+            sides[:, here] = low_bits(features(held, place * pts, pts, centre, False))
+            side_masses[here, :] = columns_of(held, place * pts, pts)
 
         def pair(index, carry, step=step):
             here = lanes((index + 2 * step) * (2 * pts), 2 * pts)
             starts = [(4 * y + x + index) * pts for y in range(2) for x in range(3)]
-            total[:, here] = pulled(near[:, here], target[:, here], sides, held, starts, pts)
+            total[here, :] = pulled(near[here, :], target[here, :], sides, side_masses, starts, pts)
             return carry
 
         lax.fori_loop(0, 2, pair, 0)
@@ -391,7 +399,8 @@
         slot = slice(leaf * SLOT, (leaf + 1) * SLOT)
         left = jnp.concatenate([local_high[:, slot], local_high[:, slot]], axis=1)
         far_part = dot(left, basis[:, here]) + dot(local_low[:, slot], basis[0:SLOT, here])
-        value = (total[:, lanes(leaf_slot(leaf) * pts, pts)] + far_part)[:fields]
+        near_part = jnp.transpose(total[lanes(leaf_slot(leaf) * pts, pts), :])
+        value = (near_part + far_part)[:fields]
         value = jnp.where(lane_index < count[leaf], value * coupling, 0.0)
         potential[:, here] = value
         sums[:, here] = jnp.sum(value * column, axis=0, keepdims=True)
@@ -457,14 +466,15 @@
     from_2 = swapped(given[1], "space", lambda i: i ^ 2)
     from_3 = swapped(given[2], "space", lambda i: i ^ 3)
     from_1 = swapped(given[0], "space", lambda i: i ^ 1)
-    near, source, target, far, nodes, spread = call(
+    near, source, target, masses, far, nodes, spread = call(
         own_kernel,
         "near_own",
         [vmem] + [hbm] * 3,
         [
-            ((ROWS, points // 2), full),
+            ((points // 2, ROWS), full),
+            ((FEATURES, points), half),
             ((points, FEATURES), half),
-            ((FEATURES, points), half),
+            ((points, ROWS), half),
             ((len(STEPS) * LEAVES, LEAVES), half),
             ((3, SLOT, SLOT), full),
             ((SLOT, LEAVES), half),
@@ -499,14 +509,14 @@
         side_kernel,
         "near_side",
         [vmem] * 6,
-        [((ROWS, points), full)],
-        [pltpu.VMEM((4 * pts, FEATURES), half)],
-        own,
+        [((points, ROWS), full)],
+        [pltpu.VMEM((FEATURES, 4 * pts), half), pltpu.VMEM((4 * pts, ROWS), half)],
         left,
         right,
         near,
         source,
         target,
+        masses,
     )
     potential, sums = call(
         functools.partial(last_kernel, depth),
@@ -515,8 +525,9 @@
         [((fields, points), full), ((1, points + 128), full)],
         [
             pltpu.VMEM((ROWS, points), half),
-            pltpu.VMEM((8 * pts, FEATURES), half),
-            pltpu.VMEM((ROWS, points), full),
+            pltpu.VMEM((FEATURES, 8 * pts), half),
+            pltpu.VMEM((8 * pts, ROWS), half),
+            pltpu.VMEM((points, ROWS), full),
             pltpu.SMEM((8,), jnp.int32),
             pltpu.SMEM((fields,), full),
             pltpu.SemaphoreType.DMA((2,)),

time: 40.1 us -> 43.8 us (1.092)
  Pallas kernels: 27.2 us -> 32.5 us
  waiting for transfers between devices: 2.96 us -> 1.18 us
    pallas_call x6, Pallas kernels: 27.2 us -> 32.5 us  [call(): pl.pallas_call(kernel, in_specs=in_specs, out_specs=[vmem] * len(outs), o...]
    ppermute x7, waiting for transfers between devices: 2.96 us -> 1.18 us  [swapped(): lax.ppermute(block, axis, [(i, partner(i)) for i in range(lax.axis_size(a...]
  transfers between devices with their start and end apart: 7 -> 7, of which waited for: 3 -> 1; matrix products, arithmetic and copies ran while one was open for 0% -> 0% of each run, Pallas kernels for 35% -> 40%
where the time goes in v3:
time: 43.8 us; the launch traced here: 43.7 us
  Pallas kernels  32.5 us (74%)
  starting transfers between devices  9.25 us (21%)
  waiting for transfers between devices  1.18 us (3%)
  between operations  0.72 us (2%)
    pallas_call x6, Pallas kernels, call(): pl.pallas_call(kernel, in_specs=in_specs, out_specs=[vmem] * len(outs), o...  32.5 us
    ppermute x7, starting transfers between devices, swapped(): lax.ppermute(block, axis, [(i, partner(i)) for i in range(lax.axis_size(a...  9.25 us
    ppermute x7, waiting for transfers between devices, swapped(): lax.ppermute(block, axis, [(i, partner(i)) for i in range(lax.axis_size(a...  1.18 us
  transfers between devices with their start and end apart: 7, of which 1 were waited for; matrix products, arithmetic and copies ran while one was open for 0% of the time, Pallas kernels for 40%

profile of v3, /device:TPU:0, one launch (start us, length us, event | category | flops | bytes accessed | tf_op | source)
XLA Modules:
  0.0 43.7 jit_solution(1867650618431829054)
XLA Ops:
  0.6 3.0 %pack.1 = (bf16[32,2048]{1,0:T(8,128)(2,1)S(1)}, bf16[128,2048]{1,0:T(8,128)(2,1)S(1)}, bf16[32,512]{1,0:T(8,128)(2,1)S(1)}, bf16[32,128]{1,0:T(8,128)(2,1)S(1)}...) custom-call(s32[8]{0:T(128)} %count_in.3, f32[3,2048]{1,0:T(4,128)} %positions_in.1, ...), custom_call_target="tpu_custom_call" | custom-call | tf_op jit(solution)/shard_map/pack/pallas_call | solution.py:427
  3.7 3.0 %collective-permute-start = (bf16[32,1664]{1,0:T(8,128)(2,1)S(1)}, bf16[32,1664]{1,0:T(8,128)(2,1)S(1)}, u32[]{:S(2)}, u32[]{:S(2)}) collective-permute-start(bf16[32,1664]{1,0:T(8,128)(2,1)S(1)} %get-tuple-element.27), channel_id=1, source_target_pairs={{0,2},{2,0},{4,6},{6,4},{8,10},{10,8},{12,14},{14,12},{16,18},{18,... | collective-permute-start | bytes 319496 | tf_op jit(solution)/shard_map/ppermute | solution.py:417
  6.7 1.5 %collective-permute-start.2 = (bf16[32,1664]{1,0:T(8,128)(2,1)S(1)}, bf16[32,1664]{1,0:T(8,128)(2,1)S(1)}, u32[]{:S(2)}, u32[]{:S(2)}) collective-permute-start(bf16[32,1664]{1,0:T(8,128)(2,1)S(1)} %get-tuple-element.29), channel_id=1, source_target_pairs={{0,6},{2,4},{4,2},{6,0},{8,14},{10,12},{12,10},{14,8},{16,22},{18,... | collective-permute-start | bytes 319496 | tf_op jit(solution)/shard_map/ppermute | solution.py:417
  8.2 0.1 collective-permute-start.1
  8.2 5.9 %near_own.1 = (f32[1024,32]{1,0:T(8,128)S(1)}, bf16[48,2048]{1,0:T(8,128)(2,1)S(1)}, bf16[2048,48]{1,0:T(8,128)(2,1)S(1)}, bf16[2048,32]{1,0:T(8,128)(2,1)S(1)},...) custom-call(bf16[32,2048]{1,0:T(8,128)(2,1)S(1)} %get-tuple-element.24.own, ...), custom_call_target="tpu_custom_call" | custom-call | tf_op jit(solution)/shard_map/near_own/pallas_call | solution.py:427
  14.1 0.0 collective-permute-done.1.from_2
  14.1 0.0 collective-permute-done.from_1
  14.1 0.0 collective-permute-done.2.from_3
  14.2 1.4 %row.1 = (bf16[32,1536]{1,0:T(8,128)(2,1)S(1)}, bf16[32,1536]{1,0:T(8,128)(2,1)S(1)}, f32[32,512]{1,0:T(8,128)S(1)}, bf16[32,3072]{1,0:T(8,128)(2,1)S(1)}, bf16[...) custom-call(bf16[32,2048]{1,0:T(8,128)(2,1)S(1)} %get-tuple-element.24.own, ...), custom_call_target="tpu_custom_call" | custom-call | tf_op jit(solution)/shard_map/row/pallas_call | solution.py:427
  15.5 2.0 %collective-permute-start.3 = (bf16[32,3072]{1,0:T(8,128)(2,1)S(1)}, bf16[32,3072]{1,0:T(8,128)(2,1)S(1)}, u32[]{:S(2)}, u32[]{:S(2)}) collective-permute-start(bf16[32,3072]{1,0:T(8,128)(2,1)S(1)} %get-tuple-element.41), channel_id=1, source_target_pairs={{0,8},{2,10},{4,12},{6,14},{8,0},{10,2},{12,4},{14,6},{16,24},{18,... | collective-permute-start | bytes 589832 | tf_op jit(solution)/shard_map/ppermute | solution.py:417
  17.5 2.5 %collective-permute-start.5 = (bf16[32,3072]{1,0:T(8,128)(2,1)S(1)}, bf16[32,3072]{1,0:T(8,128)(2,1)S(1)}, u32[]{:S(2)}, u32[]{:S(2)}) collective-permute-start(bf16[32,3072]{1,0:T(8,128)(2,1)S(1)} %get-tuple-element.43), channel_id=1, source_target_pairs={{0,24},{2,26},{4,28},{6,30},{8,16},{10,18},{12,20},{14,22},{16,8},... | collective-permute-start | bytes 589832 | tf_op jit(solution)/shard_map/ppermute | solution.py:417
  20.0 0.1 collective-permute-start.4
  20.1 11.6 %near_side.1.near = f32[2048,32]{1,0:T(8,128)S(1)} custom-call(bf16[32,1536]{1,0:T(8,128)(2,1)S(1)} %get-tuple-element.33.left, bf16[32,1536]{1,0:T(8,128)(2,1)S(1)} %get-tuple-element.34.right, f32[1024,32]{1,0:T(8,128)S(1)} %get-tuple-element.35.half, bf16[48,2048]{1,0:T(8,128)(2,1)S(1)} %get-tuple-element.36.source, ...), custom_call_target="tpu_custom_call" | custom-call | tf_op jit(solution)/shard_map/near_side/pallas_call | solution.py:427
  31.8 0.0 collective-permute-done.4.rest_1_
  31.8 0.0 collective-permute-done.3.rest_0_
  31.8 0.0 collective-permute-done.5.rest_2_
  31.8 10.0 %near_rows.1 = (f32[17,2048]{1,0:T(8,128)}, f32[1,2176]{1,0:T(1,128)S(1)}) custom-call(s32[8]{0:T(128)} %count_in.3, f32[17]{0:T(128)} %weights_in.1, f32[2048,32]{1,0:T(8,128)S(1)} %near_side.1.near, bf16[2048,48]{1,0:T(8,128)(2,1)S(1)} %get-tuple-element.37.target, bf16[128,2048]{1,0:T(8,128)(2,1)S(1)} %get-tuple-element.39.basis, ...), custom_call_target="tpu_custom_call" | custom-call | tf_op jit(solution)/shard_map/near_rows/pallas_call | solution.py:427
  41.7 0.1 collective-permute-start.6
  41.8 1.2 %collective-permute-done.6.other = f32[1,2176]{1,0:T(1,128)S(1)} collective-permute-done((f32[1,2176]{1,0:T(1,128)S(1)}, f32[1,2176]{1,0:T(1,128)S(1)}, u32[]{:S(2)}, u32[]{:S(2)}) %collective-permute-start.6) | collective-permute-done | bytes 8736 | tf_op jit(solution)/shard_map/ppermute | solution.py:417
  43.0 0.7 %mean.1 = f32[1,2048]{1,0:T(1,128)} custom-call(f32[1,2176]{1,0:T(1,128)S(1)} %get-tuple-element.45.mine, f32[1,2176]{1,0:T(1,128)S(1)} %collective-permute-done.6.other), custom_call_target="tpu_custom_call" | custom-call | tf_op jit(solution)/shard_map/mean/pallas_call | solution.py:427
Async XLA Ops:
  3.7 10.5 %collective-permute-start = (bf16[32,1664]{1,0:T(8,128)(2,1)S(1)}, bf16[32,1664]{1,0:T(8,128)(2,1)S(1)}, u32[]{:S(2)}, u32[]{:S(2)}) collective-permute-start(bf16[32,1664]{1,0:T(8,128)(2,1)S(1)} %get-tuple-element.27), channel_id=1, source_target_pairs={{0,2},{2,0},{4,6},{6,4},{8,10},{10,8},{12,14},{14,12},{16,18},{18,... | collective-permute-start | bytes 319496 | tf_op jit(solution)/shard_map/ppermute | solution.py:417
  6.7 7.4 %collective-permute-start.2 = (bf16[32,1664]{1,0:T(8,128)(2,1)S(1)}, bf16[32,1664]{1,0:T(8,128)(2,1)S(1)}, u32[]{:S(2)}, u32[]{:S(2)}) collective-permute-start(bf16[32,1664]{1,0:T(8,128)(2,1)S(1)} %get-tuple-element.29), channel_id=1, source_target_pairs={{0,6},{2,4},{4,2},{6,0},{8,14},{10,12},{12,10},{14,8},{16,22},{18,... | collective-permute-start | bytes 319496 | tf_op jit(solution)/shard_map/ppermute | solution.py:417
  8.2 5.9 %collective-permute-start.1 = (bf16[32,128]{1,0:T(8,128)(2,1)S(1)}, bf16[32,128]{1,0:T(8,128)(2,1)S(1)}, u32[]{:S(2)}, u32[]{:S(2)}) collective-permute-start(bf16[32,128]{1,0:T(8,128)(2,1)S(1)} %get-tuple-element.28), channel_id=1, source_target_pairs={{0,4},{2,6},{4,0},{6,2},{8,12},{10,14},{12,8},{14,10},{16,20},{18,... | collective-permute-start | bytes 24584 | tf_op jit(solution)/shard_map/ppermute | solution.py:417
  15.5 16.3 %collective-permute-start.3 = (bf16[32,3072]{1,0:T(8,128)(2,1)S(1)}, bf16[32,3072]{1,0:T(8,128)(2,1)S(1)}, u32[]{:S(2)}, u32[]{:S(2)}) collective-permute-start(bf16[32,3072]{1,0:T(8,128)(2,1)S(1)} %get-tuple-element.41), channel_id=1, source_target_pairs={{0,8},{2,10},{4,12},{6,14},{8,0},{10,2},{12,4},{14,6},{16,24},{18,... | collective-permute-start | bytes 589832 | tf_op jit(solution)/shard_map/ppermute | solution.py:417
  17.5 14.2 %collective-permute-start.5 = (bf16[32,3072]{1,0:T(8,128)(2,1)S(1)}, bf16[32,3072]{1,0:T(8,128)(2,1)S(1)}, u32[]{:S(2)}, u32[]{:S(2)}) collective-permute-start(bf16[32,3072]{1,0:T(8,128)(2,1)S(1)} %get-tuple-element.43), channel_id=1, source_target_pairs={{0,24},{2,26},{4,28},{6,30},{8,16},{10,18},{12,20},{14,22},{16,8},... | collective-permute-start | bytes 589832 | tf_op jit(solution)/shard_map/ppermute | solution.py:417
  20.0 11.7 %collective-permute-start.4 = (bf16[32,1024]{1,0:T(8,128)(2,1)S(1)}, bf16[32,1024]{1,0:T(8,128)(2,1)S(1)}, u32[]{:S(2)}, u32[]{:S(2)}) collective-permute-start(bf16[32,1024]{1,0:T(8,128)(2,1)S(1)} %get-tuple-element.42), channel_id=1, source_target_pairs={{0,16},{2,18},{4,20},{6,22},{8,24},{10,26},{12,28},{14,30},{16,0},... | collective-permute-start | bytes 196616 | tf_op jit(solution)/shard_map/ppermute | solution.py:417
  41.7 1.2 %collective-permute-start.6 = (f32[1,2176]{1,0:T(1,128)S(1)}, f32[1,2176]{1,0:T(1,128)S(1)}, u32[]{:S(2)}, u32[]{:S(2)}) collective-permute-start(f32[1,2176]{1,0:T(1,128)S(1)} %get-tuple-element.45.mine), channel_id=1, source_target_pairs={{0,1},{1,0},{2,3},{3,2},{4,5},{5,4},{6,7},{7,6},{8,9},{9,8},{10,11... | collective-permute-start | bytes 26120 | tf_op jit(solution)/shard_map/ppermute | solution.py:417

commit v4 on v2

--- a/solution.py
+++ b/solution.py
@@ -230,10 +230,7 @@
     for start in starts:
         place = lanes(start, pts)
         kernel = lax.rsqrt(dot(source[place, :], wanted))
-        high = low_bits(kernel)
-        low = low_bits(kernel - high.astype(jnp.float32))
-        mass = masses[:, place]
-        total = total + dot(mass, high) + dot(mass, low)
+        total = total + dot(masses[:, place], low_bits(kernel))
     return total
 
 

time: 40.1 us -> 38.7 us (0.965)
  Pallas kernels: 27.2 us -> 23.6 us
  waiting for transfers between devices: 2.96 us -> 5.47 us
    pallas_call x6, Pallas kernels: 27.2 us -> 23.6 us  [call(): pl.pallas_call(kernel, in_specs=in_specs, out_specs=[vmem] * len(outs), o...]
    ppermute x7, waiting for transfers between devices: 2.96 us -> 5.47 us  [swapped(): lax.ppermute(block, axis, [(i, partner(i)) for i in range(lax.axis_size(a...]
  transfers between devices with their start and end apart: 7 -> 7, of which waited for: 3 -> 3; matrix products, arithmetic and copies ran while one was open for 0% -> 0% of each run, Pallas kernels for 35% -> 30%
where the time goes in v4:
time: 38.7 us; the launch traced here: 38.5 us
  Pallas kernels  23.6 us (61%)
  starting transfers between devices  8.81 us (23%)
  waiting for transfers between devices  5.47 us (14%)
  between operations  0.68 us (2%)
    pallas_call x6, Pallas kernels, call(): pl.pallas_call(kernel, in_specs=in_specs, out_specs=[vmem] * len(outs), o...  23.6 us
    ppermute x7, starting transfers between devices, swapped(): lax.ppermute(block, axis, [(i, partner(i)) for i in range(lax.axis_size(a...  8.81 us
    ppermute x7, waiting for transfers between devices, swapped(): lax.ppermute(block, axis, [(i, partner(i)) for i in range(lax.axis_size(a...  5.47 us
  transfers between devices with their start and end apart: 7, of which 3 were waited for; matrix products, arithmetic and copies ran while one was open for 0% of the time, Pallas kernels for 30%

profile of v4, /device:TPU:0, one launch (start us, length us, event | category | flops | bytes accessed | tf_op | source)
XLA Modules:
  0.0 38.5 jit_solution(689035911012448754)
XLA Ops:
  0.6 3.0 %pack.1 = (bf16[32,2048]{1,0:T(8,128)(2,1)S(1)}, bf16[128,2048]{1,0:T(8,128)(2,1)S(1)}, bf16[32,512]{1,0:T(8,128)(2,1)S(1)}, bf16[32,128]{1,0:T(8,128)(2,1)S(1)}...) custom-call(s32[8]{0:T(128)} %count_in.3, f32[3,2048]{1,0:T(4,128)} %positions_in.1, ...), custom_call_target="tpu_custom_call" | custom-call | tf_op jit(solution)/shard_map/pack/pallas_call | solution.py:415
  3.7 3.0 %collective-permute-start = (bf16[32,1664]{1,0:T(8,128)(2,1)S(1)}, bf16[32,1664]{1,0:T(8,128)(2,1)S(1)}, u32[]{:S(2)}, u32[]{:S(2)}) collective-permute-start(bf16[32,1664]{1,0:T(8,128)(2,1)S(1)} %get-tuple-element.26), channel_id=1, source_target_pairs={{0,2},{2,0},{4,6},{6,4},{8,10},{10,8},{12,14},{14,12},{16,18},{18,... | collective-permute-start | bytes 319496 | tf_op jit(solution)/shard_map/ppermute | solution.py:405
  6.7 1.5 %collective-permute-start.2 = (bf16[32,1664]{1,0:T(8,128)(2,1)S(1)}, bf16[32,1664]{1,0:T(8,128)(2,1)S(1)}, u32[]{:S(2)}, u32[]{:S(2)}) collective-permute-start(bf16[32,1664]{1,0:T(8,128)(2,1)S(1)} %get-tuple-element.28), channel_id=1, source_target_pairs={{0,6},{2,4},{4,2},{6,0},{8,14},{10,12},{12,10},{14,8},{16,22},{18,... | collective-permute-start | bytes 319496 | tf_op jit(solution)/shard_map/ppermute | solution.py:405
  8.2 0.1 collective-permute-start.1
  8.2 3.8 %near_own.1 = (f32[32,1024]{1,0:T(8,128)S(1)}, bf16[2048,48]{1,0:T(8,128)(2,1)S(1)}, bf16[48,2048]{1,0:T(8,128)(2,1)S(1)}, bf16[4096,512]{1,0:T(8,128)(2,1)S(1)}...) custom-call(bf16[32,2048]{1,0:T(8,128)(2,1)S(1)} %get-tuple-element.23.own, ...), custom_call_target="tpu_custom_call" | custom-call | tf_op jit(solution)/shard_map/near_own/pallas_call | solution.py:415
  12.0 0.0 collective-permute-done.1.from_2
  12.0 0.0 collective-permute-done.from_1
  12.1 1.1 %collective-permute-done.2.from_3 = bf16[32,1664]{1,0:T(8,128)(2,1)S(1)} collective-permute-done((bf16[32,1664]{1,0:T(8,128)(2,1)S(1)}, bf16[32,1664]{1,0:T(8,128)(2,1)S(1)}, u32[]{:S(2)}, u32[]{:S(2)}) %collective-permute-start.2) | collective-permute-done | bytes 106528 | tf_op jit(solution)/shard_map/ppermute | solution.py:405
  13.2 1.3 %row.1 = (bf16[32,1536]{1,0:T(8,128)(2,1)S(1)}, bf16[32,1536]{1,0:T(8,128)(2,1)S(1)}, f32[32,512]{1,0:T(8,128)S(1)}, bf16[32,3072]{1,0:T(8,128)(2,1)S(1)}, bf16[...) custom-call(bf16[32,2048]{1,0:T(8,128)(2,1)S(1)} %get-tuple-element.23.own, ...), custom_call_target="tpu_custom_call" | custom-call | tf_op jit(solution)/shard_map/row/pallas_call | solution.py:415
  14.5 1.6 %collective-permute-start.3 = (bf16[32,3072]{1,0:T(8,128)(2,1)S(1)}, bf16[32,3072]{1,0:T(8,128)(2,1)S(1)}, u32[]{:S(2)}, u32[]{:S(2)}) collective-permute-start(bf16[32,3072]{1,0:T(8,128)(2,1)S(1)} %get-tuple-element.39), channel_id=1, source_target_pairs={{0,8},{2,10},{4,12},{6,14},{8,0},{10,2},{12,4},{14,6},{16,24},{18,... | collective-permute-start | bytes 589832 | tf_op jit(solution)/shard_map/ppermute | solution.py:405
  16.1 2.5 %collective-permute-start.5 = (bf16[32,3072]{1,0:T(8,128)(2,1)S(1)}, bf16[32,3072]{1,0:T(8,128)(2,1)S(1)}, u32[]{:S(2)}, u32[]{:S(2)}) collective-permute-start(bf16[32,3072]{1,0:T(8,128)(2,1)S(1)} %get-tuple-element.41), channel_id=1, source_target_pairs={{0,24},{2,26},{4,28},{6,30},{8,16},{10,18},{12,20},{14,22},{16,8},... | collective-permute-start | bytes 589832 | tf_op jit(solution)/shard_map/ppermute | solution.py:405
  18.5 0.1 collective-permute-start.4
  18.7 7.6 %near_side.1.near = f32[32,2048]{1,0:T(8,128)S(1)} custom-call(bf16[32,2048]{1,0:T(8,128)(2,1)S(1)} %get-tuple-element.23.own, bf16[32,1536]{1,0:T(8,128)(2,1)S(1)} %get-tuple-element.32.left, bf16[32,1536]{1,0:T(8,128)(2,1)S(1)} %get-tuple-element.33.right, f32[32,1024]{1,0:T(8,128)S(1)} %get-tuple-element.34.half, ...), custom_call_target="tpu_custom_call" | custom-call | tf_op jit(solution)/shard_map/near_side/pallas_call | solution.py:415
  26.2 3.2 %collective-permute-done.4.rest_1_ = bf16[32,1024]{1,0:T(8,128)(2,1)S(1)} collective-permute-done((bf16[32,1024]{1,0:T(8,128)(2,1)S(1)}, bf16[32,1024]{1,0:T(8,128)(2,1)S(1)}, u32[]{:S(2)}, u32[]{:S(2)}) %collective-permute-start.4) | collective-permute-done | bytes 65568 | tf_op jit(solution)/shard_map/ppermute | solution.py:405
  29.5 0.0 collective-permute-done.3.rest_0_
  29.5 0.0 collective-permute-done.5.rest_2_
  29.5 7.1 %near_rows.1 = (f32[17,2048]{1,0:T(8,128)}, f32[1,2176]{1,0:T(1,128)S(1)}) custom-call(s32[8]{0:T(128)} %count_in.3, f32[17]{0:T(128)} %weights_in.1, f32[32,2048]{1,0:T(8,128)S(1)} %near_side.1.near, bf16[48,2048]{1,0:T(8,128)(2,1)S(1)} %get-tuple-element.36.target, bf16[128,2048]{1,0:T(8,128)(2,1)S(1)} %get-tuple-element.37.basis, ...), custom_call_target="tpu_custom_call" | custom-call | tf_op jit(solution)/shard_map/near_rows/pallas_call | solution.py:415
  36.6 0.1 collective-permute-start.6
  36.7 1.2 %collective-permute-done.6.other = f32[1,2176]{1,0:T(1,128)S(1)} collective-permute-done((f32[1,2176]{1,0:T(1,128)S(1)}, f32[1,2176]{1,0:T(1,128)S(1)}, u32[]{:S(2)}, u32[]{:S(2)}) %collective-permute-start.6) | collective-permute-done | bytes 8736 | tf_op jit(solution)/shard_map/ppermute | solution.py:405
  37.9 0.7 %mean.1 = f32[1,2048]{1,0:T(1,128)} custom-call(f32[1,2176]{1,0:T(1,128)S(1)} %get-tuple-element.43.mine, f32[1,2176]{1,0:T(1,128)S(1)} %collective-permute-done.6.other), custom_call_target="tpu_custom_call" | custom-call | tf_op jit(solution)/shard_map/mean/pallas_call | solution.py:415
Async XLA Ops:
  3.7 8.4 %collective-permute-start = (bf16[32,1664]{1,0:T(8,128)(2,1)S(1)}, bf16[32,1664]{1,0:T(8,128)(2,1)S(1)}, u32[]{:S(2)}, u32[]{:S(2)}) collective-permute-start(bf16[32,1664]{1,0:T(8,128)(2,1)S(1)} %get-tuple-element.26), channel_id=1, source_target_pairs={{0,2},{2,0},{4,6},{6,4},{8,10},{10,8},{12,14},{14,12},{16,18},{18,... | collective-permute-start | bytes 319496 | tf_op jit(solution)/shard_map/ppermute | solution.py:405
  6.7 6.4 %collective-permute-start.2 = (bf16[32,1664]{1,0:T(8,128)(2,1)S(1)}, bf16[32,1664]{1,0:T(8,128)(2,1)S(1)}, u32[]{:S(2)}, u32[]{:S(2)}) collective-permute-start(bf16[32,1664]{1,0:T(8,128)(2,1)S(1)} %get-tuple-element.28), channel_id=1, source_target_pairs={{0,6},{2,4},{4,2},{6,0},{8,14},{10,12},{12,10},{14,8},{16,22},{18,... | collective-permute-start | bytes 319496 | tf_op jit(solution)/shard_map/ppermute | solution.py:405
  8.2 3.9 %collective-permute-start.1 = (bf16[32,128]{1,0:T(8,128)(2,1)S(1)}, bf16[32,128]{1,0:T(8,128)(2,1)S(1)}, u32[]{:S(2)}, u32[]{:S(2)}) collective-permute-start(bf16[32,128]{1,0:T(8,128)(2,1)S(1)} %get-tuple-element.27), channel_id=1, source_target_pairs={{0,4},{2,6},{4,0},{6,2},{8,12},{10,14},{12,8},{14,10},{16,20},{18,... | collective-permute-start | bytes 24584 | tf_op jit(solution)/shard_map/ppermute | solution.py:405
  14.5 15.0 %collective-permute-start.3 = (bf16[32,3072]{1,0:T(8,128)(2,1)S(1)}, bf16[32,3072]{1,0:T(8,128)(2,1)S(1)}, u32[]{:S(2)}, u32[]{:S(2)}) collective-permute-start(bf16[32,3072]{1,0:T(8,128)(2,1)S(1)} %get-tuple-element.39), channel_id=1, source_target_pairs={{0,8},{2,10},{4,12},{6,14},{8,0},{10,2},{12,4},{14,6},{16,24},{18,... | collective-permute-start | bytes 589832 | tf_op jit(solution)/shard_map/ppermute | solution.py:405
  16.1 13.4 %collective-permute-start.5 = (bf16[32,3072]{1,0:T(8,128)(2,1)S(1)}, bf16[32,3072]{1,0:T(8,128)(2,1)S(1)}, u32[]{:S(2)}, u32[]{:S(2)}) collective-permute-start(bf16[32,3072]{1,0:T(8,128)(2,1)S(1)} %get-tuple-element.41), channel_id=1, source_target_pairs={{0,24},{2,26},{4,28},{6,30},{8,16},{10,18},{12,20},{14,22},{16,8},... | collective-permute-start | bytes 589832 | tf_op jit(solution)/shard_map/ppermute | solution.py:405
  18.5 10.9 %collective-permute-start.4 = (bf16[32,1024]{1,0:T(8,128)(2,1)S(1)}, bf16[32,1024]{1,0:T(8,128)(2,1)S(1)}, u32[]{:S(2)}, u32[]{:S(2)}) collective-permute-start(bf16[32,1024]{1,0:T(8,128)(2,1)S(1)} %get-tuple-element.40), channel_id=1, source_target_pairs={{0,16},{2,18},{4,20},{6,22},{8,24},{10,26},{12,28},{14,30},{16,0},... | collective-permute-start | bytes 196616 | tf_op jit(solution)/shard_map/ppermute | solution.py:405
  36.6 1.2 %collective-permute-start.6 = (f32[1,2176]{1,0:T(1,128)S(1)}, f32[1,2176]{1,0:T(1,128)S(1)}, u32[]{:S(2)}, u32[]{:S(2)}) collective-permute-start(f32[1,2176]{1,0:T(1,128)S(1)} %get-tuple-element.43.mine), channel_id=1, source_target_pairs={{0,1},{1,0},{2,3},{3,2},{4,5},{5,4},{6,7},{7,6},{8,9},{9,8},{10,11... | collective-permute-start | bytes 26120 | tf_op jit(solution)/shard_map/ppermute | solution.py:405

commit v5 on v4

--- a/solution.py
+++ b/solution.py
@@ -44,10 +44,6 @@
 
 def bits(octant):
     return octant % 2, octant // 2 % 2, octant // 4
-
-
-def touching(distance):
-    return distance & (distance + 1) == 0
 
 
 def leaf_slot(octant):
@@ -136,8 +132,8 @@
     return copies
 
 
-def pack_kernel(count_in, positions_in, density_in, shift_in, own, basis, moments, totals, *rest):
-    payloads, (count, positions, density, shift, mono, sems) = rest[:3], rest[3:]
+def pack_kernel(count_in, positions_in, density_in, shift_in, own, basis, moments, payload, *rest):
+    count, positions, density, shift, mono, sems = rest
     copies = fetch(
         [(count_in, count), (positions_in, positions), (density_in, density), (shift_in, shift)], sems
     )
@@ -184,14 +180,12 @@
     moments[...] = moment
     total = dot(moment, shift[...]) + dot(rest, shift[...])
     total = jnp.concatenate(high_low(total), axis=1)
-    totals[...] = total
-    payloads[1][...] = total
-    for distance, payload in ((1, payloads[0]), (3, payloads[2])):
-        bit = jnp.where((box_x ^ distance) > box_x, 1, 0)
+    for box in range(ACROSS):
+        bit = jnp.where(box > box_x, 1, 0)
         for place in range(4):
-            payload[:, lanes(place * pts, pts)] = own[:, lanes((bit + 2 * place) * pts, pts)]
-        payload[:, lanes(4 * pts, LEAVES)] = moment
-        payload[:, lanes(4 * pts + LEAVES, 2 * SLOT)] = total
+            payload[box, :, lanes(place * pts, pts)] = own[:, lanes((bit + 2 * place) * pts, pts)]
+        payload[box, :, lanes(4 * pts, LEAVES)] = moment
+        payload[box, :, lanes(4 * pts + LEAVES, 2 * SLOT)] = total
 
 
 def features(held, start, size, centre, target):
@@ -229,8 +223,8 @@
 def pulled(total, wanted, source, masses, starts, pts):
     for start in starts:
         place = lanes(start, pts)
-        kernel = lax.rsqrt(dot(source[place, :], wanted))
-        total = total + dot(masses[:, place], low_bits(kernel))
+        kernel = lax.rsqrt(low_bits(dot(source[place, :], wanted)))
+        total = total + dot(masses[:, place], kernel)
     return total
 
 
@@ -254,19 +248,22 @@
         copy.wait()
 
 
-def row_kernel(depth, own, moments, totals, from_1, from_2, from_3, far, nodes, spread, *rest):
-    left, right, own_local, *payloads = rest
+def row_kernel(depth, own, moments, received, far, nodes, spread, left, right, given, faces_even, faces_odd):
     points = own.shape[1]
     pts = points // 8
     box_x, box_z = box_place()
     wide = 4 * pts + LEAVES
     for side, step in ((left, -1), (right, 1)):
-        side[...] = jnp.zeros(side.shape, side.dtype)
-        for distance, held in ((1, from_1), (3, from_3)):
-
-            @pl.when((box_x ^ distance) - box_x == step)
-            def _(side=side, held=held):
-                side[...] = held[:, lanes(0, wide)]
+        neighbour = box_x + step
+        inside = (neighbour >= 0) & (neighbour < ACROSS)
+
+        @pl.when(inside)
+        def _(side=side, neighbour=neighbour):
+            side[...] = received[neighbour, :, lanes(0, wide)]
+
+        @pl.when(jnp.logical_not(inside))
+        def _(side=side):
+            side[...] = jnp.zeros(side.shape, side.dtype)
 
     base = 4 * pts
     row = jnp.concatenate([left[:, lanes(base, LEAVES)], moments[...], right[:, lanes(base, LEAVES)]], axis=1)
@@ -275,17 +272,17 @@
     down = dot(row, far[above_rows, :])
     same = dot(jnp.concatenate([row[:, :LEAVES], row[:, 2 * LEAVES :]], axis=1), far[same_rows, :])
 
-    boxes = [totals[...], from_1[:, lanes(wide, 2 * SLOT)], from_2[...], from_3[:, lanes(wide, 2 * SLOT)]]
+    boxes = [received[box, :, lanes(wide, 2 * SLOT)] for box in range(ACROSS)]
     boxes_high = jnp.concatenate([held[:, :SLOT] for held in boxes], axis=1)
     boxes_low = jnp.concatenate([held[:, SLOT:] for held in boxes], axis=1)
     columns = []
-    for distance_z in range(depth):
-        gap_z = 2 * ((box_z ^ distance_z) - box_z)
+    for layer in range(depth):
+        gap_z = 2 * (layer - box_z)
         across_z = nodes[2] + gap_z.astype(jnp.float32)
         rest_z = across_z * across_z + nodes[1]
         blocks = []
-        for distance_x in range(ACROSS):
-            gap_x = 2 * (box_x - (box_x ^ distance_x))
+        for box in range(ACROSS):
+            gap_x = 2 * (box_x - box)
             across_x = nodes[0] + gap_x.astype(jnp.float32)
             distant = jnp.maximum(jnp.abs(gap_x), jnp.abs(gap_z)) >= 4
             blocks.append(lax.rsqrt(across_x * across_x + rest_z) * jnp.where(distant, 1.0 / COEFFS, 0.0))
@@ -295,27 +292,22 @@
     coarse = jnp.concatenate([coarse[:, d * SLOT : (d + 1) * SLOT] for d in range(depth)], axis=0)
     coarse_high, coarse_low = high_low(coarse)
     coarse = dot(coarse_high, spread[...]) + dot(coarse_low, spread[...])
-
-    own_local[...] = same + coarse[:ROWS]
-    for distance in range(1, depth):
-        payload = payloads[distance - 1]
-        gap = (box_z ^ distance) - box_z
-        given = coarse[distance * ROWS : (distance + 1) * ROWS]
-        if touching(distance):
-            given = given + jnp.where(gap == 1, up, 0.0) + jnp.where(gap == -1, down, 0.0)
-            bit = jnp.where(gap > 0, 1, 0)
-            for y in range(2):
-                for x in range(4):
-                    place = lanes((4 * y + x) * pts, pts)
-                    if x in (0, 3):
-                        side = left if x == 0 else right
-                        payload[:, place] = side[:, lanes((y + 2 * bit) * pts, pts)]
-                    else:
-                        payload[:, place] = own[:, lanes((x - 1 + 2 * y + 4 * bit) * pts, pts)]
-        start = payload.shape[1] - 2 * LEAVES
-        given_high, given_low = high_low(given)
-        payload[:, lanes(start, LEAVES)] = given_high
-        payload[:, lanes(start + LEAVES, LEAVES)] = given_low
+    kept = given.shape[1]
+    for layer in range(depth):
+        gap = layer - box_z
+        value = coarse[layer * ROWS : layer * ROWS + kept]
+        value = value + jnp.where(gap == 0, same[:kept], jnp.where(gap == 1, up[:kept], jnp.where(gap == -1, down[:kept], 0.0)))
+        given[layer] = value
+    odd = lax.rem(box_z, 2)
+    for faces, bit in ((faces_even, 1 - odd), (faces_odd, odd)):
+        for y in range(2):
+            for x in range(4):
+                place = lanes((4 * y + x) * pts, pts)
+                if x in (0, 3):
+                    side = left if x == 0 else right
+                    faces[:, place] = side[:, lanes((y + 2 * bit) * pts, pts)]
+                else:
+                    faces[:, place] = own[:, lanes((x - 1 + 2 * y + 4 * bit) * pts, pts)]
 
 
 def side_kernel(own, left, right, half, source, target, near, sides):
@@ -343,21 +335,24 @@
         lax.fori_loop(0, 2, layer, 0)
 
 
-def last_kernel(depth, count_in, weights_in, near, target, basis, own_local, *rest):
-    received, rest = rest[: depth - 1], rest[depth - 1 :]
+def last_kernel(depth, count_in, weights_in, near, target, basis, given, faces_even, faces_odd, *rest):
     potential, sums, held, sides, total, count, weights, sems = rest
     copies = fetch([(count_in, count), (weights_in, weights)], sems)
     fields, points = potential.shape
     pts = points // 8
     _, box_z = box_place()
     for step in range(2):
-        held[...] = jnp.zeros(held.shape, held.dtype)
-        for distance in range(1, depth):
-            if touching(distance):
-
-                @pl.when((box_z ^ distance) - box_z == 2 * step - 1)
-                def _(block=received[distance - 1]):
-                    held[...] = block[:, lanes(0, points)]
+        odd = lax.rem(box_z, 2)
+        inside = (box_z + 2 * step - 1 >= 0) & (box_z + 2 * step - 1 < depth)
+        for faces, parity in ((faces_even, 1 - step), (faces_odd, step)):
+
+            @pl.when(inside & (odd == parity))
+            def _(faces=faces):
+                held[...] = faces[...]
+
+        @pl.when(jnp.logical_not(inside))
+        def _():
+            held[...] = jnp.zeros(held.shape, held.dtype)
 
         for place in range(8):
             centre = (place % 4 - 1.5, place // 4 - 0.5, 1.5 if step else -1.5)
@@ -371,12 +366,9 @@
 
         lax.fori_loop(0, 2, pair, 0)
 
-    local = own_local[...]
-    for distance in range(1, depth):
-        block = received[distance - 1]
-        start = block.shape[1] - 2 * LEAVES
-        local = local + block[:, lanes(start, LEAVES)].astype(jnp.float32)
-        local = local + block[:, lanes(start + LEAVES, LEAVES)].astype(jnp.float32)
+    local = given[0]
+    for layer in range(1, depth):
+        local = local + given[layer]
     local_high, local_low = high_low(local)
     for copy in copies:
         copy.wait()
@@ -388,7 +380,7 @@
         slot = slice(leaf * SLOT, (leaf + 1) * SLOT)
         left = jnp.concatenate([local_high[:, slot], local_high[:, slot]], axis=1)
         far_part = dot(left, basis[:, here]) + dot(local_low[:, slot], basis[0:SLOT, here])
-        value = (total[:, lanes(leaf_slot(leaf) * pts, pts)] + far_part)[:fields]
+        value = total[0:fields, lanes(leaf_slot(leaf) * pts, pts)] + far_part[:fields]
         value = jnp.where(lane_index < count[leaf], value * coupling, 0.0)
         potential[:, here] = value
         sums[:, here] = jnp.sum(value * column, axis=0, keepdims=True)
@@ -402,7 +394,12 @@
 
 
 def swapped(block, axis, partner):
-    return lax.ppermute(block, axis, [(i, partner(i)) for i in range(lax.axis_size(axis))])
+    size = lax.axis_size(axis)
+    return lax.ppermute(block, axis, [(partner(i), i) for i in range(size) if 0 <= partner(i) < size])
+
+
+def traded(slots, groups):
+    return lax.all_to_all(slots, "space", 0, 0, axis_index_groups=groups, tiled=True)
 
 
 def per_device(positions, density, leaf_count, sigma_weights):
@@ -425,7 +422,7 @@
     half, full = jnp.bfloat16, jnp.float32
     shift = shift_table()
     face = 4 * pts + LEAVES + 2 * SLOT
-    own, basis, moments, totals, *given = call(
+    own, basis, moments, payload = call(
         pack_kernel,
         "pack",
         [hbm] * 4,
@@ -433,10 +430,7 @@
             ((ROWS, points), half),
             ((2 * SLOT, points), half),
             ((ROWS, LEAVES), half),
-            ((ROWS, 2 * SLOT), half),
-            ((ROWS, face), half),
-            ((ROWS, 2 * SLOT), half),
-            ((ROWS, face), half),
+            ((ACROSS, ROWS, face), half),
         ],
         [
             pltpu.SMEM((8,), jnp.int32),
@@ -451,9 +445,7 @@
         density,
         jnp.asarray(shift, half),
     )
-    from_2 = swapped(given[1], "space", lambda i: i ^ 2)
-    from_3 = swapped(given[2], "space", lambda i: i ^ 3)
-    from_1 = swapped(given[0], "space", lambda i: i ^ 1)
+    received = traded(payload, [[z * ACROSS + x for x in range(ACROSS)] for z in range(depth)])
     near, source, target, far, nodes, spread = call(
         own_kernel,
         "near_own",
@@ -472,26 +464,28 @@
         jnp.asarray(box_nodes()),
         jnp.asarray(shift.T.copy(), half),
     )
-    widths = [(points if touching(d) else 0) + 2 * LEAVES for d in range(1, depth)]
-    left, right, own_local, *given = call(
+    left, right, given, faces_even, faces_odd = call(
         functools.partial(row_kernel, depth),
         "row",
-        [vmem] * 9,
-        [((ROWS, 4 * pts + LEAVES), half)] * 2 + [((ROWS, LEAVES), full)] + [((ROWS, w), half) for w in widths],
+        [vmem] * 6,
+        [
+            ((ROWS, 4 * pts + LEAVES), half),
+            ((ROWS, 4 * pts + LEAVES), half),
+            ((depth, 24, LEAVES), full),
+            ((ROWS, points), half),
+            ((ROWS, points), half),
+        ],
         [],
         own,
         moments,
-        totals,
-        from_1,
-        from_2,
-        from_3,
+        received,
         far,
         nodes,
         spread,
     )
-    received = [None] * (depth - 1)
-    for d in sorted(range(1, depth), key=lambda d: (touching(d), -d)):
-        received[d - 1] = swapped(given[d - 1], "space", lambda i: i ^ (ACROSS * d))
+    given = traded(given, [[z * ACROSS + x for z in range(depth)] for x in range(ACROSS)])
+    faces_even = swapped(faces_even, "space", lambda i: i ^ ACROSS)
+    faces_odd = swapped(faces_odd, "space", lambda i: i + ACROSS if i // ACROSS % 2 else i - ACROSS)
     near, = call(
         side_kernel,
         "near_side",
@@ -508,7 +502,7 @@
     potential, sums = call(
         functools.partial(last_kernel, depth),
         "near_rows",
-        [hbm] * 2 + [vmem] * (4 + len(received)),
+        [hbm] * 2 + [vmem] * 6,
         [((fields, points), full), ((1, points + 128), full)],
         [
             pltpu.VMEM((ROWS, points), half),
@@ -523,8 +517,9 @@
         near,
         target,
         basis,
-        own_local,
-        *received,
+        given,
+        faces_even,
+        faces_odd,
     )
     if lax.axis_size("sig") == 2:
         other = swapped(sums, "sig", lambda i: i ^ 1)

time: 38.7 us -> 47 us (1.21)
  the two profiles are of different devices: /device:TPU:0 before, /device:TPU:9 now
where the time goes in v5:
time: 47 us; the launch traced here: 46.6 us
  Pallas kernels  25.2 us (54%)
  starting transfers between devices  15.5 us (33%)
  local copies, waits for them, and re-layouts  4.13 us (9%)
  waiting for transfers between devices  1.06 us (2%)
  between operations  0.71 us (2%)
    pallas_call x6, Pallas kernels, call(): pl.pallas_call(kernel, in_specs=in_specs, out_specs=[vmem] * len(outs), o...  25.2 us
    all_to_all x2, starting transfers between devices, traded(): lax.all_to_all(slots, 'space', 0, 0, axis_index_groups=groups, tiled=True)  8.23 us
    ppermute x3, starting transfers between devices, swapped(): lax.ppermute(block, axis, [(partner(i), i) for i in range(size) if 0 <= p...  7.27 us
    unnamed x4, local copies, waits for them, and re-layouts  4.13 us
  transfers between devices with their start and end apart: 5, of which 2 were waited for; matrix products, arithmetic and copies ran while one was open for 0% of the time, Pallas kernels for 25%

profile of v5, /device:TPU:9, one launch (start us, length us, event | category | flops | bytes accessed | tf_op | source)
XLA Modules:
  0.0 46.6 jit_solution(12410609202682418569)
XLA Ops:
  0.6 3.8 %pack.1 = (bf16[32,2048]{1,0:T(8,128)(2,1)S(1)}, bf16[128,2048]{1,0:T(8,128)(2,1)S(1)}, bf16[32,512]{1,0:T(8,128)(2,1)S(1)}, bf16[4,32,1664]{2,1,0:T(8,128)(2,1)}) custom-call(s32[8]{0:T(128)} %count_in.3, f32[3,2048]{1,0:T(4,128)} %positions_in.1, bf16[17,2048]{1,0:T(8,128)(2,1)} %density_in.1, bf16[512,64]{1,0:T(8,128)(2,1)} %constant.8.clone.shift_in), custom_call_target="tpu_custom_call" | custom-call | tf_op jit(solution)/shard_map/pack/pallas_call | solution.py:412
  4.5 3.5 %all-to-all-start = ((bf16[4,32,1664]{2,1,0:T(8,128)(2,1)}), bf16[4,32,1664]{2,1,0:T(8,128)(2,1)S(1)}, u32[]{:S(2)}, u32[]{:S(2)}) async-start(bf16[4,32,1664]{2,1,0:T(8,128)(2,1)} %get-tuple-element.21), calls=%async_computation | async-start | bytes 851968 | tf_op jit(solution)/shard_map/all_to_all | solution.py:402
  7.9 3.9 %near_own.1 = (f32[32,1024]{1,0:T(8,128)S(1)}, bf16[2048,48]{1,0:T(8,128)(2,1)S(1)}, bf16[48,2048]{1,0:T(8,128)(2,1)S(1)}, bf16[4096,512]{1,0:T(8,128)(2,1)S(1)}...) custom-call(bf16[32,2048]{1,0:T(8,128)(2,1)S(1)} %get-tuple-element.19.own, ...), custom_call_target="tpu_custom_call" | custom-call | tf_op jit(solution)/shard_map/near_own/pallas_call | solution.py:412
  11.8 0.0 copy-start
  11.9 1.9 %copy-done = bf16[4096,512]{1,0:T(8,128)(2,1)} copy-done((bf16[4096,512]{1,0:T(8,128)(2,1)}, bf16[4096,512]{1,0:T(8,128)(2,1)S(1)}, u32[]{:S(2)}) %copy-start) | copy-done | bytes 4194328
  13.8 0.2 all-to-all-done.received
  14.0 0.0 copy-start.1
  14.0 2.2 %copy-done.1 = bf16[4096,512]{1,0:T(8,128)(2,1)S(1)} copy-done((bf16[4096,512]{1,0:T(8,128)(2,1)S(1)}, bf16[4096,512]{1,0:T(8,128)(2,1)}, u32[]{:S(2)}) %copy-start.1) | copy-done | bytes 4194328
  16.2 1.9 %row.1 = (bf16[32,1536]{1,0:T(8,128)(2,1)S(1)}, bf16[32,1536]{1,0:T(8,128)(2,1)S(1)}, f32[4,24,512]{2,1,0:T(8,128)}, bf16[32,2048]{1,0:T(8,128)(2,1)S(1)}, bf16[32,2048]{1,0:T(8,128)(2,1)S(1)}) custom-call(bf16[32,2048]{1,0:T(8,128)(2,1)S(1)} %get-tuple-element.19.own, bf16[32,512]{1,0:T(8,128)(2,1)S(1)} %get-tuple-element.20.moments, ...), custom_call_target="tpu_custom_call" | custom-call | tf_op jit(solution)/shard_map/row/pallas_call | solution.py:412
  18.1 4.8 %all-to-all-start.1 = ((f32[4,24,512]{2,1,0:T(8,128)}), f32[4,24,512]{2,1,0:T(8,128)S(1)}, u32[]{:S(2)}, u32[]{:S(2)}) async-start(f32[4,24,512]{2,1,0:T(8,128)} %get-tuple-element.31), calls=%async_computation.1 | async-start | bytes 393216 | tf_op jit(solution)/shard_map/all_to_all | solution.py:402
  22.9 0.0 collective-permute-start
  22.9 4.2 %collective-permute-start.1 = (bf16[32,2048]{1,0:T(8,128)(2,1)S(1)}, bf16[32,2048]{1,0:T(8,128)(2,1)S(1)}, u32[]{:S(2)}, u32[]{:S(2)}) collective-permute-start(bf16[32,2048]{1,0:T(8,128)(2,1)S(1)} %get-tuple-element.33), channel_id=1, source_target_pairs={{16,8},{18,10},{20,12},{22,14},{8,16},{10,18},{12,20},{14,22},{17,... | collective-permute-start | bytes 393224 | tf_op jit(solution)/shard_map/ppermute | solution.py:398
  27.2 7.7 %near_side.1.near = f32[32,2048]{1,0:T(8,128)S(1)} custom-call(bf16[32,2048]{1,0:T(8,128)(2,1)S(1)} %get-tuple-element.19.own, bf16[32,1536]{1,0:T(8,128)(2,1)S(1)} %get-tuple-element.25.left, bf16[32,1536]{1,0:T(8,128)(2,1)S(1)} %get-tuple-element.26.right, f32[32,1024]{1,0:T(8,128)S(1)} %get-tuple-element.27.half, ...), custom_call_target="tpu_custom_call" | custom-call | tf_op jit(solution)/shard_map/near_side/pallas_call | solution.py:412
  34.9 0.0 collective-permute-done.faces_even
  34.9 0.0 collective-permute-done.1.faces_odd
  34.9 0.0 all-to-all-done.1.given
  34.9 7.2 %near_rows.1 = (f32[17,2048]{1,0:T(8,128)}, f32[1,2176]{1,0:T(1,128)S(1)}) custom-call(s32[8]{0:T(128)} %count_in.3, f32[17]{0:T(128)} %weights_in.1, f32[32,2048]{1,0:T(8,128)S(1)} %near_side.1.near, bf16[48,2048]{1,0:T(8,128)(2,1)S(1)} %get-tuple-element.29.target, bf16[128,2048]{1,0:T(8,128)(2,1)S(1)} %get-tuple-element.30.basis, ...), custom_call_target="tpu_custom_call" | custom-call | tf_op jit(solution)/shard_map/near_rows/pallas_call | solution.py:412
  42.1 3.0 %collective-permute-start.2 = (f32[1,2176]{1,0:T(1,128)S(1)}, f32[1,2176]{1,0:T(1,128)S(1)}, u32[]{:S(2)}, u32[]{:S(2)}) collective-permute-start(f32[1,2176]{1,0:T(1,128)S(1)} %get-tuple-element.35.mine), channel_id=1, source_target_pairs={{1,0},{0,1},{3,2},{2,3},{5,4},{4,5},{7,6},{6,7},{9,8},{8,9},{11,10... | collective-permute-start | bytes 26120 | tf_op jit(solution)/shard_map/ppermute | solution.py:398
  45.1 0.8 %collective-permute-done.2.other = f32[1,2176]{1,0:T(1,128)S(1)} collective-permute-done((f32[1,2176]{1,0:T(1,128)S(1)}, f32[1,2176]{1,0:T(1,128)S(1)}, u32[]{:S(2)}, u32[]{:S(2)}) %collective-permute-start.2) | collective-permute-done | bytes 8736 | tf_op jit(solution)/shard_map/ppermute | solution.py:398
  46.0 0.7 %mean.1 = f32[1,2048]{1,0:T(1,128)} custom-call(f32[1,2176]{1,0:T(1,128)S(1)} %get-tuple-element.35.mine, f32[1,2176]{1,0:T(1,128)S(1)} %collective-permute-done.2.other), custom_call_target="tpu_custom_call" | custom-call | tf_op jit(solution)/shard_map/mean/pallas_call | solution.py:412
Async XLA Ops:
  4.5 9.5 %all-to-all-start = ((bf16[4,32,1664]{2,1,0:T(8,128)(2,1)}), bf16[4,32,1664]{2,1,0:T(8,128)(2,1)S(1)}, u32[]{:S(2)}, u32[]{:S(2)}) async-start(bf16[4,32,1664]{2,1,0:T(8,128)(2,1)} %get-tuple-element.21), calls=%async_computation | async-start | bytes 851968 | tf_op jit(solution)/shard_map/all_to_all | solution.py:402
  11.8 2.0 %copy-start = (bf16[4096,512]{1,0:T(8,128)(2,1)}, bf16[4096,512]{1,0:T(8,128)(2,1)S(1)}, u32[]{:S(2)}) copy-start(bf16[4096,512]{1,0:T(8,128)(2,1)S(1)} %get-tuple-element.22.far) | copy-start | bytes 12582916
  14.0 2.2 %copy-start.1 = (bf16[4096,512]{1,0:T(8,128)(2,1)S(1)}, bf16[4096,512]{1,0:T(8,128)(2,1)}, u32[]{:S(2)}) copy-start(bf16[4096,512]{1,0:T(8,128)(2,1)} %copy-done) | copy-start | bytes 12582916
  18.1 16.8 %all-to-all-start.1 = ((f32[4,24,512]{2,1,0:T(8,128)}), f32[4,24,512]{2,1,0:T(8,128)S(1)}, u32[]{:S(2)}, u32[]{:S(2)}) async-start(f32[4,24,512]{2,1,0:T(8,128)} %get-tuple-element.31), calls=%async_computation.1 | async-start | bytes 393216 | tf_op jit(solution)/shard_map/all_to_all | solution.py:402
  22.9 12.0 %collective-permute-start = (bf16[32,2048]{1,0:T(8,128)(2,1)S(1)}, bf16[32,2048]{1,0:T(8,128)(2,1)S(1)}, u32[]{:S(2)}, u32[]{:S(2)}) collective-permute-start(bf16[32,2048]{1,0:T(8,128)(2,1)S(1)} %get-tuple-element.32), channel_id=1, source_target_pairs={{8,0},{10,2},{12,4},{14,6},{0,8},{2,10},{4,12},{6,14},{24,16},{26,... | collective-permute-start | bytes 393224 | tf_op jit(solution)/shard_map/ppermute | solution.py:398
  22.9 12.0 %collective-permute-start.1 = (bf16[32,2048]{1,0:T(8,128)(2,1)S(1)}, bf16[32,2048]{1,0:T(8,128)(2,1)S(1)}, u32[]{:S(2)}, u32[]{:S(2)}) collective-permute-start(bf16[32,2048]{1,0:T(8,128)(2,1)S(1)} %get-tuple-element.33), channel_id=1, source_target_pairs={{16,8},{18,10},{20,12},{22,14},{8,16},{10,18},{12,20},{14,22},{17,... | collective-permute-start | bytes 393224 | tf_op jit(solution)/shard_map/ppermute | solution.py:398
  42.1 3.8 %collective-permute-start.2 = (f32[1,2176]{1,0:T(1,128)S(1)}, f32[1,2176]{1,0:T(1,128)S(1)}, u32[]{:S(2)}, u32[]{:S(2)}) collective-permute-start(f32[1,2176]{1,0:T(1,128)S(1)} %get-tuple-element.35.mine), channel_id=1, source_target_pairs={{1,0},{0,1},{3,2},{2,3},{5,4},{4,5},{7,6},{6,7},{9,8},{8,9},{11,10... | collective-permute-start | bytes 26120 | tf_op jit(solution)/shard_map/ppermute | solution.py:398

commit v6 on v4

--- a/solution.py
+++ b/solution.py
@@ -226,12 +226,19 @@
     return low_bits(jnp.transpose(features(held, start, size, centre, False)))
 
 
-def pulled(total, wanted, source, masses, starts, pts):
-    for start in starts:
-        place = lanes(start, pts)
-        kernel = lax.rsqrt(dot(source[place, :], wanted))
-        total = total + dot(masses[:, place], low_bits(kernel))
-    return total
+def pulled(near, index, width, target, source, masses, starts, size, first=None):
+    pair = target.shape[1] // 4
+    for piece in range(0, pair, width):
+        here = lanes(index * pair + piece, width)
+        wanted = target[:, here]
+        total = jnp.zeros((ROWS, width), jnp.float32) if first is None else first[:, here]
+        ahead = dot(source[lanes(starts[0], size), :], wanted)
+        for place, start in enumerate(starts):
+            square = ahead
+            if place + 1 < len(starts):
+                ahead = dot(source[lanes(starts[place + 1], size), :], wanted)
+            total = total + dot(masses[:, lanes(start, size)], low_bits(lax.rsqrt(square)))
+        near[:, here] = total
 
 
 def own_kernel(own, far_in, nodes_in, spread_in, near, source, target, far, nodes, spread, sems):
@@ -244,9 +251,7 @@
         target[:, lanes(leaf_slot(leaf) * pts, pts)] = low_bits(features(own, leaf * pts, pts, centre, True))
 
     def group(index, carry):
-        here = lanes(index * (2 * pts), 2 * pts)
-        zero = jnp.zeros((ROWS, 2 * pts), jnp.float32)
-        near[:, here] = pulled(zero, target[:, here], source, own, [leaf * pts for leaf in range(8)], pts)
+        pulled(near, index, 2 * pts, target, source, own, [leaf * pts for leaf in range(8)], pts)
         return carry
 
     lax.fori_loop(0, 2, group, 0)
@@ -255,7 +260,7 @@
 
 
 def row_kernel(depth, own, moments, totals, from_1, from_2, from_3, far, nodes, spread, *rest):
-    left, right, own_local, *payloads = rest
+    left, right, own_local, faces_even, faces_odd, *distant = rest
     points = own.shape[1]
     pts = points // 8
     box_x, box_z = box_place()
@@ -287,8 +292,8 @@
         for distance_x in range(ACROSS):
             gap_x = 2 * (box_x - (box_x ^ distance_x))
             across_x = nodes[0] + gap_x.astype(jnp.float32)
-            distant = jnp.maximum(jnp.abs(gap_x), jnp.abs(gap_z)) >= 4
-            blocks.append(lax.rsqrt(across_x * across_x + rest_z) * jnp.where(distant, 1.0 / COEFFS, 0.0))
+            apart = jnp.maximum(jnp.abs(gap_x), jnp.abs(gap_z)) >= 4
+            blocks.append(lax.rsqrt(across_x * across_x + rest_z) * jnp.where(apart, 1.0 / COEFFS, 0.0))
         columns.append(jnp.concatenate(blocks, axis=0))
     columns = low_bits(jnp.concatenate(columns, axis=1))
     coarse = dot(boxes_high, columns) + dot(boxes_low, columns)
@@ -297,25 +302,26 @@
     coarse = dot(coarse_high, spread[...]) + dot(coarse_low, spread[...])
 
     own_local[...] = same + coarse[:ROWS]
-    for distance in range(1, depth):
-        payload = payloads[distance - 1]
-        gap = (box_z ^ distance) - box_z
-        given = coarse[distance * ROWS : (distance + 1) * ROWS]
+    sums = [coarse[distance * ROWS : (distance + 1) * ROWS] for distance in range(depth)]
+    for distance in range(2, depth):
+        distant[distance - 2][...] = sums[distance][: distant[0].shape[0]]
+    odd = lax.rem(box_z, 2)
+    beside = jnp.zeros_like(sums[0])
+    for distance in range(3, depth):
         if touching(distance):
-            given = given + jnp.where(gap == 1, up, 0.0) + jnp.where(gap == -1, down, 0.0)
-            bit = jnp.where(gap > 0, 1, 0)
-            for y in range(2):
-                for x in range(4):
-                    place = lanes((4 * y + x) * pts, pts)
-                    if x in (0, 3):
-                        side = left if x == 0 else right
-                        payload[:, place] = side[:, lanes((y + 2 * bit) * pts, pts)]
-                    else:
-                        payload[:, place] = own[:, lanes((x - 1 + 2 * y + 4 * bit) * pts, pts)]
-        start = payload.shape[1] - 2 * LEAVES
-        given_high, given_low = high_low(given)
-        payload[:, lanes(start, LEAVES)] = given_high
-        payload[:, lanes(start + LEAVES, LEAVES)] = given_low
+            beside = jnp.where(jnp.abs((box_z ^ distance) - box_z) == 1, sums[distance], beside)
+    for faces, bit, base in ((faces_even, 1 - odd, sums[1]), (faces_odd, odd, beside)):
+        for y in range(2):
+            for x in range(4):
+                place = lanes((2 * x + y) * pts, pts)
+                if x in (0, 3):
+                    side = left if x == 0 else right
+                    faces[:, place] = side[:, lanes((y + 2 * bit) * pts, pts)]
+                else:
+                    faces[:, place] = own[:, lanes((x - 1 + 2 * y + 4 * bit) * pts, pts)]
+        given_high, given_low = high_low(base + jnp.where(bit == 1, up, down))
+        faces[:, lanes(points, LEAVES)] = given_high
+        faces[:, lanes(points + LEAVES, LEAVES)] = given_low
 
 
 def side_kernel(own, left, right, half, source, target, near, sides):
@@ -323,9 +329,7 @@
     pts = points // 8
 
     def group(index, carry):
-        here = lanes(index * (2 * pts), 2 * pts)
-        zero = jnp.zeros((ROWS, 2 * pts), jnp.float32)
-        near[:, here] = pulled(zero, target[:, here], source, own, [leaf * pts for leaf in range(8)], pts)
+        pulled(near, index, pts, target, source, own, [leaf * pts for leaf in range(8)], pts)
         return carry
 
     near[:, lanes(0, 4 * pts)] = half[...]
@@ -336,47 +340,49 @@
             sides[lanes(place * pts, pts), :] = source_features(side, place * pts, pts, centre)
 
         def layer(index, carry, step=step, side=side):
-            here = lanes((step + 2 * index) * (2 * pts), 2 * pts)
-            near[:, here] = pulled(near[:, here], target[:, here], sides, side, [p * pts for p in range(4)], pts)
+            pulled(near, step + 2 * index, pts, target, sides, side, [p * pts for p in range(4)], pts, near)
             return carry
 
         lax.fori_loop(0, 2, layer, 0)
 
 
-def last_kernel(depth, count_in, weights_in, near, target, basis, own_local, *rest):
-    received, rest = rest[: depth - 1], rest[depth - 1 :]
+def last_kernel(depth, count_in, weights_in, near, target, basis, own_local, faces_even, faces_odd, *rest):
+    distant, rest = rest[: depth - 2], rest[depth - 2 :]
     potential, sums, held, sides, total, count, weights, sems = rest
     copies = fetch([(count_in, count), (weights_in, weights)], sems)
     fields, points = potential.shape
     pts = points // 8
     _, box_z = box_place()
     for step in range(2):
-        held[...] = jnp.zeros(held.shape, held.dtype)
-        for distance in range(1, depth):
-            if touching(distance):
-
-                @pl.when((box_z ^ distance) - box_z == 2 * step - 1)
-                def _(block=received[distance - 1]):
-                    held[...] = block[:, lanes(0, points)]
+        odd = lax.rem(box_z, 2)
+        inside = (box_z + 2 * step - 1 >= 0) & (box_z + 2 * step - 1 < depth)
+        for faces, parity in ((faces_even, 1 - step), (faces_odd, step)):
+
+            @pl.when(inside & (odd == parity))
+            def _(faces=faces):
+                held[...] = faces[:, lanes(0, points)]
+
+        @pl.when(jnp.logical_not(inside))
+        def _():
+            held[...] = jnp.zeros(held.shape, held.dtype)
 
         for place in range(8):
-            centre = (place % 4 - 1.5, place // 4 - 0.5, 1.5 if step else -1.5)
+            centre = (place // 2 - 1.5, place % 2 - 0.5, 1.5 if step else -1.5)
             sides[lanes(place * pts, pts), :] = source_features(held, place * pts, pts, centre)
 
         def pair(index, carry, step=step):
-            here = lanes((index + 2 * step) * (2 * pts), 2 * pts)
-            starts = [(4 * y + x + index) * pts for y in range(2) for x in range(3)]
-            total[:, here] = pulled(near[:, here], target[:, here], sides, held, starts, pts)
+            starts = [(2 * x + 2 * index) * pts for x in range(3)]
+            pulled(total, index + 2 * step, pts, target, sides, held, starts, 2 * pts, near)
             return carry
 
         lax.fori_loop(0, 2, pair, 0)
 
     local = own_local[...]
-    for distance in range(1, depth):
-        block = received[distance - 1]
-        start = block.shape[1] - 2 * LEAVES
-        local = local + block[:, lanes(start, LEAVES)].astype(jnp.float32)
-        local = local + block[:, lanes(start + LEAVES, LEAVES)].astype(jnp.float32)
+    for faces in (faces_even, faces_odd):
+        local = local + faces[:, lanes(points, LEAVES)].astype(jnp.float32)
+        local = local + faces[:, lanes(points + LEAVES, LEAVES)].astype(jnp.float32)
+    for block in distant:
+        local = local + jnp.concatenate([block[...], jnp.zeros((ROWS - block.shape[0], LEAVES), jnp.float32)], axis=0)
     local_high, local_low = high_low(local)
     for copy in copies:
         copy.wait()
@@ -402,7 +408,13 @@
 
 
 def swapped(block, axis, partner):
-    return lax.ppermute(block, axis, [(i, partner(i)) for i in range(lax.axis_size(axis))])
+    size = lax.axis_size(axis)
+    return lax.ppermute(block, axis, [(partner(i), i) for i in range(size) if 0 <= partner(i) < size])
+
+
+def across_layers(block, distance):
+    pairs = [(i, i ^ (ACROSS * distance)) for i in range(lax.axis_size("space"))]
+    return lax.ppermute(block, "space", [pair for pair in pairs if abs(pair[0] - pair[1]) > ACROSS])
 
 
 def per_device(positions, density, leaf_count, sigma_weights):
@@ -472,12 +484,14 @@
         jnp.asarray(box_nodes()),
         jnp.asarray(shift.T.copy(), half),
     )
-    widths = [(points if touching(d) else 0) + 2 * LEAVES for d in range(1, depth)]
-    left, right, own_local, *given = call(
+    left, right, own_local, faces_even, faces_odd, *distant = call(
         functools.partial(row_kernel, depth),
         "row",
         [vmem] * 9,
-        [((ROWS, 4 * pts + LEAVES), half)] * 2 + [((ROWS, LEAVES), full)] + [((ROWS, w), half) for w in widths],
+        [((ROWS, 4 * pts + LEAVES), half)] * 2
+        + [((ROWS, LEAVES), full)]
+        + [((ROWS, points + 2 * LEAVES), half)] * 2
+        + [((24, LEAVES), full)] * (depth - 2),
         [],
         own,
         moments,
@@ -489,9 +503,9 @@
         nodes,
         spread,
     )
-    received = [None] * (depth - 1)
-    for d in sorted(range(1, depth), key=lambda d: (touching(d), -d)):
-        received[d - 1] = swapped(given[d - 1], "space", lambda i: i ^ (ACROSS * d))
+    distant = [across_layers(block, distance + 2) for distance, block in enumerate(distant)]
+    faces_even = swapped(faces_even, "space", lambda i: i ^ ACROSS)
+    faces_odd = swapped(faces_odd, "space", lambda i: i + ACROSS if i // ACROSS % 2 else i - ACROSS)
     near, = call(
         side_kernel,
         "near_side",
@@ -508,7 +522,7 @@
     potential, sums = call(
         functools.partial(last_kernel, depth),
         "near_rows",
-        [hbm] * 2 + [vmem] * (4 + len(received)),
+        [hbm] * 2 + [vmem] * (6 + len(distant)),
         [((fields, points), full), ((1, points + 128), full)],
         [
             pltpu.VMEM((ROWS, points), half),
@@ -524,7 +538,9 @@
         target,
         basis,
         own_local,
-        *received,
+        faces_even,
+        faces_odd,
+        *distant,
     )
     if lax.axis_size("sig") == 2:
         other = swapped(sums, "sig", lambda i: i ^ 1)

time: 38.7 us -> 39.6 us (1.023)
  starting transfers between devices: 8.81 us -> 15.6 us
  Pallas kernels: 23.6 us -> 19.6 us
  waiting for transfers between devices: 5.47 us -> 3.48 us
    ppermute x7 -> x8, starting transfers between devices: 8.81 us -> 15.6 us  [the longest x2 8.71 us: across_layers(): lax.ppermute(block, 'space', [pair for pair in pairs if abs(pair[0] - pai...]
    pallas_call x6, Pallas kernels: 23.6 us -> 19.6 us  [call(): pl.pallas_call(kernel, in_specs=in_specs, out_specs=[vmem] * len(outs), o...]
    ppermute x7 -> x8, waiting for transfers between devices: 5.47 us -> 3.48 us  [the longest x6 3.46 us: swapped(): lax.ppermute(block, axis, [(partner(i), i) for i in range(size) if 0 <= p...]
  transfers between devices with their start and end apart: 7 -> 8, of which waited for: 3 -> 3; matrix products, arithmetic and copies ran while one was open for 0% -> 0% of each run, Pallas kernels for 30% -> 23%
where the time goes in v6:
time: 39.6 us; the launch traced here: 39.3 us
  Pallas kernels  19.6 us (49%)
  starting transfers between devices  15.6 us (39%)
  waiting for transfers between devices  3.48 us (9%)
  between operations  0.71 us (2%)
    pallas_call x6, Pallas kernels, call(): pl.pallas_call(kernel, in_specs=in_specs, out_specs=[vmem] * len(outs), o...  19.6 us
    ppermute x2, starting transfers between devices, across_layers(): lax.ppermute(block, 'space', [pair for pair in pairs if abs(pair[0] - pai...  8.71 us
    ppermute x6, starting transfers between devices, swapped(): lax.ppermute(block, axis, [(partner(i), i) for i in range(size) if 0 <= p...  6.88 us
    ppermute x6, waiting for transfers between devices, swapped(): lax.ppermute(block, axis, [(partner(i), i) for i in range(size) if 0 <= p...  3.46 us
  transfers between devices with their start and end apart: 8, of which 3 were waited for; matrix products, arithmetic and copies ran while one was open for 0% of the time, Pallas kernels for 23%

profile of v6, /device:TPU:0, one launch (start us, length us, event | category | flops | bytes accessed | tf_op | source)
XLA Modules:
  0.0 39.3 jit_solution(332965875371659423)
XLA Ops:
  0.6 3.0 %pack.1 = (bf16[32,2048]{1,0:T(8,128)(2,1)S(1)}, bf16[128,2048]{1,0:T(8,128)(2,1)S(1)}, bf16[32,512]{1,0:T(8,128)(2,1)S(1)}, bf16[32,128]{1,0:T(8,128)(2,1)S(1)}...) custom-call(s32[8]{0:T(128)} %count_in.3, f32[3,2048]{1,0:T(4,128)} %positions_in.1, ...), custom_call_target="tpu_custom_call" | custom-call | tf_op jit(solution)/shard_map/pack/pallas_call | solution.py:427
  3.7 3.0 %collective-permute-start = (bf16[32,1664]{1,0:T(8,128)(2,1)S(1)}, bf16[32,1664]{1,0:T(8,128)(2,1)S(1)}, u32[]{:S(2)}, u32[]{:S(2)}) collective-permute-start(bf16[32,1664]{1,0:T(8,128)(2,1)S(1)} %get-tuple-element.27), channel_id=1, source_target_pairs={{2,0},{0,2},{6,4},{4,6},{10,8},{8,10},{14,12},{12,14},{18,16},{16,... | collective-permute-start | bytes 319496 | tf_op jit(solution)/shard_map/ppermute | solution.py:412
  6.7 1.5 %collective-permute-start.2 = (bf16[32,1664]{1,0:T(8,128)(2,1)S(1)}, bf16[32,1664]{1,0:T(8,128)(2,1)S(1)}, u32[]{:S(2)}, u32[]{:S(2)}) collective-permute-start(bf16[32,1664]{1,0:T(8,128)(2,1)S(1)} %get-tuple-element.29), channel_id=1, source_target_pairs={{6,0},{4,2},{2,4},{0,6},{14,8},{12,10},{10,12},{8,14},{22,16},{20,... | collective-permute-start | bytes 319496 | tf_op jit(solution)/shard_map/ppermute | solution.py:412
  8.2 0.1 collective-permute-start.1
  8.2 2.6 %near_own.1 = (f32[32,1024]{1,0:T(8,128)S(1)}, bf16[2048,48]{1,0:T(8,128)(2,1)S(1)}, bf16[48,2048]{1,0:T(8,128)(2,1)S(1)}, bf16[4096,512]{1,0:T(8,128)(2,1)S(1)}...) custom-call(bf16[32,2048]{1,0:T(8,128)(2,1)S(1)} %get-tuple-element.24.own, ...), custom_call_target="tpu_custom_call" | custom-call | tf_op jit(solution)/shard_map/near_own/pallas_call | solution.py:427
  10.9 1.1 %collective-permute-done.1.from_2 = bf16[32,128]{1,0:T(8,128)(2,1)S(1)} collective-permute-done((bf16[32,128]{1,0:T(8,128)(2,1)S(1)}, bf16[32,128]{1,0:T(8,128)(2,1)S(1)}, u32[]{:S(2)}, u32[]{:S(2)}) %collective-permute-start.1) | collective-permute-done | bytes 8224 | tf_op jit(solution)/shard_map/ppermute | solution.py:412
  11.9 0.0 collective-permute-done.from_1
  11.9 1.2 %collective-permute-done.2.from_3 = bf16[32,1664]{1,0:T(8,128)(2,1)S(1)} collective-permute-done((bf16[32,1664]{1,0:T(8,128)(2,1)S(1)}, bf16[32,1664]{1,0:T(8,128)(2,1)S(1)}, u32[]{:S(2)}, u32[]{:S(2)}) %collective-permute-start.2) | collective-permute-done | bytes 106528 | tf_op jit(solution)/shard_map/ppermute | solution.py:412
  13.2 1.4 %row.1 = (bf16[32,1536]{1,0:T(8,128)(2,1)S(1)}, bf16[32,1536]{1,0:T(8,128)(2,1)S(1)}, f32[32,512]{1,0:T(8,128)S(1)}, bf16[32,3072]{1,0:T(8,128)(2,1)S(1)}, bf16[...) custom-call(bf16[32,2048]{1,0:T(8,128)(2,1)S(1)} %get-tuple-element.24.own, ...), custom_call_target="tpu_custom_call" | custom-call | tf_op jit(solution)/shard_map/row/pallas_call | solution.py:427
  14.5 1.6 %collective-permute-start.3 = (bf16[32,3072]{1,0:T(8,128)(2,1)S(1)}, bf16[32,3072]{1,0:T(8,128)(2,1)S(1)}, u32[]{:S(2)}, u32[]{:S(2)}) collective-permute-start(bf16[32,3072]{1,0:T(8,128)(2,1)S(1)} %get-tuple-element.40), channel_id=1, source_target_pairs={{8,0},{10,2},{12,4},{14,6},{0,8},{2,10},{4,12},{6,14},{24,16},{26,... | collective-permute-start | bytes 589832 | tf_op jit(solution)/shard_map/ppermute | solution.py:412
  16.1 0.7 %collective-permute-start.4 = (bf16[32,3072]{1,0:T(8,128)(2,1)S(1)}, bf16[32,3072]{1,0:T(8,128)(2,1)S(1)}, u32[]{:S(2)}, u32[]{:S(2)}) collective-permute-start(bf16[32,3072]{1,0:T(8,128)(2,1)S(1)} %get-tuple-element.41), channel_id=1, source_target_pairs={{16,8},{18,10},{20,12},{22,14},{8,16},{10,18},{12,20},{14,22},{17,... | collective-permute-start | bytes 589832 | tf_op jit(solution)/shard_map/ppermute | solution.py:412
  16.8 3.9 %collective-permute-start.5 = (f32[24,512]{1,0:T(8,128)S(1)}, f32[24,512]{1,0:T(8,128)S(1)}, u32[]{:S(2)}, u32[]{:S(2)}) collective-permute-start(f32[24,512]{1,0:T(8,128)S(1)} %get-tuple-element.42), channel_id=1, source_target_pairs={{0,16},{2,18},{4,20},{6,22},{8,24},{10,26},{12,28},{14,30},{16,0},... | collective-permute-start | bytes 147464 | tf_op jit(solution)/shard_map/ppermute | solution.py:417
  20.7 4.8 %collective-permute-start.6 = (f32[24,512]{1,0:T(8,128)S(1)}, f32[24,512]{1,0:T(8,128)S(1)}, u32[]{:S(2)}, u32[]{:S(2)}) collective-permute-start(f32[24,512]{1,0:T(8,128)S(1)} %get-tuple-element.43), channel_id=1, source_target_pairs={{0,24},{2,26},{4,28},{6,30},{24,0},{26,2},{28,4},{30,6},{1,25},{3,... | collective-permute-start | bytes 147464 | tf_op jit(solution)/shard_map/ppermute | solution.py:417
  25.5 6.5 %near_side.1.near = f32[32,2048]{1,0:T(8,128)S(1)} custom-call(bf16[32,2048]{1,0:T(8,128)(2,1)S(1)} %get-tuple-element.24.own, bf16[32,1536]{1,0:T(8,128)(2,1)S(1)} %get-tuple-element.33.left, bf16[32,1536]{1,0:T(8,128)(2,1)S(1)} %get-tuple-element.34.right, f32[32,1024]{1,0:T(8,128)S(1)} %get-tuple-element.35.half, ...), custom_call_target="tpu_custom_call" | custom-call | tf_op jit(solution)/shard_map/near_side/pallas_call | solution.py:427
  32.0 0.0 collective-permute-done.5.rest_0_
  32.1 0.0 collective-permute-done.6.rest_1_
  32.1 0.0 collective-permute-done.3.faces_even
  32.1 0.0 collective-permute-done.4.faces_odd
  32.1 5.3 %near_rows.1 = (f32[17,2048]{1,0:T(8,128)}, f32[1,2176]{1,0:T(1,128)S(1)}) custom-call(s32[8]{0:T(128)} %count_in.3, f32[17]{0:T(128)} %weights_in.1, f32[32,2048]{1,0:T(8,128)S(1)} %near_side.1.near, bf16[48,2048]{1,0:T(8,128)(2,1)S(1)} %get-tuple-element.37.target, bf16[128,2048]{1,0:T(8,128)(2,1)S(1)} %get-tuple-element.38.basis, ...), custom_call_target="tpu_custom_call" | custom-call | tf_op jit(solution)/shard_map/near_rows/pallas_call | solution.py:427
  37.4 0.1 collective-permute-start.7
  37.5 1.2 %collective-permute-done.7.other = f32[1,2176]{1,0:T(1,128)S(1)} collective-permute-done((f32[1,2176]{1,0:T(1,128)S(1)}, f32[1,2176]{1,0:T(1,128)S(1)}, u32[]{:S(2)}, u32[]{:S(2)}) %collective-permute-start.7) | collective-permute-done | bytes 8736 | tf_op jit(solution)/shard_map/ppermute | solution.py:412
  38.7 0.7 %mean.1 = f32[1,2048]{1,0:T(1,128)} custom-call(f32[1,2176]{1,0:T(1,128)S(1)} %get-tuple-element.45.mine, f32[1,2176]{1,0:T(1,128)S(1)} %collective-permute-done.7.other), custom_call_target="tpu_custom_call" | custom-call | tf_op jit(solution)/shard_map/mean/pallas_call | solution.py:427
Async XLA Ops:
  3.7 8.2 %collective-permute-start = (bf16[32,1664]{1,0:T(8,128)(2,1)S(1)}, bf16[32,1664]{1,0:T(8,128)(2,1)S(1)}, u32[]{:S(2)}, u32[]{:S(2)}) collective-permute-start(bf16[32,1664]{1,0:T(8,128)(2,1)S(1)} %get-tuple-element.27), channel_id=1, source_target_pairs={{2,0},{0,2},{6,4},{4,6},{10,8},{8,10},{14,12},{12,14},{18,16},{16,... | collective-permute-start | bytes 319496 | tf_op jit(solution)/shard_map/ppermute | solution.py:412
  6.7 6.4 %collective-permute-start.2 = (bf16[32,1664]{1,0:T(8,128)(2,1)S(1)}, bf16[32,1664]{1,0:T(8,128)(2,1)S(1)}, u32[]{:S(2)}, u32[]{:S(2)}) collective-permute-start(bf16[32,1664]{1,0:T(8,128)(2,1)S(1)} %get-tuple-element.29), channel_id=1, source_target_pairs={{6,0},{4,2},{2,4},{0,6},{14,8},{12,10},{10,12},{8,14},{22,16},{20,... | collective-permute-start | bytes 319496 | tf_op jit(solution)/shard_map/ppermute | solution.py:412
  8.2 3.7 %collective-permute-start.1 = (bf16[32,128]{1,0:T(8,128)(2,1)S(1)}, bf16[32,128]{1,0:T(8,128)(2,1)S(1)}, u32[]{:S(2)}, u32[]{:S(2)}) collective-permute-start(bf16[32,128]{1,0:T(8,128)(2,1)S(1)} %get-tuple-element.28), channel_id=1, source_target_pairs={{4,0},{6,2},{0,4},{2,6},{12,8},{14,10},{8,12},{10,14},{20,16},{22,... | collective-permute-start | bytes 24584 | tf_op jit(solution)/shard_map/ppermute | solution.py:412
  14.5 17.5 %collective-permute-start.3 = (bf16[32,3072]{1,0:T(8,128)(2,1)S(1)}, bf16[32,3072]{1,0:T(8,128)(2,1)S(1)}, u32[]{:S(2)}, u32[]{:S(2)}) collective-permute-start(bf16[32,3072]{1,0:T(8,128)(2,1)S(1)} %get-tuple-element.40), channel_id=1, source_target_pairs={{8,0},{10,2},{12,4},{14,6},{0,8},{2,10},{4,12},{6,14},{24,16},{26,... | collective-permute-start | bytes 589832 | tf_op jit(solution)/shard_map/ppermute | solution.py:412
  16.1 16.0 %collective-permute-start.4 = (bf16[32,3072]{1,0:T(8,128)(2,1)S(1)}, bf16[32,3072]{1,0:T(8,128)(2,1)S(1)}, u32[]{:S(2)}, u32[]{:S(2)}) collective-permute-start(bf16[32,3072]{1,0:T(8,128)(2,1)S(1)} %get-tuple-element.41), channel_id=1, source_target_pairs={{16,8},{18,10},{20,12},{22,14},{8,16},{10,18},{12,20},{14,22},{17,... | collective-permute-start | bytes 589832 | tf_op jit(solution)/shard_map/ppermute | solution.py:412
  16.8 15.3 %collective-permute-start.5 = (f32[24,512]{1,0:T(8,128)S(1)}, f32[24,512]{1,0:T(8,128)S(1)}, u32[]{:S(2)}, u32[]{:S(2)}) collective-permute-start(f32[24,512]{1,0:T(8,128)S(1)} %get-tuple-element.42), channel_id=1, source_target_pairs={{0,16},{2,18},{4,20},{6,22},{8,24},{10,26},{12,28},{14,30},{16,0},... | collective-permute-start | bytes 147464 | tf_op jit(solution)/shard_map/ppermute | solution.py:417
  20.7 11.4 %collective-permute-start.6 = (f32[24,512]{1,0:T(8,128)S(1)}, f32[24,512]{1,0:T(8,128)S(1)}, u32[]{:S(2)}, u32[]{:S(2)}) collective-permute-start(f32[24,512]{1,0:T(8,128)S(1)} %get-tuple-element.43), channel_id=1, source_target_pairs={{0,24},{2,26},{4,28},{6,30},{24,0},{26,2},{28,4},{30,6},{1,25},{3,... | collective-permute-start | bytes 147464 | tf_op jit(solution)/shard_map/ppermute | solution.py:417
  37.4 1.2 %collective-permute-start.7 = (f32[1,2176]{1,0:T(1,128)S(1)}, f32[1,2176]{1,0:T(1,128)S(1)}, u32[]{:S(2)}, u32[]{:S(2)}) collective-permute-start(f32[1,2176]{1,0:T(1,128)S(1)} %get-tuple-element.45.mine), channel_id=1, source_target_pairs={{1,0},{0,1},{3,2},{2,3},{5,4},{4,5},{7,6},{6,7},{9,8},{8,9},{11,10... | collective-permute-start | bytes 26120 | tf_op jit(solution)/shard_map/ppermute | solution.py:412

commit v7 on v6

--- a/solution.py
+++ b/solution.py
@@ -13,10 +13,11 @@
 SOFTENING = 0.1
 ACROSS = 4
 SLOT = 64
-ROWS = 32
+ROWS = 24
 LEAVES = 8 * SLOT
 MEGA = 1024 * 1024
 FEATURES = 48
+EARLY = 3
 
 
 def exponent_table(order_max):
@@ -158,11 +159,10 @@
         local.append(offset)
         high = low_bits(offset).astype(jnp.float32)
         middle = low_bits(offset - high).astype(jnp.float32)
-        low = offset - high - middle
         raw = density[:, here].astype(jnp.float32)
         mass = jnp.where(lax.broadcasted_iota(jnp.int32, raw.shape, 1) < count[leaf], raw, 0.0)
-        spare = jnp.zeros((ROWS - fields - 9, pts), jnp.float32)
-        own[:, here] = low_bits(jnp.concatenate([mass, high, middle, low, spare], axis=0))
+        spare = jnp.zeros((ROWS - fields - 6, pts), jnp.float32)
+        own[:, here] = low_bits(jnp.concatenate([mass, high, middle, spare], axis=0))
 
     axes = [2.0 * jnp.concatenate([part[a : a + 1] for part in local], axis=0) for a in range(3)]
     made = {(0, 0, 0): jnp.ones((8, pts), jnp.float32)}
@@ -195,8 +195,8 @@
 
 
 def features(held, start, size, centre, target):
-    value = held[16:32, lanes(start, size)].astype(jnp.float32)
-    x = value[1:4] + value[4:7] + value[7:10] + by_row(centre, (3, 1))
+    value = held[16:ROWS, lanes(start, size)].astype(jnp.float32)
+    x = value[1:4] + value[4:7] + by_row(centre, (3, 1))
     norm = jnp.sum(x * x, axis=0, keepdims=True)
     if target:
         norm = norm + SOFTENING * SOFTENING
@@ -226,19 +226,24 @@
     return low_bits(jnp.transpose(features(held, start, size, centre, False)))
 
 
-def pulled(near, index, width, target, source, masses, starts, size, first=None):
-    pair = target.shape[1] // 4
-    for piece in range(0, pair, width):
-        here = lanes(index * pair + piece, width)
-        wanted = target[:, here]
-        total = jnp.zeros((ROWS, width), jnp.float32) if first is None else first[:, here]
-        ahead = dot(source[lanes(starts[0], size), :], wanted)
-        for place, start in enumerate(starts):
-            square = ahead
-            if place + 1 < len(starts):
-                ahead = dot(source[lanes(starts[place + 1], size), :], wanted)
-            total = total + dot(masses[:, lanes(start, size)], low_bits(lax.rsqrt(square)))
-        near[:, here] = total
+def pulled(near, index, target, source, masses, starts, size, first=None):
+    width = target.shape[1] // 8
+    tiles = [(piece, turn) for piece in range(2) for turn in range(len(starts))]
+    places = [lanes((2 * index + piece) * width, width) for piece in range(2)]
+
+    def squares(piece, turn):
+        return dot(source[lanes(starts[turn], size), :], target[:, places[piece]])
+
+    ahead = squares(*tiles[0])
+    for place, (piece, turn) in enumerate(tiles):
+        square = ahead
+        if place + 1 < len(tiles):
+            ahead = squares(*tiles[place + 1])
+        if turn == 0:
+            total = jnp.zeros((ROWS, width), jnp.float32) if first is None else first[:, places[piece]]
+        total = total + dot(masses[:, lanes(starts[turn], size)], low_bits(lax.rsqrt(square)))
+        if turn + 1 == len(starts):
+            near[:, places[piece]] = total
 
 
 def own_kernel(own, far_in, nodes_in, spread_in, near, source, target, far, nodes, spread, sems):
@@ -251,10 +256,10 @@
         target[:, lanes(leaf_slot(leaf) * pts, pts)] = low_bits(features(own, leaf * pts, pts, centre, True))
 
     def group(index, carry):
-        pulled(near, index, 2 * pts, target, source, own, [leaf * pts for leaf in range(8)], pts)
+        pulled(near, index, target, source, own, [2 * p * pts for p in range(4)], 2 * pts)
         return carry
 
-    lax.fori_loop(0, 2, group, 0)
+    lax.fori_loop(0, EARLY, group, 0)
     for copy in copies:
         copy.wait()
 
@@ -324,33 +329,36 @@
         faces[:, lanes(points + LEAVES, LEAVES)] = given_low
 
 
-def side_kernel(own, left, right, half, source, target, near, sides):
+def side_kernel(own, left, right, early, source, target, *rest):
+    count = (len(rest) - 2) // 2
+    near, sides = rest[count], rest[-1]
+    for block, passed in zip(rest[:count], rest[count + 1 : -1]):
+        passed[...] = block[...]
     points = own.shape[1]
     pts = points // 8
 
     def group(index, carry):
-        pulled(near, index, pts, target, source, own, [leaf * pts for leaf in range(8)], pts)
+        pulled(near, index, target, source, own, [2 * p * pts for p in range(4)], 2 * pts)
         return carry
 
-    near[:, lanes(0, 4 * pts)] = half[...]
-    lax.fori_loop(2, 4, group, 0)
+    near[:, lanes(0, 2 * EARLY * pts)] = early[...]
+    lax.fori_loop(EARLY, 4, group, 0)
     for step, side in ((0, left), (1, right)):
         for place in range(4):
             centre = (1.5 if step else -1.5, place % 2 - 0.5, place // 2 - 0.5)
             sides[lanes(place * pts, pts), :] = source_features(side, place * pts, pts, centre)
 
         def layer(index, carry, step=step, side=side):
-            pulled(near, step + 2 * index, pts, target, sides, side, [p * pts for p in range(4)], pts, near)
+            pulled(near, step + 2 * index, target, sides, side, [0, 2 * pts], 2 * pts, near)
             return carry
 
         lax.fori_loop(0, 2, layer, 0)
 
 
-def last_kernel(depth, count_in, weights_in, near, target, basis, own_local, faces_even, faces_odd, *rest):
-    distant, rest = rest[: depth - 2], rest[depth - 2 :]
-    potential, sums, held, sides, total, count, weights, sems = rest
+def rows_kernel(depth, count_in, weights_in, near, target, own_local, faces_even, faces_odd, *rest):
+    total, local, scale, column, held, sides, count, weights, sems = rest
     copies = fetch([(count_in, count), (weights_in, weights)], sems)
-    fields, points = potential.shape
+    points = total.shape[1]
     pts = points // 8
     _, box_z = box_place()
     for step in range(2):
@@ -372,33 +380,43 @@
 
         def pair(index, carry, step=step):
             starts = [(2 * x + 2 * index) * pts for x in range(3)]
-            pulled(total, index + 2 * step, pts, target, sides, held, starts, 2 * pts, near)
+            pulled(total, index + 2 * step, target, sides, held, starts, 2 * pts, near)
             return carry
 
         lax.fori_loop(0, 2, pair, 0)
 
-    local = own_local[...]
+    value = own_local[...]
     for faces in (faces_even, faces_odd):
-        local = local + faces[:, lanes(points, LEAVES)].astype(jnp.float32)
-        local = local + faces[:, lanes(points + LEAVES, LEAVES)].astype(jnp.float32)
-    for block in distant:
-        local = local + jnp.concatenate([block[...], jnp.zeros((ROWS - block.shape[0], LEAVES), jnp.float32)], axis=0)
-    local_high, local_low = high_low(local)
+        value = value + faces[:, lanes(points, LEAVES)].astype(jnp.float32)
+        value = value + faces[:, lanes(points + LEAVES, LEAVES)].astype(jnp.float32)
+    local[...] = value
     for copy in copies:
         copy.wait()
-    column = by_row([weights[field] for field in range(fields)], (fields, 1))
-    lane_index = lax.broadcasted_iota(jnp.int32, (fields, pts), 1)
-    coupling = 1.0 / (128.0 * pts)
+    column[...] = by_row([weights[field] for field in range(weights.shape[0])], column.shape)
+    lane_index = lax.broadcasted_iota(jnp.int32, (1, pts), 1)
+    for leaf in range(8):
+        scale[:, leaf * pts : (leaf + 1) * pts] = jnp.where(lane_index < count[leaf], 1.0 / (128.0 * pts), 0.0)
+
+
+def last_kernel(near, basis, scale, column, local, *rest):
+    distant, (potential, sums) = rest[:-2], rest[-2:]
+    fields, points = potential.shape
+    pts = points // 8
+    value = local[...]
+    for block in distant:
+        value = value + block[...]
+    local_high, local_low = high_low(value)
+    weight = column[0:fields, 0:1]
     for leaf in range(8):
         here = slice(leaf * pts, (leaf + 1) * pts)
         slot = slice(leaf * SLOT, (leaf + 1) * SLOT)
         left = jnp.concatenate([local_high[:, slot], local_high[:, slot]], axis=1)
         far_part = dot(left, basis[:, here]) + dot(local_low[:, slot], basis[0:SLOT, here])
-        value = (total[:, lanes(leaf_slot(leaf) * pts, pts)] + far_part)[:fields]
-        value = jnp.where(lane_index < count[leaf], value * coupling, 0.0)
-        potential[:, here] = value
-        sums[:, here] = jnp.sum(value * column, axis=0, keepdims=True)
-    sums[:, points:] = jnp.broadcast_to(jnp.sum(column), (1, sums.shape[1] - points))
+        total = near[0:fields, lanes(leaf_slot(leaf) * pts, pts)] + far_part[:fields]
+        total = total * scale[:, here]
+        potential[:, here] = total
+        sums[:, here] = jnp.sum(total * weight, axis=0, keepdims=True)
+    sums[:, points:] = jnp.broadcast_to(jnp.sum(weight), (1, sums.shape[1] - points))
 
 
 def mean_kernel(mine, other, mean):
@@ -471,7 +489,7 @@
         "near_own",
         [vmem] + [hbm] * 3,
         [
-            ((ROWS, points // 2), full),
+            ((ROWS, EARLY * points // 4), full),
             ((points, FEATURES), half),
             ((FEATURES, points), half),
             ((len(STEPS) * LEAVES, LEAVES), half),
@@ -491,7 +509,7 @@
         [((ROWS, 4 * pts + LEAVES), half)] * 2
         + [((ROWS, LEAVES), full)]
         + [((ROWS, points + 2 * LEAVES), half)] * 2
-        + [((24, LEAVES), full)] * (depth - 2),
+        + [((ROWS, LEAVES), full)] * (depth - 2),
         [],
         own,
         moments,
@@ -503,14 +521,13 @@
         nodes,
         spread,
     )
-    distant = [across_layers(block, distance + 2) for distance, block in enumerate(distant)]
     faces_even = swapped(faces_even, "space", lambda i: i ^ ACROSS)
     faces_odd = swapped(faces_odd, "space", lambda i: i + ACROSS if i // ACROSS % 2 else i - ACROSS)
-    near, = call(
+    near, *distant = call(
         side_kernel,
         "near_side",
-        [vmem] * 6,
-        [((ROWS, points), full)],
+        [vmem] * (6 + len(distant)),
+        [((ROWS, points), full)] + [((ROWS, LEAVES), full)] * len(distant),
         [pltpu.VMEM((4 * pts, FEATURES), half)],
         own,
         left,
@@ -518,16 +535,17 @@
         near,
         source,
         target,
-    )
-    potential, sums = call(
-        functools.partial(last_kernel, depth),
+        *distant,
+    )
+    distant = [across_layers(block, distance + 2) for distance, block in enumerate(distant)]
+    near, local, scale, column = call(
+        functools.partial(rows_kernel, depth),
         "near_rows",
-        [hbm] * 2 + [vmem] * (6 + len(distant)),
-        [((fields, points), full), ((1, points + 128), full)],
+        [hbm] * 2 + [vmem] * 5,
+        [((ROWS, points), full), ((ROWS, LEAVES), full), ((1, points), full), ((ROWS, 128), full)],
         [
             pltpu.VMEM((ROWS, points), half),
             pltpu.VMEM((8 * pts, FEATURES), half),
-            pltpu.VMEM((ROWS, points), full),
             pltpu.SMEM((8,), jnp.int32),
             pltpu.SMEM((fields,), full),
             pltpu.SemaphoreType.DMA((2,)),
@@ -536,10 +554,21 @@
         sigma_weights,
         near,
         target,
-        basis,
         own_local,
         faces_even,
         faces_odd,
+    )
+    potential, sums = call(
+        last_kernel,
+        "evaluate",
+        [vmem] * (5 + len(distant)),
+        [((fields, points), full), ((1, points + 128), full)],
+        [],
+        near,
+        basis,
+        scale,
+        column,
+        local,
         *distant,
     )
     if lax.axis_size("sig") == 2:

time: 39.6 us -> 36.8 us (0.929)
  waiting for transfers between devices: 3.48 us -> 1.26 us
  Pallas kernels: 19.6 us -> 18.7 us
    ppermute x6, waiting for transfers between devices: 3.46 us -> 1.26 us  [swapped(): lax.ppermute(block, axis, [(partner(i), i) for i in range(size) if 0 <= p...]
    pallas_call x6 -> x7, Pallas kernels: 19.6 us -> 18.7 us  [call(): pl.pallas_call(kernel, in_specs=in_specs, out_specs=[vmem] * len(outs), o...]
  transfers between devices with their start and end apart: 8 -> 8, of which waited for: 3 -> 2; matrix products, arithmetic and copies ran while one was open for 0% -> 0% of each run, Pallas kernels for 23% -> 35%
where the time goes in v7:
time: 36.8 us; the launch traced here: 36.6 us
  Pallas kernels  18.7 us (51%)
  starting transfers between devices  15.9 us (43%)
  waiting for transfers between devices  1.26 us (3%)
  between operations  0.71 us (2%)
    pallas_call x7, Pallas kernels, call(): pl.pallas_call(kernel, in_specs=in_specs, out_specs=[vmem] * len(outs), o...  18.7 us
    ppermute x2, starting transfers between devices, across_layers(): lax.ppermute(block, 'space', [pair for pair in pairs if abs(pair[0] - pai...  8.67 us
    ppermute x6, starting transfers between devices, swapped(): lax.ppermute(block, axis, [(partner(i), i) for i in range(size) if 0 <= p...  7.22 us
    ppermute x6, waiting for transfers between devices, swapped(): lax.ppermute(block, axis, [(partner(i), i) for i in range(size) if 0 <= p...  1.26 us
  transfers between devices with their start and end apart: 8, of which 2 were waited for; matrix products, arithmetic and copies ran while one was open for 0% of the time, Pallas kernels for 35%

profile of v7, /device:TPU:0, one launch (start us, length us, event | category | flops | bytes accessed | tf_op | source)
XLA Modules:
  0.0 36.6 jit_solution(5167551206319041641)
XLA Ops:
  0.6 3.0 %pack.1 = (bf16[24,2048]{1,0:T(8,128)(2,1)S(1)}, bf16[128,2048]{1,0:T(8,128)(2,1)S(1)}, bf16[24,512]{1,0:T(8,128)(2,1)S(1)}, bf16[24,128]{1,0:T(8,128)(2,1)S(1)}...) custom-call(s32[8]{0:T(128)} %count_in.3, f32[3,2048]{1,0:T(4,128)} %positions_in.1, ...), custom_call_target="tpu_custom_call" | custom-call | tf_op jit(solution)/shard_map/pack/pallas_call | solution.py:445
  3.7 3.0 %collective-permute-start = (bf16[24,1664]{1,0:T(8,128)(2,1)S(1)}, bf16[24,1664]{1,0:T(8,128)(2,1)S(1)}, u32[]{:S(2)}, u32[]{:S(2)}) collective-permute-start(bf16[24,1664]{1,0:T(8,128)(2,1)S(1)} %get-tuple-element.34), channel_id=1, source_target_pairs={{2,0},{0,2},{6,4},{4,6},{10,8},{8,10},{14,12},{12,14},{18,16},{16,... | collective-permute-start | bytes 239624 | tf_op jit(solution)/shard_map/ppermute | solution.py:430
  6.7 1.5 %collective-permute-start.2 = (bf16[24,1664]{1,0:T(8,128)(2,1)S(1)}, bf16[24,1664]{1,0:T(8,128)(2,1)S(1)}, u32[]{:S(2)}, u32[]{:S(2)}) collective-permute-start(bf16[24,1664]{1,0:T(8,128)(2,1)S(1)} %get-tuple-element.36), channel_id=1, source_target_pairs={{6,0},{4,2},{2,4},{0,6},{14,8},{12,10},{10,12},{8,14},{22,16},{20,... | collective-permute-start | bytes 239624 | tf_op jit(solution)/shard_map/ppermute | solution.py:430
  8.2 0.1 collective-permute-start.1
  8.2 4.0 %near_own.1 = (f32[24,1536]{1,0:T(8,128)S(1)}, bf16[2048,48]{1,0:T(8,128)(2,1)S(1)}, bf16[48,2048]{1,0:T(8,128)(2,1)S(1)}, bf16[4096,512]{1,0:T(8,128)(2,1)S(1)}...) custom-call(bf16[24,2048]{1,0:T(8,128)(2,1)S(1)} %get-tuple-element.31.own, ...), custom_call_target="tpu_custom_call" | custom-call | tf_op jit(solution)/shard_map/near_own/pallas_call | solution.py:445
  12.3 0.1 collective-permute-done.1.from_2
  12.3 0.0 collective-permute-done.from_1
  12.3 0.0 collective-permute-done.2.from_3
  12.3 1.4 %row.1 = (bf16[24,1536]{1,0:T(8,128)(2,1)S(1)}, bf16[24,1536]{1,0:T(8,128)(2,1)S(1)}, f32[24,512]{1,0:T(8,128)S(1)}, bf16[24,3072]{1,0:T(8,128)(2,1)S(1)}, bf16[...) custom-call(bf16[24,2048]{1,0:T(8,128)(2,1)S(1)} %get-tuple-element.31.own, ...), custom_call_target="tpu_custom_call" | custom-call | tf_op jit(solution)/shard_map/row/pallas_call | solution.py:445
  13.7 2.0 %collective-permute-start.3 = (bf16[24,3072]{1,0:T(8,128)(2,1)S(1)}, bf16[24,3072]{1,0:T(8,128)(2,1)S(1)}, u32[]{:S(2)}, u32[]{:S(2)}) collective-permute-start(bf16[24,3072]{1,0:T(8,128)(2,1)S(1)} %get-tuple-element.49), channel_id=1, source_target_pairs={{8,0},{10,2},{12,4},{14,6},{0,8},{2,10},{4,12},{6,14},{24,16},{26,... | collective-permute-start | bytes 442376 | tf_op jit(solution)/shard_map/ppermute | solution.py:430
  15.7 0.7 %collective-permute-start.4 = (bf16[24,3072]{1,0:T(8,128)(2,1)S(1)}, bf16[24,3072]{1,0:T(8,128)(2,1)S(1)}, u32[]{:S(2)}, u32[]{:S(2)}) collective-permute-start(bf16[24,3072]{1,0:T(8,128)(2,1)S(1)} %get-tuple-element.50), channel_id=1, source_target_pairs={{16,8},{18,10},{20,12},{22,14},{8,16},{10,18},{12,20},{14,22},{17,... | collective-permute-start | bytes 442376 | tf_op jit(solution)/shard_map/ppermute | solution.py:430
  16.4 4.3 %near_side.1 = (f32[24,2048]{1,0:T(8,128)S(1)}, f32[24,512]{1,0:T(8,128)S(1)}, f32[24,512]{1,0:T(8,128)S(1)}) custom-call(bf16[24,2048]{1,0:T(8,128)(2,1)S(1)} %get-tuple-element.31.own, bf16[24,1536]{1,0:T(8,128)(2,1)S(1)} %get-tuple-element.40.left, bf16[24,1536]{1,0:T(8,128)(2,1)S(1)} %get-tuple-element.41.right, f32[24,1536]{1,0:T(8,128)S(1)} %get-tuple-element.42.early, ...), custom_call_target="tpu_custom_call" | custom-call | tf_op jit(solution)/shard_map/near_side/pallas_call | solution.py:445
  20.7 3.8 %collective-permute-start.5 = (f32[24,512]{1,0:T(8,128)S(1)}, f32[24,512]{1,0:T(8,128)S(1)}, u32[]{:S(2)}, u32[]{:S(2)}) collective-permute-start(f32[24,512]{1,0:T(8,128)S(1)} %get-tuple-element.56), channel_id=1, source_target_pairs={{0,16},{2,18},{4,20},{6,22},{8,24},{10,26},{12,28},{14,30},{16,0},... | collective-permute-start | bytes 147464 | tf_op jit(solution)/shard_map/ppermute | solution.py:435
  24.5 4.8 %collective-permute-start.6 = (f32[24,512]{1,0:T(8,128)S(1)}, f32[24,512]{1,0:T(8,128)S(1)}, u32[]{:S(2)}, u32[]{:S(2)}) collective-permute-start(f32[24,512]{1,0:T(8,128)S(1)} %get-tuple-element.57), channel_id=1, source_target_pairs={{0,24},{2,26},{4,28},{6,30},{24,0},{26,2},{28,4},{30,6},{1,25},{3,... | collective-permute-start | bytes 147464 | tf_op jit(solution)/shard_map/ppermute | solution.py:435
  29.4 0.0 collective-permute-done.3.faces_even
  29.4 0.0 collective-permute-done.4.faces_odd
  29.4 4.3 %near_rows.1 = (f32[24,2048]{1,0:T(8,128)S(1)}, f32[24,512]{1,0:T(8,128)S(1)}, f32[1,2048]{1,0:T(1,128)S(1)}, f32[24,128]{1,0:T(8,128)S(1)}) custom-call(s32[8]{0:T(128)} %count_in.3, f32[17]{0:T(128)} %weights_in.1, f32[24,2048]{1,0:T(8,128)S(1)} %get-tuple-element.47.near, bf16[48,2048]{1,0:T(8,128)(2,1)S(1)} %get-tuple-element.44.target, ...), custom_call_target="tpu_custom_call" | custom-call | tf_op jit(solution)/shard_map/near_rows/pallas_call | solution.py:445
  33.7 0.0 collective-permute-done.5.rest_0_
  33.7 0.0 collective-permute-done.6.rest_1_
  33.7 1.0 %evaluate.1 = (f32[17,2048]{1,0:T(8,128)}, f32[1,2176]{1,0:T(1,128)S(1)}) custom-call(f32[24,2048]{1,0:T(8,128)S(1)} %get-tuple-element.51.near, bf16[128,2048]{1,0:T(8,128)(2,1)S(1)} %get-tuple-element.52.basis, f32[1,2048]{1,0:T(1,128)S(1)} %get-tuple-element.53.scale, f32[24,128]{1,0:T(8,128)S(1)} %get-tuple-element.54.column, ...), custom_call_target="tpu_custom_call" | custom-call | tf_op jit(solution)/shard_map/evaluate/pallas_call | solution.py:445
  34.8 0.0 collective-permute-start.7
  34.8 1.2 %collective-permute-done.7.other = f32[1,2176]{1,0:T(1,128)S(1)} collective-permute-done((f32[1,2176]{1,0:T(1,128)S(1)}, f32[1,2176]{1,0:T(1,128)S(1)}, u32[]{:S(2)}, u32[]{:S(2)}) %collective-permute-start.7) | collective-permute-done | bytes 8736 | tf_op jit(solution)/shard_map/ppermute | solution.py:430
  35.9 0.7 %mean.1 = f32[1,2048]{1,0:T(1,128)} custom-call(f32[1,2176]{1,0:T(1,128)S(1)} %get-tuple-element.59.mine, f32[1,2176]{1,0:T(1,128)S(1)} %collective-permute-done.7.other), custom_call_target="tpu_custom_call" | custom-call | tf_op jit(solution)/shard_map/mean/pallas_call | solution.py:445
Async XLA Ops:
  3.7 8.7 %collective-permute-start = (bf16[24,1664]{1,0:T(8,128)(2,1)S(1)}, bf16[24,1664]{1,0:T(8,128)(2,1)S(1)}, u32[]{:S(2)}, u32[]{:S(2)}) collective-permute-start(bf16[24,1664]{1,0:T(8,128)(2,1)S(1)} %get-tuple-element.34), channel_id=1, source_target_pairs={{2,0},{0,2},{6,4},{4,6},{10,8},{8,10},{14,12},{12,14},{18,16},{16,... | collective-permute-start | bytes 239624 | tf_op jit(solution)/shard_map/ppermute | solution.py:430
  6.7 5.7 %collective-permute-start.2 = (bf16[24,1664]{1,0:T(8,128)(2,1)S(1)}, bf16[24,1664]{1,0:T(8,128)(2,1)S(1)}, u32[]{:S(2)}, u32[]{:S(2)}) collective-permute-start(bf16[24,1664]{1,0:T(8,128)(2,1)S(1)} %get-tuple-element.36), channel_id=1, source_target_pairs={{6,0},{4,2},{2,4},{0,6},{14,8},{12,10},{10,12},{8,14},{22,16},{20,... | collective-permute-start | bytes 239624 | tf_op jit(solution)/shard_map/ppermute | solution.py:430
  8.2 4.2 %collective-permute-start.1 = (bf16[24,128]{1,0:T(8,128)(2,1)S(1)}, bf16[24,128]{1,0:T(8,128)(2,1)S(1)}, u32[]{:S(2)}, u32[]{:S(2)}) collective-permute-start(bf16[24,128]{1,0:T(8,128)(2,1)S(1)} %get-tuple-element.35), channel_id=1, source_target_pairs={{4,0},{6,2},{0,4},{2,6},{12,8},{14,10},{8,12},{10,14},{20,16},{22,... | collective-permute-start | bytes 18440 | tf_op jit(solution)/shard_map/ppermute | solution.py:430
  13.7 15.7 %collective-permute-start.3 = (bf16[24,3072]{1,0:T(8,128)(2,1)S(1)}, bf16[24,3072]{1,0:T(8,128)(2,1)S(1)}, u32[]{:S(2)}, u32[]{:S(2)}) collective-permute-start(bf16[24,3072]{1,0:T(8,128)(2,1)S(1)} %get-tuple-element.49), channel_id=1, source_target_pairs={{8,0},{10,2},{12,4},{14,6},{0,8},{2,10},{4,12},{6,14},{24,16},{26,... | collective-permute-start | bytes 442376 | tf_op jit(solution)/shard_map/ppermute | solution.py:430
  15.7 13.7 %collective-permute-start.4 = (bf16[24,3072]{1,0:T(8,128)(2,1)S(1)}, bf16[24,3072]{1,0:T(8,128)(2,1)S(1)}, u32[]{:S(2)}, u32[]{:S(2)}) collective-permute-start(bf16[24,3072]{1,0:T(8,128)(2,1)S(1)} %get-tuple-element.50), channel_id=1, source_target_pairs={{16,8},{18,10},{20,12},{22,14},{8,16},{10,18},{12,20},{14,22},{17,... | collective-permute-start | bytes 442376 | tf_op jit(solution)/shard_map/ppermute | solution.py:430
  20.7 13.0 %collective-permute-start.5 = (f32[24,512]{1,0:T(8,128)S(1)}, f32[24,512]{1,0:T(8,128)S(1)}, u32[]{:S(2)}, u32[]{:S(2)}) collective-permute-start(f32[24,512]{1,0:T(8,128)S(1)} %get-tuple-element.56), channel_id=1, source_target_pairs={{0,16},{2,18},{4,20},{6,22},{8,24},{10,26},{12,28},{14,30},{16,0},... | collective-permute-start | bytes 147464 | tf_op jit(solution)/shard_map/ppermute | solution.py:435
  24.5 9.2 %collective-permute-start.6 = (f32[24,512]{1,0:T(8,128)S(1)}, f32[24,512]{1,0:T(8,128)S(1)}, u32[]{:S(2)}, u32[]{:S(2)}) collective-permute-start(f32[24,512]{1,0:T(8,128)S(1)} %get-tuple-element.57), channel_id=1, source_target_pairs={{0,24},{2,26},{4,28},{6,30},{24,0},{26,2},{28,4},{30,6},{1,25},{3,... | collective-permute-start | bytes 147464 | tf_op jit(solution)/shard_map/ppermute | solution.py:435
  34.8 1.2 %collective-permute-start.7 = (f32[1,2176]{1,0:T(1,128)S(1)}, f32[1,2176]{1,0:T(1,128)S(1)}, u32[]{:S(2)}, u32[]{:S(2)}) collective-permute-start(f32[1,2176]{1,0:T(1,128)S(1)} %get-tuple-element.59.mine), channel_id=1, source_target_pairs={{1,0},{0,1},{3,2},{2,3},{5,4},{4,5},{7,6},{6,7},{9,8},{8,9},{11,10... | collective-permute-start | bytes 26120 | tf_op jit(solution)/shard_map/ppermute | solution.py:430

commit v8 on v7

v8 whole, which is shorter than its diff:
```python
import functools
import math

import jax
import jax.numpy as jnp
import numpy as np
from jax import lax
from jax.experimental import pallas as pl
from jax.experimental.pallas import tpu as pltpu
from jax.sharding import PartitionSpec as P

ORDER = 5
SOFTENING = 0.1
ACROSS = 4
SLOT = 64
ROWS = 24
LEAVES = 8 * SLOT
MEGA = 1024 * 1024
FEATURES = 48


def exponent_table(order_max):
    entries_list = []
    for degree in range(order_max + 1):
        for first_power in range(degree, -1, -1):
            for second_power in range(degree - first_power, -1, -1):
                entries_list.append((first_power, second_power, degree - first_power - second_power))
    return entries_list


def node_table(count_nodes, offset_value):
    counter = np.arange(1, count_nodes + 1, dtype=np.float32)[:, None]
    stride_set = np.array([0.7548776662466927, 0.5698402909980532, 0.4142135623730951], dtype=np.float32)[None, :]
    unit_points = np.mod(counter * stride_set + np.float32(offset_value), np.float32(1.0))
    return (np.float32(2.0) * unit_points - np.float32(1.0)).astype(np.float32)


EXPONENTS = exponent_table(ORDER)
COEFFS = len(EXPONENTS)
CHECK = node_table(COEFFS, 0.5).astype(np.float64)
EQUIV = node_table(COEFFS, 0.0).astype(np.float64)
STEPS = [(sx, sz) for sz in (-1, 0, 1) for sx in (-1, 0, 1) if sx != 0 or sz != 0]


def bits(octant):
    return octant % 2, octant // 2 % 2, octant // 4


def leaf_slot(octant):
    bit_x, bit_y, bit_z = bits(octant)
    return (bit_x + 2 * bit_z) * 2 + bit_y


@functools.lru_cache(None)
def far_table():
    shape = (len(STEPS), 8, SLOT, 8, SLOT)
    table = np.zeros(shape)
    gap_nodes = 0.5 * (CHECK[None, :, :] - EQUIV[:, None, :])
    for index, (step_x, step_z) in enumerate(STEPS):
        for source in range(8):
            for target in range(8):
                s, t = bits(source), bits(target)
                gap = np.array([2 * step_x + s[0] - t[0], s[1] - t[1], 2 * step_z + s[2] - t[2]], np.float64)
                if max(abs(gap[0]), abs(gap[2])) >= 2:
                    shifted = gap_nodes - gap
                    value = 1.0 / np.sqrt(np.sum(shifted * shifted, -1) + SOFTENING * SOFTENING) / COEFFS
                    table[index, source, :COEFFS, target, :COEFFS] = value
    return table.reshape(len(STEPS) * LEAVES, LEAVES)


@functools.lru_cache(None)
def shift_table():
    table = np.zeros((8, SLOT, SLOT))
    for leaf in range(8):
        offset = [bit - 0.5 for bit in bits(leaf)]
        for k, target in enumerate(EXPONENTS):
            for i, source in enumerate(EXPONENTS):
                if all(b <= a for a, b in zip(target, source)):
                    value = 1.0
                    for a, b, h in zip(target, source, offset):
                        value *= math.comb(a, b) * 0.5**b * h ** (a - b)
                    table[leaf, i, k] = value
    return table.reshape(8 * SLOT, SLOT)


@functools.lru_cache(None)
def box_nodes():
    gaps = np.zeros((3, SLOT, SLOT))
    gaps[:, :COEFFS, :COEFFS] = np.moveaxis(CHECK[None, :, :] - EQUIV[:, None, :], -1, 0)
    gaps[1] = gaps[1] ** 2 + SOFTENING * SOFTENING
    return gaps.astype(np.float32)


def dot(left, right):
    return jnp.dot(left, right, preferred_element_type=jnp.float32)


def dot_nt(left, right):
    return lax.dot_general(left, right, (((1,), (1,)), ((), ())), preferred_element_type=jnp.float32)


def low_bits(value):
    return value.astype(jnp.bfloat16)


def high_low(value):
    high = low_bits(value)
    return high, low_bits(value - high.astype(jnp.float32))


def by_row(values, shape):
    row = lax.broadcasted_iota(jnp.int32, shape, 0)
    result = jnp.zeros(shape, jnp.float32)
    for index, value in enumerate(values):
        result = jnp.where(row == index, value, result)
    return result


def box_place():
    label = lax.axis_index("space")
    return lax.rem(label, ACROSS), lax.div(label, ACROSS)


def lanes(start, size):
    return pl.ds(start if isinstance(start, int) else pl.multiple_of(start, 128), size)


def fetch(pairs, sems):
    copies = [pltpu.make_async_copy(src, dst, sems.at[i]) for i, (src, dst) in enumerate(pairs)]
    for copy in copies:
        copy.start()
    return copies


def pack_kernel(count_in, positions_in, density_in, own, basis, count, positions, density, mono, sems):
    copies = fetch([(count_in, count), (positions_in, positions), (density_in, density)], sems)
    fields, points = density.shape
    pts = points // 8
    box_x, box_z = box_place()
    for copy in copies:
        copy.wait()
    local = []
    for leaf in range(8):
        bit_x, bit_y, bit_z = bits(leaf)
        centre = by_row(
            [2.0 * box_x.astype(jnp.float32) + (bit_x + 0.5), bit_y + 0.5, 2.0 * box_z.astype(jnp.float32) + (bit_z + 0.5)],
            (3, 1),
        )
        here = slice(leaf * pts, (leaf + 1) * pts)
        offset = positions[:, here] - centre
        local.append(offset)
        high = low_bits(offset).astype(jnp.float32)
        middle = low_bits(offset - high).astype(jnp.float32)
        raw = density[:, here].astype(jnp.float32)
        mass = jnp.where(lax.broadcasted_iota(jnp.int32, raw.shape, 1) < count[leaf], raw, 0.0)
        spare = jnp.zeros((ROWS - fields - 6, pts), jnp.float32)
        own[:, here] = low_bits(jnp.concatenate([mass, high, middle, spare], axis=0))

    axes = [2.0 * jnp.concatenate([part[a : a + 1] for part in local], axis=0) for a in range(3)]
    made = {(0, 0, 0): jnp.ones((8, pts), jnp.float32)}
    for k, powers in enumerate(EXPONENTS):
        if powers not in made:
            a = next(i for i in range(3) if powers[i] > 0)
            before = tuple(p - (i == a) for i, p in enumerate(powers))
            made[powers] = made[before] * axes[a]
        mono[k] = made[powers]
    mono[COEFFS:SLOT] = jnp.zeros((SLOT - COEFFS, 8, pts), jnp.float32)
    parts = []
    for leaf in range(8):
        here = slice(leaf * pts, (leaf + 1) * pts)
        high, low = high_low(mono[:, leaf, :])
        basis[0:SLOT, here] = high
        basis[SLOT:, here] = low
        parts.append(dot_nt(own[:, here], high))
    own[:, points:] = low_bits(jnp.concatenate(parts, axis=1))


def features(held, start, size, centre, target):
    value = held[16:ROWS, lanes(start, size)].astype(jnp.float32)
    x = value[1:4] + value[4:7] + by_row(centre, (3, 1))
    norm = jnp.sum(x * x, axis=0, keepdims=True)
    if target:
        norm = norm + SOFTENING * SOFTENING
    parts, norms = [], []
    for source, out in ((x, parts), (norm, norms)):
        left = source
        for _ in range(3):
            high = low_bits(left).astype(jnp.float32)
            out.append(high)
            left = left - high
    one = jnp.ones_like(norm)
    zero = jnp.zeros_like(norm)
    blank = jnp.zeros((3, norm.shape[1]), jnp.float32)
    blocks = []
    order = (0, 1, 0, 2, 0, 1) if target else (0, 0, 1, 0, 2, 1)
    for index, which in enumerate(order):
        coords = -2.0 * parts[which] if target else parts[which]
        if index < 3:
            pair = [one, norms[index]] if target else [norms[index], one]
        else:
            pair = [zero, zero]
        blocks += [coords, *pair, blank]
    return jnp.concatenate(blocks, axis=0)


def source_features(held, start, size, centre):
    return low_bits(jnp.transpose(features(held, start, size, centre, False)))


def pulled(near, index, target, source, masses, starts, size, first=None):
    width = target.shape[1] // 8
    tiles = [(piece, turn) for piece in range(2) for turn in range(len(starts))]
    places = [lanes((2 * index + piece) * width, width) for piece in range(2)]

    def squares(piece, turn):
        return dot(source[lanes(starts[turn], size), :], target[:, places[piece]])

    ahead = squares(*tiles[0])
    for place, (piece, turn) in enumerate(tiles):
        square = ahead
        if place + 1 < len(tiles):
            ahead = squares(*tiles[place + 1])
        if turn == 0:
            total = jnp.zeros((ROWS, width), jnp.float32) if first is None else first[:, places[piece]]
        total = total + dot(masses[:, lanes(starts[turn], size)], low_bits(lax.rsqrt(square)))
        if turn + 1 == len(starts):
            near[:, places[piece]] = total


def own_kernel(count_in, weights_in, own, *rest):
    tables, (near, source, target, scale, column), rest = rest[:4], rest[4:9], rest[9:]
    copies = fetch([*zip(tables, rest[:4]), (count_in, rest[4]), (weights_in, rest[5])], rest[6])
    count, weights = rest[4:6]
    points = near.shape[1]
    pts = points // 8
    for leaf in range(8):
        centre = [bit - 0.5 for bit in bits(leaf)]
        source[lanes(leaf * pts, pts), :] = source_features(own, leaf * pts, pts, centre)
        target[:, lanes(leaf_slot(leaf) * pts, pts)] = low_bits(features(own, leaf * pts, pts, centre, True))

    def group(index, carry):
        pulled(near, index, target, source, own, [2 * p * pts for p in range(4)], 2 * pts)
        return carry

    lax.fori_loop(0, 4, group, 0)
    for copy in copies:
        copy.wait()
    column[...] = by_row([weights[field] for field in range(weights.shape[0])], column.shape)
    lane_index = lax.broadcasted_iota(jnp.int32, (1, pts), 1)
    for leaf in range(8):
        scale[:, leaf * pts : (leaf + 1) * pts] = jnp.where(lane_index < count[leaf], 1.0 / (128.0 * pts), 0.0)


def box_columns(depth, box_x, box_z, nodes):
    blocks = []
    for box in range(ACROSS * depth):
        gap_x = 2 * (box_x - box % ACROSS)
        gap_z = 2 * (box_z - box // ACROSS)
        across_x = nodes[0] + gap_x.astype(jnp.float32)
        across_z = nodes[2] + gap_z.astype(jnp.float32)
        apart = jnp.maximum(jnp.abs(gap_x), jnp.abs(gap_z)) >= 4
        value = lax.rsqrt(across_x * across_x + across_z * across_z + nodes[1])
        blocks.append(low_bits(value * jnp.where(apart, 1.0 / COEFFS, 0.0)))
    return jnp.concatenate(blocks, axis=0)


def rest_kernel(depth, gathered, early, target, scale, column, basis, far, nodes, spread, shift, *rest):
    potential, sums, left, right, below, above, moments, sides, near, sems = rest
    fields, points = potential.shape
    pts = points // 8
    box_x, box_z = box_place()
    all_moments = pltpu.make_async_copy(gathered.at[:, :, pl.ds(points, LEAVES)], moments, sems.at[0])
    all_moments.start()
    valid, label, faces = {}, {}, {}
    for index, (step_x, step_z) in enumerate(STEPS):
        x, z = box_x + step_x, box_z + step_z
        inside = (x >= 0) & (x < ACROSS) & (z >= 0) & (z < depth)
        step = (step_x, step_z)
        valid[step] = inside
        label[step] = jnp.where(inside, x + ACROSS * z, box_x + ACROSS * box_z)
        pairs = []
        for octant in range(8):
            bit_x, bit_y, bit_z = bits(octant)
            if step_x and bit_x != (step_x < 0) or step_z and bit_z != (step_z < 0):
                continue
            if step_z:
                place = 2 * (1 + bit_x + 2 * step_x) + bit_y
                held = above if step_z > 0 else below
            else:
                place = bit_y + 2 * bit_z
                held = right if step_x > 0 else left
            pairs.append((octant * pts, held.at[:, pl.ds(place * pts, pts)]))
        faces[step] = pairs

    def copies(index, step):
        return [
            pltpu.make_async_copy(gathered.at[label[step], :, pl.ds(start, pts)], place, sems.at[1 + 4 * index + turn])
            for turn, (start, place) in enumerate(faces[step])
        ]

    for index, step in enumerate(STEPS):

        @pl.when(valid[step])
        def _(index=index, step=step):
            for copy in copies(index, step):
                copy.start()

        @pl.when(jnp.logical_not(valid[step]))
        def _(step=step):
            for _, place in faces[step]:
                place[...] = jnp.zeros(place.shape, jnp.bfloat16)

    columns = box_columns(depth, box_x, box_z, nodes)
    for index, step in enumerate(STEPS):

        @pl.when(valid[step])
        def _(index=index, step=step):
            for copy in copies(index, step):
                copy.wait()

    near[...] = early[...]
    for step, side in ((0, left), (1, right)):
        for place in range(4):
            centre = (1.5 if step else -1.5, place % 2 - 0.5, place // 2 - 0.5)
            sides[lanes(place * pts, pts), :] = source_features(side, place * pts, pts, centre)

        def layer(index, carry, step=step, side=side):
            pulled(near, step + 2 * index, target, sides, side, [0, 2 * pts], 2 * pts, near)
            return carry

        lax.fori_loop(0, 2, layer, 0)
    for step, held in ((0, below), (1, above)):
        for place in range(8):
            centre = (place // 2 - 1.5, place % 2 - 0.5, 1.5 if step else -1.5)
            sides[lanes(place * pts, pts), :] = source_features(held, place * pts, pts, centre)

        def pair(index, carry, step=step, held=held):
            starts = [(2 * x + 2 * index) * pts for x in range(3)]
            pulled(near, index + 2 * step, target, sides, held, starts, 2 * pts, near)
            return carry

        lax.fori_loop(0, 2, pair, 0)

    all_moments.wait()
    boxes = ACROSS * depth
    totals = dot(jnp.concatenate([moments[box] for box in range(boxes)], axis=0), shift[...])
    totals = jnp.concatenate([totals[box * ROWS : (box + 1) * ROWS] for box in range(boxes)], axis=1)
    totals_high, totals_low = high_low(totals)
    coarse_high, coarse_low = high_low(dot(totals_high, columns) + dot(totals_low, columns))
    value = dot(coarse_high, spread[...]) + dot(coarse_low, spread[...])
    around = [jnp.where(valid[step], moments[label[step]], jnp.bfloat16(0)) for step in STEPS]
    value = value + dot(jnp.concatenate(around, axis=1), far[...])
    local_high, local_low = high_low(value)
    weight = column[0:fields, 0:1]
    for leaf in range(8):
        here = slice(leaf * pts, (leaf + 1) * pts)
        slot = slice(leaf * SLOT, (leaf + 1) * SLOT)
        doubled = jnp.concatenate([local_high[:, slot], local_high[:, slot]], axis=1)
        far_part = dot(doubled, basis[:, here]) + dot(local_low[:, slot], basis[0:SLOT, here])
        total = near[0:fields, lanes(leaf_slot(leaf) * pts, pts)] + far_part[:fields]
        total = total * scale[:, here]
        potential[:, here] = total
        sums[:, here] = jnp.sum(total * weight, axis=0, keepdims=True)
    sums[:, points:] = jnp.broadcast_to(jnp.sum(weight), (1, sums.shape[1] - points))


def mean_kernel(mine, other, mean):
    points = mean.shape[1]
    total = mine[...] + other[...]
    mean[...] = total[:, :points] / total[:, points : points + 1]


def swapped(block, axis, partner):
    size = lax.axis_size(axis)
    return lax.ppermute(block, axis, [(partner(i), i) for i in range(size) if 0 <= partner(i) < size])


def per_device(positions, density, leaf_count, sigma_weights):
    fields, points = density.shape
    pts = points // 8
    depth = lax.axis_size("space") // ACROSS
    vmem, hbm = pl.BlockSpec(memory_space=pltpu.VMEM), pl.BlockSpec(memory_space=pltpu.HBM)

    def call(kernel, name, in_specs, outs, scratch, *args):
        return pl.pallas_call(
            kernel,
            in_specs=in_specs,
            out_specs=[vmem] * len(outs),
            out_shape=[jax.ShapeDtypeStruct(shape, dtype) for shape, dtype in outs],
            scratch_shapes=scratch,
            compiler_params=pltpu.CompilerParams(vmem_limit_bytes=24 * MEGA),
            name=name,
        )(*(pltpu.with_memory_space_constraint(a, pltpu.HBM) if s is hbm else a for s, a in zip(in_specs, args)))

    half, full = jnp.bfloat16, jnp.float32
    shift = shift_table()
    own, basis = call(
        pack_kernel,
        "pack",
        [hbm] * 3,
        [((ROWS, points + LEAVES), half), ((2 * SLOT, points), half)],
        [
            pltpu.SMEM((8,), jnp.int32),
            pltpu.VMEM((3, points), full),
            pltpu.VMEM((fields, points), half),
            pltpu.VMEM((SLOT, 8, pts), full),
            pltpu.SemaphoreType.DMA((3,)),
        ],
        leaf_count,
        positions,
        density,
    )
    gathered = lax.all_gather(own, "space")
    tables = [
        jnp.asarray(far_table(), half),
        jnp.asarray(box_nodes()),
        jnp.asarray(shift.T.copy(), half),
        jnp.asarray(shift, half),
    ]
    near, source, target, scale, column, *tables = call(
        own_kernel,
        "near_own",
        [hbm] * 2 + [vmem] + [hbm] * 4,
        [
            ((ROWS, points), full),
            ((points, FEATURES), half),
            ((FEATURES, points), half),
            ((1, points), full),
            ((ROWS, 128), full),
            *[(table.shape, table.dtype) for table in tables],
        ],
        [pltpu.SMEM((8,), jnp.int32), pltpu.SMEM((fields,), full), pltpu.SemaphoreType.DMA((6,))],
        leaf_count,
        sigma_weights,
        own,
        *tables,
    )
    potential, sums = call(
        functools.partial(rest_kernel, depth),
        "near_rest",
        [hbm] + [vmem] * 9,
        [((fields, points), full), ((1, points + 128), full)],
        [
            pltpu.VMEM((ROWS, 4 * pts), half),
            pltpu.VMEM((ROWS, 4 * pts), half),
            pltpu.VMEM((ROWS, points), half),
            pltpu.VMEM((ROWS, points), half),
            pltpu.VMEM((ACROSS * depth, ROWS, LEAVES), half),
            pltpu.VMEM((8 * pts, FEATURES), half),
            pltpu.VMEM((ROWS, points), full),
            pltpu.SemaphoreType.DMA((1 + 4 * len(STEPS),)),
        ],
        gathered,
        near,
        target,
        scale,
        column,
        basis,
        *tables,
    )
    if lax.axis_size("sig") == 2:
        other = swapped(sums, "sig", lambda i: i ^ 1)
    else:
        other = lax.psum(sums, "sig") - sums
    mean, = call(mean_kernel, "mean", [vmem] * 2, [((1, points), full)], [], sums, other)
    return potential, mean.reshape(points)


def solution(mesh):
    in_specs = (P(None, "space"), P("sig", "space"), P("space"), P("sig"))
    out_specs = (P("sig", "space"), P("space"))
    return jax.shard_map(per_device, mesh=mesh, in_specs=in_specs, out_specs=out_specs, check_vma=False)
```

time: 36.8 us -> 96.5 us (2.62)
  waiting for transfers between devices: 1.26 us -> 55.1 us
  starting transfers between devices: 15.9 us -> 0.11 us
  between operations: 0.71 us -> 14.1 us
  Pallas kernels: 18.7 us -> 22.9 us
  local copies, waits for them, and re-layouts: 0 us -> 4.12 us
    all_gather x0 -> x1, waiting for transfers between devices: none -> 53.9 us  [per_device(): gathered = lax.all_gather(own, 'space')]
    ppermute x2 -> x0, starting transfers between devices: 8.67 us -> none  [across_layers(): lax.ppermute(block, 'space', [pair for pair in pairs if abs(pair[0] - pai...]
    ppermute x6 -> x1, starting transfers between devices: 7.22 us -> 0.07 us  [swapped(): lax.ppermute(block, axis, [(partner(i), i) for i in range(size) if 0 <= p...]
    unnamed x0 -> x4, local copies, waits for them, and re-layouts: none -> 4.12 us
    pallas_call x7 -> x4, Pallas kernels: 18.7 us -> 22.9 us  [call(): pl.pallas_call(kernel, in_specs=in_specs, out_specs=[vmem] * len(outs), o...]
  transfers between devices with their start and end apart: 8 -> 2, of which waited for: 2 -> 2; matrix products, arithmetic and copies ran while one was open for 0% -> 0% of each run, Pallas kernels for 35% -> 7%
where the time goes in v8:
time: 96.5 us; the launch traced here: 96.2 us
  waiting for transfers between devices  55.1 us (57%)
  Pallas kernels  22.9 us (24%)
  between operations  14.1 us (15%)
  local copies, waits for them, and re-layouts  4.12 us (4%)
    all_gather x1, waiting for transfers between devices, per_device(): gathered = lax.all_gather(own, 'space')  53.9 us
    pallas_call x4, Pallas kernels, call(): pl.pallas_call(kernel, in_specs=in_specs, out_specs=[vmem] * len(outs), o...  22.9 us
    unnamed x4, local copies, waits for them, and re-layouts  4.12 us
  transfers between devices with their start and end apart: 2, of which 2 were waited for; matrix products, arithmetic and copies ran while one was open for 0% of the time, Pallas kernels for 7%

profile of v8, /device:TPU:0, one launch (start us, length us, event | category | flops | bytes accessed | tf_op | source)
XLA Modules:
  0.0 96.2 jit_solution(8186564018363431727)
XLA Ops:
  7.2 0.0 all-gather.3.cloned.1.call-start
  7.2 4.0 %pack.1 = (bf16[24,2560]{1,0:T(8,128)(2,1)}, bf16[128,2048]{1,0:T(8,128)(2,1)S(1)}) custom-call(s32[8]{0:T(128)} %count_in.3, f32[3,2048]{1,0:T(4,128)} %positions_in.1, bf16[17,2048]{1,0:T(8,128)(2,1)} %density_in.1), custom_call_target="tpu_custom_call" | custom-call | tf_op jit(solution)/shard_map/pack/pallas_call | solution.py:385
  11.2 0.0 all-gather.3.cloned.1.call-update
  11.3 7.0 %near_own.1 = (f32[24,2048]{1,0:T(8,128)S(1)}, bf16[2048,48]{1,0:T(8,128)(2,1)}, bf16[48,2048]{1,0:T(8,128)(2,1)S(1)}, f32[1,2048]{1,0:T(1,128)S(1)}, f32[24,128...) custom-call(s32[8]{0:T(128)} %count_in.3, ...), custom_call_target="tpu_custom_call" | custom-call | tf_op jit(solution)/shard_map/near_own/pallas_call | solution.py:385
  18.3 0.0 copy-start
  18.3 1.9 %copy-done = bf16[4096,512]{1,0:T(8,128)(2,1)} copy-done((bf16[4096,512]{1,0:T(8,128)(2,1)}, bf16[4096,512]{1,0:T(8,128)(2,1)S(1)}, u32[]{:S(2)}) %copy-start) | copy-done | bytes 4194328
  20.2 53.9 %all-gather.3.cloned.1.call-done = bf16[384,2560]{1,0:T(8,128)(2,1)} async-done(((bf16[24,2560]{1,0:T(8,128)(2,1)}), bf16[384,2560]{1,0:T(8,128)(2,1)}) %all-gather.3.cloned.1.call-update) | async-done | bytes 1966096 | tf_op jit(solution)/shard_map/all_gather | solution.py:413
  74.2 0.0 copy-start.1
  74.2 2.2 %copy-done.1 = bf16[4096,512]{1,0:T(8,128)(2,1)S(1)} copy-done((bf16[4096,512]{1,0:T(8,128)(2,1)S(1)}, bf16[4096,512]{1,0:T(8,128)(2,1)}, u32[]{:S(2)}) %copy-start.1) | copy-done | bytes 4194328
  76.3 11.1 %near_rest.1 = (f32[17,2048]{1,0:T(8,128)}, f32[1,2176]{1,0:T(1,128)S(1)}) custom-call(bf16[16,24,2560]{2,1,0:T(8,128)(2,1)} %bitcast.2, f32[24,2048]{1,0:T(8,128)S(1)} %get-tuple-element.15.early, bf16[48,2048]{1,0:T(8,128)(2,1)S(1)} %get-tuple-element.16.target, f32[1,2048]{1,0:T(1,128)S(1)} %get-tuple-element.17.scale, ...), custom_call_target="tpu_custom_call" | custom-call | tf_op jit(solution)/shard_map/near_rest/pallas_call | solution.py:385
  87.5 0.1 collective-permute-start
  87.6 1.2 %collective-permute-done.other = f32[1,2176]{1,0:T(1,128)S(1)} collective-permute-done((f32[1,2176]{1,0:T(1,128)S(1)}, f32[1,2176]{1,0:T(1,128)S(1)}, u32[]{:S(2)}, u32[]{:S(2)}) %collective-permute-start) | collective-permute-done | bytes 8736 | tf_op jit(solution)/shard_map/ppermute | solution.py:375
  88.7 0.7 mean.1
Async XLA Ops:
  7.2 67.0 %all-gather.3.cloned.1.call-start = ((), (), s32[]{:S(2)}) async-start(), calls=%async_computation | async-start | bytes 2088960 | tf_op jit(solution)/shard_map/all_gather | solution.py:413
  18.3 1.9 %copy-start = (bf16[4096,512]{1,0:T(8,128)(2,1)}, bf16[4096,512]{1,0:T(8,128)(2,1)S(1)}, u32[]{:S(2)}) copy-start(bf16[4096,512]{1,0:T(8,128)(2,1)S(1)} %get-tuple-element.20.far) | copy-start | bytes 12582916
  74.2 2.2 %copy-start.1 = (bf16[4096,512]{1,0:T(8,128)(2,1)S(1)}, bf16[4096,512]{1,0:T(8,128)(2,1)}, u32[]{:S(2)}) copy-start(bf16[4096,512]{1,0:T(8,128)(2,1)} %copy-done) | copy-start | bytes 12582916
  87.5 1.2 %collective-permute-start = (f32[1,2176]{1,0:T(1,128)S(1)}, f32[1,2176]{1,0:T(1,128)S(1)}, u32[]{:S(2)}, u32[]{:S(2)}) collective-permute-start(f32[1,2176]{1,0:T(1,128)S(1)} %get-tuple-element.25.mine), channel_id=1, source_target_pairs={{1,0},{0,1},{3,2},{2,3},{5,4},{4,5},{7,6},{6,7},{9,8},{8,9},{11,10... | collective-permute-start | bytes 26120 | tf_op jit(solution)/shard_map/ppermute | solution.py:375
Sparse Core Ops, SparseCore 0:
  11.4 62.7 all-gather.2

commit v9 on v8

--- a/solution.py
+++ b/solution.py
@@ -17,6 +17,7 @@
 LEAVES = 8 * SLOT
 MEGA = 1024 * 1024
 FEATURES = 48
+EARLY = 2
 
 
 def exponent_table(order_max):
@@ -132,8 +133,11 @@
     return copies
 
 
-def pack_kernel(count_in, positions_in, density_in, own, basis, count, positions, density, mono, sems):
-    copies = fetch([(count_in, count), (positions_in, positions), (density_in, density)], sems)
+def pack_kernel(count_in, positions_in, density_in, shift_in, own, basis, moments, totals, *rest):
+    payloads, (count, positions, density, shift, mono, sems) = rest[:2], rest[2:]
+    copies = fetch(
+        [(count_in, count), (positions_in, positions), (density_in, density), (shift_in, shift)], sems
+    )
     fields, points = density.shape
     pts = points // 8
     box_x, box_z = box_place()
@@ -172,7 +176,15 @@
         basis[0:SLOT, here] = high
         basis[SLOT:, here] = low
         parts.append(dot_nt(own[:, here], high))
-    own[:, points:] = low_bits(jnp.concatenate(parts, axis=1))
+    moment, rest = high_low(jnp.concatenate(parts, axis=1))
+    moments[...] = moment
+    total = dot(moment, shift[...]) + dot(rest, shift[...])
+    totals[...] = jnp.concatenate(high_low(total), axis=1)
+    for distance, payload in zip((1, 3), payloads):
+        bit = jnp.where((box_x ^ distance) > box_x, 1, 0)
+        for place in range(4):
+            payload[:, lanes(place * pts, pts)] = own[:, lanes((bit + 2 * place) * pts, pts)]
+        payload[:, lanes(4 * pts, LEAVES)] = moment
 
 
 def features(held, start, size, centre, target):
@@ -227,28 +239,14 @@
             near[:, places[piece]] = total
 
 
-def own_kernel(count_in, weights_in, own, *rest):
-    tables, (near, source, target, scale, column), rest = rest[:4], rest[4:9], rest[9:]
-    copies = fetch([*zip(tables, rest[:4]), (count_in, rest[4]), (weights_in, rest[5])], rest[6])
-    count, weights = rest[4:6]
-    points = near.shape[1]
-    pts = points // 8
-    for leaf in range(8):
-        centre = [bit - 0.5 for bit in bits(leaf)]
-        source[lanes(leaf * pts, pts), :] = source_features(own, leaf * pts, pts, centre)
-        target[:, lanes(leaf_slot(leaf) * pts, pts)] = low_bits(features(own, leaf * pts, pts, centre, True))
+def own_groups(near, first, last, target, source, own):
+    pts = source.shape[0] // 8
 
     def group(index, carry):
         pulled(near, index, target, source, own, [2 * p * pts for p in range(4)], 2 * pts)
         return carry
 
-    lax.fori_loop(0, 4, group, 0)
-    for copy in copies:
-        copy.wait()
-    column[...] = by_row([weights[field] for field in range(weights.shape[0])], column.shape)
-    lane_index = lax.broadcasted_iota(jnp.int32, (1, pts), 1)
-    for leaf in range(8):
-        scale[:, leaf * pts : (leaf + 1) * pts] = jnp.where(lane_index < count[leaf], 1.0 / (128.0 * pts), 0.0)
+    lax.fori_loop(first, last, group, 0)
 
 
 def box_columns(depth, box_x, box_z, nodes):
@@ -264,92 +262,139 @@
     return jnp.concatenate(blocks, axis=0)
 
 
-def rest_kernel(depth, gathered, early, target, scale, column, basis, far, nodes, spread, shift, *rest):
-    potential, sums, left, right, below, above, moments, sides, near, sems = rest
-    fields, points = potential.shape
+def own_kernel(depth, count_in, weights_in, own, *rest):
+    tables, outs, rest = rest[:3], rest[3:11], rest[11:]
+    near, source, target, scale, column, columns, far, spread = outs
+    nodes, count, weights, sems = rest
+    copies = fetch([*zip(tables, (far, spread, nodes)), (count_in, count), (weights_in, weights)], sems)
+    points = own.shape[1]
+    pts = points // 8
+    for leaf in range(8):
+        centre = [bit - 0.5 for bit in bits(leaf)]
+        source[lanes(leaf * pts, pts), :] = source_features(own, leaf * pts, pts, centre)
+        target[:, lanes(leaf_slot(leaf) * pts, pts)] = low_bits(features(own, leaf * pts, pts, centre, True))
+    own_groups(near, 0, EARLY, target, source, own)
+    for copy in copies:
+        copy.wait()
+    columns[...] = box_columns(depth, *box_place(), nodes)
+    column[...] = by_row([weights[field] for field in range(weights.shape[0])], column.shape)
+    lane_index = lax.broadcasted_iota(jnp.int32, (1, pts), 1)
+    for leaf in range(8):
+        scale[:, leaf * pts : (leaf + 1) * pts] = jnp.where(lane_index < count[leaf], 1.0 / (128.0 * pts), 0.0)
+
+
+def faces_of(faces, bit, given, own, left, right):
+    points = own.shape[1]
+    pts = points // 8
+    for y in range(2):
+        for x in range(4):
+            place = lanes((2 * x + y) * pts, pts)
+            if x in (0, 3):
+                side = left if x == 0 else right
+                faces[:, place] = side[:, lanes((y + 2 * bit) * pts, pts)]
+            else:
+                faces[:, place] = own[:, lanes((x - 1 + 2 * y + 4 * bit) * pts, pts)]
+    given_high, given_low = high_low(given)
+    faces[:, lanes(points, LEAVES)] = given_high
+    faces[:, lanes(points + LEAVES, LEAVES)] = given_low
+
+
+def row_kernel(own, moments, from_1, from_3, far, left, right, same, other, faces_even):
+    points = own.shape[1]
     pts = points // 8
     box_x, box_z = box_place()
-    all_moments = pltpu.make_async_copy(gathered.at[:, :, pl.ds(points, LEAVES)], moments, sems.at[0])
-    all_moments.start()
-    valid, label, faces = {}, {}, {}
-    for index, (step_x, step_z) in enumerate(STEPS):
-        x, z = box_x + step_x, box_z + step_z
-        inside = (x >= 0) & (x < ACROSS) & (z >= 0) & (z < depth)
-        step = (step_x, step_z)
-        valid[step] = inside
-        label[step] = jnp.where(inside, x + ACROSS * z, box_x + ACROSS * box_z)
-        pairs = []
-        for octant in range(8):
-            bit_x, bit_y, bit_z = bits(octant)
-            if step_x and bit_x != (step_x < 0) or step_z and bit_z != (step_z < 0):
-                continue
-            if step_z:
-                place = 2 * (1 + bit_x + 2 * step_x) + bit_y
-                held = above if step_z > 0 else below
-            else:
-                place = bit_y + 2 * bit_z
-                held = right if step_x > 0 else left
-            pairs.append((octant * pts, held.at[:, pl.ds(place * pts, pts)]))
-        faces[step] = pairs
-
-    def copies(index, step):
-        return [
-            pltpu.make_async_copy(gathered.at[label[step], :, pl.ds(start, pts)], place, sems.at[1 + 4 * index + turn])
-            for turn, (start, place) in enumerate(faces[step])
-        ]
-
-    for index, step in enumerate(STEPS):
-
-        @pl.when(valid[step])
-        def _(index=index, step=step):
-            for copy in copies(index, step):
-                copy.start()
-
-        @pl.when(jnp.logical_not(valid[step]))
-        def _(step=step):
-            for _, place in faces[step]:
-                place[...] = jnp.zeros(place.shape, jnp.bfloat16)
-
-    columns = box_columns(depth, box_x, box_z, nodes)
-    for index, step in enumerate(STEPS):
-
-        @pl.when(valid[step])
-        def _(index=index, step=step):
-            for copy in copies(index, step):
-                copy.wait()
-
-    near[...] = early[...]
+    for side, step in ((left, -1), (right, 1)):
+        side[...] = jnp.zeros(side.shape, side.dtype)
+        for distance, held in ((1, from_1), (3, from_3)):
+
+            @pl.when((box_x ^ distance) - box_x == step)
+            def _(side=side, held=held):
+                side[...] = held[...]
+
+    base = 4 * pts
+    row = jnp.concatenate([left[:, lanes(base, LEAVES)], moments[...], right[:, lanes(base, LEAVES)]], axis=1)
+    below_rows, same_rows, above_rows = pl.ds(0, 3 * LEAVES), pl.ds(3 * LEAVES, 2 * LEAVES), pl.ds(5 * LEAVES, 3 * LEAVES)
+    up = dot(row, far[below_rows, :])
+    down = dot(row, far[above_rows, :])
+    same[...] = dot(jnp.concatenate([row[:, :LEAVES], row[:, 2 * LEAVES :]], axis=1), far[same_rows, :])
+    odd = lax.rem(box_z, 2)
+    faces_of(faces_even, 1 - odd, jnp.where(odd == 0, up, down), own, left, right)
+    other[...] = jnp.where(odd == 0, down, up)
+
+
+def middle_kernel(own, left, right, other, early, source, target, near, faces_odd):
+    points = own.shape[1]
+    _, box_z = box_place()
+    faces_of(faces_odd, lax.rem(box_z, 2), other[...], own, left, right)
+    near[:, lanes(0, EARLY * points // 4)] = early[...]
+    own_groups(near, EARLY, 4, target, source, own)
+
+
+def side_kernel(left, right, early, target, near, sides):
+    pts = early.shape[1] // 8
     for step, side in ((0, left), (1, right)):
         for place in range(4):
             centre = (1.5 if step else -1.5, place % 2 - 0.5, place // 2 - 0.5)
             sides[lanes(place * pts, pts), :] = source_features(side, place * pts, pts, centre)
 
         def layer(index, carry, step=step, side=side):
-            pulled(near, step + 2 * index, target, sides, side, [0, 2 * pts], 2 * pts, near)
+            pulled(near, step + 2 * index, target, sides, side, [0, 2 * pts], 2 * pts, early)
             return carry
 
         lax.fori_loop(0, 2, layer, 0)
-    for step, held in ((0, below), (1, above)):
+
+
+def layer_pulls(near, early, step, inside, target, faces, sides):
+    points = early.shape[1]
+    pts = points // 8
+
+    @pl.when(inside)
+    def _():
         for place in range(8):
-            centre = (place // 2 - 1.5, place % 2 - 0.5, 1.5 if step else -1.5)
-            sides[lanes(place * pts, pts), :] = source_features(held, place * pts, pts, centre)
-
-        def pair(index, carry, step=step, held=held):
+            height = jnp.where(step == 1, 1.5, -1.5)
+            centre = (place // 2 - 1.5, place % 2 - 0.5, height)
+            sides[lanes(place * pts, pts), :] = source_features(faces, place * pts, pts, centre)
+
+        def pair(index, carry):
             starts = [(2 * x + 2 * index) * pts for x in range(3)]
-            pulled(near, index + 2 * step, target, sides, held, starts, 2 * pts, near)
+            pulled(near, index + 2 * step, target, sides, faces, starts, 2 * pts, early)
             return carry
 
         lax.fori_loop(0, 2, pair, 0)
 
-    all_moments.wait()
-    boxes = ACROSS * depth
-    totals = dot(jnp.concatenate([moments[box] for box in range(boxes)], axis=0), shift[...])
-    totals = jnp.concatenate([totals[box * ROWS : (box + 1) * ROWS] for box in range(boxes)], axis=1)
-    totals_high, totals_low = high_low(totals)
-    coarse_high, coarse_low = high_low(dot(totals_high, columns) + dot(totals_low, columns))
-    value = dot(coarse_high, spread[...]) + dot(coarse_low, spread[...])
-    around = [jnp.where(valid[step], moments[label[step]], jnp.bfloat16(0)) for step in STEPS]
-    value = value + dot(jnp.concatenate(around, axis=1), far[...])
+    @pl.when(jnp.logical_not(inside))
+    def _():
+        here = lanes(step * (points // 2), points // 2)
+        near[:, here] = early[:, here]
+
+
+def even_kernel(early, target, faces, near, sides):
+    _, box_z = box_place()
+    points = early.shape[1]
+    step = 1 - lax.rem(box_z, 2)
+    other = lanes((1 - step) * (points // 2), points // 2)
+    near[:, other] = early[:, other]
+    layer_pulls(near, early, step, box_z >= 0, target, faces, sides)
+
+
+def last_kernel(depth, early, target, faces_even, faces_odd, basis, scale, column, columns, spread, same, boxes, *rest):
+    potential, sums, near, sides = rest
+    fields, points = potential.shape
+    pts = points // 8
+    _, box_z = box_place()
+    step = lax.rem(box_z, 2)
+    other = lanes((1 - step) * (points // 2), points // 2)
+    near[:, other] = early[:, other]
+    inside = (box_z + 2 * step - 1 >= 0) & (box_z + 2 * step - 1 < depth)
+    layer_pulls(near, early, step, inside, target, faces_odd, sides)
+
+    totals_high = jnp.concatenate([boxes[box][:, :SLOT] for box in range(ACROSS * depth)], axis=1)
+    totals_low = jnp.concatenate([boxes[box][:, SLOT:] for box in range(ACROSS * depth)], axis=1)
+    coarse_high, coarse_low = high_low(dot(totals_high, columns[...]) + dot(totals_low, columns[...]))
+    value = same[...] + dot(coarse_high, spread[...]) + dot(coarse_low, spread[...])
+    for faces in (faces_even, faces_odd):
+        value = value + faces[:, lanes(points, LEAVES)].astype(jnp.float32)
+        value = value + faces[:, lanes(points + LEAVES, LEAVES)].astype(jnp.float32)
     local_high, local_low = high_low(value)
     weight = column[0:fields, 0:1]
     for leaf in range(8):
@@ -394,69 +439,122 @@
 
     half, full = jnp.bfloat16, jnp.float32
     shift = shift_table()
-    own, basis = call(
+    side_shape = ((ROWS, 4 * pts + LEAVES), half)
+    faces_shape = ((ROWS, points + 2 * LEAVES), half)
+    near_shape, sums_shape = ((ROWS, points), full), ((ROWS, LEAVES), full)
+    rows_scratch = pltpu.VMEM((8 * pts, FEATURES), half)
+    own, basis, moments, totals, *given = call(
         pack_kernel,
         "pack",
-        [hbm] * 3,
-        [((ROWS, points + LEAVES), half), ((2 * SLOT, points), half)],
+        [hbm] * 4,
+        [
+            ((ROWS, points), half),
+            ((2 * SLOT, points), half),
+            ((ROWS, LEAVES), half),
+            ((ROWS, 2 * SLOT), half),
+            side_shape,
+            side_shape,
+        ],
         [
             pltpu.SMEM((8,), jnp.int32),
             pltpu.VMEM((3, points), full),
             pltpu.VMEM((fields, points), half),
+            pltpu.VMEM((LEAVES, SLOT), half),
             pltpu.VMEM((SLOT, 8, pts), full),
-            pltpu.SemaphoreType.DMA((3,)),
+            pltpu.SemaphoreType.DMA((4,)),
         ],
         leaf_count,
         positions,
         density,
-    )
-    gathered = lax.all_gather(own, "space")
-    tables = [
-        jnp.asarray(far_table(), half),
-        jnp.asarray(box_nodes()),
-        jnp.asarray(shift.T.copy(), half),
         jnp.asarray(shift, half),
-    ]
-    near, source, target, scale, column, *tables = call(
-        own_kernel,
+    )
+    boxes = lax.all_gather(totals, "space")
+    from_1 = swapped(given[0], "space", lambda i: i ^ 1)
+    from_3 = swapped(given[1], "space", lambda i: i ^ 3)
+    near, source, target, scale, column, columns, far, spread = call(
+        functools.partial(own_kernel, depth),
         "near_own",
-        [hbm] * 2 + [vmem] + [hbm] * 4,
+        [hbm] * 2 + [vmem] + [hbm] * 3,
         [
-            ((ROWS, points), full),
+            ((ROWS, EARLY * points // 4), full),
             ((points, FEATURES), half),
             ((FEATURES, points), half),
             ((1, points), full),
             ((ROWS, 128), full),
-            *[(table.shape, table.dtype) for table in tables],
+            ((ACROSS * depth * SLOT, SLOT), half),
+            ((len(STEPS) * LEAVES, LEAVES), half),
+            ((SLOT, LEAVES), half),
         ],
-        [pltpu.SMEM((8,), jnp.int32), pltpu.SMEM((fields,), full), pltpu.SemaphoreType.DMA((6,))],
+        [
+            pltpu.VMEM((3, SLOT, SLOT), full),
+            pltpu.SMEM((8,), jnp.int32),
+            pltpu.SMEM((fields,), full),
+            pltpu.SemaphoreType.DMA((5,)),
+        ],
         leaf_count,
         sigma_weights,
         own,
-        *tables,
-    )
-    potential, sums = call(
-        functools.partial(rest_kernel, depth),
-        "near_rest",
-        [hbm] + [vmem] * 9,
-        [((fields, points), full), ((1, points + 128), full)],
-        [
-            pltpu.VMEM((ROWS, 4 * pts), half),
-            pltpu.VMEM((ROWS, 4 * pts), half),
-            pltpu.VMEM((ROWS, points), half),
-            pltpu.VMEM((ROWS, points), half),
-            pltpu.VMEM((ACROSS * depth, ROWS, LEAVES), half),
-            pltpu.VMEM((8 * pts, FEATURES), half),
-            pltpu.VMEM((ROWS, points), full),
-            pltpu.SemaphoreType.DMA((1 + 4 * len(STEPS),)),
-        ],
-        gathered,
+        jnp.asarray(far_table(), half),
+        jnp.asarray(shift.T.copy(), half),
+        jnp.asarray(box_nodes()),
+    )
+    left, right, same, other, faces_even = call(
+        row_kernel,
+        "row",
+        [vmem] * 5,
+        [side_shape, side_shape, sums_shape, sums_shape, faces_shape],
+        [],
+        own,
+        moments,
+        from_1,
+        from_3,
+        far,
+    )
+    faces_even = swapped(faces_even, "space", lambda i: i ^ ACROSS)
+    near, faces_odd = call(
+        middle_kernel,
+        "near_middle",
+        [vmem] * 7,
+        [near_shape, faces_shape],
+        [],
+        own,
+        left,
+        right,
+        other,
+        near,
+        source,
+        target,
+    )
+    faces_odd = swapped(faces_odd, "space", lambda i: i + ACROSS if i // ACROSS % 2 else i - ACROSS)
+    near, = call(
+        side_kernel,
+        "near_side",
+        [vmem] * 4,
+        [near_shape],
+        [pltpu.VMEM((4 * pts, FEATURES), half)],
+        left,
+        right,
         near,
         target,
+    )
+    near, = call(even_kernel, "near_even", [vmem] * 3, [near_shape], [rows_scratch], near, target, faces_even)
+    potential, sums = call(
+        functools.partial(last_kernel, depth),
+        "near_odd",
+        [vmem] * 11,
+        [((fields, points), full), ((1, points + 128), full)],
+        [pltpu.VMEM((ROWS, points), full), rows_scratch],
+        near,
+        target,
+        faces_even,
+        faces_odd,
+        basis,
         scale,
         column,
-        basis,
-        *tables,
+        columns,
+        spread,
+        same,
+        boxes,
     )
     if lax.axis_size("sig") == 2:
         other = swapped(sums, "sig", lambda i: i ^ 1)

time: 96.5 us -> 65.9 us (0.68)
  waiting for transfers between devices: 55.1 us -> 2.08 us
  blocking collectives: 0 us -> 39.4 us
  between operations: 14.1 us -> 0.67 us
  starting transfers between devices: 0.11 us -> 6.76 us
  Pallas kernels: 22.9 us -> 16.7 us
  local copies, waits for them, and re-layouts: 4.12 us -> 0 us
    all_gather x1 -> x0, waiting for transfers between devices: 53.9 us -> none  [per_device(): gathered = lax.all_gather(own, 'space')]
    all_gather x0 -> x1, blocking collectives: none -> 39.4 us  [per_device(): boxes = lax.all_gather(totals, 'space')]
    ppermute x1 -> x5, starting transfers between devices: 0.07 us -> 6.76 us  [swapped(): lax.ppermute(block, axis, [(partner(i), i) for i in range(size) if 0 <= p...]
    pallas_call x4 -> x8, Pallas kernels: 22.9 us -> 16.7 us  [call(): pl.pallas_call(kernel, in_specs=in_specs, out_specs=[vmem] * len(outs), o...]
    unnamed x4 -> x0, local copies, waits for them, and re-layouts: 4.12 us -> none
    ppermute x1 -> x5, waiting for transfers between devices: 1.16 us -> 2.08 us  [swapped(): lax.ppermute(block, axis, [(partner(i), i) for i in range(size) if 0 <= p...]
  transfers between devices with their start and end apart: 2 -> 5, of which waited for: 2 -> 2; matrix products, arithmetic and copies ran while one was open for 0% -> 0% of each run, Pallas kernels for 7% -> 16%
where the time goes in v9:
time: 65.9 us; the launch traced here: 65.7 us
  blocking collectives  39.4 us (60%)
  Pallas kernels  16.7 us (25%)
  starting transfers between devices  6.76 us (10%)
  waiting for transfers between devices  2.08 us (3%)
  between operations  0.67 us (1%)
    all_gather x1, blocking collectives, per_device(): boxes = lax.all_gather(totals, 'space')  39.4 us
    pallas_call x8, Pallas kernels, call(): pl.pallas_call(kernel, in_specs=in_specs, out_specs=[vmem] * len(outs), o...  16.7 us
    ppermute x5, starting transfers between devices, swapped(): lax.ppermute(block, axis, [(partner(i), i) for i in range(size) if 0 <= p...  6.76 us
    ppermute x5, waiting for transfers between devices, swapped(): lax.ppermute(block, axis, [(partner(i), i) for i in range(size) if 0 <= p...  2.08 us
  transfers between devices with their start and end apart: 5, of which 2 were waited for; matrix products, arithmetic and copies ran while one was open for 0% of the time, Pallas kernels for 16%

profile of v9, /device:TPU:0, one launch (start us, length us, event | category | flops | bytes accessed | tf_op | source)
XLA Modules:
  0.0 65.7 jit_solution(9936978421939444935)
XLA Ops:
  0.6 3.0 %pack.1 = (bf16[24,2048]{1,0:T(8,128)(2,1)S(1)}, bf16[128,2048]{1,0:T(8,128)(2,1)S(1)}, bf16[24,512]{1,0:T(8,128)(2,1)S(1)}, bf16[24,128]{1,0:T(8,128)(2,1)S(1)}...) custom-call(s32[8]{0:T(128)} %count_in.3, f32[3,2048]{1,0:T(4,128)} %positions_in.1, ...), custom_call_target="tpu_custom_call" | custom-call | tf_op jit(solution)/shard_map/pack/pallas_call | solution.py:430
  3.7 3.0 %collective-permute-start = (bf16[24,1536]{1,0:T(8,128)(2,1)S(1)}, bf16[24,1536]{1,0:T(8,128)(2,1)S(1)}, u32[]{:S(2)}, u32[]{:S(2)}) collective-permute-start(bf16[24,1536]{1,0:T(8,128)(2,1)S(1)} %get-tuple-element.27), channel_id=1, source_target_pairs={{2,0},{0,2},{6,4},{4,6},{10,8},{8,10},{14,12},{12,14},{18,16},{16,... | collective-permute-start | bytes 221192 | tf_op jit(solution)/shard_map/ppermute | solution.py:420
  6.7 1.5 %collective-permute-start.1 = (bf16[24,1536]{1,0:T(8,128)(2,1)S(1)}, bf16[24,1536]{1,0:T(8,128)(2,1)S(1)}, u32[]{:S(2)}, u32[]{:S(2)}) collective-permute-start(bf16[24,1536]{1,0:T(8,128)(2,1)S(1)} %get-tuple-element.28), channel_id=1, source_target_pairs={{6,0},{4,2},{2,4},{0,6},{14,8},{12,10},{10,12},{8,14},{22,16},{20,... | collective-permute-start | bytes 221192 | tf_op jit(solution)/shard_map/ppermute | solution.py:420
  8.2 3.0 %near_own.1 = (f32[24,1024]{1,0:T(8,128)S(1)}, bf16[2048,48]{1,0:T(8,128)(2,1)S(1)}, bf16[48,2048]{1,0:T(8,128)(2,1)S(1)}, f32[1,2048]{1,0:T(1,128)S(1)}, f32[24...) custom-call(s32[8]{0:T(128)} %count_in.3, ...), custom_call_target="tpu_custom_call" | custom-call | tf_op jit(solution)/shard_map/near_own/pallas_call | solution.py:430
  11.2 0.0 collective-permute-done.from_1
  11.2 0.9 %collective-permute-done.1.from_3 = bf16[24,1536]{1,0:T(8,128)(2,1)S(1)} collective-permute-done((bf16[24,1536]{1,0:T(8,128)(2,1)S(1)}, bf16[24,1536]{1,0:T(8,128)(2,1)S(1)}, u32[]{:S(2)}, u32[]{:S(2)}) %collective-permute-start.1) | collective-permute-done | bytes 73760 | tf_op jit(solution)/shard_map/ppermute | solution.py:420
  12.1 0.8 %row.1 = (bf16[24,1536]{1,0:T(8,128)(2,1)S(1)}, bf16[24,1536]{1,0:T(8,128)(2,1)S(1)}, f32[24,512]{1,0:T(8,128)S(1)}, f32[24,512]{1,0:T(8,128)S(1)}, bf16[24,3072]{1,0:T(8,128)(2,1)S(1)}) custom-call(bf16[24,2048]{1,0:T(8,128)(2,1)S(1)} %get-tuple-element.25.own, bf16[24,512]{1,0:T(8,128)(2,1)S(1)} %get-tuple-element.26.moments, ...), custom_call_target="tpu_custom_call" | custom-call | tf_op jit(solution)/shard_map/row/pallas_call | solution.py:430
  12.9 1.6 %collective-permute-start.2 = (bf16[24,3072]{1,0:T(8,128)(2,1)S(1)}, bf16[24,3072]{1,0:T(8,128)(2,1)S(1)}, u32[]{:S(2)}, u32[]{:S(2)}) collective-permute-start(bf16[24,3072]{1,0:T(8,128)(2,1)S(1)} %get-tuple-element.37), channel_id=1, source_target_pairs={{8,0},{10,2},{12,4},{14,6},{0,8},{2,10},{4,12},{6,14},{24,16},{26,... | collective-permute-start | bytes 442376 | tf_op jit(solution)/shard_map/ppermute | solution.py:420
  14.5 2.5 %near_middle.1 = (f32[24,2048]{1,0:T(8,128)S(1)}, bf16[24,3072]{1,0:T(8,128)(2,1)S(1)}) custom-call(bf16[24,2048]{1,0:T(8,128)(2,1)S(1)} %get-tuple-element.25.own, bf16[24,1536]{1,0:T(8,128)(2,1)S(1)} %get-tuple-element.30.left, bf16[24,1536]{1,0:T(8,128)(2,1)S(1)} %get-tuple-element.31.right, f32[24,512]{1,0:T(8,128)S(1)} %get-tuple-element.32.other, ...), custom_call_target="tpu_custom_call" | custom-call | tf_op jit(solution)/shard_map/near_middle/pallas_call | solution.py:430
  17.0 0.7 %collective-permute-start.3 = (bf16[24,3072]{1,0:T(8,128)(2,1)S(1)}, bf16[24,3072]{1,0:T(8,128)(2,1)S(1)}, u32[]{:S(2)}, u32[]{:S(2)}) collective-permute-start(bf16[24,3072]{1,0:T(8,128)(2,1)S(1)} %get-tuple-element.38), channel_id=1, source_target_pairs={{16,8},{18,10},{20,12},{22,14},{8,16},{10,18},{12,20},{14,22},{17,... | collective-permute-start | bytes 442376 | tf_op jit(solution)/shard_map/ppermute | solution.py:420
  17.6 39.4 %all-gather = bf16[384,128]{1,0:T(8,128)(2,1)S(1)} all-gather(bf16[24,128]{1,0:T(8,128)(2,1)S(1)} %get-tuple-element.45), channel_id=2, replica_groups=mesh['space'=16,'sig'=2] {'space'}, dimensions={0}, use_global_device_ids=true | all-gather | bytes 104448 | tf_op jit(solution)/shard_map/all_gather | solution.py:471
  57.1 3.2 %near_side.1.early = f32[24,2048]{1,0:T(8,128)S(1)} custom-call(bf16[24,1536]{1,0:T(8,128)(2,1)S(1)} %get-tuple-element.30.left, bf16[24,1536]{1,0:T(8,128)(2,1)S(1)} %get-tuple-element.31.right, f32[24,2048]{1,0:T(8,128)S(1)} %get-tuple-element.36.early, bf16[48,2048]{1,0:T(8,128)(2,1)S(1)} %get-tuple-element.35.target), custom_call_target="tpu_custom_call" | custom-call | tf_op jit(solution)/shard_map/near_side/pallas_call | solution.py:430
  60.3 0.0 collective-permute-done.2.faces.faces_even
  60.3 2.1 %near_even.1.early = f32[24,2048]{1,0:T(8,128)S(1)} custom-call(f32[24,2048]{1,0:T(8,128)S(1)} %near_side.1.early, bf16[48,2048]{1,0:T(8,128)(2,1)S(1)} %get-tuple-element.35.target, bf16[24,3072]{1,0:T(8,128)(2,1)S(1)} %collective-permute-done.2.faces.faces_even), custom_call_target="tpu_custom_call" | custom-call | tf_op jit(solution)/shard_map/near_even/pallas_call | solution.py:430
  62.4 0.0 collective-permute-done.3.faces_odd
  62.4 1.4 %near_odd.1 = (f32[17,2048]{1,0:T(8,128)}, f32[1,2176]{1,0:T(1,128)S(1)}) custom-call(f32[24,2048]{1,0:T(8,128)S(1)} %near_even.1.early, bf16[48,2048]{1,0:T(8,128)(2,1)S(1)} %get-tuple-element.35.target, bf16[24,3072]{1,0:T(8,128)(2,1)S(1)} %collective-permute-done.2.faces.faces_even, bf16[24,3072]{1,0:T(8,128)(2,1)S(1)} %collective-permute-done.3.faces_odd, ...), custom_call_target="tpu_custom_call" | custom-call | tf_op jit(solution)/shard_map/near_odd/pallas_call | solution.py:430
  63.9 0.0 collective-permute-start.4
  63.9 1.2 %collective-permute-done.4.other = f32[1,2176]{1,0:T(1,128)S(1)} collective-permute-done((f32[1,2176]{1,0:T(1,128)S(1)}, f32[1,2176]{1,0:T(1,128)S(1)}, u32[]{:S(2)}, u32[]{:S(2)}) %collective-permute-start.4) | collective-permute-done | bytes 8736 | tf_op jit(solution)/shard_map/ppermute | solution.py:420
  65.0 0.7 %mean.1 = f32[1,2048]{1,0:T(1,128)} custom-call(f32[1,2176]{1,0:T(1,128)S(1)} %get-tuple-element.47.mine, f32[1,2176]{1,0:T(1,128)S(1)} %collective-permute-done.4.other), custom_call_target="tpu_custom_call" | custom-call | tf_op jit(solution)/shard_map/mean/pallas_call | solution.py:430
Async XLA Ops:
  3.7 7.5 %collective-permute-start = (bf16[24,1536]{1,0:T(8,128)(2,1)S(1)}, bf16[24,1536]{1,0:T(8,128)(2,1)S(1)}, u32[]{:S(2)}, u32[]{:S(2)}) collective-permute-start(bf16[24,1536]{1,0:T(8,128)(2,1)S(1)} %get-tuple-element.27), channel_id=1, source_target_pairs={{2,0},{0,2},{6,4},{4,6},{10,8},{8,10},{14,12},{12,14},{18,16},{16,... | collective-permute-start | bytes 221192 | tf_op jit(solution)/shard_map/ppermute | solution.py:420
  6.7 5.4 %collective-permute-start.1 = (bf16[24,1536]{1,0:T(8,128)(2,1)S(1)}, bf16[24,1536]{1,0:T(8,128)(2,1)S(1)}, u32[]{:S(2)}, u32[]{:S(2)}) collective-permute-start(bf16[24,1536]{1,0:T(8,128)(2,1)S(1)} %get-tuple-element.28), channel_id=1, source_target_pairs={{6,0},{4,2},{2,4},{0,6},{14,8},{12,10},{10,12},{8,14},{22,16},{20,... | collective-permute-start | bytes 221192 | tf_op jit(solution)/shard_map/ppermute | solution.py:420
  12.9 47.4 %collective-permute-start.2 = (bf16[24,3072]{1,0:T(8,128)(2,1)S(1)}, bf16[24,3072]{1,0:T(8,128)(2,1)S(1)}, u32[]{:S(2)}, u32[]{:S(2)}) collective-permute-start(bf16[24,3072]{1,0:T(8,128)(2,1)S(1)} %get-tuple-element.37), channel_id=1, source_target_pairs={{8,0},{10,2},{12,4},{14,6},{0,8},{2,10},{4,12},{6,14},{24,16},{26,... | collective-permute-start | bytes 442376 | tf_op jit(solution)/shard_map/ppermute | solution.py:420
  17.0 45.5 %collective-permute-start.3 = (bf16[24,3072]{1,0:T(8,128)(2,1)S(1)}, bf16[24,3072]{1,0:T(8,128)(2,1)S(1)}, u32[]{:S(2)}, u32[]{:S(2)}) collective-permute-start(bf16[24,3072]{1,0:T(8,128)(2,1)S(1)} %get-tuple-element.38), channel_id=1, source_target_pairs={{16,8},{18,10},{20,12},{22,14},{8,16},{10,18},{12,20},{14,22},{17,... | collective-permute-start | bytes 442376 | tf_op jit(solution)/shard_map/ppermute | solution.py:420
  63.9 1.2 %collective-permute-start.4 = (f32[1,2176]{1,0:T(1,128)S(1)}, f32[1,2176]{1,0:T(1,128)S(1)}, u32[]{:S(2)}, u32[]{:S(2)}) collective-permute-start(f32[1,2176]{1,0:T(1,128)S(1)} %get-tuple-element.47.mine), channel_id=1, source_target_pairs={{1,0},{0,1},{3,2},{2,3},{5,4},{4,5},{7,6},{6,7},{9,8},{8,9},{11,10... | collective-permute-start | bytes 26120 | tf_op jit(solution)/shard_map/ppermute | solution.py:420

commit v10 on v9

--- a/solution.py
+++ b/solution.py
@@ -179,7 +179,7 @@
     moment, rest = high_low(jnp.concatenate(parts, axis=1))
     moments[...] = moment
     total = dot(moment, shift[...]) + dot(rest, shift[...])
-    totals[...] = jnp.concatenate(high_low(total), axis=1)
+    totals[...] = jnp.broadcast_to(jnp.concatenate(high_low(total), axis=1)[None], totals.shape)
     for distance, payload in zip((1, 3), payloads):
         bit = jnp.where((box_x ^ distance) > box_x, 1, 0)
         for place in range(4):
@@ -451,7 +451,7 @@
             ((ROWS, points), half),
             ((2 * SLOT, points), half),
             ((ROWS, LEAVES), half),
-            ((ROWS, 2 * SLOT), half),
+            ((ACROSS * depth, ROWS, 2 * SLOT), half),
             side_shape,
             side_shape,
         ],
@@ -468,7 +468,7 @@
         density,
         jnp.asarray(shift, half),
     )
-    boxes = lax.all_gather(totals, "space")
+    boxes = lax.all_to_all(totals, "space", 0, 0, tiled=True)
     from_1 = swapped(given[0], "space", lambda i: i ^ 1)
     from_3 = swapped(given[1], "space", lambda i: i ^ 3)
     near, source, target, scale, column, columns, far, spread = call(

time: 65.9 us -> 36.1 us (0.55)
  the two profiles are of different devices: /device:TPU:0 before, /device:TPU:9 now
where the time goes in v10:
time: 36.1 us; the launch traced here: 35.9 us
  Pallas kernels  19.5 us (54%)
  starting transfers between devices  14.8 us (41%)
  waiting for transfers between devices  0.84 us (2%)
  between operations  0.69 us (2%)
    pallas_call x8, Pallas kernels, call(): pl.pallas_call(kernel, in_specs=in_specs, out_specs=[vmem] * len(outs), o...  19.5 us
    ppermute x5, starting transfers between devices, swapped(): lax.ppermute(block, axis, [(partner(i), i) for i in range(size) if 0 <= p...  9.12 us
    all_to_all x1, starting transfers between devices, per_device(): boxes = lax.all_to_all(totals, 'space', 0, 0, tiled=True)  5.71 us
    ppermute x5, waiting for transfers between devices, swapped(): lax.ppermute(block, axis, [(partner(i), i) for i in range(size) if 0 <= p...  0.84 us
  transfers between devices with their start and end apart: 6, of which 1 were waited for; matrix products, arithmetic and copies ran while one was open for 0% of the time, Pallas kernels for 33%

profile of v10, /device:TPU:9, one launch (start us, length us, event | category | flops | bytes accessed | tf_op | source)
XLA Modules:
  0.0 35.9 jit_solution(11469032501712320111)
XLA Ops:
  0.6 3.7 %pack.1 = (bf16[24,2048]{1,0:T(8,128)(2,1)S(1)}, bf16[128,2048]{1,0:T(8,128)(2,1)S(1)}, bf16[24,512]{1,0:T(8,128)(2,1)S(1)}, bf16[16,24,128]{2,1,0:T(8,128)(2,1)...) custom-call(s32[8]{0:T(128)} %count_in.3, f32[3,2048]{1,0:T(4,128)} %positions_in.1, ...), custom_call_target="tpu_custom_call" | custom-call | tf_op jit(solution)/shard_map/pack/pallas_call | solution.py:430
  4.3 1.3 %collective-permute-start = (bf16[24,1536]{1,0:T(8,128)(2,1)S(1)}, bf16[24,1536]{1,0:T(8,128)(2,1)S(1)}, u32[]{:S(2)}, u32[]{:S(2)}) collective-permute-start(bf16[24,1536]{1,0:T(8,128)(2,1)S(1)} %get-tuple-element.27), channel_id=1, source_target_pairs={{2,0},{0,2},{6,4},{4,6},{10,8},{8,10},{14,12},{12,14},{18,16},{16,... | collective-permute-start | bytes 221192 | tf_op jit(solution)/shard_map/ppermute | solution.py:420
  5.6 1.2 %collective-permute-start.1 = (bf16[24,1536]{1,0:T(8,128)(2,1)S(1)}, bf16[24,1536]{1,0:T(8,128)(2,1)S(1)}, u32[]{:S(2)}, u32[]{:S(2)}) collective-permute-start(bf16[24,1536]{1,0:T(8,128)(2,1)S(1)} %get-tuple-element.28), channel_id=1, source_target_pairs={{6,0},{4,2},{2,4},{0,6},{14,8},{12,10},{10,12},{8,14},{22,16},{20,... | collective-permute-start | bytes 221192 | tf_op jit(solution)/shard_map/ppermute | solution.py:420
  6.8 5.7 %all-to-all-start = ((bf16[16,24,128]{2,1,0:T(8,128)(2,1)}), bf16[16,24,128]{2,1,0:T(8,128)(2,1)S(1)}, u32[]{:S(2)}, u32[]{:S(2)}) async-start(bf16[16,24,128]{2,1,0:T(8,128)(2,1)} %get-tuple-element.45), calls=%async_computation | async-start | bytes 196608 | tf_op jit(solution)/shard_map/all_to_all | solution.py:471
  12.5 3.0 %near_own.1 = (f32[24,1024]{1,0:T(8,128)S(1)}, bf16[2048,48]{1,0:T(8,128)(2,1)S(1)}, bf16[48,2048]{1,0:T(8,128)(2,1)S(1)}, f32[1,2048]{1,0:T(1,128)S(1)}, f32[24...) custom-call(s32[8]{0:T(128)} %count_in.3, ...), custom_call_target="tpu_custom_call" | custom-call | tf_op jit(solution)/shard_map/near_own/pallas_call | solution.py:430
  15.5 0.0 collective-permute-done.from_1
  15.5 0.0 collective-permute-done.1.from_3
  15.5 0.9 %row.1 = (bf16[24,1536]{1,0:T(8,128)(2,1)S(1)}, bf16[24,1536]{1,0:T(8,128)(2,1)S(1)}, f32[24,512]{1,0:T(8,128)S(1)}, f32[24,512]{1,0:T(8,128)S(1)}, bf16[24,3072]{1,0:T(8,128)(2,1)S(1)}) custom-call(bf16[24,2048]{1,0:T(8,128)(2,1)S(1)} %get-tuple-element.25.own, bf16[24,512]{1,0:T(8,128)(2,1)S(1)} %get-tuple-element.26.moments, ...), custom_call_target="tpu_custom_call" | custom-call | tf_op jit(solution)/shard_map/row/pallas_call | solution.py:430
  16.4 0.1 collective-permute-start.2
  16.5 2.5 %near_middle.1 = (f32[24,2048]{1,0:T(8,128)S(1)}, bf16[24,3072]{1,0:T(8,128)(2,1)S(1)}) custom-call(bf16[24,2048]{1,0:T(8,128)(2,1)S(1)} %get-tuple-element.25.own, bf16[24,1536]{1,0:T(8,128)(2,1)S(1)} %get-tuple-element.30.left, bf16[24,1536]{1,0:T(8,128)(2,1)S(1)} %get-tuple-element.31.right, f32[24,512]{1,0:T(8,128)S(1)} %get-tuple-element.32.other, ...), custom_call_target="tpu_custom_call" | custom-call | tf_op jit(solution)/shard_map/near_middle/pallas_call | solution.py:430
  19.0 4.2 %collective-permute-start.3 = (bf16[24,3072]{1,0:T(8,128)(2,1)S(1)}, bf16[24,3072]{1,0:T(8,128)(2,1)S(1)}, u32[]{:S(2)}, u32[]{:S(2)}) collective-permute-start(bf16[24,3072]{1,0:T(8,128)(2,1)S(1)} %get-tuple-element.38), channel_id=1, source_target_pairs={{16,8},{18,10},{20,12},{22,14},{8,16},{10,18},{12,20},{14,22},{17,... | collective-permute-start | bytes 442376 | tf_op jit(solution)/shard_map/ppermute | solution.py:420
  23.2 3.2 %near_side.1.early = f32[24,2048]{1,0:T(8,128)S(1)} custom-call(bf16[24,1536]{1,0:T(8,128)(2,1)S(1)} %get-tuple-element.30.left, bf16[24,1536]{1,0:T(8,128)(2,1)S(1)} %get-tuple-element.31.right, f32[24,2048]{1,0:T(8,128)S(1)} %get-tuple-element.36.early, bf16[48,2048]{1,0:T(8,128)(2,1)S(1)} %get-tuple-element.35.target), custom_call_target="tpu_custom_call" | custom-call | tf_op jit(solution)/shard_map/near_side/pallas_call | solution.py:430
  26.4 0.0 collective-permute-done.2.faces.faces_even
  26.4 2.1 %near_even.1.early = f32[24,2048]{1,0:T(8,128)S(1)} custom-call(f32[24,2048]{1,0:T(8,128)S(1)} %near_side.1.early, bf16[48,2048]{1,0:T(8,128)(2,1)S(1)} %get-tuple-element.35.target, bf16[24,3072]{1,0:T(8,128)(2,1)S(1)} %collective-permute-done.2.faces.faces_even), custom_call_target="tpu_custom_call" | custom-call | tf_op jit(solution)/shard_map/near_even/pallas_call | solution.py:430
  28.5 0.0 all-to-all-done.boxes
  28.5 0.0 collective-permute-done.3.faces_odd
  28.6 3.5 %near_odd.1 = (f32[17,2048]{1,0:T(8,128)}, f32[1,2176]{1,0:T(1,128)S(1)}) custom-call(f32[24,2048]{1,0:T(8,128)S(1)} %near_even.1.early, bf16[48,2048]{1,0:T(8,128)(2,1)S(1)} %get-tuple-element.35.target, bf16[24,3072]{1,0:T(8,128)(2,1)S(1)} %collective-permute-done.2.faces.faces_even, bf16[24,3072]{1,0:T(8,128)(2,1)S(1)} %collective-permute-done.3.faces_odd, ...), custom_call_target="tpu_custom_call" | custom-call | tf_op jit(solution)/shard_map/near_odd/pallas_call | solution.py:430
  32.0 2.3 %collective-permute-start.4 = (f32[1,2176]{1,0:T(1,128)S(1)}, f32[1,2176]{1,0:T(1,128)S(1)}, u32[]{:S(2)}, u32[]{:S(2)}) collective-permute-start(f32[1,2176]{1,0:T(1,128)S(1)} %get-tuple-element.47.mine), channel_id=1, source_target_pairs={{1,0},{0,1},{3,2},{2,3},{5,4},{4,5},{7,6},{6,7},{9,8},{8,9},{11,10... | collective-permute-start | bytes 26120 | tf_op jit(solution)/shard_map/ppermute | solution.py:420
  34.4 0.8 %collective-permute-done.4.other = f32[1,2176]{1,0:T(1,128)S(1)} collective-permute-done((f32[1,2176]{1,0:T(1,128)S(1)}, f32[1,2176]{1,0:T(1,128)S(1)}, u32[]{:S(2)}, u32[]{:S(2)}) %collective-permute-start.4) | collective-permute-done | bytes 8736 | tf_op jit(solution)/shard_map/ppermute | solution.py:420
  35.2 0.7 %mean.1 = f32[1,2048]{1,0:T(1,128)} custom-call(f32[1,2176]{1,0:T(1,128)S(1)} %get-tuple-element.47.mine, f32[1,2176]{1,0:T(1,128)S(1)} %collective-permute-done.4.other), custom_call_target="tpu_custom_call" | custom-call | tf_op jit(solution)/shard_map/mean/pallas_call | solution.py:430
Async XLA Ops:
  4.3 11.2 %collective-permute-start = (bf16[24,1536]{1,0:T(8,128)(2,1)S(1)}, bf16[24,1536]{1,0:T(8,128)(2,1)S(1)}, u32[]{:S(2)}, u32[]{:S(2)}) collective-permute-start(bf16[24,1536]{1,0:T(8,128)(2,1)S(1)} %get-tuple-element.27), channel_id=1, source_target_pairs={{2,0},{0,2},{6,4},{4,6},{10,8},{8,10},{14,12},{12,14},{18,16},{16,... | collective-permute-start | bytes 221192 | tf_op jit(solution)/shard_map/ppermute | solution.py:420
  5.6 9.9 %collective-permute-start.1 = (bf16[24,1536]{1,0:T(8,128)(2,1)S(1)}, bf16[24,1536]{1,0:T(8,128)(2,1)S(1)}, u32[]{:S(2)}, u32[]{:S(2)}) collective-permute-start(bf16[24,1536]{1,0:T(8,128)(2,1)S(1)} %get-tuple-element.28), channel_id=1, source_target_pairs={{6,0},{4,2},{2,4},{0,6},{14,8},{12,10},{10,12},{8,14},{22,16},{20,... | collective-permute-start | bytes 221192 | tf_op jit(solution)/shard_map/ppermute | solution.py:420
  6.8 21.7 %all-to-all-start = ((bf16[16,24,128]{2,1,0:T(8,128)(2,1)}), bf16[16,24,128]{2,1,0:T(8,128)(2,1)S(1)}, u32[]{:S(2)}, u32[]{:S(2)}) async-start(bf16[16,24,128]{2,1,0:T(8,128)(2,1)} %get-tuple-element.45), calls=%async_computation | async-start | bytes 196608 | tf_op jit(solution)/shard_map/all_to_all | solution.py:471
  16.4 10.0 %collective-permute-start.2 = (bf16[24,3072]{1,0:T(8,128)(2,1)S(1)}, bf16[24,3072]{1,0:T(8,128)(2,1)S(1)}, u32[]{:S(2)}, u32[]{:S(2)}) collective-permute-start(bf16[24,3072]{1,0:T(8,128)(2,1)S(1)} %get-tuple-element.37), channel_id=1, source_target_pairs={{8,0},{10,2},{12,4},{14,6},{0,8},{2,10},{4,12},{6,14},{24,16},{26,... | collective-permute-start | bytes 442376 | tf_op jit(solution)/shard_map/ppermute | solution.py:420
  19.0 9.5 %collective-permute-start.3 = (bf16[24,3072]{1,0:T(8,128)(2,1)S(1)}, bf16[24,3072]{1,0:T(8,128)(2,1)S(1)}, u32[]{:S(2)}, u32[]{:S(2)}) collective-permute-start(bf16[24,3072]{1,0:T(8,128)(2,1)S(1)} %get-tuple-element.38), channel_id=1, source_target_pairs={{16,8},{18,10},{20,12},{22,14},{8,16},{10,18},{12,20},{14,22},{17,... | collective-permute-start | bytes 442376 | tf_op jit(solution)/shard_map/ppermute | solution.py:420
  32.0 3.2 %collective-permute-start.4 = (f32[1,2176]{1,0:T(1,128)S(1)}, f32[1,2176]{1,0:T(1,128)S(1)}, u32[]{:S(2)}, u32[]{:S(2)}) collective-permute-start(f32[1,2176]{1,0:T(1,128)S(1)} %get-tuple-element.47.mine), channel_id=1, source_target_pairs={{1,0},{0,1},{3,2},{2,3},{5,4},{4,5},{7,6},{6,7},{9,8},{8,9},{11,10... | collective-permute-start | bytes 26120 | tf_op jit(solution)/shard_map/ppermute | solution.py:420

commit v11 on v9

--- a/solution.py
+++ b/solution.py
@@ -179,12 +179,14 @@
     moment, rest = high_low(jnp.concatenate(parts, axis=1))
     moments[...] = moment
     total = dot(moment, shift[...]) + dot(rest, shift[...])
-    totals[...] = jnp.concatenate(high_low(total), axis=1)
+    total = jnp.concatenate(high_low(total), axis=1)
+    totals[...] = total
     for distance, payload in zip((1, 3), payloads):
         bit = jnp.where((box_x ^ distance) > box_x, 1, 0)
         for place in range(4):
             payload[:, lanes(place * pts, pts)] = own[:, lanes((bit + 2 * place) * pts, pts)]
         payload[:, lanes(4 * pts, LEAVES)] = moment
+        payload[:, lanes(4 * pts + LEAVES, 2 * SLOT)] = total
 
 
 def features(held, start, size, centre, target):
@@ -251,9 +253,9 @@
 
 def box_columns(depth, box_x, box_z, nodes):
     blocks = []
-    for box in range(ACROSS * depth):
-        gap_x = 2 * (box_x - box % ACROSS)
-        gap_z = 2 * (box_z - box // ACROSS)
+    for layer, distance in [(layer, distance) for layer in range(depth) for distance in range(ACROSS)]:
+        gap_x = 2 * (box_x - (box_x ^ distance))
+        gap_z = 2 * (box_z - layer)
         across_x = nodes[0] + gap_x.astype(jnp.float32)
         across_z = nodes[2] + gap_z.astype(jnp.float32)
         apart = jnp.maximum(jnp.abs(gap_x), jnp.abs(gap_z)) >= 4
@@ -283,6 +285,17 @@
         scale[:, leaf * pts : (leaf + 1) * pts] = jnp.where(lane_index < count[leaf], 1.0 / (128.0 * pts), 0.0)
 
 
+def spread_first(value, node):
+    starts = [leaf * SLOT + node for leaf in range(8)]
+    return jnp.concatenate([jnp.broadcast_to(value[:, s : s + 1], (ROWS, SLOT)) for s in starts], axis=1)
+
+
+def decoded(coded):
+    value = coded.astype(jnp.float32)
+    node = lax.broadcasted_iota(jnp.int32, value.shape, 1) % SLOT
+    return jnp.where(node == 0, 0.0, value) + spread_first(value, 0) + spread_first(value, COEFFS)
+
+
 def faces_of(faces, bit, given, own, left, right):
     points = own.shape[1]
     pts = points // 8
@@ -294,12 +307,14 @@
                 faces[:, place] = side[:, lanes((y + 2 * bit) * pts, pts)]
             else:
                 faces[:, place] = own[:, lanes((x - 1 + 2 * y + 4 * bit) * pts, pts)]
-    given_high, given_low = high_low(given)
-    faces[:, lanes(points, LEAVES)] = given_high
-    faces[:, lanes(points + LEAVES, LEAVES)] = given_low
-
-
-def row_kernel(own, moments, from_1, from_3, far, left, right, same, other, faces_even):
+    node = lax.broadcasted_iota(jnp.int32, given.shape, 1) % SLOT
+    base = spread_first(given, 0)
+    base_high = low_bits(base).astype(jnp.float32)
+    coded = jnp.where(node == 0, base_high, jnp.where(node == COEFFS, base - base_high, given - base))
+    faces[:, lanes(points, LEAVES)] = low_bits(coded)
+
+
+def row_kernel(own, moments, totals, from_1, from_2, from_3, far, left, right, same, other, faces_even, rows):
     points = own.shape[1]
     pts = points // 8
     box_x, box_z = box_place()
@@ -309,9 +324,12 @@
 
             @pl.when((box_x ^ distance) - box_x == step)
             def _(side=side, held=held):
-                side[...] = held[...]
+                side[...] = held[:, lanes(0, side.shape[1])]
 
     base = 4 * pts
+    ends = lanes(base + LEAVES, 2 * SLOT)
+    row = jnp.concatenate([totals[...], from_1[:, ends], from_2[...], from_3[:, ends]], axis=1)
+    rows[...] = jnp.broadcast_to(row[None], rows.shape)
     row = jnp.concatenate([left[:, lanes(base, LEAVES)], moments[...], right[:, lanes(base, LEAVES)]], axis=1)
     below_rows, same_rows, above_rows = pl.ds(0, 3 * LEAVES), pl.ds(3 * LEAVES, 2 * LEAVES), pl.ds(5 * LEAVES, 3 * LEAVES)
     up = dot(row, far[below_rows, :])
@@ -330,7 +348,8 @@
     own_groups(near, EARLY, 4, target, source, own)
 
 
-def side_kernel(left, right, early, target, near, sides):
+def side_kernel(left, right, early, target, rows, near, passed, sides):
+    passed[...] = rows[...]
     pts = early.shape[1] // 8
     for step, side in ((0, left), (1, right)):
         for place in range(4):
@@ -388,13 +407,13 @@
     inside = (box_z + 2 * step - 1 >= 0) & (box_z + 2 * step - 1 < depth)
     layer_pulls(near, early, step, inside, target, faces_odd, sides)
 
-    totals_high = jnp.concatenate([boxes[box][:, :SLOT] for box in range(ACROSS * depth)], axis=1)
-    totals_low = jnp.concatenate([boxes[box][:, SLOT:] for box in range(ACROSS * depth)], axis=1)
+    pieces = [boxes[layer][:, 2 * SLOT * turn : 2 * SLOT * (turn + 1)] for layer in range(depth) for turn in range(ACROSS)]
+    totals_high = jnp.concatenate([piece[:, :SLOT] for piece in pieces], axis=1)
+    totals_low = jnp.concatenate([piece[:, SLOT:] for piece in pieces], axis=1)
     coarse_high, coarse_low = high_low(dot(totals_high, columns[...]) + dot(totals_low, columns[...]))
     value = same[...] + dot(coarse_high, spread[...]) + dot(coarse_low, spread[...])
     for faces in (faces_even, faces_odd):
-        value = value + faces[:, lanes(points, LEAVES)].astype(jnp.float32)
-        value = value + faces[:, lanes(points + LEAVES, LEAVES)].astype(jnp.float32)
+        value = value + decoded(faces[:, lanes(points, LEAVES)])
     local_high, local_low = high_low(value)
     weight = column[0:fields, 0:1]
     for leaf in range(8):
@@ -440,7 +459,9 @@
     half, full = jnp.bfloat16, jnp.float32
     shift = shift_table()
     side_shape = ((ROWS, 4 * pts + LEAVES), half)
-    faces_shape = ((ROWS, points + 2 * LEAVES), half)
+    given_shape = ((ROWS, 4 * pts + LEAVES + 2 * SLOT), half)
+    faces_shape = ((ROWS, points + LEAVES), half)
+    rows_shape = ((depth, ROWS, 2 * SLOT * ACROSS), half)
     near_shape, sums_shape = ((ROWS, points), full), ((ROWS, LEAVES), full)
     rows_scratch = pltpu.VMEM((8 * pts, FEATURES), half)
     own, basis, moments, totals, *given = call(
@@ -452,8 +473,8 @@
             ((2 * SLOT, points), half),
             ((ROWS, LEAVES), half),
             ((ROWS, 2 * SLOT), half),
-            side_shape,
-            side_shape,
+            given_shape,
+            given_shape,
         ],
         [
             pltpu.SMEM((8,), jnp.int32),
@@ -468,7 +489,7 @@
         density,
         jnp.asarray(shift, half),
     )
-    boxes = lax.all_gather(totals, "space")
+    from_2 = swapped(totals, "space", lambda i: i ^ 2)
     from_1 = swapped(given[0], "space", lambda i: i ^ 1)
     from_3 = swapped(given[1], "space", lambda i: i ^ 3)
     near, source, target, scale, column, columns, far, spread = call(
@@ -498,15 +519,17 @@
         jnp.asarray(shift.T.copy(), half),
         jnp.asarray(box_nodes()),
     )
-    left, right, same, other, faces_even = call(
+    left, right, same, other, faces_even, rows = call(
         row_kernel,
         "row",
-        [vmem] * 5,
-        [side_shape, side_shape, sums_shape, sums_shape, faces_shape],
+        [vmem] * 7,
+        [side_shape, side_shape, sums_shape, sums_shape, faces_shape, rows_shape],
         [],
         own,
         moments,
+        totals,
         from_1,
+        from_2,
         from_3,
         far,
     )
@@ -526,17 +549,20 @@
         target,
     )
     faces_odd = swapped(faces_odd, "space", lambda i: i + ACROSS if i // ACROSS % 2 else i - ACROSS)
-    near, = call(
+    near, rows = call(
         side_kernel,
         "near_side",
-        [vmem] * 4,
-        [near_shape],
+        [vmem] * 5,
+        [near_shape, rows_shape],
         [pltpu.VMEM((4 * pts, FEATURES), half)],
         left,
         right,
         near,
         target,
-    )
+        rows,
+    )
+    columns_of_boxes = [[z * ACROSS + x for z in range(depth)] for x in range(ACROSS)]
+    boxes = lax.all_to_all(rows, "space", 0, 0, axis_index_groups=columns_of_boxes, tiled=True)
     near, = call(even_kernel, "near_even", [vmem] * 3, [near_shape], [rows_scratch], near, target, faces_even)
     potential, sums = call(
         functools.partial(last_kernel, depth),

time: 65.9 us -> 37.3 us (0.57)
  the two profiles are of different devices: /device:TPU:0 before, /device:TPU:17 now
where the time goes in v11:
time: 37.3 us; the launch traced here: 37.1 us
  Pallas kernels  19.3 us (52%)
  starting transfers between devices  13.7 us (37%)
  waiting for transfers between devices  3.36 us (9%)
  between operations  0.69 us (2%)
    pallas_call x8, Pallas kernels, call(): pl.pallas_call(kernel, in_specs=in_specs, out_specs=[vmem] * len(outs), o...  19.3 us
    ppermute x6, starting transfers between devices, swapped(): lax.ppermute(block, axis, [(partner(i), i) for i in range(size) if 0 <= p...  9.04 us
    all_to_all x1, starting transfers between devices, per_device(): lax.all_to_all(rows, 'space', 0, 0, axis_index_groups=columns_of_boxes, t...  4.65 us
    ppermute x6, waiting for transfers between devices, swapped(): lax.ppermute(block, axis, [(partner(i), i) for i in range(size) if 0 <= p...  3.36 us
  transfers between devices with their start and end apart: 7, of which 3 were waited for; matrix products, arithmetic and copies ran while one was open for 0% of the time, Pallas kernels for 14%

profile of v11, /device:TPU:17, one launch (start us, length us, event | category | flops | bytes accessed | tf_op | source)
XLA Modules:
  0.0 37.1 jit_solution(8563411406088370203)
XLA Ops:
  0.6 3.0 %pack.1 = (bf16[24,2048]{1,0:T(8,128)(2,1)S(1)}, bf16[128,2048]{1,0:T(8,128)(2,1)S(1)}, bf16[24,512]{1,0:T(8,128)(2,1)S(1)}, bf16[24,128]{1,0:T(8,128)(2,1)S(1)}...) custom-call(s32[8]{0:T(128)} %count_in.3, f32[3,2048]{1,0:T(4,128)} %positions_in.1, ...), custom_call_target="tpu_custom_call" | custom-call | tf_op jit(solution)/shard_map/pack/pallas_call | solution.py:449
  3.7 1.3 %collective-permute-start = (bf16[24,1664]{1,0:T(8,128)(2,1)S(1)}, bf16[24,1664]{1,0:T(8,128)(2,1)S(1)}, u32[]{:S(2)}, u32[]{:S(2)}) collective-permute-start(bf16[24,1664]{1,0:T(8,128)(2,1)S(1)} %get-tuple-element.31), channel_id=1, source_target_pairs={{2,0},{0,2},{6,4},{4,6},{10,8},{8,10},{14,12},{12,14},{18,16},{16,... | collective-permute-start | bytes 239624 | tf_op jit(solution)/shard_map/ppermute | solution.py:439
  5.0 1.2 %collective-permute-start.2 = (bf16[24,1664]{1,0:T(8,128)(2,1)S(1)}, bf16[24,1664]{1,0:T(8,128)(2,1)S(1)}, u32[]{:S(2)}, u32[]{:S(2)}) collective-permute-start(bf16[24,1664]{1,0:T(8,128)(2,1)S(1)} %get-tuple-element.32), channel_id=1, source_target_pairs={{6,0},{4,2},{2,4},{0,6},{14,8},{12,10},{10,12},{8,14},{22,16},{20,... | collective-permute-start | bytes 239624 | tf_op jit(solution)/shard_map/ppermute | solution.py:439
  6.2 0.2 collective-permute-start.1
  6.4 3.0 %near_own.1 = (f32[24,1024]{1,0:T(8,128)S(1)}, bf16[2048,48]{1,0:T(8,128)(2,1)S(1)}, bf16[48,2048]{1,0:T(8,128)(2,1)S(1)}, f32[1,2048]{1,0:T(1,128)S(1)}, f32[24...) custom-call(s32[8]{0:T(128)} %count_in.3, ...), custom_call_target="tpu_custom_call" | custom-call | tf_op jit(solution)/shard_map/near_own/pallas_call | solution.py:449
  9.4 0.0 collective-permute-done.1.from_2
  9.4 0.0 collective-permute-done.from_1
  9.4 0.9 %collective-permute-done.2.from_3 = bf16[24,1664]{1,0:T(8,128)(2,1)S(1)} collective-permute-done((bf16[24,1664]{1,0:T(8,128)(2,1)S(1)}, bf16[24,1664]{1,0:T(8,128)(2,1)S(1)}, u32[]{:S(2)}, u32[]{:S(2)}) %collective-permute-start.2) | collective-permute-done | bytes 79904 | tf_op jit(solution)/shard_map/ppermute | solution.py:439
  10.3 0.8 %row.1 = (bf16[24,1536]{1,0:T(8,128)(2,1)S(1)}, bf16[24,1536]{1,0:T(8,128)(2,1)S(1)}, f32[24,512]{1,0:T(8,128)S(1)}, f32[24,512]{1,0:T(8,128)S(1)}, bf16[24,2560...) custom-call(bf16[24,2048]{1,0:T(8,128)(2,1)S(1)} %get-tuple-element.28.own, ...), custom_call_target="tpu_custom_call" | custom-call | tf_op jit(solution)/shard_map/row/pallas_call | solution.py:449
  11.1 2.5 %near_middle.1 = (f32[24,2048]{1,0:T(8,128)S(1)}, bf16[24,2560]{1,0:T(8,128)(2,1)S(1)}) custom-call(bf16[24,2048]{1,0:T(8,128)(2,1)S(1)} %get-tuple-element.28.own, bf16[24,1536]{1,0:T(8,128)(2,1)S(1)} %get-tuple-element.34.left, bf16[24,1536]{1,0:T(8,128)(2,1)S(1)} %get-tuple-element.35.right, f32[24,512]{1,0:T(8,128)S(1)} %get-tuple-element.36.other, ...), custom_call_target="tpu_custom_call" | custom-call | tf_op jit(solution)/shard_map/near_middle/pallas_call | solution.py:449
  13.7 3.6 %near_side.1 = (f32[24,2048]{1,0:T(8,128)S(1)}, bf16[4,24,512]{2,1,0:T(8,128)(2,1)}) custom-call(bf16[24,1536]{1,0:T(8,128)(2,1)S(1)} %get-tuple-element.34.left, bf16[24,1536]{1,0:T(8,128)(2,1)S(1)} %get-tuple-element.35.right, f32[24,2048]{1,0:T(8,128)S(1)} %get-tuple-element.40.early, bf16[48,2048]{1,0:T(8,128)(2,1)S(1)} %get-tuple-element.39.target, ...), custom_call_target="tpu_custom_call" | custom-call | tf_op jit(solution)/shard_map/near_side/pallas_call | solution.py:449
  17.3 4.6 %all-to-all-start = ((bf16[4,24,512]{2,1,0:T(8,128)(2,1)}), bf16[4,24,512]{2,1,0:T(8,128)(2,1)S(1)}, u32[]{:S(2)}, u32[]{:S(2)}) async-start(bf16[4,24,512]{2,1,0:T(8,128)(2,1)} %get-tuple-element.51), calls=%async_computation | async-start | bytes 196608 | tf_op jit(solution)/shard_map/all_to_all | solution.py:565
  21.9 1.2 %collective-permute-start.3 = (bf16[24,2560]{1,0:T(8,128)(2,1)S(1)}, bf16[24,2560]{1,0:T(8,128)(2,1)S(1)}, u32[]{:S(2)}, u32[]{:S(2)}) collective-permute-start(bf16[24,2560]{1,0:T(8,128)(2,1)S(1)} %get-tuple-element.43), channel_id=1, source_target_pairs={{8,0},{10,2},{12,4},{14,6},{0,8},{2,10},{4,12},{6,14},{24,16},{26,... | collective-permute-start | bytes 368648 | tf_op jit(solution)/shard_map/ppermute | solution.py:439
  23.1 1.9 %collective-permute-start.4 = (bf16[24,2560]{1,0:T(8,128)(2,1)S(1)}, bf16[24,2560]{1,0:T(8,128)(2,1)S(1)}, u32[]{:S(2)}, u32[]{:S(2)}) collective-permute-start(bf16[24,2560]{1,0:T(8,128)(2,1)S(1)} %get-tuple-element.44), channel_id=1, source_target_pairs={{16,8},{18,10},{20,12},{22,14},{8,16},{10,18},{12,20},{14,22},{17,... | collective-permute-start | bytes 368648 | tf_op jit(solution)/shard_map/ppermute | solution.py:439
  25.0 1.6 %collective-permute-done.3.faces.faces_even = bf16[24,2560]{1,0:T(8,128)(2,1)S(1)} collective-permute-done((bf16[24,2560]{1,0:T(8,128)(2,1)S(1)}, bf16[24,2560]{1,0:T(8,128)(2,1)S(1)}, u32[]{:S(2)}, u32[]{:S(2)}) %collective-permute-start.3) | collective-permute-done | bytes 122912 | tf_op jit(solution)/shard_map/ppermute | solution.py:439
  26.7 2.1 %near_even.1.early = f32[24,2048]{1,0:T(8,128)S(1)} custom-call(f32[24,2048]{1,0:T(8,128)S(1)} %get-tuple-element.42.early, bf16[48,2048]{1,0:T(8,128)(2,1)S(1)} %get-tuple-element.39.target, bf16[24,2560]{1,0:T(8,128)(2,1)S(1)} %collective-permute-done.3.faces.faces_even), custom_call_target="tpu_custom_call" | custom-call | tf_op jit(solution)/shard_map/near_even/pallas_call | solution.py:449
  28.8 0.0 collective-permute-done.4.faces_odd
  28.8 0.0 all-to-all-done.boxes
  28.8 3.5 %near_odd.1 = (f32[17,2048]{1,0:T(8,128)}, f32[1,2176]{1,0:T(1,128)S(1)}) custom-call(f32[24,2048]{1,0:T(8,128)S(1)} %near_even.1.early, bf16[48,2048]{1,0:T(8,128)(2,1)S(1)} %get-tuple-element.39.target, bf16[24,2560]{1,0:T(8,128)(2,1)S(1)} %collective-permute-done.3.faces.faces_even, bf16[24,2560]{1,0:T(8,128)(2,1)S(1)} %collective-permute-done.4.faces_odd, ...), custom_call_target="tpu_custom_call" | custom-call | tf_op jit(solution)/shard_map/near_odd/pallas_call | solution.py:449
  32.3 3.2 %collective-permute-start.5 = (f32[1,2176]{1,0:T(1,128)S(1)}, f32[1,2176]{1,0:T(1,128)S(1)}, u32[]{:S(2)}, u32[]{:S(2)}) collective-permute-start(f32[1,2176]{1,0:T(1,128)S(1)} %get-tuple-element.53.mine), channel_id=1, source_target_pairs={{1,0},{0,1},{3,2},{2,3},{5,4},{4,5},{7,6},{6,7},{9,8},{8,9},{11,10... | collective-permute-start | bytes 26120 | tf_op jit(solution)/shard_map/ppermute | solution.py:439
  35.6 0.8 %collective-permute-done.5.other = f32[1,2176]{1,0:T(1,128)S(1)} collective-permute-done((f32[1,2176]{1,0:T(1,128)S(1)}, f32[1,2176]{1,0:T(1,128)S(1)}, u32[]{:S(2)}, u32[]{:S(2)}) %collective-permute-start.5) | collective-permute-done | bytes 8736 | tf_op jit(solution)/shard_map/ppermute | solution.py:439
  36.4 0.7 %mean.1 = f32[1,2048]{1,0:T(1,128)} custom-call(f32[1,2176]{1,0:T(1,128)S(1)} %get-tuple-element.53.mine, f32[1,2176]{1,0:T(1,128)S(1)} %collective-permute-done.5.other), custom_call_target="tpu_custom_call" | custom-call | tf_op jit(solution)/shard_map/mean/pallas_call | solution.py:449
Async XLA Ops:
  3.7 5.7 %collective-permute-start = (bf16[24,1664]{1,0:T(8,128)(2,1)S(1)}, bf16[24,1664]{1,0:T(8,128)(2,1)S(1)}, u32[]{:S(2)}, u32[]{:S(2)}) collective-permute-start(bf16[24,1664]{1,0:T(8,128)(2,1)S(1)} %get-tuple-element.31), channel_id=1, source_target_pairs={{2,0},{0,2},{6,4},{4,6},{10,8},{8,10},{14,12},{12,14},{18,16},{16,... | collective-permute-start | bytes 239624 | tf_op jit(solution)/shard_map/ppermute | solution.py:439
  5.0 5.3 %collective-permute-start.2 = (bf16[24,1664]{1,0:T(8,128)(2,1)S(1)}, bf16[24,1664]{1,0:T(8,128)(2,1)S(1)}, u32[]{:S(2)}, u32[]{:S(2)}) collective-permute-start(bf16[24,1664]{1,0:T(8,128)(2,1)S(1)} %get-tuple-element.32), channel_id=1, source_target_pairs={{6,0},{4,2},{2,4},{0,6},{14,8},{12,10},{10,12},{8,14},{22,16},{20,... | collective-permute-start | bytes 239624 | tf_op jit(solution)/shard_map/ppermute | solution.py:439
  6.2 3.2 %collective-permute-start.1 = (bf16[24,128]{1,0:T(8,128)(2,1)S(1)}, bf16[24,128]{1,0:T(8,128)(2,1)S(1)}, u32[]{:S(2)}, u32[]{:S(2)}) collective-permute-start(bf16[24,128]{1,0:T(8,128)(2,1)S(1)} %get-tuple-element.30.totals), channel_id=1, source_target_pairs={{4,0},{6,2},{0,4},{2,6},{12,8},{14,10},{8,12},{10,14},{20,16},{22,... | collective-permute-start | bytes 18440 | tf_op jit(solution)/shard_map/ppermute | solution.py:439
  17.3 11.5 %all-to-all-start = ((bf16[4,24,512]{2,1,0:T(8,128)(2,1)}), bf16[4,24,512]{2,1,0:T(8,128)(2,1)S(1)}, u32[]{:S(2)}, u32[]{:S(2)}) async-start(bf16[4,24,512]{2,1,0:T(8,128)(2,1)} %get-tuple-element.51), calls=%async_computation | async-start | bytes 196608 | tf_op jit(solution)/shard_map/all_to_all | solution.py:565
  21.9 4.7 %collective-permute-start.3 = (bf16[24,2560]{1,0:T(8,128)(2,1)S(1)}, bf16[24,2560]{1,0:T(8,128)(2,1)S(1)}, u32[]{:S(2)}, u32[]{:S(2)}) collective-permute-start(bf16[24,2560]{1,0:T(8,128)(2,1)S(1)} %get-tuple-element.43), channel_id=1, source_target_pairs={{8,0},{10,2},{12,4},{14,6},{0,8},{2,10},{4,12},{6,14},{24,16},{26,... | collective-permute-start | bytes 368648 | tf_op jit(solution)/shard_map/ppermute | solution.py:439
  23.1 5.7 %collective-permute-start.4 = (bf16[24,2560]{1,0:T(8,128)(2,1)S(1)}, bf16[24,2560]{1,0:T(8,128)(2,1)S(1)}, u32[]{:S(2)}, u32[]{:S(2)}) collective-permute-start(bf16[24,2560]{1,0:T(8,128)(2,1)S(1)} %get-tuple-element.44), channel_id=1, source_target_pairs={{16,8},{18,10},{20,12},{22,14},{8,16},{10,18},{12,20},{14,22},{17,... | collective-permute-start | bytes 368648 | tf_op jit(solution)/shard_map/ppermute | solution.py:439
  32.3 4.1 %collective-permute-start.5 = (f32[1,2176]{1,0:T(1,128)S(1)}, f32[1,2176]{1,0:T(1,128)S(1)}, u32[]{:S(2)}, u32[]{:S(2)}) collective-permute-start(f32[1,2176]{1,0:T(1,128)S(1)} %get-tuple-element.53.mine), channel_id=1, source_target_pairs={{1,0},{0,1},{3,2},{2,3},{5,4},{4,5},{7,6},{6,7},{9,8},{8,9},{11,10... | collective-permute-start | bytes 26120 | tf_op jit(solution)/shard_map/ppermute | solution.py:439

commit v12 on v10

--- a/solution.py
+++ b/solution.py
@@ -115,6 +115,10 @@
     for index, value in enumerate(values):
         result = jnp.where(row == index, value, result)
     return result
+
+
+def turn_of():
+    return lax.rem(lax.axis_index("sig"), 2)
 
 
 def box_place():
@@ -180,7 +184,8 @@
     moments[...] = moment
     total = dot(moment, shift[...]) + dot(rest, shift[...])
     totals[...] = jnp.broadcast_to(jnp.concatenate(high_low(total), axis=1)[None], totals.shape)
-    for distance, payload in zip((1, 3), payloads):
+    for turn, payload in enumerate(payloads):
+        distance = jnp.where(turn_of() == turn, 1, 3)
         bit = jnp.where((box_x ^ distance) > box_x, 1, 0)
         for place in range(4):
             payload[:, lanes(place * pts, pts)] = own[:, lanes((bit + 2 * place) * pts, pts)]
@@ -283,6 +288,17 @@
         scale[:, leaf * pts : (leaf + 1) * pts] = jnp.where(lane_index < count[leaf], 1.0 / (128.0 * pts), 0.0)
 
 
+def spread_first(value, node):
+    starts = [leaf * SLOT + node for leaf in range(8)]
+    return jnp.concatenate([jnp.broadcast_to(value[:, s : s + 1], (ROWS, SLOT)) for s in starts], axis=1)
+
+
+def decoded(coded):
+    value = coded.astype(jnp.float32)
+    node = lax.broadcasted_iota(jnp.int32, value.shape, 1) % SLOT
+    return jnp.where(node == 0, 0.0, value) + spread_first(value, 0) + spread_first(value, COEFFS)
+
+
 def faces_of(faces, bit, given, own, left, right):
     points = own.shape[1]
     pts = points // 8
@@ -294,18 +310,21 @@
                 faces[:, place] = side[:, lanes((y + 2 * bit) * pts, pts)]
             else:
                 faces[:, place] = own[:, lanes((x - 1 + 2 * y + 4 * bit) * pts, pts)]
-    given_high, given_low = high_low(given)
-    faces[:, lanes(points, LEAVES)] = given_high
-    faces[:, lanes(points + LEAVES, LEAVES)] = given_low
-
-
-def row_kernel(own, moments, from_1, from_3, far, left, right, same, other, faces_even):
+    node = lax.broadcasted_iota(jnp.int32, given.shape, 1) % SLOT
+    base = spread_first(given, 0)
+    base_high = low_bits(base).astype(jnp.float32)
+    coded = jnp.where(node == 0, base_high, jnp.where(node == COEFFS, base - base_high, given - base))
+    faces[:, lanes(points, LEAVES)] = low_bits(coded)
+
+
+def row_kernel(own, moments, first, second, far, left, right, same, other, faces):
     points = own.shape[1]
     pts = points // 8
     box_x, box_z = box_place()
     for side, step in ((left, -1), (right, 1)):
         side[...] = jnp.zeros(side.shape, side.dtype)
-        for distance, held in ((1, from_1), (3, from_3)):
+        for turn, held in ((0, first), (1, second)):
+            distance = jnp.where(turn_of() == turn, 1, 3)
 
             @pl.when((box_x ^ distance) - box_x == step)
             def _(side=side, held=held):
@@ -317,15 +336,15 @@
     up = dot(row, far[below_rows, :])
     down = dot(row, far[above_rows, :])
     same[...] = dot(jnp.concatenate([row[:, :LEAVES], row[:, 2 * LEAVES :]], axis=1), far[same_rows, :])
-    odd = lax.rem(box_z, 2)
-    faces_of(faces_even, 1 - odd, jnp.where(odd == 0, up, down), own, left, right)
-    other[...] = jnp.where(odd == 0, down, up)
-
-
-def middle_kernel(own, left, right, other, early, source, target, near, faces_odd):
+    above = 1 - lax.rem(box_z + turn_of(), 2)
+    faces_of(faces, above, jnp.where(above == 1, up, down), own, left, right)
+    other[...] = jnp.where(above == 1, down, up)
+
+
+def middle_kernel(own, left, right, other, early, source, target, near, faces):
     points = own.shape[1]
     _, box_z = box_place()
-    faces_of(faces_odd, lax.rem(box_z, 2), other[...], own, left, right)
+    faces_of(faces, lax.rem(box_z + turn_of(), 2), other[...], own, left, right)
     near[:, lanes(0, EARLY * points // 4)] = early[...]
     own_groups(near, EARLY, 4, target, source, own)
 
@@ -368,33 +387,28 @@
         near[:, here] = early[:, here]
 
 
-def even_kernel(early, target, faces, near, sides):
+def one_layer(depth, turn, early, target, faces, near, sides):
+    points = early.shape[1]
     _, box_z = box_place()
-    points = early.shape[1]
-    step = 1 - lax.rem(box_z, 2)
+    step = 1 - lax.rem(box_z + turn_of() + turn, 2)
     other = lanes((1 - step) * (points // 2), points // 2)
     near[:, other] = early[:, other]
-    layer_pulls(near, early, step, box_z >= 0, target, faces, sides)
-
-
-def last_kernel(depth, early, target, faces_even, faces_odd, basis, scale, column, columns, spread, same, boxes, *rest):
+    layer = box_z + 2 * step - 1
+    layer_pulls(near, early, step, (layer >= 0) & (layer < depth), target, faces, sides)
+
+
+def last_kernel(depth, early, target, faces_first, faces_second, basis, scale, column, columns, spread, same, boxes, *rest):
     potential, sums, near, sides = rest
     fields, points = potential.shape
     pts = points // 8
-    _, box_z = box_place()
-    step = lax.rem(box_z, 2)
-    other = lanes((1 - step) * (points // 2), points // 2)
-    near[:, other] = early[:, other]
-    inside = (box_z + 2 * step - 1 >= 0) & (box_z + 2 * step - 1 < depth)
-    layer_pulls(near, early, step, inside, target, faces_odd, sides)
+    one_layer(depth, 1, early, target, faces_second, near, sides)
 
     totals_high = jnp.concatenate([boxes[box][:, :SLOT] for box in range(ACROSS * depth)], axis=1)
     totals_low = jnp.concatenate([boxes[box][:, SLOT:] for box in range(ACROSS * depth)], axis=1)
     coarse_high, coarse_low = high_low(dot(totals_high, columns[...]) + dot(totals_low, columns[...]))
     value = same[...] + dot(coarse_high, spread[...]) + dot(coarse_low, spread[...])
-    for faces in (faces_even, faces_odd):
-        value = value + faces[:, lanes(points, LEAVES)].astype(jnp.float32)
-        value = value + faces[:, lanes(points + LEAVES, LEAVES)].astype(jnp.float32)
+    for faces in (faces_first, faces_second):
+        value = value + decoded(faces[:, lanes(points, LEAVES)])
     local_high, local_low = high_low(value)
     weight = column[0:fields, 0:1]
     for leaf in range(8):
@@ -420,6 +434,21 @@
     return lax.ppermute(block, axis, [(partner(i), i) for i in range(size) if 0 <= partner(i) < size])
 
 
+def taken_in_turns(block, turn, partners):
+    boxes, cores = lax.axis_size("space"), lax.axis_size("sig")
+    pairs = []
+    for box in range(boxes):
+        for core in range(cores):
+            other = partners[(turn + core) % 2](box)
+            if 0 <= other < boxes:
+                pairs.append((other * cores + core, box * cores + core))
+    return lax.ppermute(block, ("space", "sig"), pairs)
+
+
+def beside(i):
+    return i + ACROSS if i // ACROSS % 2 else i - ACROSS
+
+
 def per_device(positions, density, leaf_count, sigma_weights):
     fields, points = density.shape
     pts = points // 8
@@ -427,6 +456,7 @@
     vmem, hbm = pl.BlockSpec(memory_space=pltpu.VMEM), pl.BlockSpec(memory_space=pltpu.HBM)
 
     def call(kernel, name, in_specs, outs, scratch, *args):
+        work = {"near_own": 3, "near_middle": 3, "near_side": 3, "near_first": 2, "near_second": 3}.get(name, 1)
         return pl.pallas_call(
             kernel,
             in_specs=in_specs,
@@ -434,13 +464,14 @@
             out_shape=[jax.ShapeDtypeStruct(shape, dtype) for shape, dtype in outs],
             scratch_shapes=scratch,
             compiler_params=pltpu.CompilerParams(vmem_limit_bytes=24 * MEGA),
+            cost_estimate=pl.CostEstimate(flops=work * 10**9, transcendentals=0, bytes_accessed=work * 10**6),
             name=name,
         )(*(pltpu.with_memory_space_constraint(a, pltpu.HBM) if s is hbm else a for s, a in zip(in_specs, args)))
 
     half, full = jnp.bfloat16, jnp.float32
     shift = shift_table()
     side_shape = ((ROWS, 4 * pts + LEAVES), half)
-    faces_shape = ((ROWS, points + 2 * LEAVES), half)
+    faces_shape = ((ROWS, points + LEAVES), half)
     near_shape, sums_shape = ((ROWS, points), full), ((ROWS, LEAVES), full)
     rows_scratch = pltpu.VMEM((8 * pts, FEATURES), half)
     own, basis, moments, totals, *given = call(
@@ -469,8 +500,8 @@
         jnp.asarray(shift, half),
     )
     boxes = lax.all_to_all(totals, "space", 0, 0, tiled=True)
-    from_1 = swapped(given[0], "space", lambda i: i ^ 1)
-    from_3 = swapped(given[1], "space", lambda i: i ^ 3)
+    along_row = (lambda i: i ^ 1, lambda i: i ^ 3)
+    first, second = [taken_in_turns(block, turn, along_row) for turn, block in enumerate(given)]
     near, source, target, scale, column, columns, far, spread = call(
         functools.partial(own_kernel, depth),
         "near_own",
@@ -498,7 +529,7 @@
         jnp.asarray(shift.T.copy(), half),
         jnp.asarray(box_nodes()),
     )
-    left, right, same, other, faces_even = call(
+    left, right, same, other, faces_first = call(
         row_kernel,
         "row",
         [vmem] * 5,
@@ -506,12 +537,13 @@
         [],
         own,
         moments,
-        from_1,
-        from_3,
+        first,
+        second,
         far,
     )
-    faces_even = swapped(faces_even, "space", lambda i: i ^ ACROSS)
-    near, faces_odd = call(
+    layers = (lambda i: i ^ ACROSS, beside)
+    faces_first = taken_in_turns(faces_first, 0, layers)
+    near, faces_second = call(
         middle_kernel,
         "near_middle",
         [vmem] * 7,
@@ -525,7 +557,7 @@
         source,
         target,
     )
-    faces_odd = swapped(faces_odd, "space", lambda i: i + ACROSS if i // ACROSS % 2 else i - ACROSS)
+    faces_second = taken_in_turns(faces_second, 1, layers)
     near, = call(
         side_kernel,
         "near_side",
@@ -537,17 +569,26 @@
         near,
         target,
     )
-    near, = call(even_kernel, "near_even", [vmem] * 3, [near_shape], [rows_scratch], near, target, faces_even)
+    near, = call(
+        functools.partial(one_layer, depth, 0),
+        "near_first",
+        [vmem] * 3,
+        [near_shape],
+        [rows_scratch],
+        near,
+        target,
+        faces_first,
+    )
     potential, sums = call(
         functools.partial(last_kernel, depth),
-        "near_odd",
+        "near_second",
         [vmem] * 11,
         [((fields, points), full), ((1, points + 128), full)],
         [pltpu.VMEM((ROWS, points), full), rows_scratch],
         near,
         target,
-        faces_even,
-        faces_odd,
+        faces_first,
+        faces_second,
         basis,
         scale,
         column,

time: 36.1 us -> 41.1 us (1.14)
  the two profiles are of different devices: /device:TPU:9 before, /device:TPU:17 now
where the time goes in v12:
time: 41.1 us; the launch traced here: 40.8 us
  Pallas kernels  19.6 us (48%)
  starting transfers between devices  17 us (41%)
  waiting for transfers between devices  3.54 us (9%)
  between operations  0.69 us (2%)
    pallas_call x8, Pallas kernels, call(): pl.pallas_call(kernel, in_specs=in_specs, out_specs=[vmem] * len(outs), o...  19.6 us
    ppermute x4, starting transfers between devices, taken_in_turns(): return lax.ppermute(block, ('space', 'sig'), pairs)  6.74 us
    all_to_all x1, starting transfers between devices, per_device(): boxes = lax.all_to_all(totals, 'space', 0, 0, tiled=True)  6.58 us
    ppermute x1, starting transfers between devices, swapped(): lax.ppermute(block, axis, [(partner(i), i) for i in range(size) if 0 <= p...  3.71 us
    ppermute x4, waiting for transfers between devices, taken_in_turns(): return lax.ppermute(block, ('space', 'sig'), pairs)  2.7 us
    ppermute x1, waiting for transfers between devices, swapped(): lax.ppermute(block, axis, [(partner(i), i) for i in range(size) if 0 <= p...  0.83 us
  transfers between devices with their start and end apart: 6, of which 3 were waited for; matrix products, arithmetic and copies ran while one was open for 0% of the time, Pallas kernels for 29%

profile of v12, /device:TPU:17, one launch (start us, length us, event | category | flops | bytes accessed | tf_op | source)
XLA Modules:
  0.0 40.8 jit_solution(18305507843748887590)
XLA Ops:
  0.6 3.7 %pack.1 = (bf16[24,2048]{1,0:T(8,128)(2,1)S(1)}, bf16[128,2048]{1,0:T(8,128)(2,1)S(1)}, bf16[24,512]{1,0:T(8,128)(2,1)S(1)}, bf16[16,24,128]{2,1,0:T(8,128)(2,1)...) custom-call(s32[8]{0:T(128)} %count_in.3, f32[3,2048]{1,0:T(4,128)} %positions_in.1, ...), custom_call_target="tpu_custom_call" | custom-call | flops 1000000000 | bytes 1000000 | tf_op jit(solution)/shard_map/pack/pallas_call | solution.py:460
  4.3 6.6 %all-to-all-start = ((bf16[16,24,128]{2,1,0:T(8,128)(2,1)}), bf16[16,24,128]{2,1,0:T(8,128)(2,1)S(1)}, u32[]{:S(2)}, u32[]{:S(2)}) async-start(bf16[16,24,128]{2,1,0:T(8,128)(2,1)} %get-tuple-element.45), calls=%async_computation | async-start | bytes 196608 | tf_op jit(solution)/shard_map/all_to_all | solution.py:502
  10.9 2.1 %collective-permute-start = (bf16[24,1536]{1,0:T(8,128)(2,1)S(1)}, bf16[24,1536]{1,0:T(8,128)(2,1)S(1)}, u32[]{:S(2)}, u32[]{:S(2)}) collective-permute-start(bf16[24,1536]{1,0:T(8,128)(2,1)S(1)} %get-tuple-element.27), channel_id=1, source_target_pairs={{2,0},{7,1},{0,2},{5,3},{6,4},{3,5},{4,6},{1,7},{10,8},{15,9},{8,1... | collective-permute-start | bytes 221192 | tf_op jit(solution)/shard_map/ppermute | solution.py:445
  13.0 0.3 collective-permute-start.1
  13.3 3.0 %near_own.1 = (f32[24,1024]{1,0:T(8,128)S(1)}, bf16[2048,48]{1,0:T(8,128)(2,1)S(1)}, bf16[48,2048]{1,0:T(8,128)(2,1)S(1)}, f32[1,2048]{1,0:T(1,128)S(1)}, f32[24...) custom-call(s32[8]{0:T(128)} %count_in.3, ...), custom_call_target="tpu_custom_call" | custom-call | flops 3000000000 | bytes 3000000 | tf_op jit(solution)/shard_map/near_own/pallas_call | solution.py:460
  16.3 0.0 collective-permute-done.first
  16.3 1.1 %collective-permute-done.1.second = bf16[24,1536]{1,0:T(8,128)(2,1)S(1)} collective-permute-done((bf16[24,1536]{1,0:T(8,128)(2,1)S(1)}, bf16[24,1536]{1,0:T(8,128)(2,1)S(1)}, u32[]{:S(2)}, u32[]{:S(2)}) %collective-permute-start.1) | collective-permute-done | bytes 73760 | tf_op jit(solution)/shard_map/ppermute | solution.py:445
  17.4 0.8 %row.1 = (bf16[24,1536]{1,0:T(8,128)(2,1)S(1)}, bf16[24,1536]{1,0:T(8,128)(2,1)S(1)}, f32[24,512]{1,0:T(8,128)S(1)}, f32[24,512]{1,0:T(8,128)S(1)}, bf16[24,2560]{1,0:T(8,128)(2,1)S(1)}) custom-call(bf16[24,2048]{1,0:T(8,128)(2,1)S(1)} %get-tuple-element.25.own, bf16[24,512]{1,0:T(8,128)(2,1)S(1)} %get-tuple-element.26.moments, ...), custom_call_target="tpu_custom_call" | custom-call | flops 1000000000 | bytes 1000000 | tf_op jit(solution)/shard_map/row/pallas_call | solution.py:460
  18.2 2.5 %collective-permute-start.2 = (bf16[24,2560]{1,0:T(8,128)(2,1)S(1)}, bf16[24,2560]{1,0:T(8,128)(2,1)S(1)}, u32[]{:S(2)}, u32[]{:S(2)}) collective-permute-start(bf16[24,2560]{1,0:T(8,128)(2,1)S(1)} %get-tuple-element.37), channel_id=1, source_target_pairs={{8,0},{10,2},{12,4},{14,6},{0,8},{17,9},{2,10},{19,11},{4,12},{21,... | collective-permute-start | bytes 368648 | tf_op jit(solution)/shard_map/ppermute | solution.py:445
  20.7 2.6 %near_middle.1 = (f32[24,2048]{1,0:T(8,128)S(1)}, bf16[24,2560]{1,0:T(8,128)(2,1)S(1)}) custom-call(bf16[24,2048]{1,0:T(8,128)(2,1)S(1)} %get-tuple-element.25.own, bf16[24,1536]{1,0:T(8,128)(2,1)S(1)} %get-tuple-element.30.left, bf16[24,1536]{1,0:T(8,128)(2,1)S(1)} %get-tuple-element.31.right, f32[24,512]{1,0:T(8,128)S(1)} %get-tuple-element.32.other, ...), custom_call_target="tpu_custom_call" | custom-call | flops 3000000000 | bytes 3000000 | tf_op jit(solution)/shard_map/near_middle/pallas_call | solution.py:460
  23.3 3.2 %near_side.1.early = f32[24,2048]{1,0:T(8,128)S(1)} custom-call(bf16[24,1536]{1,0:T(8,128)(2,1)S(1)} %get-tuple-element.30.left, bf16[24,1536]{1,0:T(8,128)(2,1)S(1)} %get-tuple-element.31.right, f32[24,2048]{1,0:T(8,128)S(1)} %get-tuple-element.36.early, bf16[48,2048]{1,0:T(8,128)(2,1)S(1)} %get-tuple-element.35.target), custom_call_target="tpu_custom_call" | custom-call | flops 3000000000 | bytes 3000000 | tf_op jit(solution)/shard_map/near_side/pallas_call | solution.py:460
  26.5 1.9 %collective-permute-start.3 = (bf16[24,2560]{1,0:T(8,128)(2,1)S(1)}, bf16[24,2560]{1,0:T(8,128)(2,1)S(1)}, u32[]{:S(2)}, u32[]{:S(2)}) collective-permute-start(bf16[24,2560]{1,0:T(8,128)(2,1)S(1)} %get-tuple-element.38), channel_id=1, source_target_pairs={{9,1},{11,3},{13,5},{15,7},{16,8},{1,9},{18,10},{3,11},{20,12},{5,... | collective-permute-start | bytes 368648 | tf_op jit(solution)/shard_map/ppermute | solution.py:445
  28.4 0.0 collective-permute-done.2.faces.faces_first
  28.4 2.1 %near_first.1.early = f32[24,2048]{1,0:T(8,128)S(1)} custom-call(f32[24,2048]{1,0:T(8,128)S(1)} %near_side.1.early, bf16[48,2048]{1,0:T(8,128)(2,1)S(1)} %get-tuple-element.35.target, bf16[24,2560]{1,0:T(8,128)(2,1)S(1)} %collective-permute-done.2.faces.faces_first), custom_call_target="tpu_custom_call" | custom-call | flops 2000000000 | bytes 2000000 | tf_op jit(solution)/shard_map/near_first/pallas_call | solution.py:460
  30.6 0.0 all-to-all-done.boxes
  30.6 1.6 %collective-permute-done.3.faces_second = bf16[24,2560]{1,0:T(8,128)(2,1)S(1)} collective-permute-done((bf16[24,2560]{1,0:T(8,128)(2,1)S(1)}, bf16[24,2560]{1,0:T(8,128)(2,1)S(1)}, u32[]{:S(2)}, u32[]{:S(2)}) %collective-permute-start.3) | collective-permute-done | bytes 122912 | tf_op jit(solution)/shard_map/ppermute | solution.py:445
  32.1 3.5 %near_second.1 = (f32[17,2048]{1,0:T(8,128)}, f32[1,2176]{1,0:T(1,128)S(1)}) custom-call(f32[24,2048]{1,0:T(8,128)S(1)} %near_first.1.early, bf16[48,2048]{1,0:T(8,128)(2,1)S(1)} %get-tuple-element.35.target, bf16[24,2560]{1,0:T(8,128)(2,1)S(1)} %collective-permute-done.2.faces.faces_first, bf16[24,2560]{1,0:T(8,128)(2,1)S(1)} %collective-permute-done.3.faces_second, ...), custom_call_target="tpu_custom_call" | custom-call | flops 3000000000 | bytes 3000000 | tf_op jit(solution)/shard_map/near_second/pallas_call | solution.py:460
  35.6 3.7 %collective-permute-start.4 = (f32[1,2176]{1,0:T(1,128)S(1)}, f32[1,2176]{1,0:T(1,128)S(1)}, u32[]{:S(2)}, u32[]{:S(2)}) collective-permute-start(f32[1,2176]{1,0:T(1,128)S(1)} %get-tuple-element.47.mine), channel_id=1, source_target_pairs={{1,0},{0,1},{3,2},{2,3},{5,4},{4,5},{7,6},{6,7},{9,8},{8,9},{11,10... | collective-permute-start | bytes 26120 | tf_op jit(solution)/shard_map/ppermute | solution.py:434
  39.3 0.8 %collective-permute-done.4.other = f32[1,2176]{1,0:T(1,128)S(1)} collective-permute-done((f32[1,2176]{1,0:T(1,128)S(1)}, f32[1,2176]{1,0:T(1,128)S(1)}, u32[]{:S(2)}, u32[]{:S(2)}) %collective-permute-start.4) | collective-permute-done | bytes 8736 | tf_op jit(solution)/shard_map/ppermute | solution.py:434
  40.2 0.7 %mean.1 = f32[1,2048]{1,0:T(1,128)} custom-call(f32[1,2176]{1,0:T(1,128)S(1)} %get-tuple-element.47.mine, f32[1,2176]{1,0:T(1,128)S(1)} %collective-permute-done.4.other), custom_call_target="tpu_custom_call" | custom-call | flops 1000000000 | bytes 1000000 | tf_op jit(solution)/shard_map/mean/pallas_call | solution.py:460
Async XLA Ops:
  4.3 26.2 %all-to-all-start = ((bf16[16,24,128]{2,1,0:T(8,128)(2,1)}), bf16[16,24,128]{2,1,0:T(8,128)(2,1)S(1)}, u32[]{:S(2)}, u32[]{:S(2)}) async-start(bf16[16,24,128]{2,1,0:T(8,128)(2,1)} %get-tuple-element.45), calls=%async_computation | async-start | bytes 196608 | tf_op jit(solution)/shard_map/all_to_all | solution.py:502
  10.9 5.4 %collective-permute-start = (bf16[24,1536]{1,0:T(8,128)(2,1)S(1)}, bf16[24,1536]{1,0:T(8,128)(2,1)S(1)}, u32[]{:S(2)}, u32[]{:S(2)}) collective-permute-start(bf16[24,1536]{1,0:T(8,128)(2,1)S(1)} %get-tuple-element.27), channel_id=1, source_target_pairs={{2,0},{7,1},{0,2},{5,3},{6,4},{3,5},{4,6},{1,7},{10,8},{15,9},{8,1... | collective-permute-start | bytes 221192 | tf_op jit(solution)/shard_map/ppermute | solution.py:445
  13.0 4.4 %collective-permute-start.1 = (bf16[24,1536]{1,0:T(8,128)(2,1)S(1)}, bf16[24,1536]{1,0:T(8,128)(2,1)S(1)}, u32[]{:S(2)}, u32[]{:S(2)}) collective-permute-start(bf16[24,1536]{1,0:T(8,128)(2,1)S(1)} %get-tuple-element.28), channel_id=1, source_target_pairs={{6,0},{3,1},{4,2},{1,3},{2,4},{7,5},{0,6},{5,7},{14,8},{11,9},{12,... | collective-permute-start | bytes 221192 | tf_op jit(solution)/shard_map/ppermute | solution.py:445
  18.2 10.2 %collective-permute-start.2 = (bf16[24,2560]{1,0:T(8,128)(2,1)S(1)}, bf16[24,2560]{1,0:T(8,128)(2,1)S(1)}, u32[]{:S(2)}, u32[]{:S(2)}) collective-permute-start(bf16[24,2560]{1,0:T(8,128)(2,1)S(1)} %get-tuple-element.37), channel_id=1, source_target_pairs={{8,0},{10,2},{12,4},{14,6},{0,8},{17,9},{2,10},{19,11},{4,12},{21,... | collective-permute-start | bytes 368648 | tf_op jit(solution)/shard_map/ppermute | solution.py:445
  26.5 5.6 %collective-permute-start.3 = (bf16[24,2560]{1,0:T(8,128)(2,1)S(1)}, bf16[24,2560]{1,0:T(8,128)(2,1)S(1)}, u32[]{:S(2)}, u32[]{:S(2)}) collective-permute-start(bf16[24,2560]{1,0:T(8,128)(2,1)S(1)} %get-tuple-element.38), channel_id=1, source_target_pairs={{9,1},{11,3},{13,5},{15,7},{16,8},{1,9},{18,10},{3,11},{20,12},{5,... | collective-permute-start | bytes 368648 | tf_op jit(solution)/shard_map/ppermute | solution.py:445
  35.6 4.5 %collective-permute-start.4 = (f32[1,2176]{1,0:T(1,128)S(1)}, f32[1,2176]{1,0:T(1,128)S(1)}, u32[]{:S(2)}, u32[]{:S(2)}) collective-permute-start(f32[1,2176]{1,0:T(1,128)S(1)} %get-tuple-element.47.mine), channel_id=1, source_target_pairs={{1,0},{0,1},{3,2},{2,3},{5,4},{4,5},{7,6},{6,7},{9,8},{8,9},{11,10... | collective-permute-start | bytes 26120 | tf_op jit(solution)/shard_map/ppermute | solution.py:434

commit v13 on v11

--- a/solution.py
+++ b/solution.py
@@ -221,41 +221,45 @@
     return low_bits(jnp.transpose(features(held, start, size, centre, False)))
 
 
-def pulled(near, index, target, source, masses, starts, size, first=None):
+def pulled(near, jobs, target, size, first=None):
     width = target.shape[1] // 8
-    tiles = [(piece, turn) for piece in range(2) for turn in range(len(starts))]
-    places = [lanes((2 * index + piece) * width, width) for piece in range(2)]
-
-    def squares(piece, turn):
-        return dot(source[lanes(starts[turn], size), :], target[:, places[piece]])
-
-    ahead = squares(*tiles[0])
-    for place, (piece, turn) in enumerate(tiles):
+    tiles = []
+    for group, source, masses, starts in jobs:
+        for piece in range(2):
+            here = lanes((2 * group + piece) * width, width)
+            for turn, start in enumerate(starts):
+                tiles.append((here, source, masses, lanes(start, size), turn == 0, turn + 1 == len(starts)))
+
+    def squares(tile):
+        return dot(tile[1][tile[3], :], target[:, tile[0]])
+
+    ahead, kernel, total = squares(tiles[0]), None, None
+    for turn in range(len(tiles) + 1):
         square = ahead
-        if place + 1 < len(tiles):
-            ahead = squares(*tiles[place + 1])
-        if turn == 0:
-            total = jnp.zeros((ROWS, width), jnp.float32) if first is None else first[:, places[piece]]
-        total = total + dot(masses[:, lanes(starts[turn], size)], low_bits(lax.rsqrt(square)))
-        if turn + 1 == len(starts):
-            near[:, places[piece]] = total
+        if turn + 1 < len(tiles):
+            ahead = squares(tiles[turn + 1])
+        if turn > 0:
+            here, _, masses, place, opens, closes = tiles[turn - 1]
+            if opens:
+                total = jnp.zeros((ROWS, width), jnp.float32) if first is None else first[:, here]
+            total = total + dot(masses[:, place], kernel)
+            if closes:
+                near[:, here] = total
+        if turn < len(tiles):
+            kernel = low_bits(lax.rsqrt(square))
 
 
 def own_groups(near, first, last, target, source, own):
     pts = source.shape[0] // 8
-
-    def group(index, carry):
-        pulled(near, index, target, source, own, [2 * p * pts for p in range(4)], 2 * pts)
-        return carry
-
-    lax.fori_loop(first, last, group, 0)
+    starts = [2 * p * pts for p in range(4)]
+    pulled(near, [(group, source, own, starts) for group in range(first, last)], target, 2 * pts)
 
 
 def box_columns(depth, box_x, box_z, nodes):
     blocks = []
-    for layer, distance in [(layer, distance) for layer in range(depth) for distance in range(ACROSS)]:
+    for turn, distance in [(turn, distance) for turn in range(depth) for distance in range(ACROSS)]:
         gap_x = 2 * (box_x - (box_x ^ distance))
-        gap_z = 2 * (box_z - layer)
+        gap_z = 2 * (box_z - ((box_z ^ turn) if depth == 4 else turn))
         across_x = nodes[0] + gap_x.astype(jnp.float32)
         across_z = nodes[2] + gap_z.astype(jnp.float32)
         apart = jnp.maximum(jnp.abs(gap_x), jnp.abs(gap_z)) >= 4
@@ -296,7 +300,7 @@
     return jnp.where(node == 0, 0.0, value) + spread_first(value, 0) + spread_first(value, COEFFS)
 
 
-def faces_of(faces, bit, given, own, left, right):
+def faces_of(faces, bit, given, own, left, right, rows=None):
     points = own.shape[1]
     pts = points // 8
     for y in range(2):
@@ -312,6 +316,8 @@
     base_high = low_bits(base).astype(jnp.float32)
     coded = jnp.where(node == 0, base_high, jnp.where(node == COEFFS, base - base_high, given - base))
     faces[:, lanes(points, LEAVES)] = low_bits(coded)
+    if rows is not None:
+        faces[:, lanes(points + LEAVES, rows.shape[1])] = rows
 
 
 def row_kernel(own, moments, totals, from_1, from_2, from_3, far, left, right, same, other, faces_even, rows):
@@ -329,14 +335,14 @@
     base = 4 * pts
     ends = lanes(base + LEAVES, 2 * SLOT)
     row = jnp.concatenate([totals[...], from_1[:, ends], from_2[...], from_3[:, ends]], axis=1)
-    rows[...] = jnp.broadcast_to(row[None], rows.shape)
-    row = jnp.concatenate([left[:, lanes(base, LEAVES)], moments[...], right[:, lanes(base, LEAVES)]], axis=1)
+    rows[...] = row
+    around = jnp.concatenate([left[:, lanes(base, LEAVES)], moments[...], right[:, lanes(base, LEAVES)]], axis=1)
     below_rows, same_rows, above_rows = pl.ds(0, 3 * LEAVES), pl.ds(3 * LEAVES, 2 * LEAVES), pl.ds(5 * LEAVES, 3 * LEAVES)
-    up = dot(row, far[below_rows, :])
-    down = dot(row, far[above_rows, :])
-    same[...] = dot(jnp.concatenate([row[:, :LEAVES], row[:, 2 * LEAVES :]], axis=1), far[same_rows, :])
+    up = dot(around, far[below_rows, :])
+    down = dot(around, far[above_rows, :])
+    same[...] = dot(jnp.concatenate([around[:, :LEAVES], around[:, 2 * LEAVES :]], axis=1), far[same_rows, :])
     odd = lax.rem(box_z, 2)
-    faces_of(faces_even, 1 - odd, jnp.where(odd == 0, up, down), own, left, right)
+    faces_of(faces_even, 1 - odd, jnp.where(odd == 0, up, down), own, left, right, row)
     other[...] = jnp.where(odd == 0, down, up)
 
 
@@ -348,19 +354,18 @@
     own_groups(near, EARLY, 4, target, source, own)
 
 
-def side_kernel(left, right, early, target, rows, near, passed, sides):
-    passed[...] = rows[...]
+def side_kernel(left, right, early, target, rows, faces_even, near, both, sides_left, sides_right):
     pts = early.shape[1] // 8
-    for step, side in ((0, left), (1, right)):
+    width = rows.shape[1]
+    both[:, lanes(0, width)] = rows[...]
+    both[:, lanes(width, width)] = faces_even[:, lanes(faces_even.shape[1] - width, width)]
+    jobs = []
+    for step, side, held in ((0, left, sides_left), (1, right, sides_right)):
         for place in range(4):
             centre = (1.5 if step else -1.5, place % 2 - 0.5, place // 2 - 0.5)
-            sides[lanes(place * pts, pts), :] = source_features(side, place * pts, pts, centre)
-
-        def layer(index, carry, step=step, side=side):
-            pulled(near, step + 2 * index, target, sides, side, [0, 2 * pts], 2 * pts, early)
-            return carry
-
-        lax.fori_loop(0, 2, layer, 0)
+            held[lanes(place * pts, pts), :] = source_features(side, place * pts, pts, centre)
+        jobs += [(step, held, side, [0, 2 * pts]), (step + 2, held, side, [0, 2 * pts])]
+    pulled(near, jobs, target, 2 * pts, early)
 
 
 def layer_pulls(near, early, step, inside, target, faces, sides):
@@ -374,12 +379,8 @@
             centre = (place // 2 - 1.5, place % 2 - 0.5, height)
             sides[lanes(place * pts, pts), :] = source_features(faces, place * pts, pts, centre)
 
-        def pair(index, carry):
-            starts = [(2 * x + 2 * index) * pts for x in range(3)]
-            pulled(near, index + 2 * step, target, sides, faces, starts, 2 * pts, early)
-            return carry
-
-        lax.fori_loop(0, 2, pair, 0)
+        jobs = [(i + 2 * step, sides, faces, [2 * (x + i) * pts for x in range(3)]) for i in range(2)]
+        pulled(near, jobs, target, 2 * pts, early)
 
     @pl.when(jnp.logical_not(inside))
     def _():
@@ -396,8 +397,8 @@
     layer_pulls(near, early, step, box_z >= 0, target, faces, sides)
 
 
-def last_kernel(depth, early, target, faces_even, faces_odd, basis, scale, column, columns, spread, same, boxes, *rest):
-    potential, sums, near, sides = rest
+def last_kernel(depth, early, target, faces_even, faces_odd, basis, scale, column, columns, spread, same, *rest):
+    held, (potential, sums, near, sides) = rest[:-4], rest[-4:]
     fields, points = potential.shape
     pts = points // 8
     _, box_z = box_place()
@@ -407,7 +408,14 @@
     inside = (box_z + 2 * step - 1 >= 0) & (box_z + 2 * step - 1 < depth)
     layer_pulls(near, early, step, inside, target, faces_odd, sides)
 
-    pieces = [boxes[layer][:, 2 * SLOT * turn : 2 * SLOT * (turn + 1)] for layer in range(depth) for turn in range(ACROSS)]
+    if depth == 4:
+        rows, distant = held
+        width = rows.shape[1]
+        near_rows = faces_even[:, lanes(faces_even.shape[1] - width, width)]
+        layers = [rows[...], near_rows, distant[:, lanes(0, width)], distant[:, lanes(width, width)]]
+    else:
+        layers = [held[0][layer] for layer in range(depth)]
+    pieces = [layer[:, 2 * SLOT * turn : 2 * SLOT * (turn + 1)] for layer in layers for turn in range(ACROSS)]
     totals_high = jnp.concatenate([piece[:, :SLOT] for piece in pieces], axis=1)
     totals_low = jnp.concatenate([piece[:, SLOT:] for piece in pieces], axis=1)
     coarse_high, coarse_low = high_low(dot(totals_high, columns[...]) + dot(totals_low, columns[...]))
@@ -461,7 +469,9 @@
     side_shape = ((ROWS, 4 * pts + LEAVES), half)
     given_shape = ((ROWS, 4 * pts + LEAVES + 2 * SLOT), half)
     faces_shape = ((ROWS, points + LEAVES), half)
-    rows_shape = ((depth, ROWS, 2 * SLOT * ACROSS), half)
+    even_shape = ((ROWS, points + LEAVES + 2 * SLOT * ACROSS), half)
+    rows_shape = ((ROWS, 2 * SLOT * ACROSS), half)
+    both_shape = ((ROWS, 4 * SLOT * ACROSS), half)
     near_shape, sums_shape = ((ROWS, points), full), ((ROWS, LEAVES), full)
     rows_scratch = pltpu.VMEM((8 * pts, FEATURES), half)
     own, basis, moments, totals, *given = call(
@@ -523,7 +533,7 @@
         row_kernel,
         "row",
         [vmem] * 7,
-        [side_shape, side_shape, sums_shape, sums_shape, faces_shape, rows_shape],
+        [side_shape, side_shape, sums_shape, sums_shape, even_shape, rows_shape],
         [],
         own,
         moments,
@@ -549,25 +559,29 @@
         target,
     )
     faces_odd = swapped(faces_odd, "space", lambda i: i + ACROSS if i // ACROSS % 2 else i - ACROSS)
-    near, rows = call(
+    near, both = call(
         side_kernel,
         "near_side",
-        [vmem] * 5,
-        [near_shape, rows_shape],
-        [pltpu.VMEM((4 * pts, FEATURES), half)],
+        [vmem] * 6,
+        [near_shape, both_shape],
+        [pltpu.VMEM((4 * pts, FEATURES), half)] * 2,
         left,
         right,
         near,
         target,
         rows,
+        faces_even,
     )
-    columns_of_boxes = [[z * ACROSS + x for z in range(depth)] for x in range(ACROSS)]
-    boxes = lax.all_to_all(rows, "space", 0, 0, axis_index_groups=columns_of_boxes, tiled=True)
+    if depth == 4:
+        held = [rows, swapped(both, "space", lambda i: i ^ (2 * ACROSS))]
+    else:
+        groups = [[z * ACROSS + x for z in range(depth)] for x in range(ACROSS)]
+        held = [lax.all_gather(rows, "space", axis_index_groups=groups)]
     near, = call(even_kernel, "near_even", [vmem] * 3, [near_shape], [rows_scratch], near, target, faces_even)
     potential, sums = call(
         functools.partial(last_kernel, depth),
         "near_odd",
-        [vmem] * 11,
+        [vmem] * (10 + len(held)),
         [((fields, points), full), ((1, points + 128), full)],
         [pltpu.VMEM((ROWS, points), full), rows_scratch],
         near,
@@ -580,7 +594,7 @@
         columns,
         spread,
         same,
-        boxes,
+        *held,
     )
     if lax.axis_size("sig") == 2:
         other = swapped(sums, "sig", lambda i: i ^ 1)

time: 37.3 us -> 31.2 us (0.84)
  the two profiles are of different devices: /device:TPU:17 before, /device:TPU:9 now
where the time goes in v13:
time: 31.2 us; the launch traced here: 31 us
  Pallas kernels  15.5 us (50%)
  starting transfers between devices  10.3 us (33%)
  waiting for transfers between devices  4.53 us (15%)
  between operations  0.7 us (2%)
    pallas_call x8, Pallas kernels, call(): pl.pallas_call(kernel, in_specs=in_specs, out_specs=[vmem] * len(outs), o...  15.5 us
    ppermute x7, starting transfers between devices, swapped(): lax.ppermute(block, axis, [(partner(i), i) for i in range(size) if 0 <= p...  10.3 us
    ppermute x7, waiting for transfers between devices, swapped(): lax.ppermute(block, axis, [(partner(i), i) for i in range(size) if 0 <= p...  4.53 us
  transfers between devices with their start and end apart: 7, of which 3 were waited for; matrix products, arithmetic and copies ran while one was open for 0% of the time, Pallas kernels for 26%

profile of v13, /device:TPU:9, one launch (start us, length us, event | category | flops | bytes accessed | tf_op | source)
XLA Modules:
  0.0 31.0 jit_solution(12961603799761092132)
XLA Ops:
  0.6 3.0 %pack.1 = (bf16[24,2048]{1,0:T(8,128)(2,1)S(1)}, bf16[128,2048]{1,0:T(8,128)(2,1)S(1)}, bf16[24,512]{1,0:T(8,128)(2,1)S(1)}, bf16[24,128]{1,0:T(8,128)(2,1)S(1)}...) custom-call(s32[8]{0:T(128)} %count_in.3, f32[3,2048]{1,0:T(4,128)} %positions_in.1, ...), custom_call_target="tpu_custom_call" | custom-call | tf_op jit(solution)/shard_map/pack/pallas_call | solution.py:457
  3.7 1.3 %collective-permute-start = (bf16[24,1664]{1,0:T(8,128)(2,1)S(1)}, bf16[24,1664]{1,0:T(8,128)(2,1)S(1)}, u32[]{:S(2)}, u32[]{:S(2)}) collective-permute-start(bf16[24,1664]{1,0:T(8,128)(2,1)S(1)} %get-tuple-element.31), channel_id=1, source_target_pairs={{2,0},{0,2},{6,4},{4,6},{10,8},{8,10},{14,12},{12,14},{18,16},{16,... | collective-permute-start | bytes 239624 | tf_op jit(solution)/shard_map/ppermute | solution.py:447
  5.0 1.2 %collective-permute-start.2 = (bf16[24,1664]{1,0:T(8,128)(2,1)S(1)}, bf16[24,1664]{1,0:T(8,128)(2,1)S(1)}, u32[]{:S(2)}, u32[]{:S(2)}) collective-permute-start(bf16[24,1664]{1,0:T(8,128)(2,1)S(1)} %get-tuple-element.32), channel_id=1, source_target_pairs={{6,0},{4,2},{2,4},{0,6},{14,8},{12,10},{10,12},{8,14},{22,16},{20,... | collective-permute-start | bytes 239624 | tf_op jit(solution)/shard_map/ppermute | solution.py:447
  6.2 0.2 collective-permute-start.1
  6.4 2.4 %near_own.1 = (f32[24,1024]{1,0:T(8,128)S(1)}, bf16[2048,48]{1,0:T(8,128)(2,1)S(1)}, bf16[48,2048]{1,0:T(8,128)(2,1)S(1)}, f32[1,2048]{1,0:T(1,128)S(1)}, f32[24...) custom-call(s32[8]{0:T(128)} %count_in.3, ...), custom_call_target="tpu_custom_call" | custom-call | tf_op jit(solution)/shard_map/near_own/pallas_call | solution.py:457
  8.8 0.0 collective-permute-done.1.from_2
  8.8 0.0 collective-permute-done.from_1
  8.8 1.5 %collective-permute-done.2.from_3 = bf16[24,1664]{1,0:T(8,128)(2,1)S(1)} collective-permute-done((bf16[24,1664]{1,0:T(8,128)(2,1)S(1)}, bf16[24,1664]{1,0:T(8,128)(2,1)S(1)}, u32[]{:S(2)}, u32[]{:S(2)}) %collective-permute-start.2) | collective-permute-done | bytes 79904 | tf_op jit(solution)/shard_map/ppermute | solution.py:447
  10.3 0.8 %row.1 = (bf16[24,1536]{1,0:T(8,128)(2,1)S(1)}, bf16[24,1536]{1,0:T(8,128)(2,1)S(1)}, f32[24,512]{1,0:T(8,128)S(1)}, f32[24,512]{1,0:T(8,128)S(1)}, bf16[24,3072...) custom-call(bf16[24,2048]{1,0:T(8,128)(2,1)S(1)} %get-tuple-element.28.own, bf16[24,512]{1,0:T(8,128)(2,1)S(1)} %get-tuple-element.29.moments, ...), custom_call_target="tpu_custom_call" | custom-call | tf_op jit(solution)/shard_map/row/pallas_call | solution.py:457
  11.1 0.2 collective-permute-start.3
  11.3 1.9 %near_middle.1 = (f32[24,2048]{1,0:T(8,128)S(1)}, bf16[24,2560]{1,0:T(8,128)(2,1)S(1)}) custom-call(bf16[24,2048]{1,0:T(8,128)(2,1)S(1)} %get-tuple-element.28.own, bf16[24,1536]{1,0:T(8,128)(2,1)S(1)} %get-tuple-element.34.left, bf16[24,1536]{1,0:T(8,128)(2,1)S(1)} %get-tuple-element.35.right, f32[24,512]{1,0:T(8,128)S(1)} %get-tuple-element.36.other, ...), custom_call_target="tpu_custom_call" | custom-call | tf_op jit(solution)/shard_map/near_middle/pallas_call | solution.py:457
  13.3 4.3 %collective-permute-start.4 = (bf16[24,2560]{1,0:T(8,128)(2,1)S(1)}, bf16[24,2560]{1,0:T(8,128)(2,1)S(1)}, u32[]{:S(2)}, u32[]{:S(2)}) collective-permute-start(bf16[24,2560]{1,0:T(8,128)(2,1)S(1)} %get-tuple-element.44), channel_id=1, source_target_pairs={{16,8},{18,10},{20,12},{22,14},{8,16},{10,18},{12,20},{14,22},{17,... | collective-permute-start | bytes 368648 | tf_op jit(solution)/shard_map/ppermute | solution.py:447
  17.6 0.0 collective-permute-done.3.faces_even.faces
  17.6 2.0 %near_side.1 = (f32[24,2048]{1,0:T(8,128)S(1)}, bf16[24,1024]{1,0:T(8,128)(2,1)S(1)}) custom-call(bf16[24,1536]{1,0:T(8,128)(2,1)S(1)} %get-tuple-element.34.left, bf16[24,1536]{1,0:T(8,128)(2,1)S(1)} %get-tuple-element.35.right, f32[24,2048]{1,0:T(8,128)S(1)} %get-tuple-element.40.early, bf16[48,2048]{1,0:T(8,128)(2,1)S(1)} %get-tuple-element.39.target, ...), custom_call_target="tpu_custom_call" | custom-call | tf_op jit(solution)/shard_map/near_side/pallas_call | solution.py:457
  19.6 0.0 collective-permute-start.5
  19.7 1.6 %near_even.1.early = f32[24,2048]{1,0:T(8,128)S(1)} custom-call(f32[24,2048]{1,0:T(8,128)S(1)} %get-tuple-element.43.early, bf16[48,2048]{1,0:T(8,128)(2,1)S(1)} %get-tuple-element.39.target, bf16[24,3072]{1,0:T(8,128)(2,1)S(1)} %collective-permute-done.3.faces_even.faces), custom_call_target="tpu_custom_call" | custom-call | tf_op jit(solution)/shard_map/near_even/pallas_call | solution.py:457
  21.3 0.0 collective-permute-done.4.faces_odd
  21.3 2.2 %collective-permute-done.5.rest_1_ = bf16[24,1024]{1,0:T(8,128)(2,1)S(1)} collective-permute-done((bf16[24,1024]{1,0:T(8,128)(2,1)S(1)}, bf16[24,1024]{1,0:T(8,128)(2,1)S(1)}, u32[]{:S(2)}, u32[]{:S(2)}) %collective-permute-start.5) | collective-permute-done | bytes 49184 | tf_op jit(solution)/shard_map/ppermute | solution.py:447
  23.5 3.0 %near_odd.1 = (f32[17,2048]{1,0:T(8,128)}, f32[1,2176]{1,0:T(1,128)S(1)}) custom-call(f32[24,2048]{1,0:T(8,128)S(1)} %near_even.1.early, bf16[48,2048]{1,0:T(8,128)(2,1)S(1)} %get-tuple-element.39.target, bf16[24,3072]{1,0:T(8,128)(2,1)S(1)} %collective-permute-done.3.faces_even.faces, bf16[24,2560]{1,0:T(8,128)(2,1)S(1)} %collective-permute-done.4.faces_odd, ...), custom_call_target="tpu_custom_call" | custom-call | tf_op jit(solution)/shard_map/near_odd/pallas_call | solution.py:457
  26.5 3.0 %collective-permute-start.6 = (f32[1,2176]{1,0:T(1,128)S(1)}, f32[1,2176]{1,0:T(1,128)S(1)}, u32[]{:S(2)}, u32[]{:S(2)}) collective-permute-start(f32[1,2176]{1,0:T(1,128)S(1)} %get-tuple-element.53.mine), channel_id=1, source_target_pairs={{1,0},{0,1},{3,2},{2,3},{5,4},{4,5},{7,6},{6,7},{9,8},{8,9},{11,10... | collective-permute-start | bytes 26120 | tf_op jit(solution)/shard_map/ppermute | solution.py:447
  29.5 0.8 %collective-permute-done.6.other = f32[1,2176]{1,0:T(1,128)S(1)} collective-permute-done((f32[1,2176]{1,0:T(1,128)S(1)}, f32[1,2176]{1,0:T(1,128)S(1)}, u32[]{:S(2)}, u32[]{:S(2)}) %collective-permute-start.6) | collective-permute-done | bytes 8736 | tf_op jit(solution)/shard_map/ppermute | solution.py:447
  30.4 0.7 %mean.1 = f32[1,2048]{1,0:T(1,128)} custom-call(f32[1,2176]{1,0:T(1,128)S(1)} %get-tuple-element.53.mine, f32[1,2176]{1,0:T(1,128)S(1)} %collective-permute-done.6.other), custom_call_target="tpu_custom_call" | custom-call | tf_op jit(solution)/shard_map/mean/pallas_call | solution.py:457
Async XLA Ops:
  3.7 5.1 %collective-permute-start = (bf16[24,1664]{1,0:T(8,128)(2,1)S(1)}, bf16[24,1664]{1,0:T(8,128)(2,1)S(1)}, u32[]{:S(2)}, u32[]{:S(2)}) collective-permute-start(bf16[24,1664]{1,0:T(8,128)(2,1)S(1)} %get-tuple-element.31), channel_id=1, source_target_pairs={{2,0},{0,2},{6,4},{4,6},{10,8},{8,10},{14,12},{12,14},{18,16},{16,... | collective-permute-start | bytes 239624 | tf_op jit(solution)/shard_map/ppermute | solution.py:447
  5.0 5.3 %collective-permute-start.2 = (bf16[24,1664]{1,0:T(8,128)(2,1)S(1)}, bf16[24,1664]{1,0:T(8,128)(2,1)S(1)}, u32[]{:S(2)}, u32[]{:S(2)}) collective-permute-start(bf16[24,1664]{1,0:T(8,128)(2,1)S(1)} %get-tuple-element.32), channel_id=1, source_target_pairs={{6,0},{4,2},{2,4},{0,6},{14,8},{12,10},{10,12},{8,14},{22,16},{20,... | collective-permute-start | bytes 239624 | tf_op jit(solution)/shard_map/ppermute | solution.py:447
  6.2 2.6 %collective-permute-start.1 = (bf16[24,128]{1,0:T(8,128)(2,1)S(1)}, bf16[24,128]{1,0:T(8,128)(2,1)S(1)}, u32[]{:S(2)}, u32[]{:S(2)}) collective-permute-start(bf16[24,128]{1,0:T(8,128)(2,1)S(1)} %get-tuple-element.30.totals), channel_id=1, source_target_pairs={{4,0},{6,2},{0,4},{2,6},{12,8},{14,10},{8,12},{10,14},{20,16},{22,... | collective-permute-start | bytes 18440 | tf_op jit(solution)/shard_map/ppermute | solution.py:447
  11.1 6.5 %collective-permute-start.3 = (bf16[24,3072]{1,0:T(8,128)(2,1)S(1)}, bf16[24,3072]{1,0:T(8,128)(2,1)S(1)}, u32[]{:S(2)}, u32[]{:S(2)}) collective-permute-start(bf16[24,3072]{1,0:T(8,128)(2,1)S(1)} %get-tuple-element.42), channel_id=1, source_target_pairs={{8,0},{10,2},{12,4},{14,6},{0,8},{2,10},{4,12},{6,14},{24,16},{26,... | collective-permute-start | bytes 442376 | tf_op jit(solution)/shard_map/ppermute | solution.py:447
  13.3 8.0 %collective-permute-start.4 = (bf16[24,2560]{1,0:T(8,128)(2,1)S(1)}, bf16[24,2560]{1,0:T(8,128)(2,1)S(1)}, u32[]{:S(2)}, u32[]{:S(2)}) collective-permute-start(bf16[24,2560]{1,0:T(8,128)(2,1)S(1)} %get-tuple-element.44), channel_id=1, source_target_pairs={{16,8},{18,10},{20,12},{22,14},{8,16},{10,18},{12,20},{14,22},{17,... | collective-permute-start | bytes 368648 | tf_op jit(solution)/shard_map/ppermute | solution.py:447
  19.6 3.8 %collective-permute-start.5 = (bf16[24,1024]{1,0:T(8,128)(2,1)S(1)}, bf16[24,1024]{1,0:T(8,128)(2,1)S(1)}, u32[]{:S(2)}, u32[]{:S(2)}) collective-permute-start(bf16[24,1024]{1,0:T(8,128)(2,1)S(1)} %get-tuple-element.51), channel_id=1, source_target_pairs={{16,0},{18,2},{20,4},{22,6},{24,8},{26,10},{28,12},{30,14},{0,16},... | collective-permute-start | bytes 147464 | tf_op jit(solution)/shard_map/ppermute | solution.py:447
  26.5 3.9 %collective-permute-start.6 = (f32[1,2176]{1,0:T(1,128)S(1)}, f32[1,2176]{1,0:T(1,128)S(1)}, u32[]{:S(2)}, u32[]{:S(2)}) collective-permute-start(f32[1,2176]{1,0:T(1,128)S(1)} %get-tuple-element.53.mine), channel_id=1, source_target_pairs={{1,0},{0,1},{3,2},{2,3},{5,4},{4,5},{7,6},{6,7},{9,8},{8,9},{11,10... | collective-permute-start | bytes 26120 | tf_op jit(solution)/shard_map/ppermute | solution.py:447

commit v14 on v13

--- a/solution.py
+++ b/solution.py
@@ -420,8 +420,8 @@
     totals_low = jnp.concatenate([piece[:, SLOT:] for piece in pieces], axis=1)
     coarse_high, coarse_low = high_low(dot(totals_high, columns[...]) + dot(totals_low, columns[...]))
     value = same[...] + dot(coarse_high, spread[...]) + dot(coarse_low, spread[...])
-    for faces in (faces_even, faces_odd):
-        value = value + decoded(faces[:, lanes(points, LEAVES)])
+    value = value + decoded(faces_even[:, lanes(points, LEAVES)])
+    value = value + jnp.where(inside, decoded(faces_odd[:, lanes(points, LEAVES)]), 0.0)
     local_high, local_low = high_low(value)
     weight = column[0:fields, 0:1]
     for leaf in range(8):
@@ -444,7 +444,7 @@
 
 def swapped(block, axis, partner):
     size = lax.axis_size(axis)
-    return lax.ppermute(block, axis, [(partner(i), i) for i in range(size) if 0 <= partner(i) < size])
+    return lax.ppermute(block, axis, [(partner(i) if 0 <= partner(i) < size else i, i) for i in range(size)])
 
 
 def per_device(positions, density, leaf_count, sigma_weights):

time: 31.2 us -> 31.2 us (level)
  no operation moved by 1% of the time
where the time goes in v14:
time: 31.2 us; the launch traced here: 31.1 us
  Pallas kernels  15.5 us (50%)
  starting transfers between devices  10.3 us (33%)
  waiting for transfers between devices  4.53 us (15%)
  between operations  0.7 us (2%)
    pallas_call x8, Pallas kernels, call(): pl.pallas_call(kernel, in_specs=in_specs, out_specs=[vmem] * len(outs), o...  15.5 us
    ppermute x7, starting transfers between devices, swapped(): lax.ppermute(block, axis, [(partner(i) if 0 <= partner(i) < size else i,...  10.3 us
    ppermute x7, waiting for transfers between devices, swapped(): lax.ppermute(block, axis, [(partner(i) if 0 <= partner(i) < size else i,...  4.53 us
  transfers between devices with their start and end apart: 7, of which 3 were waited for; matrix products, arithmetic and copies ran while one was open for 0% of the time, Pallas kernels for 26%

profile of v14, /device:TPU:9, one launch (start us, length us, event | category | flops | bytes accessed | tf_op | source)
XLA Modules:
  0.0 31.1 jit_solution(10740575624769356722)
XLA Ops:
  0.6 3.0 %pack.1 = (bf16[24,2048]{1,0:T(8,128)(2,1)S(1)}, bf16[128,2048]{1,0:T(8,128)(2,1)S(1)}, bf16[24,512]{1,0:T(8,128)(2,1)S(1)}, bf16[24,128]{1,0:T(8,128)(2,1)S(1)}...) custom-call(s32[8]{0:T(128)} %count_in.3, f32[3,2048]{1,0:T(4,128)} %positions_in.1, ...), custom_call_target="tpu_custom_call" | custom-call | tf_op jit(solution)/shard_map/pack/pallas_call | solution.py:457
  3.7 1.3 %collective-permute-start = (bf16[24,1664]{1,0:T(8,128)(2,1)S(1)}, bf16[24,1664]{1,0:T(8,128)(2,1)S(1)}, u32[]{:S(2)}, u32[]{:S(2)}) collective-permute-start(bf16[24,1664]{1,0:T(8,128)(2,1)S(1)} %get-tuple-element.31), channel_id=1, source_target_pairs={{2,0},{0,2},{6,4},{4,6},{10,8},{8,10},{14,12},{12,14},{18,16},{16,... | collective-permute-start | bytes 239624 | tf_op jit(solution)/shard_map/ppermute | solution.py:447
  5.0 1.2 %collective-permute-start.2 = (bf16[24,1664]{1,0:T(8,128)(2,1)S(1)}, bf16[24,1664]{1,0:T(8,128)(2,1)S(1)}, u32[]{:S(2)}, u32[]{:S(2)}) collective-permute-start(bf16[24,1664]{1,0:T(8,128)(2,1)S(1)} %get-tuple-element.32), channel_id=1, source_target_pairs={{6,0},{4,2},{2,4},{0,6},{14,8},{12,10},{10,12},{8,14},{22,16},{20,... | collective-permute-start | bytes 239624 | tf_op jit(solution)/shard_map/ppermute | solution.py:447
  6.2 0.2 collective-permute-start.1
  6.4 2.4 %near_own.1 = (f32[24,1024]{1,0:T(8,128)S(1)}, bf16[2048,48]{1,0:T(8,128)(2,1)S(1)}, bf16[48,2048]{1,0:T(8,128)(2,1)S(1)}, f32[1,2048]{1,0:T(1,128)S(1)}, f32[24...) custom-call(s32[8]{0:T(128)} %count_in.3, ...), custom_call_target="tpu_custom_call" | custom-call | tf_op jit(solution)/shard_map/near_own/pallas_call | solution.py:457
  8.8 0.0 collective-permute-done.1.from_2
  8.8 0.0 collective-permute-done.from_1
  8.8 1.5 %collective-permute-done.2.from_3 = bf16[24,1664]{1,0:T(8,128)(2,1)S(1)} collective-permute-done((bf16[24,1664]{1,0:T(8,128)(2,1)S(1)}, bf16[24,1664]{1,0:T(8,128)(2,1)S(1)}, u32[]{:S(2)}, u32[]{:S(2)}) %collective-permute-start.2) | collective-permute-done | bytes 79904 | tf_op jit(solution)/shard_map/ppermute | solution.py:447
  10.3 0.8 %row.1 = (bf16[24,1536]{1,0:T(8,128)(2,1)S(1)}, bf16[24,1536]{1,0:T(8,128)(2,1)S(1)}, f32[24,512]{1,0:T(8,128)S(1)}, f32[24,512]{1,0:T(8,128)S(1)}, bf16[24,3072...) custom-call(bf16[24,2048]{1,0:T(8,128)(2,1)S(1)} %get-tuple-element.28.own, bf16[24,512]{1,0:T(8,128)(2,1)S(1)} %get-tuple-element.29.moments, ...), custom_call_target="tpu_custom_call" | custom-call | tf_op jit(solution)/shard_map/row/pallas_call | solution.py:457
  11.1 0.2 collective-permute-start.3
  11.3 1.9 %near_middle.1 = (f32[24,2048]{1,0:T(8,128)S(1)}, bf16[24,2560]{1,0:T(8,128)(2,1)S(1)}) custom-call(bf16[24,2048]{1,0:T(8,128)(2,1)S(1)} %get-tuple-element.28.own, bf16[24,1536]{1,0:T(8,128)(2,1)S(1)} %get-tuple-element.34.left, bf16[24,1536]{1,0:T(8,128)(2,1)S(1)} %get-tuple-element.35.right, f32[24,512]{1,0:T(8,128)S(1)} %get-tuple-element.36.other, ...), custom_call_target="tpu_custom_call" | custom-call | tf_op jit(solution)/shard_map/near_middle/pallas_call | solution.py:457
  13.3 4.3 %collective-permute-start.4 = (bf16[24,2560]{1,0:T(8,128)(2,1)S(1)}, bf16[24,2560]{1,0:T(8,128)(2,1)S(1)}, u32[]{:S(2)}, u32[]{:S(2)}) collective-permute-start(bf16[24,2560]{1,0:T(8,128)(2,1)S(1)} %get-tuple-element.44), channel_id=1, source_target_pairs={{0,0},{2,2},{4,4},{6,6},{16,8},{18,10},{20,12},{22,14},{8,16},{10,... | collective-permute-start | bytes 368648 | tf_op jit(solution)/shard_map/ppermute | solution.py:447
  17.6 0.0 collective-permute-done.3.faces_even.faces
  17.6 2.0 %near_side.1 = (f32[24,2048]{1,0:T(8,128)S(1)}, bf16[24,1024]{1,0:T(8,128)(2,1)S(1)}) custom-call(bf16[24,1536]{1,0:T(8,128)(2,1)S(1)} %get-tuple-element.34.left, bf16[24,1536]{1,0:T(8,128)(2,1)S(1)} %get-tuple-element.35.right, f32[24,2048]{1,0:T(8,128)S(1)} %get-tuple-element.40.early, bf16[48,2048]{1,0:T(8,128)(2,1)S(1)} %get-tuple-element.39.target, ...), custom_call_target="tpu_custom_call" | custom-call | tf_op jit(solution)/shard_map/near_side/pallas_call | solution.py:457
  19.6 0.0 collective-permute-start.5
  19.7 1.6 %near_even.1.early = f32[24,2048]{1,0:T(8,128)S(1)} custom-call(f32[24,2048]{1,0:T(8,128)S(1)} %get-tuple-element.43.early, bf16[48,2048]{1,0:T(8,128)(2,1)S(1)} %get-tuple-element.39.target, bf16[24,3072]{1,0:T(8,128)(2,1)S(1)} %collective-permute-done.3.faces_even.faces), custom_call_target="tpu_custom_call" | custom-call | tf_op jit(solution)/shard_map/near_even/pallas_call | solution.py:457
  21.3 0.0 collective-permute-done.4.faces_odd
  21.3 2.2 %collective-permute-done.5.rest_1_ = bf16[24,1024]{1,0:T(8,128)(2,1)S(1)} collective-permute-done((bf16[24,1024]{1,0:T(8,128)(2,1)S(1)}, bf16[24,1024]{1,0:T(8,128)(2,1)S(1)}, u32[]{:S(2)}, u32[]{:S(2)}) %collective-permute-start.5) | collective-permute-done | bytes 49184 | tf_op jit(solution)/shard_map/ppermute | solution.py:447
  23.5 3.0 %near_odd.1 = (f32[17,2048]{1,0:T(8,128)}, f32[1,2176]{1,0:T(1,128)S(1)}) custom-call(f32[24,2048]{1,0:T(8,128)S(1)} %near_even.1.early, bf16[48,2048]{1,0:T(8,128)(2,1)S(1)} %get-tuple-element.39.target, bf16[24,3072]{1,0:T(8,128)(2,1)S(1)} %collective-permute-done.3.faces_even.faces, bf16[24,2560]{1,0:T(8,128)(2,1)S(1)} %collective-permute-done.4.faces_odd, ...), custom_call_target="tpu_custom_call" | custom-call | tf_op jit(solution)/shard_map/near_odd/pallas_call | solution.py:457
  26.5 3.0 %collective-permute-start.6 = (f32[1,2176]{1,0:T(1,128)S(1)}, f32[1,2176]{1,0:T(1,128)S(1)}, u32[]{:S(2)}, u32[]{:S(2)}) collective-permute-start(f32[1,2176]{1,0:T(1,128)S(1)} %get-tuple-element.53.mine), channel_id=1, source_target_pairs={{1,0},{0,1},{3,2},{2,3},{5,4},{4,5},{7,6},{6,7},{9,8},{8,9},{11,10... | collective-permute-start | bytes 26120 | tf_op jit(solution)/shard_map/ppermute | solution.py:447
  29.5 0.8 %collective-permute-done.6.other = f32[1,2176]{1,0:T(1,128)S(1)} collective-permute-done((f32[1,2176]{1,0:T(1,128)S(1)}, f32[1,2176]{1,0:T(1,128)S(1)}, u32[]{:S(2)}, u32[]{:S(2)}) %collective-permute-start.6) | collective-permute-done | bytes 8736 | tf_op jit(solution)/shard_map/ppermute | solution.py:447
  30.4 0.7 %mean.1 = f32[1,2048]{1,0:T(1,128)} custom-call(f32[1,2176]{1,0:T(1,128)S(1)} %get-tuple-element.53.mine, f32[1,2176]{1,0:T(1,128)S(1)} %collective-permute-done.6.other), custom_call_target="tpu_custom_call" | custom-call | tf_op jit(solution)/shard_map/mean/pallas_call | solution.py:457
Async XLA Ops:
  3.7 5.1 %collective-permute-start = (bf16[24,1664]{1,0:T(8,128)(2,1)S(1)}, bf16[24,1664]{1,0:T(8,128)(2,1)S(1)}, u32[]{:S(2)}, u32[]{:S(2)}) collective-permute-start(bf16[24,1664]{1,0:T(8,128)(2,1)S(1)} %get-tuple-element.31), channel_id=1, source_target_pairs={{2,0},{0,2},{6,4},{4,6},{10,8},{8,10},{14,12},{12,14},{18,16},{16,... | collective-permute-start | bytes 239624 | tf_op jit(solution)/shard_map/ppermute | solution.py:447
  5.0 5.3 %collective-permute-start.2 = (bf16[24,1664]{1,0:T(8,128)(2,1)S(1)}, bf16[24,1664]{1,0:T(8,128)(2,1)S(1)}, u32[]{:S(2)}, u32[]{:S(2)}) collective-permute-start(bf16[24,1664]{1,0:T(8,128)(2,1)S(1)} %get-tuple-element.32), channel_id=1, source_target_pairs={{6,0},{4,2},{2,4},{0,6},{14,8},{12,10},{10,12},{8,14},{22,16},{20,... | collective-permute-start | bytes 239624 | tf_op jit(solution)/shard_map/ppermute | solution.py:447
  6.2 2.6 %collective-permute-start.1 = (bf16[24,128]{1,0:T(8,128)(2,1)S(1)}, bf16[24,128]{1,0:T(8,128)(2,1)S(1)}, u32[]{:S(2)}, u32[]{:S(2)}) collective-permute-start(bf16[24,128]{1,0:T(8,128)(2,1)S(1)} %get-tuple-element.30.totals), channel_id=1, source_target_pairs={{4,0},{6,2},{0,4},{2,6},{12,8},{14,10},{8,12},{10,14},{20,16},{22,... | collective-permute-start | bytes 18440 | tf_op jit(solution)/shard_map/ppermute | solution.py:447
  11.1 6.5 %collective-permute-start.3 = (bf16[24,3072]{1,0:T(8,128)(2,1)S(1)}, bf16[24,3072]{1,0:T(8,128)(2,1)S(1)}, u32[]{:S(2)}, u32[]{:S(2)}) collective-permute-start(bf16[24,3072]{1,0:T(8,128)(2,1)S(1)} %get-tuple-element.42), channel_id=1, source_target_pairs={{8,0},{10,2},{12,4},{14,6},{0,8},{2,10},{4,12},{6,14},{24,16},{26,... | collective-permute-start | bytes 442376 | tf_op jit(solution)/shard_map/ppermute | solution.py:447
  13.3 8.0 %collective-permute-start.4 = (bf16[24,2560]{1,0:T(8,128)(2,1)S(1)}, bf16[24,2560]{1,0:T(8,128)(2,1)S(1)}, u32[]{:S(2)}, u32[]{:S(2)}) collective-permute-start(bf16[24,2560]{1,0:T(8,128)(2,1)S(1)} %get-tuple-element.44), channel_id=1, source_target_pairs={{0,0},{2,2},{4,4},{6,6},{16,8},{18,10},{20,12},{22,14},{8,16},{10,... | collective-permute-start | bytes 368648 | tf_op jit(solution)/shard_map/ppermute | solution.py:447
  19.6 3.8 %collective-permute-start.5 = (bf16[24,1024]{1,0:T(8,128)(2,1)S(1)}, bf16[24,1024]{1,0:T(8,128)(2,1)S(1)}, u32[]{:S(2)}, u32[]{:S(2)}) collective-permute-start(bf16[24,1024]{1,0:T(8,128)(2,1)S(1)} %get-tuple-element.51), channel_id=1, source_target_pairs={{16,0},{18,2},{20,4},{22,6},{24,8},{26,10},{28,12},{30,14},{0,16},... | collective-permute-start | bytes 147464 | tf_op jit(solution)/shard_map/ppermute | solution.py:447
  26.5 3.9 %collective-permute-start.6 = (f32[1,2176]{1,0:T(1,128)S(1)}, f32[1,2176]{1,0:T(1,128)S(1)}, u32[]{:S(2)}, u32[]{:S(2)}) collective-permute-start(f32[1,2176]{1,0:T(1,128)S(1)} %get-tuple-element.53.mine), channel_id=1, source_target_pairs={{1,0},{0,1},{3,2},{2,3},{5,4},{4,5},{7,6},{6,7},{9,8},{8,9},{11,10... | collective-permute-start | bytes 26120 | tf_op jit(solution)/shard_map/ppermute | solution.py:447

commit v15 on v14

--- a/solution.py
+++ b/solution.py
@@ -444,7 +444,18 @@
 
 def swapped(block, axis, partner):
     size = lax.axis_size(axis)
-    return lax.ppermute(block, axis, [(partner(i) if 0 <= partner(i) < size else i, i) for i in range(size)])
+    return lax.ppermute(block, axis, [(partner(i), i) for i in range(size)])
+
+
+def swapped_odd(block):
+    boxes, cores = lax.axis_size("space"), lax.axis_size("sig")
+    pairs = []
+    for box in range(boxes):
+        other = box + ACROSS if box // ACROSS % 2 else box - ACROSS
+        for core in range(cores):
+            source = other * cores + core if 0 <= other < boxes else box * cores + (core ^ 1)
+            pairs.append((source, box * cores + core))
+    return lax.ppermute(block, ("space", "sig"), pairs)
 
 
 def per_device(positions, density, leaf_count, sigma_weights):
@@ -558,7 +569,7 @@
         source,
         target,
     )
-    faces_odd = swapped(faces_odd, "space", lambda i: i + ACROSS if i // ACROSS % 2 else i - ACROSS)
+    faces_odd = swapped_odd(faces_odd)
     near, both = call(
         side_kernel,
         "near_side",

time: 31.2 us -> 29.4 us (0.942)
  the two profiles are of different devices: /device:TPU:9 before, /device:TPU:17 now
where the time goes in v15:
time: 29.4 us; the launch traced here: 29.2 us
  Pallas kernels  15.5 us (53%)
  starting transfers between devices  8.6 us (29%)
  waiting for transfers between devices  4.46 us (15%)
  between operations  0.68 us (2%)
    pallas_call x8, Pallas kernels, call(): pl.pallas_call(kernel, in_specs=in_specs, out_specs=[vmem] * len(outs), o...  15.5 us
    ppermute x6, starting transfers between devices, swapped(): return lax.ppermute(block, axis, [(partner(i), i) for i in range(size)])  8.6 us
    ppermute x6, waiting for transfers between devices, swapped(): return lax.ppermute(block, axis, [(partner(i), i) for i in range(size)])  4.46 us
  transfers between devices with their start and end apart: 7, of which 4 were waited for; matrix products, arithmetic and copies ran while one was open for 0% of the time, Pallas kernels for 27%

profile of v15, /device:TPU:17, one launch (start us, length us, event | category | flops | bytes accessed | tf_op | source)
XLA Modules:
  0.0 29.2 jit_solution(17338115392139962720)
XLA Ops:
  0.6 3.0 %pack.1 = (bf16[24,2048]{1,0:T(8,128)(2,1)S(1)}, bf16[128,2048]{1,0:T(8,128)(2,1)S(1)}, bf16[24,512]{1,0:T(8,128)(2,1)S(1)}, bf16[24,128]{1,0:T(8,128)(2,1)S(1)}...) custom-call(s32[8]{0:T(128)} %count_in.3, f32[3,2048]{1,0:T(4,128)} %positions_in.1, ...), custom_call_target="tpu_custom_call" | custom-call | tf_op jit(solution)/shard_map/pack/pallas_call | solution.py:468
  3.7 1.3 %collective-permute-start = (bf16[24,1664]{1,0:T(8,128)(2,1)S(1)}, bf16[24,1664]{1,0:T(8,128)(2,1)S(1)}, u32[]{:S(2)}, u32[]{:S(2)}) collective-permute-start(bf16[24,1664]{1,0:T(8,128)(2,1)S(1)} %get-tuple-element.31), channel_id=1, source_target_pairs={{2,0},{0,2},{6,4},{4,6},{10,8},{8,10},{14,12},{12,14},{18,16},{16,... | collective-permute-start | bytes 239624 | tf_op jit(solution)/shard_map/ppermute | solution.py:447
  5.0 1.2 %collective-permute-start.2 = (bf16[24,1664]{1,0:T(8,128)(2,1)S(1)}, bf16[24,1664]{1,0:T(8,128)(2,1)S(1)}, u32[]{:S(2)}, u32[]{:S(2)}) collective-permute-start(bf16[24,1664]{1,0:T(8,128)(2,1)S(1)} %get-tuple-element.32), channel_id=1, source_target_pairs={{6,0},{4,2},{2,4},{0,6},{14,8},{12,10},{10,12},{8,14},{22,16},{20,... | collective-permute-start | bytes 239624 | tf_op jit(solution)/shard_map/ppermute | solution.py:447
  6.2 0.2 collective-permute-start.1
  6.4 2.4 %near_own.1 = (f32[24,1024]{1,0:T(8,128)S(1)}, bf16[2048,48]{1,0:T(8,128)(2,1)S(1)}, bf16[48,2048]{1,0:T(8,128)(2,1)S(1)}, f32[1,2048]{1,0:T(1,128)S(1)}, f32[24...) custom-call(s32[8]{0:T(128)} %count_in.3, ...), custom_call_target="tpu_custom_call" | custom-call | tf_op jit(solution)/shard_map/near_own/pallas_call | solution.py:468
  8.8 0.0 collective-permute-done.1.from_2
  8.8 0.0 collective-permute-done.from_1
  8.8 1.5 %collective-permute-done.2.from_3 = bf16[24,1664]{1,0:T(8,128)(2,1)S(1)} collective-permute-done((bf16[24,1664]{1,0:T(8,128)(2,1)S(1)}, bf16[24,1664]{1,0:T(8,128)(2,1)S(1)}, u32[]{:S(2)}, u32[]{:S(2)}) %collective-permute-start.2) | collective-permute-done | bytes 79904 | tf_op jit(solution)/shard_map/ppermute | solution.py:447
  10.3 0.8 %row.1 = (bf16[24,1536]{1,0:T(8,128)(2,1)S(1)}, bf16[24,1536]{1,0:T(8,128)(2,1)S(1)}, f32[24,512]{1,0:T(8,128)S(1)}, f32[24,512]{1,0:T(8,128)S(1)}, bf16[24,3072...) custom-call(bf16[24,2048]{1,0:T(8,128)(2,1)S(1)} %get-tuple-element.28.own, bf16[24,512]{1,0:T(8,128)(2,1)S(1)} %get-tuple-element.29.moments, ...), custom_call_target="tpu_custom_call" | custom-call | tf_op jit(solution)/shard_map/row/pallas_call | solution.py:468
  11.1 1.4 %collective-permute-start.3 = (bf16[24,3072]{1,0:T(8,128)(2,1)S(1)}, bf16[24,3072]{1,0:T(8,128)(2,1)S(1)}, u32[]{:S(2)}, u32[]{:S(2)}) collective-permute-start(bf16[24,3072]{1,0:T(8,128)(2,1)S(1)} %get-tuple-element.42), channel_id=1, source_target_pairs={{8,0},{10,2},{12,4},{14,6},{0,8},{2,10},{4,12},{6,14},{24,16},{26,... | collective-permute-start | bytes 442376 | tf_op jit(solution)/shard_map/ppermute | solution.py:447
  12.5 1.9 %near_middle.1 = (f32[24,2048]{1,0:T(8,128)S(1)}, bf16[24,2560]{1,0:T(8,128)(2,1)S(1)}) custom-call(bf16[24,2048]{1,0:T(8,128)(2,1)S(1)} %get-tuple-element.28.own, bf16[24,1536]{1,0:T(8,128)(2,1)S(1)} %get-tuple-element.34.left, bf16[24,1536]{1,0:T(8,128)(2,1)S(1)} %get-tuple-element.35.right, f32[24,512]{1,0:T(8,128)S(1)} %get-tuple-element.36.other, ...), custom_call_target="tpu_custom_call" | custom-call | tf_op jit(solution)/shard_map/near_middle/pallas_call | solution.py:468
  14.4 0.0 collective-permute-start.4
  14.4 0.8 %collective-permute-done.3.faces_even.faces = bf16[24,3072]{1,0:T(8,128)(2,1)S(1)} collective-permute-done((bf16[24,3072]{1,0:T(8,128)(2,1)S(1)}, bf16[24,3072]{1,0:T(8,128)(2,1)S(1)}, u32[]{:S(2)}, u32[]{:S(2)}) %collective-permute-start.3) | collective-permute-done | bytes 147488 | tf_op jit(solution)/shard_map/ppermute | solution.py:447
  15.2 2.0 %near_side.1 = (f32[24,2048]{1,0:T(8,128)S(1)}, bf16[24,1024]{1,0:T(8,128)(2,1)S(1)}) custom-call(bf16[24,1536]{1,0:T(8,128)(2,1)S(1)} %get-tuple-element.34.left, bf16[24,1536]{1,0:T(8,128)(2,1)S(1)} %get-tuple-element.35.right, f32[24,2048]{1,0:T(8,128)S(1)} %get-tuple-element.40.early, bf16[48,2048]{1,0:T(8,128)(2,1)S(1)} %get-tuple-element.39.target, ...), custom_call_target="tpu_custom_call" | custom-call | tf_op jit(solution)/shard_map/near_side/pallas_call | solution.py:468
  17.2 0.9 %collective-permute-start.5 = (bf16[24,1024]{1,0:T(8,128)(2,1)S(1)}, bf16[24,1024]{1,0:T(8,128)(2,1)S(1)}, u32[]{:S(2)}, u32[]{:S(2)}) collective-permute-start(bf16[24,1024]{1,0:T(8,128)(2,1)S(1)} %get-tuple-element.51), channel_id=1, source_target_pairs={{16,0},{18,2},{20,4},{22,6},{24,8},{26,10},{28,12},{30,14},{0,16},... | collective-permute-start | bytes 147464 | tf_op jit(solution)/shard_map/ppermute | solution.py:447
  18.1 1.6 %near_even.1.early = f32[24,2048]{1,0:T(8,128)S(1)} custom-call(f32[24,2048]{1,0:T(8,128)S(1)} %get-tuple-element.43.early, bf16[48,2048]{1,0:T(8,128)(2,1)S(1)} %get-tuple-element.39.target, bf16[24,3072]{1,0:T(8,128)(2,1)S(1)} %collective-permute-done.3.faces_even.faces), custom_call_target="tpu_custom_call" | custom-call | tf_op jit(solution)/shard_map/near_even/pallas_call | solution.py:468
  19.7 0.0 collective-permute-done.4.faces_odd
  19.7 1.4 %collective-permute-done.5.rest_1_ = bf16[24,1024]{1,0:T(8,128)(2,1)S(1)} collective-permute-done((bf16[24,1024]{1,0:T(8,128)(2,1)S(1)}, bf16[24,1024]{1,0:T(8,128)(2,1)S(1)}, u32[]{:S(2)}, u32[]{:S(2)}) %collective-permute-start.5) | collective-permute-done | bytes 49184 | tf_op jit(solution)/shard_map/ppermute | solution.py:447
  21.1 3.0 %near_odd.1 = (f32[17,2048]{1,0:T(8,128)}, f32[1,2176]{1,0:T(1,128)S(1)}) custom-call(f32[24,2048]{1,0:T(8,128)S(1)} %near_even.1.early, bf16[48,2048]{1,0:T(8,128)(2,1)S(1)} %get-tuple-element.39.target, bf16[24,3072]{1,0:T(8,128)(2,1)S(1)} %collective-permute-done.3.faces_even.faces, bf16[24,2560]{1,0:T(8,128)(2,1)S(1)} %collective-permute-done.4.faces_odd, ...), custom_call_target="tpu_custom_call" | custom-call | tf_op jit(solution)/shard_map/near_odd/pallas_call | solution.py:468
  24.1 3.6 %collective-permute-start.6 = (f32[1,2176]{1,0:T(1,128)S(1)}, f32[1,2176]{1,0:T(1,128)S(1)}, u32[]{:S(2)}, u32[]{:S(2)}) collective-permute-start(f32[1,2176]{1,0:T(1,128)S(1)} %get-tuple-element.53.mine), channel_id=1, source_target_pairs={{1,0},{0,1},{3,2},{2,3},{5,4},{4,5},{7,6},{6,7},{9,8},{8,9},{11,10... | collective-permute-start | bytes 26120 | tf_op jit(solution)/shard_map/ppermute | solution.py:447
  27.7 0.8 %collective-permute-done.6.other = f32[1,2176]{1,0:T(1,128)S(1)} collective-permute-done((f32[1,2176]{1,0:T(1,128)S(1)}, f32[1,2176]{1,0:T(1,128)S(1)}, u32[]{:S(2)}, u32[]{:S(2)}) %collective-permute-start.6) | collective-permute-done | bytes 8736 | tf_op jit(solution)/shard_map/ppermute | solution.py:447
  28.6 0.7 %mean.1 = f32[1,2048]{1,0:T(1,128)} custom-call(f32[1,2176]{1,0:T(1,128)S(1)} %get-tuple-element.53.mine, f32[1,2176]{1,0:T(1,128)S(1)} %collective-permute-done.6.other), custom_call_target="tpu_custom_call" | custom-call | tf_op jit(solution)/shard_map/mean/pallas_call | solution.py:468
Async XLA Ops:
  3.7 5.1 %collective-permute-start = (bf16[24,1664]{1,0:T(8,128)(2,1)S(1)}, bf16[24,1664]{1,0:T(8,128)(2,1)S(1)}, u32[]{:S(2)}, u32[]{:S(2)}) collective-permute-start(bf16[24,1664]{1,0:T(8,128)(2,1)S(1)} %get-tuple-element.31), channel_id=1, source_target_pairs={{2,0},{0,2},{6,4},{4,6},{10,8},{8,10},{14,12},{12,14},{18,16},{16,... | collective-permute-start | bytes 239624 | tf_op jit(solution)/shard_map/ppermute | solution.py:447
  5.0 5.3 %collective-permute-start.2 = (bf16[24,1664]{1,0:T(8,128)(2,1)S(1)}, bf16[24,1664]{1,0:T(8,128)(2,1)S(1)}, u32[]{:S(2)}, u32[]{:S(2)}) collective-permute-start(bf16[24,1664]{1,0:T(8,128)(2,1)S(1)} %get-tuple-element.32), channel_id=1, source_target_pairs={{6,0},{4,2},{2,4},{0,6},{14,8},{12,10},{10,12},{8,14},{22,16},{20,... | collective-permute-start | bytes 239624 | tf_op jit(solution)/shard_map/ppermute | solution.py:447
  6.2 2.6 %collective-permute-start.1 = (bf16[24,128]{1,0:T(8,128)(2,1)S(1)}, bf16[24,128]{1,0:T(8,128)(2,1)S(1)}, u32[]{:S(2)}, u32[]{:S(2)}) collective-permute-start(bf16[24,128]{1,0:T(8,128)(2,1)S(1)} %get-tuple-element.30.totals), channel_id=1, source_target_pairs={{4,0},{6,2},{0,4},{2,6},{12,8},{14,10},{8,12},{10,14},{20,16},{22,... | collective-permute-start | bytes 18440 | tf_op jit(solution)/shard_map/ppermute | solution.py:447
  11.1 4.1 %collective-permute-start.3 = (bf16[24,3072]{1,0:T(8,128)(2,1)S(1)}, bf16[24,3072]{1,0:T(8,128)(2,1)S(1)}, u32[]{:S(2)}, u32[]{:S(2)}) collective-permute-start(bf16[24,3072]{1,0:T(8,128)(2,1)S(1)} %get-tuple-element.42), channel_id=1, source_target_pairs={{8,0},{10,2},{12,4},{14,6},{0,8},{2,10},{4,12},{6,14},{24,16},{26,... | collective-permute-start | bytes 442376 | tf_op jit(solution)/shard_map/ppermute | solution.py:447
  14.4 5.3 %collective-permute-start.4 = (bf16[24,2560]{1,0:T(8,128)(2,1)S(1)}, bf16[24,2560]{1,0:T(8,128)(2,1)S(1)}, u32[]{:S(2)}, u32[]{:S(2)}) collective-permute-start(bf16[24,2560]{1,0:T(8,128)(2,1)S(1)} %get-tuple-element.44), channel_id=1, source_target_pairs={{1,0},{0,1},{3,2},{2,3},{5,4},{4,5},{7,6},{6,7},{16,8},{17,9},{18,... | collective-permute-start | bytes 368648 | tf_op jit(solution)/shard_map/ppermute | solution.py:458
  17.2 3.9 %collective-permute-start.5 = (bf16[24,1024]{1,0:T(8,128)(2,1)S(1)}, bf16[24,1024]{1,0:T(8,128)(2,1)S(1)}, u32[]{:S(2)}, u32[]{:S(2)}) collective-permute-start(bf16[24,1024]{1,0:T(8,128)(2,1)S(1)} %get-tuple-element.51), channel_id=1, source_target_pairs={{16,0},{18,2},{20,4},{22,6},{24,8},{26,10},{28,12},{30,14},{0,16},... | collective-permute-start | bytes 147464 | tf_op jit(solution)/shard_map/ppermute | solution.py:447
  24.1 4.5 %collective-permute-start.6 = (f32[1,2176]{1,0:T(1,128)S(1)}, f32[1,2176]{1,0:T(1,128)S(1)}, u32[]{:S(2)}, u32[]{:S(2)}) collective-permute-start(f32[1,2176]{1,0:T(1,128)S(1)} %get-tuple-element.53.mine), channel_id=1, source_target_pairs={{1,0},{0,1},{3,2},{2,3},{5,4},{4,5},{7,6},{6,7},{9,8},{8,9},{11,10... | collective-permute-start | bytes 26120 | tf_op jit(solution)/shard_map/ppermute | solution.py:447

commit v16 on v15

--- a/solution.py
+++ b/solution.py
@@ -17,7 +17,7 @@
 LEAVES = 8 * SLOT
 MEGA = 1024 * 1024
 FEATURES = 48
-EARLY = 2
+EARLY = 3
 
 
 def exponent_table(order_max):
@@ -40,6 +40,7 @@
 COEFFS = len(EXPONENTS)
 CHECK = node_table(COEFFS, 0.5).astype(np.float64)
 EQUIV = node_table(COEFFS, 0.0).astype(np.float64)
+HEAVY = [EXPONENTS.index(e) for e in ((0, 0, 0), (2, 0, 0), (0, 2, 0), (0, 0, 2), (4, 0, 0), (0, 4, 0), (0, 0, 4), (2, 0, 2))]
 STEPS = [(sx, sz) for sz in (-1, 0, 1) for sx in (-1, 0, 1) if sx != 0 or sz != 0]
 
 
@@ -88,6 +89,7 @@
 def box_nodes():
     gaps = np.zeros((3, SLOT, SLOT))
     gaps[:, :COEFFS, :COEFFS] = np.moveaxis(CHECK[None, :, :] - EQUIV[:, None, :], -1, 0)
+    gaps[:, COEFFS:] = gaps[:, HEAVY]
     gaps[1] = gaps[1] ** 2 + SOFTENING * SOFTENING
     return gaps.astype(np.float32)
 
@@ -102,6 +104,12 @@
 
 def low_bits(value):
     return value.astype(jnp.bfloat16)
+
+
+def heavy_table():
+    table = np.zeros((SLOT, SLOT), np.float32)
+    table[HEAVY, np.arange(COEFFS, SLOT)] = 1.0
+    return table
 
 
 def high_low(value):
@@ -133,10 +141,10 @@
     return copies
 
 
-def pack_kernel(count_in, positions_in, density_in, shift_in, own, basis, moments, totals, *rest):
-    payloads, (count, positions, density, shift, mono, sems) = rest[:2], rest[2:]
+def pack_kernel(count_in, positions_in, density_in, shift_in, heavy_in, own, basis, moments, totals, *rest):
+    payloads, (count, positions, density, shift, heavy, mono, sems) = rest[:2], rest[2:]
     copies = fetch(
-        [(count_in, count), (positions_in, positions), (density_in, density), (shift_in, shift)], sems
+        [(count_in, count), (positions_in, positions), (density_in, density), (shift_in, shift), (heavy_in, heavy)], sems
     )
     fields, points = density.shape
     pts = points // 8
@@ -179,7 +187,9 @@
     moment, rest = high_low(jnp.concatenate(parts, axis=1))
     moments[...] = moment
     total = dot(moment, shift[...]) + dot(rest, shift[...])
-    total = jnp.concatenate(high_low(total), axis=1)
+    total_high, total_low = high_low(total)
+    total = low_bits(total_high.astype(jnp.float32) + dot(total_low, heavy[...]))
+    total = jnp.concatenate([total, jnp.zeros_like(total)], axis=1)
     totals[...] = total
     for distance, payload in zip((1, 3), payloads):
         bit = jnp.where((box_x ^ distance) > box_x, 1, 0)
@@ -320,9 +330,13 @@
         faces[:, lanes(points + LEAVES, rows.shape[1])] = rows
 
 
-def row_kernel(own, moments, totals, from_1, from_2, from_3, far, left, right, same, other, faces_even, rows):
-    points = own.shape[1]
-    pts = points // 8
+def sums_for(above, left, moments, right, far):
+    base = left.shape[1] - LEAVES
+    around = jnp.concatenate([left[:, lanes(base, LEAVES)], moments[...], right[:, lanes(base, LEAVES)]], axis=1)
+    return dot(around, far[lanes(jnp.where(above == 1, 0, 5 * LEAVES), 3 * LEAVES), :])
+
+
+def row_kernel(own, moments, totals, from_1, from_2, from_3, far, left, right, faces_even, rows):
     box_x, box_z = box_place()
     for side, step in ((left, -1), (right, 1)):
         side[...] = jnp.zeros(side.shape, side.dtype)
@@ -332,24 +346,22 @@
             def _(side=side, held=held):
                 side[...] = held[:, lanes(0, side.shape[1])]
 
-    base = 4 * pts
-    ends = lanes(base + LEAVES, 2 * SLOT)
-    row = jnp.concatenate([totals[...], from_1[:, ends], from_2[...], from_3[:, ends]], axis=1)
+    ends = lanes(left.shape[1], 2 * SLOT)
+    row = [totals[...], from_1[:, ends], from_2[...], from_3[:, ends]]
+    row = jnp.concatenate([box[:, :SLOT] for box in row], axis=1)
     rows[...] = row
-    around = jnp.concatenate([left[:, lanes(base, LEAVES)], moments[...], right[:, lanes(base, LEAVES)]], axis=1)
-    below_rows, same_rows, above_rows = pl.ds(0, 3 * LEAVES), pl.ds(3 * LEAVES, 2 * LEAVES), pl.ds(5 * LEAVES, 3 * LEAVES)
-    up = dot(around, far[below_rows, :])
-    down = dot(around, far[above_rows, :])
-    same[...] = dot(jnp.concatenate([around[:, :LEAVES], around[:, 2 * LEAVES :]], axis=1), far[same_rows, :])
-    odd = lax.rem(box_z, 2)
-    faces_of(faces_even, 1 - odd, jnp.where(odd == 0, up, down), own, left, right, row)
-    other[...] = jnp.where(odd == 0, down, up)
-
-
-def middle_kernel(own, left, right, other, early, source, target, near, faces_odd):
+    above = 1 - lax.rem(box_z, 2)
+    faces_of(faces_even, above, sums_for(above, left, moments, right, far), own, left, right, row)
+
+
+def middle_kernel(own, left, right, moments, far, early, source, target, near, faces_odd, same):
     points = own.shape[1]
     _, box_z = box_place()
-    faces_of(faces_odd, lax.rem(box_z, 2), other[...], own, left, right)
+    above = lax.rem(box_z, 2)
+    faces_of(faces_odd, above, sums_for(above, left, moments, right, far), own, left, right)
+    base = left.shape[1] - LEAVES
+    beside = jnp.concatenate([left[:, lanes(base, LEAVES)], right[:, lanes(base, LEAVES)]], axis=1)
+    same[...] = dot(beside, far[lanes(3 * LEAVES, 2 * LEAVES), :])
     near[:, lanes(0, EARLY * points // 4)] = early[...]
     own_groups(near, EARLY, 4, target, source, own)
 
@@ -415,10 +427,7 @@
         layers = [rows[...], near_rows, distant[:, lanes(0, width)], distant[:, lanes(width, width)]]
     else:
         layers = [held[0][layer] for layer in range(depth)]
-    pieces = [layer[:, 2 * SLOT * turn : 2 * SLOT * (turn + 1)] for layer in layers for turn in range(ACROSS)]
-    totals_high = jnp.concatenate([piece[:, :SLOT] for piece in pieces], axis=1)
-    totals_low = jnp.concatenate([piece[:, SLOT:] for piece in pieces], axis=1)
-    coarse_high, coarse_low = high_low(dot(totals_high, columns[...]) + dot(totals_low, columns[...]))
+    coarse_high, coarse_low = high_low(dot(jnp.concatenate(layers, axis=1), columns[...]))
     value = same[...] + dot(coarse_high, spread[...]) + dot(coarse_low, spread[...])
     value = value + decoded(faces_even[:, lanes(points, LEAVES)])
     value = value + jnp.where(inside, decoded(faces_odd[:, lanes(points, LEAVES)]), 0.0)
@@ -480,15 +489,15 @@
     side_shape = ((ROWS, 4 * pts + LEAVES), half)
     given_shape = ((ROWS, 4 * pts + LEAVES + 2 * SLOT), half)
     faces_shape = ((ROWS, points + LEAVES), half)
-    even_shape = ((ROWS, points + LEAVES + 2 * SLOT * ACROSS), half)
-    rows_shape = ((ROWS, 2 * SLOT * ACROSS), half)
-    both_shape = ((ROWS, 4 * SLOT * ACROSS), half)
+    even_shape = ((ROWS, points + LEAVES + SLOT * ACROSS), half)
+    rows_shape = ((ROWS, SLOT * ACROSS), half)
+    both_shape = ((ROWS, 2 * SLOT * ACROSS), half)
     near_shape, sums_shape = ((ROWS, points), full), ((ROWS, LEAVES), full)
     rows_scratch = pltpu.VMEM((8 * pts, FEATURES), half)
     own, basis, moments, totals, *given = call(
         pack_kernel,
         "pack",
-        [hbm] * 4,
+        [hbm] * 5,
         [
             ((ROWS, points), half),
             ((2 * SLOT, points), half),
@@ -502,13 +511,15 @@
             pltpu.VMEM((3, points), full),
             pltpu.VMEM((fields, points), half),
             pltpu.VMEM((LEAVES, SLOT), half),
+            pltpu.VMEM((SLOT, SLOT), half),
             pltpu.VMEM((SLOT, 8, pts), full),
-            pltpu.SemaphoreType.DMA((4,)),
+            pltpu.SemaphoreType.DMA((5,)),
         ],
         leaf_count,
         positions,
         density,
         jnp.asarray(shift, half),
+        jnp.asarray(heavy_table(), half),
     )
     from_2 = swapped(totals, "space", lambda i: i ^ 2)
     from_1 = swapped(given[0], "space", lambda i: i ^ 1)
@@ -540,11 +551,11 @@
         jnp.asarray(shift.T.copy(), half),
         jnp.asarray(box_nodes()),
     )
-    left, right, same, other, faces_even, rows = call(
+    left, right, faces_even, rows = call(
         row_kernel,
         "row",
         [vmem] * 7,
-        [side_shape, side_shape, sums_shape, sums_shape, even_shape, rows_shape],
+        [side_shape, side_shape, even_shape, rows_shape],
         [],
         own,
         moments,
@@ -555,16 +566,17 @@
         far,
     )
     faces_even = swapped(faces_even, "space", lambda i: i ^ ACROSS)
-    near, faces_odd = call(
+    near, faces_odd, same = call(
         middle_kernel,
         "near_middle",
-        [vmem] * 7,
-        [near_shape, faces_shape],
+        [vmem] * 8,
+        [near_shape, faces_shape, sums_shape],
         [],
         own,
         left,
         right,
-        other,
+        moments,
+        far,
         near,
         source,
         target,

time: 29.4 us -> 28.6 us (0.973)
  waiting for transfers between devices: 4.46 us -> 3.95 us
    ppermute x6, waiting for transfers between devices: 4.46 us -> 3.94 us  [swapped(): return lax.ppermute(block, axis, [(partner(i), i) for i in range(size)])]
  transfers between devices with their start and end apart: 7 -> 7, of which waited for: 4 -> 4; matrix products, arithmetic and copies ran while one was open for 0% -> 0% of each run, Pallas kernels for 27% -> 29%
where the time goes in v16:
time: 28.6 us; the launch traced here: 28.4 us
  Pallas kernels  15.5 us (54%)
  starting transfers between devices  8.34 us (29%)
  waiting for transfers between devices  3.95 us (14%)
  between operations  0.69 us (2%)
    pallas_call x8, Pallas kernels, call(): pl.pallas_call(kernel, in_specs=in_specs, out_specs=[vmem] * len(outs), o...  15.5 us
    ppermute x6, starting transfers between devices, swapped(): return lax.ppermute(block, axis, [(partner(i), i) for i in range(size)])  8.34 us
    ppermute x6, waiting for transfers between devices, swapped(): return lax.ppermute(block, axis, [(partner(i), i) for i in range(size)])  3.94 us
  transfers between devices with their start and end apart: 7, of which 4 were waited for; matrix products, arithmetic and copies ran while one was open for 0% of the time, Pallas kernels for 29%

profile of v16, /device:TPU:17, one launch (start us, length us, event | category | flops | bytes accessed | tf_op | source)
XLA Modules:
  0.0 28.4 jit_solution(332617308583690166)
XLA Ops:
  0.6 3.1 %pack.1 = (bf16[24,2048]{1,0:T(8,128)(2,1)S(1)}, bf16[128,2048]{1,0:T(8,128)(2,1)S(1)}, bf16[24,512]{1,0:T(8,128)(2,1)S(1)}, bf16[24,128]{1,0:T(8,128)(2,1)S(1)}...) custom-call(s32[8]{0:T(128)} %count_in.3, f32[3,2048]{1,0:T(4,128)} %positions_in.1, ...), custom_call_target="tpu_custom_call" | custom-call | tf_op jit(solution)/shard_map/pack/pallas_call | solution.py:477
  3.7 1.3 %collective-permute-start = (bf16[24,1664]{1,0:T(8,128)(2,1)S(1)}, bf16[24,1664]{1,0:T(8,128)(2,1)S(1)}, u32[]{:S(2)}, u32[]{:S(2)}) collective-permute-start(bf16[24,1664]{1,0:T(8,128)(2,1)S(1)} %get-tuple-element.30), channel_id=1, source_target_pairs={{2,0},{0,2},{6,4},{4,6},{10,8},{8,10},{14,12},{12,14},{18,16},{16,... | collective-permute-start | bytes 239624 | tf_op jit(solution)/shard_map/ppermute | solution.py:456
  5.0 1.2 %collective-permute-start.2 = (bf16[24,1664]{1,0:T(8,128)(2,1)S(1)}, bf16[24,1664]{1,0:T(8,128)(2,1)S(1)}, u32[]{:S(2)}, u32[]{:S(2)}) collective-permute-start(bf16[24,1664]{1,0:T(8,128)(2,1)S(1)} %get-tuple-element.31), channel_id=1, source_target_pairs={{6,0},{4,2},{2,4},{0,6},{14,8},{12,10},{10,12},{8,14},{22,16},{20,... | collective-permute-start | bytes 239624 | tf_op jit(solution)/shard_map/ppermute | solution.py:456
  6.2 0.2 collective-permute-start.1
  6.4 3.1 %near_own.1 = (f32[24,1536]{1,0:T(8,128)S(1)}, bf16[2048,48]{1,0:T(8,128)(2,1)S(1)}, bf16[48,2048]{1,0:T(8,128)(2,1)S(1)}, f32[1,2048]{1,0:T(1,128)S(1)}, f32[24...) custom-call(s32[8]{0:T(128)} %count_in.3, ...), custom_call_target="tpu_custom_call" | custom-call | tf_op jit(solution)/shard_map/near_own/pallas_call | solution.py:477
  9.6 0.0 collective-permute-done.1.from_2
  9.6 0.0 collective-permute-done.from_1
  9.6 0.7 %collective-permute-done.2.from_3 = bf16[24,1664]{1,0:T(8,128)(2,1)S(1)} collective-permute-done((bf16[24,1664]{1,0:T(8,128)(2,1)S(1)}, bf16[24,1664]{1,0:T(8,128)(2,1)S(1)}, u32[]{:S(2)}, u32[]{:S(2)}) %collective-permute-start.2) | collective-permute-done | bytes 79904 | tf_op jit(solution)/shard_map/ppermute | solution.py:456
  10.3 0.5 %row.1 = (bf16[24,1536]{1,0:T(8,128)(2,1)S(1)}, bf16[24,1536]{1,0:T(8,128)(2,1)S(1)}, bf16[24,2816]{1,0:T(8,128)(2,1)S(1)}, bf16[24,256]{1,0:T(8,128)(2,1)S(1)}) custom-call(bf16[24,2048]{1,0:T(8,128)(2,1)S(1)} %get-tuple-element.27.own, bf16[24,512]{1,0:T(8,128)(2,1)S(1)} %get-tuple-element.28.moments, bf16[24,128]{1,0:T(8,128)(2,1)S(1)} %get-tuple-element.29.totals, ...), custom_call_target="tpu_custom_call" | custom-call | tf_op jit(solution)/shard_map/row/pallas_call | solution.py:477
  10.8 1.4 %collective-permute-start.3 = (bf16[24,2816]{1,0:T(8,128)(2,1)S(1)}, bf16[24,2816]{1,0:T(8,128)(2,1)S(1)}, u32[]{:S(2)}, u32[]{:S(2)}) collective-permute-start(bf16[24,2816]{1,0:T(8,128)(2,1)S(1)} %get-tuple-element.40), channel_id=1, source_target_pairs={{8,0},{10,2},{12,4},{14,6},{0,8},{2,10},{4,12},{6,14},{24,16},{26,... | collective-permute-start | bytes 405512 | tf_op jit(solution)/shard_map/ppermute | solution.py:456
  12.2 1.5 %near_middle.1 = (f32[24,2048]{1,0:T(8,128)S(1)}, bf16[24,2560]{1,0:T(8,128)(2,1)S(1)}, f32[24,512]{1,0:T(8,128)S(1)}) custom-call(bf16[24,2048]{1,0:T(8,128)(2,1)S(1)} %get-tuple-element.27.own, bf16[24,1536]{1,0:T(8,128)(2,1)S(1)} %get-tuple-element.33.left, bf16[24,1536]{1,0:T(8,128)(2,1)S(1)} %get-tuple-element.34.right, ...), custom_call_target="tpu_custom_call" | custom-call | tf_op jit(solution)/shard_map/near_middle/pallas_call | solution.py:477
  13.7 0.0 collective-permute-start.4
  13.7 1.0 %collective-permute-done.3.faces_even.faces = bf16[24,2816]{1,0:T(8,128)(2,1)S(1)} collective-permute-done((bf16[24,2816]{1,0:T(8,128)(2,1)S(1)}, bf16[24,2816]{1,0:T(8,128)(2,1)S(1)}, u32[]{:S(2)}, u32[]{:S(2)}) %collective-permute-start.3) | collective-permute-done | bytes 135200 | tf_op jit(solution)/shard_map/ppermute | solution.py:456
  14.8 2.0 %near_side.1 = (f32[24,2048]{1,0:T(8,128)S(1)}, bf16[24,512]{1,0:T(8,128)(2,1)S(1)}) custom-call(bf16[24,1536]{1,0:T(8,128)(2,1)S(1)} %get-tuple-element.33.left, bf16[24,1536]{1,0:T(8,128)(2,1)S(1)} %get-tuple-element.34.right, f32[24,2048]{1,0:T(8,128)S(1)} %get-tuple-element.38.early, bf16[48,2048]{1,0:T(8,128)(2,1)S(1)} %get-tuple-element.37.target, ...), custom_call_target="tpu_custom_call" | custom-call | tf_op jit(solution)/shard_map/near_side/pallas_call | solution.py:477
  16.8 0.7 %collective-permute-start.5 = (bf16[24,512]{1,0:T(8,128)(2,1)S(1)}, bf16[24,512]{1,0:T(8,128)(2,1)S(1)}, u32[]{:S(2)}, u32[]{:S(2)}) collective-permute-start(bf16[24,512]{1,0:T(8,128)(2,1)S(1)} %get-tuple-element.49), channel_id=1, source_target_pairs={{16,0},{18,2},{20,4},{22,6},{24,8},{26,10},{28,12},{30,14},{0,16},... | collective-permute-start | bytes 73736 | tf_op jit(solution)/shard_map/ppermute | solution.py:456
  17.4 1.6 %near_even.1.early = f32[24,2048]{1,0:T(8,128)S(1)} custom-call(f32[24,2048]{1,0:T(8,128)S(1)} %get-tuple-element.41.early, bf16[48,2048]{1,0:T(8,128)(2,1)S(1)} %get-tuple-element.37.target, bf16[24,2816]{1,0:T(8,128)(2,1)S(1)} %collective-permute-done.3.faces_even.faces), custom_call_target="tpu_custom_call" | custom-call | tf_op jit(solution)/shard_map/near_even/pallas_call | solution.py:477
  19.0 0.0 collective-permute-done.4.faces_odd
  19.0 1.3 %collective-permute-done.5.rest_1_ = bf16[24,512]{1,0:T(8,128)(2,1)S(1)} collective-permute-done((bf16[24,512]{1,0:T(8,128)(2,1)S(1)}, bf16[24,512]{1,0:T(8,128)(2,1)S(1)}, u32[]{:S(2)}, u32[]{:S(2)}) %collective-permute-start.5) | collective-permute-done | bytes 24608 | tf_op jit(solution)/shard_map/ppermute | solution.py:456
  20.4 2.9 %near_odd.1 = (f32[17,2048]{1,0:T(8,128)}, f32[1,2176]{1,0:T(1,128)S(1)}) custom-call(f32[24,2048]{1,0:T(8,128)S(1)} %near_even.1.early, bf16[48,2048]{1,0:T(8,128)(2,1)S(1)} %get-tuple-element.37.target, bf16[24,2816]{1,0:T(8,128)(2,1)S(1)} %collective-permute-done.3.faces_even.faces, bf16[24,2560]{1,0:T(8,128)(2,1)S(1)} %collective-permute-done.4.faces_odd, ...), custom_call_target="tpu_custom_call" | custom-call | tf_op jit(solution)/shard_map/near_odd/pallas_call | solution.py:477
  23.3 3.6 %collective-permute-start.6 = (f32[1,2176]{1,0:T(1,128)S(1)}, f32[1,2176]{1,0:T(1,128)S(1)}, u32[]{:S(2)}, u32[]{:S(2)}) collective-permute-start(f32[1,2176]{1,0:T(1,128)S(1)} %get-tuple-element.51.mine), channel_id=1, source_target_pairs={{1,0},{0,1},{3,2},{2,3},{5,4},{4,5},{7,6},{6,7},{9,8},{8,9},{11,10... | collective-permute-start | bytes 26120 | tf_op jit(solution)/shard_map/ppermute | solution.py:456
  26.9 0.8 %collective-permute-done.6.other = f32[1,2176]{1,0:T(1,128)S(1)} collective-permute-done((f32[1,2176]{1,0:T(1,128)S(1)}, f32[1,2176]{1,0:T(1,128)S(1)}, u32[]{:S(2)}, u32[]{:S(2)}) %collective-permute-start.6) | collective-permute-done | bytes 8736 | tf_op jit(solution)/shard_map/ppermute | solution.py:456
  27.8 0.7 %mean.1 = f32[1,2048]{1,0:T(1,128)} custom-call(f32[1,2176]{1,0:T(1,128)S(1)} %get-tuple-element.51.mine, f32[1,2176]{1,0:T(1,128)S(1)} %collective-permute-done.6.other), custom_call_target="tpu_custom_call" | custom-call | tf_op jit(solution)/shard_map/mean/pallas_call | solution.py:477
Async XLA Ops:
  3.7 5.9 %collective-permute-start = (bf16[24,1664]{1,0:T(8,128)(2,1)S(1)}, bf16[24,1664]{1,0:T(8,128)(2,1)S(1)}, u32[]{:S(2)}, u32[]{:S(2)}) collective-permute-start(bf16[24,1664]{1,0:T(8,128)(2,1)S(1)} %get-tuple-element.30), channel_id=1, source_target_pairs={{2,0},{0,2},{6,4},{4,6},{10,8},{8,10},{14,12},{12,14},{18,16},{16,... | collective-permute-start | bytes 239624 | tf_op jit(solution)/shard_map/ppermute | solution.py:456
  5.0 5.3 %collective-permute-start.2 = (bf16[24,1664]{1,0:T(8,128)(2,1)S(1)}, bf16[24,1664]{1,0:T(8,128)(2,1)S(1)}, u32[]{:S(2)}, u32[]{:S(2)}) collective-permute-start(bf16[24,1664]{1,0:T(8,128)(2,1)S(1)} %get-tuple-element.31), channel_id=1, source_target_pairs={{6,0},{4,2},{2,4},{0,6},{14,8},{12,10},{10,12},{8,14},{22,16},{20,... | collective-permute-start | bytes 239624 | tf_op jit(solution)/shard_map/ppermute | solution.py:456
  6.2 3.3 %collective-permute-start.1 = (bf16[24,128]{1,0:T(8,128)(2,1)S(1)}, bf16[24,128]{1,0:T(8,128)(2,1)S(1)}, u32[]{:S(2)}, u32[]{:S(2)}) collective-permute-start(bf16[24,128]{1,0:T(8,128)(2,1)S(1)} %get-tuple-element.29.totals), channel_id=1, source_target_pairs={{4,0},{6,2},{0,4},{2,6},{12,8},{14,10},{8,12},{10,14},{20,16},{22,... | collective-permute-start | bytes 18440 | tf_op jit(solution)/shard_map/ppermute | solution.py:456
  10.8 3.9 %collective-permute-start.3 = (bf16[24,2816]{1,0:T(8,128)(2,1)S(1)}, bf16[24,2816]{1,0:T(8,128)(2,1)S(1)}, u32[]{:S(2)}, u32[]{:S(2)}) collective-permute-start(bf16[24,2816]{1,0:T(8,128)(2,1)S(1)} %get-tuple-element.40), channel_id=1, source_target_pairs={{8,0},{10,2},{12,4},{14,6},{0,8},{2,10},{4,12},{6,14},{24,16},{26,... | collective-permute-start | bytes 405512 | tf_op jit(solution)/shard_map/ppermute | solution.py:456
  13.7 5.3 %collective-permute-start.4 = (bf16[24,2560]{1,0:T(8,128)(2,1)S(1)}, bf16[24,2560]{1,0:T(8,128)(2,1)S(1)}, u32[]{:S(2)}, u32[]{:S(2)}) collective-permute-start(bf16[24,2560]{1,0:T(8,128)(2,1)S(1)} %get-tuple-element.42), channel_id=1, source_target_pairs={{1,0},{0,1},{3,2},{2,3},{5,4},{4,5},{7,6},{6,7},{16,8},{17,9},{18,... | collective-permute-start | bytes 368648 | tf_op jit(solution)/shard_map/ppermute | solution.py:467
  16.8 3.6 %collective-permute-start.5 = (bf16[24,512]{1,0:T(8,128)(2,1)S(1)}, bf16[24,512]{1,0:T(8,128)(2,1)S(1)}, u32[]{:S(2)}, u32[]{:S(2)}) collective-permute-start(bf16[24,512]{1,0:T(8,128)(2,1)S(1)} %get-tuple-element.49), channel_id=1, source_target_pairs={{16,0},{18,2},{20,4},{22,6},{24,8},{26,10},{28,12},{30,14},{0,16},... | collective-permute-start | bytes 73736 | tf_op jit(solution)/shard_map/ppermute | solution.py:456
  23.3 4.4 %collective-permute-start.6 = (f32[1,2176]{1,0:T(1,128)S(1)}, f32[1,2176]{1,0:T(1,128)S(1)}, u32[]{:S(2)}, u32[]{:S(2)}) collective-permute-start(f32[1,2176]{1,0:T(1,128)S(1)} %get-tuple-element.51.mine), channel_id=1, source_target_pairs={{1,0},{0,1},{3,2},{2,3},{5,4},{4,5},{7,6},{6,7},{9,8},{8,9},{11,10... | collective-permute-start | bytes 26120 | tf_op jit(solution)/shard_map/ppermute | solution.py:456

commit v17 on v16

--- a/solution.py
+++ b/solution.py
@@ -366,11 +366,8 @@
     own_groups(near, EARLY, 4, target, source, own)
 
 
-def side_kernel(left, right, early, target, rows, faces_even, near, both, sides_left, sides_right):
+def side_kernel(left, right, early, target, near, sides_left, sides_right):
     pts = early.shape[1] // 8
-    width = rows.shape[1]
-    both[:, lanes(0, width)] = rows[...]
-    both[:, lanes(width, width)] = faces_even[:, lanes(faces_even.shape[1] - width, width)]
     jobs = []
     for step, side, held in ((0, left, sides_left), (1, right, sides_right)):
         for place in range(4):
@@ -400,26 +397,37 @@
         near[:, here] = early[:, here]
 
 
-def even_kernel(early, target, faces, near, sides):
+def even_kernel(early, target, faces, rows, near, both, sides):
     _, box_z = box_place()
     points = early.shape[1]
+    width = rows.shape[1]
+    both[:, lanes(0, width)] = rows[...]
+    both[:, lanes(width, width)] = faces[:, lanes(faces.shape[1] - width, width)]
     step = 1 - lax.rem(box_z, 2)
     other = lanes((1 - step) * (points // 2), points // 2)
     near[:, other] = early[:, other]
     layer_pulls(near, early, step, box_z >= 0, target, faces, sides)
 
 
-def last_kernel(depth, early, target, faces_even, faces_odd, basis, scale, column, columns, spread, same, *rest):
-    held, (potential, sums, near, sides) = rest[:-4], rest[-4:]
+def odd_inside(depth):
+    _, box_z = box_place()
+    step = lax.rem(box_z, 2)
+    return step, (box_z + 2 * step - 1 >= 0) & (box_z + 2 * step - 1 < depth)
+
+
+def odd_kernel(depth, early, target, faces, near, sides):
+    points = early.shape[1]
+    step, inside = odd_inside(depth)
+    other = lanes((1 - step) * (points // 2), points // 2)
+    near[:, other] = early[:, other]
+    layer_pulls(near, early, step, inside, target, faces, sides)
+
+
+def last_kernel(depth, near, faces_even, faces_odd, basis, scale, column, columns, spread, same, *rest):
+    held, (potential, sums) = rest[:-2], rest[-2:]
     fields, points = potential.shape
     pts = points // 8
-    _, box_z = box_place()
-    step = lax.rem(box_z, 2)
-    other = lanes((1 - step) * (points // 2), points // 2)
-    near[:, other] = early[:, other]
-    inside = (box_z + 2 * step - 1 >= 0) & (box_z + 2 * step - 1 < depth)
-    layer_pulls(near, early, step, inside, target, faces_odd, sides)
-
+    _, inside = odd_inside(depth)
     if depth == 4:
         rows, distant = held
         width = rows.shape[1]
@@ -582,33 +590,50 @@
         target,
     )
     faces_odd = swapped_odd(faces_odd)
-    near, both = call(
+    near, = call(
         side_kernel,
         "near_side",
-        [vmem] * 6,
-        [near_shape, both_shape],
+        [vmem] * 4,
+        [near_shape],
         [pltpu.VMEM((4 * pts, FEATURES), half)] * 2,
         left,
         right,
         near,
         target,
+    )
+    near, both = call(
+        even_kernel,
+        "near_even",
+        [vmem] * 4,
+        [near_shape, both_shape],
+        [rows_scratch],
+        near,
+        target,
+        faces_even,
         rows,
-        faces_even,
     )
     if depth == 4:
         held = [rows, swapped(both, "space", lambda i: i ^ (2 * ACROSS))]
     else:
         groups = [[z * ACROSS + x for z in range(depth)] for x in range(ACROSS)]
         held = [lax.all_gather(rows, "space", axis_index_groups=groups)]
-    near, = call(even_kernel, "near_even", [vmem] * 3, [near_shape], [rows_scratch], near, target, faces_even)
+    near, = call(
+        functools.partial(odd_kernel, depth),
+        "near_odd",
+        [vmem] * 3,
+        [near_shape],
+        [rows_scratch],
+        near,
+        target,
+        faces_odd,
+    )
     potential, sums = call(
         functools.partial(last_kernel, depth),
-        "near_odd",
-        [vmem] * (10 + len(held)),
+        "evaluate",
+        [vmem] * (9 + len(held)),
         [((fields, points), full), ((1, points + 128), full)],
-        [pltpu.VMEM((ROWS, points), full), rows_scratch],
+        [],
         near,
-        target,
         faces_even,
         faces_odd,
         basis,

time: 28.6 us -> 28.3 us (0.990)
  the two profiles are of different devices: /device:TPU:17 before, /device:TPU:9 now
where the time goes in v17:
time: 28.3 us; the launch traced here: 28.1 us
  Pallas kernels  15.5 us (55%)
  starting transfers between devices  9.9 us (35%)
  waiting for transfers between devices  2.1 us (7%)
  between operations  0.68 us (2%)
    pallas_call x9, Pallas kernels, call(): pl.pallas_call(kernel, in_specs=in_specs, out_specs=[vmem] * len(outs), o...  15.5 us
    ppermute x6, starting transfers between devices, swapped(): return lax.ppermute(block, axis, [(partner(i), i) for i in range(size)])  7.46 us
    ppermute x1, starting transfers between devices, swapped_odd(): return lax.ppermute(block, ('space', 'sig'), pairs)  2.44 us
    ppermute x6, waiting for transfers between devices, swapped(): return lax.ppermute(block, axis, [(partner(i), i) for i in range(size)])  2.09 us
  transfers between devices with their start and end apart: 7, of which 3 were waited for; matrix products, arithmetic and copies ran while one was open for 0% of the time, Pallas kernels for 35%

profile of v17, /device:TPU:9, one launch (start us, length us, event | category | flops | bytes accessed | tf_op | source)
XLA Modules:
  0.0 28.1 jit_solution(17405752650973744011)
XLA Ops:
  0.6 3.1 %pack.1 = (bf16[24,2048]{1,0:T(8,128)(2,1)S(1)}, bf16[128,2048]{1,0:T(8,128)(2,1)S(1)}, bf16[24,512]{1,0:T(8,128)(2,1)S(1)}, bf16[24,128]{1,0:T(8,128)(2,1)S(1)}...) custom-call(s32[8]{0:T(128)} %count_in.3, f32[3,2048]{1,0:T(4,128)} %positions_in.1, ...), custom_call_target="tpu_custom_call" | custom-call | tf_op jit(solution)/shard_map/pack/pallas_call | solution.py:485
  3.7 1.3 %collective-permute-start = (bf16[24,1664]{1,0:T(8,128)(2,1)S(1)}, bf16[24,1664]{1,0:T(8,128)(2,1)S(1)}, u32[]{:S(2)}, u32[]{:S(2)}) collective-permute-start(bf16[24,1664]{1,0:T(8,128)(2,1)S(1)} %get-tuple-element.30), channel_id=1, source_target_pairs={{2,0},{0,2},{6,4},{4,6},{10,8},{8,10},{14,12},{12,14},{18,16},{16,... | collective-permute-start | bytes 239624 | tf_op jit(solution)/shard_map/ppermute | solution.py:464
  5.0 1.2 %collective-permute-start.2 = (bf16[24,1664]{1,0:T(8,128)(2,1)S(1)}, bf16[24,1664]{1,0:T(8,128)(2,1)S(1)}, u32[]{:S(2)}, u32[]{:S(2)}) collective-permute-start(bf16[24,1664]{1,0:T(8,128)(2,1)S(1)} %get-tuple-element.31), channel_id=1, source_target_pairs={{6,0},{4,2},{2,4},{0,6},{14,8},{12,10},{10,12},{8,14},{22,16},{20,... | collective-permute-start | bytes 239624 | tf_op jit(solution)/shard_map/ppermute | solution.py:464
  6.2 0.2 collective-permute-start.1
  6.4 3.1 %near_own.1 = (f32[24,1536]{1,0:T(8,128)S(1)}, bf16[2048,48]{1,0:T(8,128)(2,1)S(1)}, bf16[48,2048]{1,0:T(8,128)(2,1)S(1)}, f32[1,2048]{1,0:T(1,128)S(1)}, f32[24...) custom-call(s32[8]{0:T(128)} %count_in.3, ...), custom_call_target="tpu_custom_call" | custom-call | tf_op jit(solution)/shard_map/near_own/pallas_call | solution.py:485
  9.6 0.0 collective-permute-done.1.from_2
  9.6 0.0 collective-permute-done.from_1
  9.6 0.7 %collective-permute-done.2.from_3 = bf16[24,1664]{1,0:T(8,128)(2,1)S(1)} collective-permute-done((bf16[24,1664]{1,0:T(8,128)(2,1)S(1)}, bf16[24,1664]{1,0:T(8,128)(2,1)S(1)}, u32[]{:S(2)}, u32[]{:S(2)}) %collective-permute-start.2) | collective-permute-done | bytes 79904 | tf_op jit(solution)/shard_map/ppermute | solution.py:464
  10.3 0.5 %row.1 = (bf16[24,1536]{1,0:T(8,128)(2,1)S(1)}, bf16[24,1536]{1,0:T(8,128)(2,1)S(1)}, bf16[24,2816]{1,0:T(8,128)(2,1)S(1)}, bf16[24,256]{1,0:T(8,128)(2,1)S(1)}) custom-call(bf16[24,2048]{1,0:T(8,128)(2,1)S(1)} %get-tuple-element.27.own, bf16[24,512]{1,0:T(8,128)(2,1)S(1)} %get-tuple-element.28.moments, bf16[24,128]{1,0:T(8,128)(2,1)S(1)} %get-tuple-element.29.totals, ...), custom_call_target="tpu_custom_call" | custom-call | tf_op jit(solution)/shard_map/row/pallas_call | solution.py:485
  10.8 0.2 collective-permute-start.3
  11.1 1.5 %near_middle.1 = (f32[24,2048]{1,0:T(8,128)S(1)}, bf16[24,2560]{1,0:T(8,128)(2,1)S(1)}, f32[24,512]{1,0:T(8,128)S(1)}) custom-call(bf16[24,2048]{1,0:T(8,128)(2,1)S(1)} %get-tuple-element.27.own, bf16[24,1536]{1,0:T(8,128)(2,1)S(1)} %get-tuple-element.33.left, bf16[24,1536]{1,0:T(8,128)(2,1)S(1)} %get-tuple-element.34.right, ...), custom_call_target="tpu_custom_call" | custom-call | tf_op jit(solution)/shard_map/near_middle/pallas_call | solution.py:485
  12.6 2.4 %collective-permute-start.4 = (bf16[24,2560]{1,0:T(8,128)(2,1)S(1)}, bf16[24,2560]{1,0:T(8,128)(2,1)S(1)}, u32[]{:S(2)}, u32[]{:S(2)}) collective-permute-start(bf16[24,2560]{1,0:T(8,128)(2,1)S(1)} %get-tuple-element.42), channel_id=1, source_target_pairs={{1,0},{0,1},{3,2},{2,3},{5,4},{4,5},{7,6},{6,7},{16,8},{17,9},{18,... | collective-permute-start | bytes 368648 | tf_op jit(solution)/shard_map/ppermute | solution.py:475
  15.0 2.0 %near_side.1.early = f32[24,2048]{1,0:T(8,128)S(1)} custom-call(bf16[24,1536]{1,0:T(8,128)(2,1)S(1)} %get-tuple-element.33.left, bf16[24,1536]{1,0:T(8,128)(2,1)S(1)} %get-tuple-element.34.right, f32[24,2048]{1,0:T(8,128)S(1)} %get-tuple-element.38.early, bf16[48,2048]{1,0:T(8,128)(2,1)S(1)} %get-tuple-element.37.target), custom_call_target="tpu_custom_call" | custom-call | tf_op jit(solution)/shard_map/near_side/pallas_call | solution.py:485
  17.1 0.0 collective-permute-done.3.faces.faces_even
  17.1 1.6 %near_even.1 = (f32[24,2048]{1,0:T(8,128)S(1)}, bf16[24,512]{1,0:T(8,128)(2,1)S(1)}) custom-call(f32[24,2048]{1,0:T(8,128)S(1)} %near_side.1.early, bf16[48,2048]{1,0:T(8,128)(2,1)S(1)} %get-tuple-element.37.target, bf16[24,2816]{1,0:T(8,128)(2,1)S(1)} %collective-permute-done.3.faces.faces_even, bf16[24,256]{1,0:T(8,128)(2,1)S(1)} %get-tuple-element.40.rows.rest_0_), custom_call_target="tpu_custom_call" | custom-call | tf_op jit(solution)/shard_map/near_even/pallas_call | solution.py:485
  18.7 1.5 %collective-permute-start.5 = (bf16[24,512]{1,0:T(8,128)(2,1)S(1)}, bf16[24,512]{1,0:T(8,128)(2,1)S(1)}, u32[]{:S(2)}, u32[]{:S(2)}) collective-permute-start(bf16[24,512]{1,0:T(8,128)(2,1)S(1)} %get-tuple-element.49), channel_id=1, source_target_pairs={{16,0},{18,2},{20,4},{22,6},{24,8},{26,10},{28,12},{30,14},{0,16},... | collective-permute-start | bytes 73736 | tf_op jit(solution)/shard_map/ppermute | solution.py:464
  20.2 0.0 collective-permute-done.4.faces.faces_odd
  20.2 1.6 %near_odd.1.near = f32[24,2048]{1,0:T(8,128)S(1)} custom-call(f32[24,2048]{1,0:T(8,128)S(1)} %get-tuple-element.41.early, bf16[48,2048]{1,0:T(8,128)(2,1)S(1)} %get-tuple-element.37.target, bf16[24,2560]{1,0:T(8,128)(2,1)S(1)} %collective-permute-done.4.faces.faces_odd), custom_call_target="tpu_custom_call" | custom-call | tf_op jit(solution)/shard_map/near_odd/pallas_call | solution.py:485
  21.8 0.5 %collective-permute-done.5.rest_1_ = bf16[24,512]{1,0:T(8,128)(2,1)S(1)} collective-permute-done((bf16[24,512]{1,0:T(8,128)(2,1)S(1)}, bf16[24,512]{1,0:T(8,128)(2,1)S(1)}, u32[]{:S(2)}, u32[]{:S(2)}) %collective-permute-start.5) | collective-permute-done | bytes 24608 | tf_op jit(solution)/shard_map/ppermute | solution.py:464
  22.3 1.3 %evaluate.1 = (f32[17,2048]{1,0:T(8,128)}, f32[1,2176]{1,0:T(1,128)S(1)}) custom-call(f32[24,2048]{1,0:T(8,128)S(1)} %near_odd.1.near, bf16[24,2816]{1,0:T(8,128)(2,1)S(1)} %collective-permute-done.3.faces.faces_even, bf16[24,2560]{1,0:T(8,128)(2,1)S(1)} %collective-permute-done.4.faces.faces_odd, bf16[128,2048]{1,0:T(8,128)(2,1)S(1)} %get-tuple-element.43.basis, ...), custom_call_target="tpu_custom_call" | custom-call | tf_op jit(solution)/shard_map/evaluate/pallas_call | solution.py:485
  23.6 3.0 %collective-permute-start.6 = (f32[1,2176]{1,0:T(1,128)S(1)}, f32[1,2176]{1,0:T(1,128)S(1)}, u32[]{:S(2)}, u32[]{:S(2)}) collective-permute-start(f32[1,2176]{1,0:T(1,128)S(1)} %get-tuple-element.51.mine), channel_id=1, source_target_pairs={{1,0},{0,1},{3,2},{2,3},{5,4},{4,5},{7,6},{6,7},{9,8},{8,9},{11,10... | collective-permute-start | bytes 26120 | tf_op jit(solution)/shard_map/ppermute | solution.py:464
  26.6 0.8 %collective-permute-done.6.other = f32[1,2176]{1,0:T(1,128)S(1)} collective-permute-done((f32[1,2176]{1,0:T(1,128)S(1)}, f32[1,2176]{1,0:T(1,128)S(1)}, u32[]{:S(2)}, u32[]{:S(2)}) %collective-permute-start.6) | collective-permute-done | bytes 8736 | tf_op jit(solution)/shard_map/ppermute | solution.py:464
  27.5 0.7 %mean.1 = f32[1,2048]{1,0:T(1,128)} custom-call(f32[1,2176]{1,0:T(1,128)S(1)} %get-tuple-element.51.mine, f32[1,2176]{1,0:T(1,128)S(1)} %collective-permute-done.6.other), custom_call_target="tpu_custom_call" | custom-call | tf_op jit(solution)/shard_map/mean/pallas_call | solution.py:485
Async XLA Ops:
  3.7 5.9 %collective-permute-start = (bf16[24,1664]{1,0:T(8,128)(2,1)S(1)}, bf16[24,1664]{1,0:T(8,128)(2,1)S(1)}, u32[]{:S(2)}, u32[]{:S(2)}) collective-permute-start(bf16[24,1664]{1,0:T(8,128)(2,1)S(1)} %get-tuple-element.30), channel_id=1, source_target_pairs={{2,0},{0,2},{6,4},{4,6},{10,8},{8,10},{14,12},{12,14},{18,16},{16,... | collective-permute-start | bytes 239624 | tf_op jit(solution)/shard_map/ppermute | solution.py:464
  5.0 5.3 %collective-permute-start.2 = (bf16[24,1664]{1,0:T(8,128)(2,1)S(1)}, bf16[24,1664]{1,0:T(8,128)(2,1)S(1)}, u32[]{:S(2)}, u32[]{:S(2)}) collective-permute-start(bf16[24,1664]{1,0:T(8,128)(2,1)S(1)} %get-tuple-element.31), channel_id=1, source_target_pairs={{6,0},{4,2},{2,4},{0,6},{14,8},{12,10},{10,12},{8,14},{22,16},{20,... | collective-permute-start | bytes 239624 | tf_op jit(solution)/shard_map/ppermute | solution.py:464
  6.2 3.3 %collective-permute-start.1 = (bf16[24,128]{1,0:T(8,128)(2,1)S(1)}, bf16[24,128]{1,0:T(8,128)(2,1)S(1)}, u32[]{:S(2)}, u32[]{:S(2)}) collective-permute-start(bf16[24,128]{1,0:T(8,128)(2,1)S(1)} %get-tuple-element.29.totals), channel_id=1, source_target_pairs={{4,0},{6,2},{0,4},{2,6},{12,8},{14,10},{8,12},{10,14},{20,16},{22,... | collective-permute-start | bytes 18440 | tf_op jit(solution)/shard_map/ppermute | solution.py:464
  10.8 6.2 %collective-permute-start.3 = (bf16[24,2816]{1,0:T(8,128)(2,1)S(1)}, bf16[24,2816]{1,0:T(8,128)(2,1)S(1)}, u32[]{:S(2)}, u32[]{:S(2)}) collective-permute-start(bf16[24,2816]{1,0:T(8,128)(2,1)S(1)} %get-tuple-element.39), channel_id=1, source_target_pairs={{8,0},{10,2},{12,4},{14,6},{0,8},{2,10},{4,12},{6,14},{24,16},{26,... | collective-permute-start | bytes 405512 | tf_op jit(solution)/shard_map/ppermute | solution.py:464
  12.6 7.6 %collective-permute-start.4 = (bf16[24,2560]{1,0:T(8,128)(2,1)S(1)}, bf16[24,2560]{1,0:T(8,128)(2,1)S(1)}, u32[]{:S(2)}, u32[]{:S(2)}) collective-permute-start(bf16[24,2560]{1,0:T(8,128)(2,1)S(1)} %get-tuple-element.42), channel_id=1, source_target_pairs={{1,0},{0,1},{3,2},{2,3},{5,4},{4,5},{7,6},{6,7},{16,8},{17,9},{18,... | collective-permute-start | bytes 368648 | tf_op jit(solution)/shard_map/ppermute | solution.py:475
  18.7 3.6 %collective-permute-start.5 = (bf16[24,512]{1,0:T(8,128)(2,1)S(1)}, bf16[24,512]{1,0:T(8,128)(2,1)S(1)}, u32[]{:S(2)}, u32[]{:S(2)}) collective-permute-start(bf16[24,512]{1,0:T(8,128)(2,1)S(1)} %get-tuple-element.49), channel_id=1, source_target_pairs={{16,0},{18,2},{20,4},{22,6},{24,8},{26,10},{28,12},{30,14},{0,16},... | collective-permute-start | bytes 73736 | tf_op jit(solution)/shard_map/ppermute | solution.py:464
  23.6 3.8 %collective-permute-start.6 = (f32[1,2176]{1,0:T(1,128)S(1)}, f32[1,2176]{1,0:T(1,128)S(1)}, u32[]{:S(2)}, u32[]{:S(2)}) collective-permute-start(f32[1,2176]{1,0:T(1,128)S(1)} %get-tuple-element.51.mine), channel_id=1, source_target_pairs={{1,0},{0,1},{3,2},{2,3},{5,4},{4,5},{7,6},{6,7},{9,8},{8,9},{11,10... | collective-permute-start | bytes 26120 | tf_op jit(solution)/shard_map/ppermute | solution.py:464

commit v18 on v17

--- a/solution.py
+++ b/solution.py
@@ -590,6 +590,22 @@
         target,
     )
     faces_odd = swapped_odd(faces_odd)
+    near, both = call(
+        even_kernel,
+        "near_even",
+        [vmem] * 4,
+        [near_shape, both_shape],
+        [rows_scratch],
+        near,
+        target,
+        faces_even,
+        rows,
+    )
+    if depth == 4:
+        held = [rows, swapped(both, "space", lambda i: i ^ (2 * ACROSS))]
+    else:
+        groups = [[z * ACROSS + x for z in range(depth)] for x in range(ACROSS)]
+        held = [lax.all_gather(rows, "space", axis_index_groups=groups)]
     near, = call(
         side_kernel,
         "near_side",
@@ -601,22 +617,6 @@
         near,
         target,
     )
-    near, both = call(
-        even_kernel,
-        "near_even",
-        [vmem] * 4,
-        [near_shape, both_shape],
-        [rows_scratch],
-        near,
-        target,
-        faces_even,
-        rows,
-    )
-    if depth == 4:
-        held = [rows, swapped(both, "space", lambda i: i ^ (2 * ACROSS))]
-    else:
-        groups = [[z * ACROSS + x for z in range(depth)] for x in range(ACROSS)]
-        held = [lax.all_gather(rows, "space", axis_index_groups=groups)]
     near, = call(
         functools.partial(odd_kernel, depth),
         "near_odd",

time: 28.3 us -> 28.1 us (level)
  waiting for transfers between devices: 2.1 us -> 1.59 us
  starting transfers between devices: 9.9 us -> 10.2 us
    ppermute x6, waiting for transfers between devices: 2.09 us -> 1.58 us  [swapped(): return lax.ppermute(block, axis, [(partner(i), i) for i in range(size)])]
    ppermute x6, starting transfers between devices: 7.46 us -> 7.74 us  [swapped(): return lax.ppermute(block, axis, [(partner(i), i) for i in range(size)])]
  transfers between devices with their start and end apart: 7 -> 7, of which waited for: 3 -> 2; matrix products, arithmetic and copies ran while one was open for 0% -> 0% of each run, Pallas kernels for 35% -> 35%
where the time goes in v18:
time: 28.1 us; the launch traced here: 27.9 us
  Pallas kernels  15.5 us (55%)
  starting transfers between devices  10.2 us (36%)
  waiting for transfers between devices  1.59 us (6%)
  between operations  0.69 us (2%)
    pallas_call x9, Pallas kernels, call(): pl.pallas_call(kernel, in_specs=in_specs, out_specs=[vmem] * len(outs), o...  15.5 us
    ppermute x6, starting transfers between devices, swapped(): return lax.ppermute(block, axis, [(partner(i), i) for i in range(size)])  7.74 us
    ppermute x1, starting transfers between devices, swapped_odd(): return lax.ppermute(block, ('space', 'sig'), pairs)  2.44 us
    ppermute x6, waiting for transfers between devices, swapped(): return lax.ppermute(block, axis, [(partner(i), i) for i in range(size)])  1.58 us
  transfers between devices with their start and end apart: 7, of which 2 were waited for; matrix products, arithmetic and copies ran while one was open for 0% of the time, Pallas kernels for 35%

profile of v18, /device:TPU:9, one launch (start us, length us, event | category | flops | bytes accessed | tf_op | source)
XLA Modules:
  0.0 27.9 jit_solution(16515896291411752213)
XLA Ops:
  0.6 3.1 %pack.1 = (bf16[24,2048]{1,0:T(8,128)(2,1)S(1)}, bf16[128,2048]{1,0:T(8,128)(2,1)S(1)}, bf16[24,512]{1,0:T(8,128)(2,1)S(1)}, bf16[24,128]{1,0:T(8,128)(2,1)S(1)}...) custom-call(s32[8]{0:T(128)} %count_in.3, f32[3,2048]{1,0:T(4,128)} %positions_in.1, ...), custom_call_target="tpu_custom_call" | custom-call | tf_op jit(solution)/shard_map/pack/pallas_call | solution.py:485
  3.7 1.3 %collective-permute-start = (bf16[24,1664]{1,0:T(8,128)(2,1)S(1)}, bf16[24,1664]{1,0:T(8,128)(2,1)S(1)}, u32[]{:S(2)}, u32[]{:S(2)}) collective-permute-start(bf16[24,1664]{1,0:T(8,128)(2,1)S(1)} %get-tuple-element.30), channel_id=1, source_target_pairs={{2,0},{0,2},{6,4},{4,6},{10,8},{8,10},{14,12},{12,14},{18,16},{16,... | collective-permute-start | bytes 239624 | tf_op jit(solution)/shard_map/ppermute | solution.py:464
  5.0 1.2 %collective-permute-start.2 = (bf16[24,1664]{1,0:T(8,128)(2,1)S(1)}, bf16[24,1664]{1,0:T(8,128)(2,1)S(1)}, u32[]{:S(2)}, u32[]{:S(2)}) collective-permute-start(bf16[24,1664]{1,0:T(8,128)(2,1)S(1)} %get-tuple-element.31), channel_id=1, source_target_pairs={{6,0},{4,2},{2,4},{0,6},{14,8},{12,10},{10,12},{8,14},{22,16},{20,... | collective-permute-start | bytes 239624 | tf_op jit(solution)/shard_map/ppermute | solution.py:464
  6.2 0.2 collective-permute-start.1
  6.4 3.1 %near_own.1 = (f32[24,1536]{1,0:T(8,128)S(1)}, bf16[2048,48]{1,0:T(8,128)(2,1)S(1)}, bf16[48,2048]{1,0:T(8,128)(2,1)S(1)}, f32[1,2048]{1,0:T(1,128)S(1)}, f32[24...) custom-call(s32[8]{0:T(128)} %count_in.3, ...), custom_call_target="tpu_custom_call" | custom-call | tf_op jit(solution)/shard_map/near_own/pallas_call | solution.py:485
  9.6 0.0 collective-permute-done.1.from_2
  9.6 0.0 collective-permute-done.from_1
  9.6 0.7 %collective-permute-done.2.from_3 = bf16[24,1664]{1,0:T(8,128)(2,1)S(1)} collective-permute-done((bf16[24,1664]{1,0:T(8,128)(2,1)S(1)}, bf16[24,1664]{1,0:T(8,128)(2,1)S(1)}, u32[]{:S(2)}, u32[]{:S(2)}) %collective-permute-start.2) | collective-permute-done | bytes 79904 | tf_op jit(solution)/shard_map/ppermute | solution.py:464
  10.3 0.5 %row.1 = (bf16[24,1536]{1,0:T(8,128)(2,1)S(1)}, bf16[24,1536]{1,0:T(8,128)(2,1)S(1)}, bf16[24,2816]{1,0:T(8,128)(2,1)S(1)}, bf16[24,256]{1,0:T(8,128)(2,1)S(1)}) custom-call(bf16[24,2048]{1,0:T(8,128)(2,1)S(1)} %get-tuple-element.27.own, bf16[24,512]{1,0:T(8,128)(2,1)S(1)} %get-tuple-element.28.moments, bf16[24,128]{1,0:T(8,128)(2,1)S(1)} %get-tuple-element.29.totals, ...), custom_call_target="tpu_custom_call" | custom-call | tf_op jit(solution)/shard_map/row/pallas_call | solution.py:485
  10.8 0.2 collective-permute-start.3
  11.1 1.5 %near_middle.1 = (f32[24,2048]{1,0:T(8,128)S(1)}, bf16[24,2560]{1,0:T(8,128)(2,1)S(1)}, f32[24,512]{1,0:T(8,128)S(1)}) custom-call(bf16[24,2048]{1,0:T(8,128)(2,1)S(1)} %get-tuple-element.27.own, bf16[24,1536]{1,0:T(8,128)(2,1)S(1)} %get-tuple-element.33.left, bf16[24,1536]{1,0:T(8,128)(2,1)S(1)} %get-tuple-element.34.right, ...), custom_call_target="tpu_custom_call" | custom-call | tf_op jit(solution)/shard_map/near_middle/pallas_call | solution.py:485
  12.6 2.4 %collective-permute-start.4 = (bf16[24,2560]{1,0:T(8,128)(2,1)S(1)}, bf16[24,2560]{1,0:T(8,128)(2,1)S(1)}, u32[]{:S(2)}, u32[]{:S(2)}) collective-permute-start(bf16[24,2560]{1,0:T(8,128)(2,1)S(1)} %get-tuple-element.42), channel_id=1, source_target_pairs={{1,0},{0,1},{3,2},{2,3},{5,4},{4,5},{7,6},{6,7},{16,8},{17,9},{18,... | collective-permute-start | bytes 368648 | tf_op jit(solution)/shard_map/ppermute | solution.py:475
  15.0 0.0 collective-permute-done.3.faces.faces_even
  15.0 1.6 %near_even.1 = (f32[24,2048]{1,0:T(8,128)S(1)}, bf16[24,512]{1,0:T(8,128)(2,1)S(1)}) custom-call(f32[24,2048]{1,0:T(8,128)S(1)} %get-tuple-element.38.early, bf16[48,2048]{1,0:T(8,128)(2,1)S(1)} %get-tuple-element.37.target, bf16[24,2816]{1,0:T(8,128)(2,1)S(1)} %collective-permute-done.3.faces.faces_even, bf16[24,256]{1,0:T(8,128)(2,1)S(1)} %get-tuple-element.40.rows.rest_0_), custom_call_target="tpu_custom_call" | custom-call | tf_op jit(solution)/shard_map/near_even/pallas_call | solution.py:485
  16.6 2.0 %collective-permute-start.5 = (bf16[24,512]{1,0:T(8,128)(2,1)S(1)}, bf16[24,512]{1,0:T(8,128)(2,1)S(1)}, u32[]{:S(2)}, u32[]{:S(2)}) collective-permute-start(bf16[24,512]{1,0:T(8,128)(2,1)S(1)} %get-tuple-element.49), channel_id=1, source_target_pairs={{16,0},{18,2},{20,4},{22,6},{24,8},{26,10},{28,12},{30,14},{0,16},... | collective-permute-start | bytes 73736 | tf_op jit(solution)/shard_map/ppermute | solution.py:464
  18.7 2.0 %near_side.1.early = f32[24,2048]{1,0:T(8,128)S(1)} custom-call(bf16[24,1536]{1,0:T(8,128)(2,1)S(1)} %get-tuple-element.33.left, bf16[24,1536]{1,0:T(8,128)(2,1)S(1)} %get-tuple-element.34.right, f32[24,2048]{1,0:T(8,128)S(1)} %get-tuple-element.41.early, bf16[48,2048]{1,0:T(8,128)(2,1)S(1)} %get-tuple-element.37.target), custom_call_target="tpu_custom_call" | custom-call | tf_op jit(solution)/shard_map/near_side/pallas_call | solution.py:485
  20.7 0.0 collective-permute-done.4.faces.faces_odd
  20.7 1.6 %near_odd.1.near = f32[24,2048]{1,0:T(8,128)S(1)} custom-call(f32[24,2048]{1,0:T(8,128)S(1)} %near_side.1.early, bf16[48,2048]{1,0:T(8,128)(2,1)S(1)} %get-tuple-element.37.target, bf16[24,2560]{1,0:T(8,128)(2,1)S(1)} %collective-permute-done.4.faces.faces_odd), custom_call_target="tpu_custom_call" | custom-call | tf_op jit(solution)/shard_map/near_odd/pallas_call | solution.py:485
  22.3 0.0 collective-permute-done.5.rest_1_
  22.3 1.3 %evaluate.1 = (f32[17,2048]{1,0:T(8,128)}, f32[1,2176]{1,0:T(1,128)S(1)}) custom-call(f32[24,2048]{1,0:T(8,128)S(1)} %near_odd.1.near, bf16[24,2816]{1,0:T(8,128)(2,1)S(1)} %collective-permute-done.3.faces.faces_even, bf16[24,2560]{1,0:T(8,128)(2,1)S(1)} %collective-permute-done.4.faces.faces_odd, bf16[128,2048]{1,0:T(8,128)(2,1)S(1)} %get-tuple-element.43.basis, ...), custom_call_target="tpu_custom_call" | custom-call | tf_op jit(solution)/shard_map/evaluate/pallas_call | solution.py:485
  23.7 2.7 %collective-permute-start.6 = (f32[1,2176]{1,0:T(1,128)S(1)}, f32[1,2176]{1,0:T(1,128)S(1)}, u32[]{:S(2)}, u32[]{:S(2)}) collective-permute-start(f32[1,2176]{1,0:T(1,128)S(1)} %get-tuple-element.51.mine), channel_id=1, source_target_pairs={{1,0},{0,1},{3,2},{2,3},{5,4},{4,5},{7,6},{6,7},{9,8},{8,9},{11,10... | collective-permute-start | bytes 26120 | tf_op jit(solution)/shard_map/ppermute | solution.py:464
  26.4 0.8 %collective-permute-done.6.other = f32[1,2176]{1,0:T(1,128)S(1)} collective-permute-done((f32[1,2176]{1,0:T(1,128)S(1)}, f32[1,2176]{1,0:T(1,128)S(1)}, u32[]{:S(2)}, u32[]{:S(2)}) %collective-permute-start.6) | collective-permute-done | bytes 8736 | tf_op jit(solution)/shard_map/ppermute | solution.py:464
  27.3 0.7 %mean.1 = f32[1,2048]{1,0:T(1,128)} custom-call(f32[1,2176]{1,0:T(1,128)S(1)} %get-tuple-element.51.mine, f32[1,2176]{1,0:T(1,128)S(1)} %collective-permute-done.6.other), custom_call_target="tpu_custom_call" | custom-call | tf_op jit(solution)/shard_map/mean/pallas_call | solution.py:485
Async XLA Ops:
  3.7 5.9 %collective-permute-start = (bf16[24,1664]{1,0:T(8,128)(2,1)S(1)}, bf16[24,1664]{1,0:T(8,128)(2,1)S(1)}, u32[]{:S(2)}, u32[]{:S(2)}) collective-permute-start(bf16[24,1664]{1,0:T(8,128)(2,1)S(1)} %get-tuple-element.30), channel_id=1, source_target_pairs={{2,0},{0,2},{6,4},{4,6},{10,8},{8,10},{14,12},{12,14},{18,16},{16,... | collective-permute-start | bytes 239624 | tf_op jit(solution)/shard_map/ppermute | solution.py:464
  5.0 5.3 %collective-permute-start.2 = (bf16[24,1664]{1,0:T(8,128)(2,1)S(1)}, bf16[24,1664]{1,0:T(8,128)(2,1)S(1)}, u32[]{:S(2)}, u32[]{:S(2)}) collective-permute-start(bf16[24,1664]{1,0:T(8,128)(2,1)S(1)} %get-tuple-element.31), channel_id=1, source_target_pairs={{6,0},{4,2},{2,4},{0,6},{14,8},{12,10},{10,12},{8,14},{22,16},{20,... | collective-permute-start | bytes 239624 | tf_op jit(solution)/shard_map/ppermute | solution.py:464
  6.2 3.3 %collective-permute-start.1 = (bf16[24,128]{1,0:T(8,128)(2,1)S(1)}, bf16[24,128]{1,0:T(8,128)(2,1)S(1)}, u32[]{:S(2)}, u32[]{:S(2)}) collective-permute-start(bf16[24,128]{1,0:T(8,128)(2,1)S(1)} %get-tuple-element.29.totals), channel_id=1, source_target_pairs={{4,0},{6,2},{0,4},{2,6},{12,8},{14,10},{8,12},{10,14},{20,16},{22,... | collective-permute-start | bytes 18440 | tf_op jit(solution)/shard_map/ppermute | solution.py:464
  10.8 4.2 %collective-permute-start.3 = (bf16[24,2816]{1,0:T(8,128)(2,1)S(1)}, bf16[24,2816]{1,0:T(8,128)(2,1)S(1)}, u32[]{:S(2)}, u32[]{:S(2)}) collective-permute-start(bf16[24,2816]{1,0:T(8,128)(2,1)S(1)} %get-tuple-element.39), channel_id=1, source_target_pairs={{8,0},{10,2},{12,4},{14,6},{0,8},{2,10},{4,12},{6,14},{24,16},{26,... | collective-permute-start | bytes 405512 | tf_op jit(solution)/shard_map/ppermute | solution.py:464
  12.6 8.1 %collective-permute-start.4 = (bf16[24,2560]{1,0:T(8,128)(2,1)S(1)}, bf16[24,2560]{1,0:T(8,128)(2,1)S(1)}, u32[]{:S(2)}, u32[]{:S(2)}) collective-permute-start(bf16[24,2560]{1,0:T(8,128)(2,1)S(1)} %get-tuple-element.42), channel_id=1, source_target_pairs={{1,0},{0,1},{3,2},{2,3},{5,4},{4,5},{7,6},{6,7},{16,8},{17,9},{18,... | collective-permute-start | bytes 368648 | tf_op jit(solution)/shard_map/ppermute | solution.py:475
  16.6 5.7 %collective-permute-start.5 = (bf16[24,512]{1,0:T(8,128)(2,1)S(1)}, bf16[24,512]{1,0:T(8,128)(2,1)S(1)}, u32[]{:S(2)}, u32[]{:S(2)}) collective-permute-start(bf16[24,512]{1,0:T(8,128)(2,1)S(1)} %get-tuple-element.49), channel_id=1, source_target_pairs={{16,0},{18,2},{20,4},{22,6},{24,8},{26,10},{28,12},{30,14},{0,16},... | collective-permute-start | bytes 73736 | tf_op jit(solution)/shard_map/ppermute | solution.py:464
  23.7 3.6 %collective-permute-start.6 = (f32[1,2176]{1,0:T(1,128)S(1)}, f32[1,2176]{1,0:T(1,128)S(1)}, u32[]{:S(2)}, u32[]{:S(2)}) collective-permute-start(f32[1,2176]{1,0:T(1,128)S(1)} %get-tuple-element.51.mine), channel_id=1, source_target_pairs={{1,0},{0,1},{3,2},{2,3},{5,4},{4,5},{7,6},{6,7},{9,8},{8,9},{11,10... | collective-permute-start | bytes 26120 | tf_op jit(solution)/shard_map/ppermute | solution.py:464

commit v19 on v17

--- a/solution.py
+++ b/solution.py
@@ -354,7 +354,18 @@
     faces_of(faces_even, above, sums_for(above, left, moments, right, far), own, left, right, row)
 
 
-def middle_kernel(own, left, right, moments, far, early, source, target, near, faces_odd, same):
+def side_pulls(near, left, right, early, target, sides_left, sides_right):
+    pts = early.shape[1] // 8
+    jobs = []
+    for step, side, held in ((0, left, sides_left), (1, right, sides_right)):
+        for place in range(4):
+            centre = (1.5 if step else -1.5, place % 2 - 0.5, place // 2 - 0.5)
+            held[lanes(place * pts, pts), :] = source_features(side, place * pts, pts, centre)
+        jobs += [(step, held, side, [0, 2 * pts]), (step + 2, held, side, [0, 2 * pts])]
+    pulled(near, jobs, target, 2 * pts, early)
+
+
+def middle_kernel(own, left, right, moments, far, early, source, target, near, faces_odd, same, *sides):
     points = own.shape[1]
     _, box_z = box_place()
     above = lax.rem(box_z, 2)
@@ -365,16 +376,28 @@
     near[:, lanes(0, EARLY * points // 4)] = early[...]
     own_groups(near, EARLY, 4, target, source, own)
 
-
-def side_kernel(left, right, early, target, near, sides_left, sides_right):
-    pts = early.shape[1] // 8
-    jobs = []
-    for step, side, held in ((0, left, sides_left), (1, right, sides_right)):
-        for place in range(4):
-            centre = (1.5 if step else -1.5, place % 2 - 0.5, place // 2 - 0.5)
-            held[lanes(place * pts, pts), :] = source_features(side, place * pts, pts, centre)
-        jobs += [(step, held, side, [0, 2 * pts]), (step + 2, held, side, [0, 2 * pts])]
-    pulled(near, jobs, target, 2 * pts, early)
+    @pl.when(above == 1)
+    def _():
+        side_pulls(near, left, right, near, target, *sides)
+
+
+def side_kernel(left, right, early, target, near, *sides):
+    _, box_z = box_place()
+    odd = lax.rem(box_z, 2) == 1
+
+    @pl.when(odd)
+    def _():
+        near[...] = early[...]
+
+    @pl.when(jnp.logical_not(odd))
+    def _():
+        side_pulls(near, left, right, early, target, *sides)
+
+
+def both_kernel(rows, faces, both):
+    width = rows.shape[1]
+    both[:, lanes(0, width)] = rows[...]
+    both[:, lanes(width, width)] = faces[:, lanes(faces.shape[1] - width, width)]
 
 
 def layer_pulls(near, early, step, inside, target, faces, sides):
@@ -397,12 +420,9 @@
         near[:, here] = early[:, here]
 
 
-def even_kernel(early, target, faces, rows, near, both, sides):
+def even_kernel(early, target, faces, near, sides):
     _, box_z = box_place()
     points = early.shape[1]
-    width = rows.shape[1]
-    both[:, lanes(0, width)] = rows[...]
-    both[:, lanes(width, width)] = faces[:, lanes(faces.shape[1] - width, width)]
     step = 1 - lax.rem(box_z, 2)
     other = lanes((1 - step) * (points // 2), points // 2)
     near[:, other] = early[:, other]
@@ -501,6 +521,7 @@
     rows_shape = ((ROWS, SLOT * ACROSS), half)
     both_shape = ((ROWS, 2 * SLOT * ACROSS), half)
     near_shape, sums_shape = ((ROWS, points), full), ((ROWS, LEAVES), full)
+    side_scratch = [pltpu.VMEM((4 * pts, FEATURES), half)] * 2
     rows_scratch = pltpu.VMEM((8 * pts, FEATURES), half)
     own, basis, moments, totals, *given = call(
         pack_kernel,
@@ -579,7 +600,7 @@
         "near_middle",
         [vmem] * 8,
         [near_shape, faces_shape, sums_shape],
-        [],
+        side_scratch,
         own,
         left,
         right,
@@ -595,28 +616,19 @@
         "near_side",
         [vmem] * 4,
         [near_shape],
-        [pltpu.VMEM((4 * pts, FEATURES), half)] * 2,
+        side_scratch,
         left,
         right,
         near,
         target,
     )
-    near, both = call(
-        even_kernel,
-        "near_even",
-        [vmem] * 4,
-        [near_shape, both_shape],
-        [rows_scratch],
-        near,
-        target,
-        faces_even,
-        rows,
-    )
     if depth == 4:
+        both, = call(both_kernel, "row_pairs", [vmem] * 2, [both_shape], [], rows, faces_even)
         held = [rows, swapped(both, "space", lambda i: i ^ (2 * ACROSS))]
     else:
         groups = [[z * ACROSS + x for z in range(depth)] for x in range(ACROSS)]
         held = [lax.all_gather(rows, "space", axis_index_groups=groups)]
+    near, = call(even_kernel, "near_even", [vmem] * 3, [near_shape], [rows_scratch], near, target, faces_even)
     near, = call(
         functools.partial(odd_kernel, depth),
         "near_odd",

time: 28.3 us -> 27.8 us (0.982)
  the two profiles are of different devices: /device:TPU:9 before, /device:TPU:0 now
where the time goes in v19:
time: 27.8 us; the launch traced here: 27.7 us
  Pallas kernels  14.1 us (51%)
  starting transfers between devices  8.79 us (32%)
  waiting for transfers between devices  4.07 us (15%)
  between operations  0.69 us (2%)
    pallas_call x10, Pallas kernels, call(): pl.pallas_call(kernel, in_specs=in_specs, out_specs=[vmem] * len(outs), o...  14.1 us
    ppermute x6, starting transfers between devices, swapped(): return lax.ppermute(block, axis, [(partner(i), i) for i in range(size)])  8.79 us
    ppermute x6, waiting for transfers between devices, swapped(): return lax.ppermute(block, axis, [(partner(i), i) for i in range(size)])  4.07 us
  transfers between devices with their start and end apart: 7, of which 3 were waited for; matrix products, arithmetic and copies ran while one was open for 0% of the time, Pallas kernels for 31%

profile of v19, /device:TPU:0, one launch (start us, length us, event | category | flops | bytes accessed | tf_op | source)
XLA Modules:
  0.0 27.7 jit_solution(7768665395751063352)
XLA Ops:
  0.6 3.1 %pack.1 = (bf16[24,2048]{1,0:T(8,128)(2,1)S(1)}, bf16[128,2048]{1,0:T(8,128)(2,1)S(1)}, bf16[24,512]{1,0:T(8,128)(2,1)S(1)}, bf16[24,128]{1,0:T(8,128)(2,1)S(1)}...) custom-call(s32[8]{0:T(128)} %count_in.3, f32[3,2048]{1,0:T(4,128)} %positions_in.1, ...), custom_call_target="tpu_custom_call" | custom-call | tf_op jit(solution)/shard_map/pack/pallas_call | solution.py:505
  3.7 3.0 %collective-permute-start = (bf16[24,1664]{1,0:T(8,128)(2,1)S(1)}, bf16[24,1664]{1,0:T(8,128)(2,1)S(1)}, u32[]{:S(2)}, u32[]{:S(2)}) collective-permute-start(bf16[24,1664]{1,0:T(8,128)(2,1)S(1)} %get-tuple-element.28), channel_id=1, source_target_pairs={{2,0},{0,2},{6,4},{4,6},{10,8},{8,10},{14,12},{12,14},{18,16},{16,... | collective-permute-start | bytes 239624 | tf_op jit(solution)/shard_map/ppermute | solution.py:484
  6.7 1.5 %collective-permute-start.2 = (bf16[24,1664]{1,0:T(8,128)(2,1)S(1)}, bf16[24,1664]{1,0:T(8,128)(2,1)S(1)}, u32[]{:S(2)}, u32[]{:S(2)}) collective-permute-start(bf16[24,1664]{1,0:T(8,128)(2,1)S(1)} %get-tuple-element.29), channel_id=1, source_target_pairs={{6,0},{4,2},{2,4},{0,6},{14,8},{12,10},{10,12},{8,14},{22,16},{20,... | collective-permute-start | bytes 239624 | tf_op jit(solution)/shard_map/ppermute | solution.py:484
  8.2 0.1 collective-permute-start.1
  8.3 3.1 %near_own.1 = (f32[24,1536]{1,0:T(8,128)S(1)}, bf16[2048,48]{1,0:T(8,128)(2,1)S(1)}, bf16[48,2048]{1,0:T(8,128)(2,1)S(1)}, f32[1,2048]{1,0:T(1,128)S(1)}, f32[24...) custom-call(s32[8]{0:T(128)} %count_in.3, ...), custom_call_target="tpu_custom_call" | custom-call | tf_op jit(solution)/shard_map/near_own/pallas_call | solution.py:505
  11.4 1.0 %collective-permute-done.1.from_2 = bf16[24,128]{1,0:T(8,128)(2,1)S(1)} collective-permute-done((bf16[24,128]{1,0:T(8,128)(2,1)S(1)}, bf16[24,128]{1,0:T(8,128)(2,1)S(1)}, u32[]{:S(2)}, u32[]{:S(2)}) %collective-permute-start.1) | collective-permute-done | bytes 6176 | tf_op jit(solution)/shard_map/ppermute | solution.py:484
  12.4 0.0 collective-permute-done.from_1
  12.4 0.0 collective-permute-done.2.from_3
  12.4 0.5 %row.1 = (bf16[24,1536]{1,0:T(8,128)(2,1)S(1)}, bf16[24,1536]{1,0:T(8,128)(2,1)S(1)}, bf16[24,2816]{1,0:T(8,128)(2,1)S(1)}, bf16[24,256]{1,0:T(8,128)(2,1)S(1)}) custom-call(bf16[24,2048]{1,0:T(8,128)(2,1)S(1)} %get-tuple-element.25.own, bf16[24,512]{1,0:T(8,128)(2,1)S(1)} %get-tuple-element.26.moments, bf16[24,128]{1,0:T(8,128)(2,1)S(1)} %get-tuple-element.27.totals, ...), custom_call_target="tpu_custom_call" | custom-call | tf_op jit(solution)/shard_map/row/pallas_call | solution.py:505
  12.9 1.6 %collective-permute-start.3 = (bf16[24,2816]{1,0:T(8,128)(2,1)S(1)}, bf16[24,2816]{1,0:T(8,128)(2,1)S(1)}, u32[]{:S(2)}, u32[]{:S(2)}) collective-permute-start(bf16[24,2816]{1,0:T(8,128)(2,1)S(1)} %get-tuple-element.37), channel_id=1, source_target_pairs={{8,0},{10,2},{12,4},{14,6},{0,8},{2,10},{4,12},{6,14},{24,16},{26,... | collective-permute-start | bytes 405512 | tf_op jit(solution)/shard_map/ppermute | solution.py:484
  14.6 1.5 %near_middle.1 = (f32[24,2048]{1,0:T(8,128)S(1)}, bf16[24,2560]{1,0:T(8,128)(2,1)S(1)}, f32[24,512]{1,0:T(8,128)S(1)}) custom-call(bf16[24,2048]{1,0:T(8,128)(2,1)S(1)} %get-tuple-element.25.own, bf16[24,1536]{1,0:T(8,128)(2,1)S(1)} %get-tuple-element.31.left, bf16[24,1536]{1,0:T(8,128)(2,1)S(1)} %get-tuple-element.32.right, ...), custom_call_target="tpu_custom_call" | custom-call | tf_op jit(solution)/shard_map/near_middle/pallas_call | solution.py:505
  16.1 0.0 collective-permute-start.4
  16.1 1.9 %collective-permute-done.3.faces.faces_even = bf16[24,2816]{1,0:T(8,128)(2,1)S(1)} collective-permute-done((bf16[24,2816]{1,0:T(8,128)(2,1)S(1)}, bf16[24,2816]{1,0:T(8,128)(2,1)S(1)}, u32[]{:S(2)}, u32[]{:S(2)}) %collective-permute-start.3) | collective-permute-done | bytes 135200 | tf_op jit(solution)/shard_map/ppermute | solution.py:484
  18.0 2.6 %collective-permute-start.5 = (bf16[24,512]{1,0:T(8,128)(2,1)S(1)}, bf16[24,512]{1,0:T(8,128)(2,1)S(1)}, u32[]{:S(2)}, u32[]{:S(2)}) collective-permute-start(bf16[24,512]{1,0:T(8,128)(2,1)S(1)} %row_pairs.1), channel_id=1, source_target_pairs={{16,0},{18,2},{20,4},{22,6},{24,8},{26,10},{28,12},{30,14},{0,16},... | collective-permute-start | bytes 73736 | tf_op jit(solution)/shard_map/ppermute | solution.py:484
  20.6 2.0 %near_side.1.early = f32[24,2048]{1,0:T(8,128)S(1)} custom-call(bf16[24,1536]{1,0:T(8,128)(2,1)S(1)} %get-tuple-element.31.left, bf16[24,1536]{1,0:T(8,128)(2,1)S(1)} %get-tuple-element.32.right, f32[24,2048]{1,0:T(8,128)S(1)} %get-tuple-element.36.early, bf16[48,2048]{1,0:T(8,128)(2,1)S(1)} %get-tuple-element.35.target), custom_call_target="tpu_custom_call" | custom-call | tf_op jit(solution)/shard_map/near_side/pallas_call | solution.py:505
  22.6 1.8 %near_even.1.early = f32[24,2048]{1,0:T(8,128)S(1)} custom-call(f32[24,2048]{1,0:T(8,128)S(1)} %near_side.1.early, bf16[48,2048]{1,0:T(8,128)(2,1)S(1)} %get-tuple-element.35.target, bf16[24,2816]{1,0:T(8,128)(2,1)S(1)} %collective-permute-done.3.faces.faces_even), custom_call_target="tpu_custom_call" | custom-call | tf_op jit(solution)/shard_map/near_even/pallas_call | solution.py:505
  24.4 0.0 collective-permute-done.4.faces.faces_odd
  24.5 0.0 collective-permute-done.5.rest_1_
  24.5 1.3 %evaluate.1 = (f32[17,2048]{1,0:T(8,128)}, f32[1,2176]{1,0:T(1,128)S(1)}) custom-call(f32[24,2048]{1,0:T(8,128)S(1)} %near_odd.1.near, bf16[24,2816]{1,0:T(8,128)(2,1)S(1)} %collective-permute-done.3.faces.faces_even, bf16[24,2560]{1,0:T(8,128)(2,1)S(1)} %collective-permute-done.4.faces.faces_odd, bf16[128,2048]{1,0:T(8,128)(2,1)S(1)} %get-tuple-element.39.basis, ...), custom_call_target="tpu_custom_call" | custom-call | tf_op jit(solution)/shard_map/evaluate/pallas_call | solution.py:505
  25.8 0.0 collective-permute-start.6
  25.8 1.2 %collective-permute-done.6.other = f32[1,2176]{1,0:T(1,128)S(1)} collective-permute-done((f32[1,2176]{1,0:T(1,128)S(1)}, f32[1,2176]{1,0:T(1,128)S(1)}, u32[]{:S(2)}, u32[]{:S(2)}) %collective-permute-start.6) | collective-permute-done | bytes 8736 | tf_op jit(solution)/shard_map/ppermute | solution.py:484
  27.0 0.7 %mean.1 = f32[1,2048]{1,0:T(1,128)} custom-call(f32[1,2176]{1,0:T(1,128)S(1)} %get-tuple-element.47.mine, f32[1,2176]{1,0:T(1,128)S(1)} %collective-permute-done.6.other), custom_call_target="tpu_custom_call" | custom-call | tf_op jit(solution)/shard_map/mean/pallas_call | solution.py:505
  (2 shorter events, 0.0 us)
Async XLA Ops:
  3.7 8.7 %collective-permute-start = (bf16[24,1664]{1,0:T(8,128)(2,1)S(1)}, bf16[24,1664]{1,0:T(8,128)(2,1)S(1)}, u32[]{:S(2)}, u32[]{:S(2)}) collective-permute-start(bf16[24,1664]{1,0:T(8,128)(2,1)S(1)} %get-tuple-element.28), channel_id=1, source_target_pairs={{2,0},{0,2},{6,4},{4,6},{10,8},{8,10},{14,12},{12,14},{18,16},{16,... | collective-permute-start | bytes 239624 | tf_op jit(solution)/shard_map/ppermute | solution.py:484
  6.7 5.7 %collective-permute-start.2 = (bf16[24,1664]{1,0:T(8,128)(2,1)S(1)}, bf16[24,1664]{1,0:T(8,128)(2,1)S(1)}, u32[]{:S(2)}, u32[]{:S(2)}) collective-permute-start(bf16[24,1664]{1,0:T(8,128)(2,1)S(1)} %get-tuple-element.29), channel_id=1, source_target_pairs={{6,0},{4,2},{2,4},{0,6},{14,8},{12,10},{10,12},{8,14},{22,16},{20,... | collective-permute-start | bytes 239624 | tf_op jit(solution)/shard_map/ppermute | solution.py:484
  8.2 4.2 %collective-permute-start.1 = (bf16[24,128]{1,0:T(8,128)(2,1)S(1)}, bf16[24,128]{1,0:T(8,128)(2,1)S(1)}, u32[]{:S(2)}, u32[]{:S(2)}) collective-permute-start(bf16[24,128]{1,0:T(8,128)(2,1)S(1)} %get-tuple-element.27.totals), channel_id=1, source_target_pairs={{4,0},{6,2},{0,4},{2,6},{12,8},{14,10},{8,12},{10,14},{20,16},{22,... | collective-permute-start | bytes 18440 | tf_op jit(solution)/shard_map/ppermute | solution.py:484
  12.9 5.1 %collective-permute-start.3 = (bf16[24,2816]{1,0:T(8,128)(2,1)S(1)}, bf16[24,2816]{1,0:T(8,128)(2,1)S(1)}, u32[]{:S(2)}, u32[]{:S(2)}) collective-permute-start(bf16[24,2816]{1,0:T(8,128)(2,1)S(1)} %get-tuple-element.37), channel_id=1, source_target_pairs={{8,0},{10,2},{12,4},{14,6},{0,8},{2,10},{4,12},{6,14},{24,16},{26,... | collective-permute-start | bytes 405512 | tf_op jit(solution)/shard_map/ppermute | solution.py:484
  16.1 8.3 %collective-permute-start.4 = (bf16[24,2560]{1,0:T(8,128)(2,1)S(1)}, bf16[24,2560]{1,0:T(8,128)(2,1)S(1)}, u32[]{:S(2)}, u32[]{:S(2)}) collective-permute-start(bf16[24,2560]{1,0:T(8,128)(2,1)S(1)} %get-tuple-element.38), channel_id=1, source_target_pairs={{1,0},{0,1},{3,2},{2,3},{5,4},{4,5},{7,6},{6,7},{16,8},{17,9},{18,... | collective-permute-start | bytes 368648 | tf_op jit(solution)/shard_map/ppermute | solution.py:495
  18.0 6.5 %collective-permute-start.5 = (bf16[24,512]{1,0:T(8,128)(2,1)S(1)}, bf16[24,512]{1,0:T(8,128)(2,1)S(1)}, u32[]{:S(2)}, u32[]{:S(2)}) collective-permute-start(bf16[24,512]{1,0:T(8,128)(2,1)S(1)} %row_pairs.1), channel_id=1, source_target_pairs={{16,0},{18,2},{20,4},{22,6},{24,8},{26,10},{28,12},{30,14},{0,16},... | collective-permute-start | bytes 73736 | tf_op jit(solution)/shard_map/ppermute | solution.py:484
  25.8 1.2 %collective-permute-start.6 = (f32[1,2176]{1,0:T(1,128)S(1)}, f32[1,2176]{1,0:T(1,128)S(1)}, u32[]{:S(2)}, u32[]{:S(2)}) collective-permute-start(f32[1,2176]{1,0:T(1,128)S(1)} %get-tuple-element.47.mine), channel_id=1, source_target_pairs={{1,0},{0,1},{3,2},{2,3},{5,4},{4,5},{7,6},{6,7},{9,8},{8,9},{11,10... | collective-permute-start | bytes 26120 | tf_op jit(solution)/shard_map/ppermute | solution.py:484

commit v20 on v19

--- a/solution.py
+++ b/solution.py
@@ -141,8 +141,8 @@
     return copies
 
 
-def pack_kernel(count_in, positions_in, density_in, shift_in, heavy_in, own, basis, moments, totals, *rest):
-    payloads, (count, positions, density, shift, heavy, mono, sems) = rest[:2], rest[2:]
+def pack_kernel(count_in, positions_in, density_in, shift_in, heavy_in, own, mono, moments, totals, *rest):
+    payloads, (count, positions, density, shift, heavy, sems) = rest[:2], rest[2:]
     copies = fetch(
         [(count_in, count), (positions_in, positions), (density_in, density), (shift_in, shift), (heavy_in, heavy)], sems
     )
@@ -180,10 +180,7 @@
     parts = []
     for leaf in range(8):
         here = slice(leaf * pts, (leaf + 1) * pts)
-        high, low = high_low(mono[:, leaf, :])
-        basis[0:SLOT, here] = high
-        basis[SLOT:, here] = low
-        parts.append(dot_nt(own[:, here], high))
+        parts.append(dot_nt(own[:, here], low_bits(mono[:, leaf, :])))
     moment, rest = high_low(jnp.concatenate(parts, axis=1))
     moments[...] = moment
     total = dot(moment, shift[...]) + dot(rest, shift[...])
@@ -278,10 +275,9 @@
     return jnp.concatenate(blocks, axis=0)
 
 
-def own_kernel(depth, count_in, weights_in, own, *rest):
-    tables, outs, rest = rest[:3], rest[3:11], rest[11:]
-    near, source, target, scale, column, columns, far, spread = outs
-    nodes, count, weights, sems = rest
+def own_kernel(count_in, weights_in, own, *rest):
+    tables, outs, (count, weights, sems) = rest[:3], rest[3:11], rest[11:]
+    near, source, target, scale, column, far, spread, nodes = outs
     copies = fetch([*zip(tables, (far, spread, nodes)), (count_in, count), (weights_in, weights)], sems)
     points = own.shape[1]
     pts = points // 8
@@ -292,7 +288,6 @@
     own_groups(near, 0, EARLY, target, source, own)
     for copy in copies:
         copy.wait()
-    columns[...] = box_columns(depth, *box_place(), nodes)
     column[...] = by_row([weights[field] for field in range(weights.shape[0])], column.shape)
     lane_index = lax.broadcasted_iota(jnp.int32, (1, pts), 1)
     for leaf in range(8):
@@ -354,10 +349,10 @@
     faces_of(faces_even, above, sums_for(above, left, moments, right, far), own, left, right, row)
 
 
-def side_pulls(near, left, right, early, target, sides_left, sides_right):
+def side_pulls(near, faces, early, target, scratch):
     pts = early.shape[1] // 8
     jobs = []
-    for step, side, held in ((0, left, sides_left), (1, right, sides_right)):
+    for (step, side), held in zip(faces, scratch):
         for place in range(4):
             centre = (1.5 if step else -1.5, place % 2 - 0.5, place // 2 - 0.5)
             held[lanes(place * pts, pts), :] = source_features(side, place * pts, pts, centre)
@@ -365,9 +360,16 @@
     pulled(near, jobs, target, 2 * pts, early)
 
 
-def middle_kernel(own, left, right, moments, far, early, source, target, near, faces_odd, same, *sides):
+def middle_kernel(depth, own, left, right, moments, far, early, source, target, nodes, mono, *rest):
+    (near, faces_odd, same, columns, basis), sides = rest[:5], rest[5:]
     points = own.shape[1]
-    _, box_z = box_place()
+    pts = points // 8
+    box_x, box_z = box_place()
+    columns[...] = box_columns(depth, box_x, box_z, nodes)
+    for leaf in range(8):
+        high, low = high_low(mono[:, leaf, :])
+        basis[0:SLOT, lanes(leaf * pts, pts)] = high
+        basis[SLOT:, lanes(leaf * pts, pts)] = low
     above = lax.rem(box_z, 2)
     faces_of(faces_odd, above, sums_for(above, left, moments, right, far), own, left, right)
     base = left.shape[1] - LEAVES
@@ -378,10 +380,14 @@
 
     @pl.when(above == 1)
     def _():
-        side_pulls(near, left, right, near, target, *sides)
-
-
-def side_kernel(left, right, early, target, near, *sides):
+        side_pulls(near, [(0, left), (1, right)], near, target, sides)
+
+    @pl.when(above == 0)
+    def _():
+        side_pulls(near, [(0, left)], near, target, sides)
+
+
+def side_kernel(right, early, target, near, held):
     _, box_z = box_place()
     odd = lax.rem(box_z, 2) == 1
 
@@ -391,7 +397,11 @@
 
     @pl.when(jnp.logical_not(odd))
     def _():
-        side_pulls(near, left, right, early, target, *sides)
+        pts = early.shape[1] // 8
+        for group in (0, 2):
+            here = lanes(2 * group * pts, 2 * pts)
+            near[:, here] = early[:, here]
+        side_pulls(near, [(1, right)], early, target, [held])
 
 
 def both_kernel(rows, faces, both):
@@ -523,13 +533,13 @@
     near_shape, sums_shape = ((ROWS, points), full), ((ROWS, LEAVES), full)
     side_scratch = [pltpu.VMEM((4 * pts, FEATURES), half)] * 2
     rows_scratch = pltpu.VMEM((8 * pts, FEATURES), half)
-    own, basis, moments, totals, *given = call(
+    own, mono, moments, totals, *given = call(
         pack_kernel,
         "pack",
         [hbm] * 5,
         [
             ((ROWS, points), half),
-            ((2 * SLOT, points), half),
+            ((SLOT, 8, pts), full),
             ((ROWS, LEAVES), half),
             ((ROWS, 2 * SLOT), half),
             given_shape,
@@ -541,7 +551,6 @@
             pltpu.VMEM((fields, points), half),
             pltpu.VMEM((LEAVES, SLOT), half),
             pltpu.VMEM((SLOT, SLOT), half),
-            pltpu.VMEM((SLOT, 8, pts), full),
             pltpu.SemaphoreType.DMA((5,)),
         ],
         leaf_count,
@@ -553,8 +562,8 @@
     from_2 = swapped(totals, "space", lambda i: i ^ 2)
     from_1 = swapped(given[0], "space", lambda i: i ^ 1)
     from_3 = swapped(given[1], "space", lambda i: i ^ 3)
-    near, source, target, scale, column, columns, far, spread = call(
-        functools.partial(own_kernel, depth),
+    near, source, target, scale, column, far, spread, nodes = call(
+        own_kernel,
         "near_own",
         [hbm] * 2 + [vmem] + [hbm] * 3,
         [
@@ -563,12 +572,11 @@
             ((FEATURES, points), half),
             ((1, points), full),
             ((ROWS, 128), full),
-            ((ACROSS * depth * SLOT, SLOT), half),
             ((len(STEPS) * LEAVES, LEAVES), half),
             ((SLOT, LEAVES), half),
+            ((3, SLOT, SLOT), full),
         ],
         [
-            pltpu.VMEM((3, SLOT, SLOT), full),
             pltpu.SMEM((8,), jnp.int32),
             pltpu.SMEM((fields,), full),
             pltpu.SemaphoreType.DMA((5,)),
@@ -595,11 +603,17 @@
         far,
     )
     faces_even = swapped(faces_even, "space", lambda i: i ^ ACROSS)
-    near, faces_odd, same = call(
-        middle_kernel,
+    near, faces_odd, same, columns, basis = call(
+        functools.partial(middle_kernel, depth),
         "near_middle",
-        [vmem] * 8,
-        [near_shape, faces_shape, sums_shape],
+        [vmem] * 10,
+        [
+            near_shape,
+            faces_shape,
+            sums_shape,
+            ((ACROSS * depth * SLOT, SLOT), half),
+            ((2 * SLOT, points), half),
+        ],
         side_scratch,
         own,
         left,
@@ -609,15 +623,16 @@
         near,
         source,
         target,
+        nodes,
+        mono,
     )
     faces_odd = swapped_odd(faces_odd)
     near, = call(
         side_kernel,
         "near_side",
-        [vmem] * 4,
+        [vmem] * 3,
         [near_shape],
-        side_scratch,
-        left,
+        side_scratch[:1],
         right,
         near,
         target,

time: 27.8 us -> 27.7 us (level)
  waiting for transfers between devices: 4.07 us -> 2.64 us
  Pallas kernels: 14.1 us -> 15.2 us
    ppermute x6, waiting for transfers between devices: 4.07 us -> 2.63 us  [swapped(): return lax.ppermute(block, axis, [(partner(i), i) for i in range(size)])]
    pallas_call x10, Pallas kernels: 14.1 us -> 15.2 us  [call(): pl.pallas_call(kernel, in_specs=in_specs, out_specs=[vmem] * len(outs), o...]
  transfers between devices with their start and end apart: 7 -> 7, of which waited for: 3 -> 3; matrix products, arithmetic and copies ran while one was open for 0% -> 0% of each run, Pallas kernels for 31% -> 39%
where the time goes in v20:
time: 27.7 us; the launch traced here: 27.5 us
  Pallas kernels  15.2 us (55%)
  starting transfers between devices  8.95 us (32%)
  waiting for transfers between devices  2.64 us (10%)
  between operations  0.71 us (3%)
    pallas_call x10, Pallas kernels, call(): pl.pallas_call(kernel, in_specs=in_specs, out_specs=[vmem] * len(outs), o...  15.2 us
    ppermute x6, starting transfers between devices, swapped(): return lax.ppermute(block, axis, [(partner(i), i) for i in range(size)])  8.95 us
    ppermute x6, waiting for transfers between devices, swapped(): return lax.ppermute(block, axis, [(partner(i), i) for i in range(size)])  2.63 us
  transfers between devices with their start and end apart: 7, of which 3 were waited for; matrix products, arithmetic and copies ran while one was open for 0% of the time, Pallas kernels for 39%

profile of v20, /device:TPU:0, one launch (start us, length us, event | category | flops | bytes accessed | tf_op | source)
XLA Modules:
  0.0 27.5 jit_solution(5069528372861675238)
XLA Ops:
  0.6 2.0 %pack.1 = (bf16[24,2048]{1,0:T(8,128)(2,1)S(1)}, f32[64,8,256]{2,1,0:T(8,128)S(1)}, bf16[24,512]{1,0:T(8,128)(2,1)S(1)}, bf16[24,128]{1,0:T(8,128)(2,1)S(1)}, bf...) custom-call(s32[8]{0:T(128)} %count_in.3, f32[3,2048]{1,0:T(4,128)} %positions_in.1, ...), custom_call_target="tpu_custom_call" | custom-call | tf_op jit(solution)/shard_map/pack/pallas_call | solution.py:515
  2.7 3.0 %collective-permute-start = (bf16[24,1664]{1,0:T(8,128)(2,1)S(1)}, bf16[24,1664]{1,0:T(8,128)(2,1)S(1)}, u32[]{:S(2)}, u32[]{:S(2)}) collective-permute-start(bf16[24,1664]{1,0:T(8,128)(2,1)S(1)} %get-tuple-element.30), channel_id=1, source_target_pairs={{2,0},{0,2},{6,4},{4,6},{10,8},{8,10},{14,12},{12,14},{18,16},{16,... | collective-permute-start | bytes 239624 | tf_op jit(solution)/shard_map/ppermute | solution.py:494
  5.7 1.5 %collective-permute-start.2 = (bf16[24,1664]{1,0:T(8,128)(2,1)S(1)}, bf16[24,1664]{1,0:T(8,128)(2,1)S(1)}, u32[]{:S(2)}, u32[]{:S(2)}) collective-permute-start(bf16[24,1664]{1,0:T(8,128)(2,1)S(1)} %get-tuple-element.31), channel_id=1, source_target_pairs={{6,0},{4,2},{2,4},{0,6},{14,8},{12,10},{10,12},{8,14},{22,16},{20,... | collective-permute-start | bytes 239624 | tf_op jit(solution)/shard_map/ppermute | solution.py:494
  7.2 0.1 collective-permute-start.1
  7.2 3.0 %near_own.1 = (f32[24,1536]{1,0:T(8,128)S(1)}, bf16[2048,48]{1,0:T(8,128)(2,1)S(1)}, bf16[48,2048]{1,0:T(8,128)(2,1)S(1)}, f32[1,2048]{1,0:T(1,128)S(1)}, f32[24...) custom-call(s32[8]{0:T(128)} %count_in.3, ...), custom_call_target="tpu_custom_call" | custom-call | tf_op jit(solution)/shard_map/near_own/pallas_call | solution.py:515
  10.2 1.1 %collective-permute-done.1.from_2 = bf16[24,128]{1,0:T(8,128)(2,1)S(1)} collective-permute-done((bf16[24,128]{1,0:T(8,128)(2,1)S(1)}, bf16[24,128]{1,0:T(8,128)(2,1)S(1)}, u32[]{:S(2)}, u32[]{:S(2)}) %collective-permute-start.1) | collective-permute-done | bytes 6176 | tf_op jit(solution)/shard_map/ppermute | solution.py:494
  11.3 0.0 collective-permute-done.from_1
  11.3 0.0 collective-permute-done.2.from_3
  11.3 0.5 %row.1 = (bf16[24,1536]{1,0:T(8,128)(2,1)S(1)}, bf16[24,1536]{1,0:T(8,128)(2,1)S(1)}, bf16[24,2816]{1,0:T(8,128)(2,1)S(1)}, bf16[24,256]{1,0:T(8,128)(2,1)S(1)}) custom-call(bf16[24,2048]{1,0:T(8,128)(2,1)S(1)} %get-tuple-element.27.own, bf16[24,512]{1,0:T(8,128)(2,1)S(1)} %get-tuple-element.28.moments, bf16[24,128]{1,0:T(8,128)(2,1)S(1)} %get-tuple-element.29.totals, ...), custom_call_target="tpu_custom_call" | custom-call | tf_op jit(solution)/shard_map/row/pallas_call | solution.py:515
  11.9 1.6 %collective-permute-start.3 = (bf16[24,2816]{1,0:T(8,128)(2,1)S(1)}, bf16[24,2816]{1,0:T(8,128)(2,1)S(1)}, u32[]{:S(2)}, u32[]{:S(2)}) collective-permute-start(bf16[24,2816]{1,0:T(8,128)(2,1)S(1)} %get-tuple-element.41), channel_id=1, source_target_pairs={{8,0},{10,2},{12,4},{14,6},{0,8},{2,10},{4,12},{6,14},{24,16},{26,... | collective-permute-start | bytes 405512 | tf_op jit(solution)/shard_map/ppermute | solution.py:494
  13.5 4.7 %near_middle.1 = (f32[24,2048]{1,0:T(8,128)S(1)}, bf16[24,2560]{1,0:T(8,128)(2,1)S(1)}, f32[24,512]{1,0:T(8,128)S(1)}, bf16[1024,64]{1,0:T(8,128)(2,1)S(1)}, bf16[128,2048]{1,0:T(8,128)(2,1)S(1)}) custom-call(bf16[24,2048]{1,0:T(8,128)(2,1)S(1)} %get-tuple-element.27.own, bf16[24,1536]{1,0:T(8,128)(2,1)S(1)} %get-tuple-element.34.left, ...), custom_call_target="tpu_custom_call" | custom-call | tf_op jit(solution)/shard_map/near_middle/pallas_call | solution.py:515
  18.1 0.0 collective-permute-start.4
  18.2 0.0 collective-permute-done.3.faces.faces_even
  18.2 2.7 %collective-permute-start.5 = (bf16[24,512]{1,0:T(8,128)(2,1)S(1)}, bf16[24,512]{1,0:T(8,128)(2,1)S(1)}, u32[]{:S(2)}, u32[]{:S(2)}) collective-permute-start(bf16[24,512]{1,0:T(8,128)(2,1)S(1)} %row_pairs.1), channel_id=1, source_target_pairs={{16,0},{18,2},{20,4},{22,6},{24,8},{26,10},{28,12},{30,14},{0,16},... | collective-permute-start | bytes 73736 | tf_op jit(solution)/shard_map/ppermute | solution.py:494
  20.9 1.2 %near_side.1.early = f32[24,2048]{1,0:T(8,128)S(1)} custom-call(bf16[24,1536]{1,0:T(8,128)(2,1)S(1)} %get-tuple-element.33.right, f32[24,2048]{1,0:T(8,128)S(1)} %get-tuple-element.40.early, bf16[48,2048]{1,0:T(8,128)(2,1)S(1)} %get-tuple-element.37.target), custom_call_target="tpu_custom_call" | custom-call | tf_op jit(solution)/shard_map/near_side/pallas_call | solution.py:515
  22.1 1.8 %near_even.1.early = f32[24,2048]{1,0:T(8,128)S(1)} custom-call(f32[24,2048]{1,0:T(8,128)S(1)} %near_side.1.early, bf16[48,2048]{1,0:T(8,128)(2,1)S(1)} %get-tuple-element.37.target, bf16[24,2816]{1,0:T(8,128)(2,1)S(1)} %collective-permute-done.3.faces.faces_even), custom_call_target="tpu_custom_call" | custom-call | tf_op jit(solution)/shard_map/near_even/pallas_call | solution.py:515
  23.9 0.0 collective-permute-done.4.faces.faces_odd
  23.9 0.4 %collective-permute-done.5.rest_1_ = bf16[24,512]{1,0:T(8,128)(2,1)S(1)} collective-permute-done((bf16[24,512]{1,0:T(8,128)(2,1)S(1)}, bf16[24,512]{1,0:T(8,128)(2,1)S(1)}, u32[]{:S(2)}, u32[]{:S(2)}) %collective-permute-start.5) | collective-permute-done | bytes 24608 | tf_op jit(solution)/shard_map/ppermute | solution.py:494
  24.3 1.3 %evaluate.1 = (f32[17,2048]{1,0:T(8,128)}, f32[1,2176]{1,0:T(1,128)S(1)}) custom-call(f32[24,2048]{1,0:T(8,128)S(1)} %near_odd.1.near, bf16[24,2816]{1,0:T(8,128)(2,1)S(1)} %collective-permute-done.3.faces.faces_even, bf16[24,2560]{1,0:T(8,128)(2,1)S(1)} %collective-permute-done.4.faces.faces_odd, bf16[128,2048]{1,0:T(8,128)(2,1)S(1)} %get-tuple-element.43.basis, ...), custom_call_target="tpu_custom_call" | custom-call | tf_op jit(solution)/shard_map/evaluate/pallas_call | solution.py:515
  25.6 0.0 collective-permute-start.6
  25.6 1.2 %collective-permute-done.6.other = f32[1,2176]{1,0:T(1,128)S(1)} collective-permute-done((f32[1,2176]{1,0:T(1,128)S(1)}, f32[1,2176]{1,0:T(1,128)S(1)}, u32[]{:S(2)}, u32[]{:S(2)}) %collective-permute-start.6) | collective-permute-done | bytes 8736 | tf_op jit(solution)/shard_map/ppermute | solution.py:494
  26.8 0.7 %mean.1 = f32[1,2048]{1,0:T(1,128)} custom-call(f32[1,2176]{1,0:T(1,128)S(1)} %get-tuple-element.51.mine, f32[1,2176]{1,0:T(1,128)S(1)} %collective-permute-done.6.other), custom_call_target="tpu_custom_call" | custom-call | tf_op jit(solution)/shard_map/mean/pallas_call | solution.py:515
  (2 shorter events, 0.0 us)
Async XLA Ops:
  2.7 8.7 %collective-permute-start = (bf16[24,1664]{1,0:T(8,128)(2,1)S(1)}, bf16[24,1664]{1,0:T(8,128)(2,1)S(1)}, u32[]{:S(2)}, u32[]{:S(2)}) collective-permute-start(bf16[24,1664]{1,0:T(8,128)(2,1)S(1)} %get-tuple-element.30), channel_id=1, source_target_pairs={{2,0},{0,2},{6,4},{4,6},{10,8},{8,10},{14,12},{12,14},{18,16},{16,... | collective-permute-start | bytes 239624 | tf_op jit(solution)/shard_map/ppermute | solution.py:494
  5.7 5.7 %collective-permute-start.2 = (bf16[24,1664]{1,0:T(8,128)(2,1)S(1)}, bf16[24,1664]{1,0:T(8,128)(2,1)S(1)}, u32[]{:S(2)}, u32[]{:S(2)}) collective-permute-start(bf16[24,1664]{1,0:T(8,128)(2,1)S(1)} %get-tuple-element.31), channel_id=1, source_target_pairs={{6,0},{4,2},{2,4},{0,6},{14,8},{12,10},{10,12},{8,14},{22,16},{20,... | collective-permute-start | bytes 239624 | tf_op jit(solution)/shard_map/ppermute | solution.py:494
  7.2 4.2 %collective-permute-start.1 = (bf16[24,128]{1,0:T(8,128)(2,1)S(1)}, bf16[24,128]{1,0:T(8,128)(2,1)S(1)}, u32[]{:S(2)}, u32[]{:S(2)}) collective-permute-start(bf16[24,128]{1,0:T(8,128)(2,1)S(1)} %get-tuple-element.29.totals), channel_id=1, source_target_pairs={{4,0},{6,2},{0,4},{2,6},{12,8},{14,10},{8,12},{10,14},{20,16},{22,... | collective-permute-start | bytes 18440 | tf_op jit(solution)/shard_map/ppermute | solution.py:494
  11.9 6.3 %collective-permute-start.3 = (bf16[24,2816]{1,0:T(8,128)(2,1)S(1)}, bf16[24,2816]{1,0:T(8,128)(2,1)S(1)}, u32[]{:S(2)}, u32[]{:S(2)}) collective-permute-start(bf16[24,2816]{1,0:T(8,128)(2,1)S(1)} %get-tuple-element.41), channel_id=1, source_target_pairs={{8,0},{10,2},{12,4},{14,6},{0,8},{2,10},{4,12},{6,14},{24,16},{26,... | collective-permute-start | bytes 405512 | tf_op jit(solution)/shard_map/ppermute | solution.py:494
  18.1 5.7 %collective-permute-start.4 = (bf16[24,2560]{1,0:T(8,128)(2,1)S(1)}, bf16[24,2560]{1,0:T(8,128)(2,1)S(1)}, u32[]{:S(2)}, u32[]{:S(2)}) collective-permute-start(bf16[24,2560]{1,0:T(8,128)(2,1)S(1)} %get-tuple-element.42), channel_id=1, source_target_pairs={{1,0},{0,1},{3,2},{2,3},{5,4},{4,5},{7,6},{6,7},{16,8},{17,9},{18,... | collective-permute-start | bytes 368648 | tf_op jit(solution)/shard_map/ppermute | solution.py:505
  18.2 6.1 %collective-permute-start.5 = (bf16[24,512]{1,0:T(8,128)(2,1)S(1)}, bf16[24,512]{1,0:T(8,128)(2,1)S(1)}, u32[]{:S(2)}, u32[]{:S(2)}) collective-permute-start(bf16[24,512]{1,0:T(8,128)(2,1)S(1)} %row_pairs.1), channel_id=1, source_target_pairs={{16,0},{18,2},{20,4},{22,6},{24,8},{26,10},{28,12},{30,14},{0,16},... | collective-permute-start | bytes 73736 | tf_op jit(solution)/shard_map/ppermute | solution.py:494
  25.6 1.2 %collective-permute-start.6 = (f32[1,2176]{1,0:T(1,128)S(1)}, f32[1,2176]{1,0:T(1,128)S(1)}, u32[]{:S(2)}, u32[]{:S(2)}) collective-permute-start(f32[1,2176]{1,0:T(1,128)S(1)} %get-tuple-element.51.mine), channel_id=1, source_target_pairs={{1,0},{0,1},{3,2},{2,3},{5,4},{4,5},{7,6},{6,7},{9,8},{8,9},{11,10... | collective-permute-start | bytes 26120 | tf_op jit(solution)/shard_map/ppermute | solution.py:494

commit v21 on v19

--- a/solution.py
+++ b/solution.py
@@ -112,6 +112,15 @@
     return table
 
 
+def power_table():
+    table = np.zeros((3, SLOT, 16), np.float32)
+    for axis in range(3):
+        for k, powers in enumerate(EXPONENTS):
+            table[axis, k, powers[axis]] = 1.0
+            table[axis, k, 8 + powers[axis]] = 1.0
+    return table.reshape(3 * SLOT, 16)
+
+
 def high_low(value):
     high = low_bits(value)
     return high, low_bits(value - high.astype(jnp.float32))
@@ -141,10 +150,18 @@
     return copies
 
 
-def pack_kernel(count_in, positions_in, density_in, shift_in, heavy_in, own, basis, moments, totals, *rest):
-    payloads, (count, positions, density, shift, heavy, mono, sems) = rest[:2], rest[2:]
+def pack_kernel(count_in, positions_in, density_in, shift_in, heavy_in, powers_in, own, basis, moments, totals, *rest):
+    payloads, (count, positions, density, shift, heavy, powers, sems) = rest[:2], rest[2:]
     copies = fetch(
-        [(count_in, count), (positions_in, positions), (density_in, density), (shift_in, shift), (heavy_in, heavy)], sems
+        [
+            (count_in, count),
+            (positions_in, positions),
+            (density_in, density),
+            (shift_in, shift),
+            (heavy_in, heavy),
+            (powers_in, powers),
+        ],
+        sems,
     )
     fields, points = density.shape
     pts = points // 8
@@ -168,22 +185,24 @@
         spare = jnp.zeros((ROWS - fields - 6, pts), jnp.float32)
         own[:, here] = low_bits(jnp.concatenate([mass, high, middle, spare], axis=0))
 
-    axes = [2.0 * jnp.concatenate([part[a : a + 1] for part in local], axis=0) for a in range(3)]
-    made = {(0, 0, 0): jnp.ones((8, pts), jnp.float32)}
-    for k, powers in enumerate(EXPONENTS):
-        if powers not in made:
-            a = next(i for i in range(3) if powers[i] > 0)
-            before = tuple(p - (i == a) for i, p in enumerate(powers))
-            made[powers] = made[before] * axes[a]
-        mono[k] = made[powers]
-    mono[COEFFS:SLOT] = jnp.zeros((SLOT - COEFFS, 8, pts), jnp.float32)
+    scaled = 2.0 * jnp.concatenate(local, axis=1)
+    row = lax.broadcasted_iota(jnp.int32, (8, points), 0)
+    value = None
+    for axis in range(3):
+        base = jnp.broadcast_to(scaled[axis : axis + 1], (8, points))
+        power = jnp.ones((8, points), jnp.float32)
+        for degree in range(1, ORDER + 1):
+            power = power * jnp.where(row >= degree, base, 1.0)
+        pieces = jnp.concatenate(high_low(power), axis=0)
+        picked = dot(powers[axis * SLOT : (axis + 1) * SLOT, :], pieces)
+        value = picked if value is None else value * picked
+    high, low = high_low(value)
+    basis[0:SLOT, :] = high
+    basis[SLOT:, :] = low
     parts = []
     for leaf in range(8):
         here = slice(leaf * pts, (leaf + 1) * pts)
-        high, low = high_low(mono[:, leaf, :])
-        basis[0:SLOT, here] = high
-        basis[SLOT:, here] = low
-        parts.append(dot_nt(own[:, here], high))
+        parts.append(dot_nt(own[:, here], high[:, here]))
     moment, rest = high_low(jnp.concatenate(parts, axis=1))
     moments[...] = moment
     total = dot(moment, shift[...]) + dot(rest, shift[...])
@@ -279,9 +298,8 @@
 
 
 def own_kernel(depth, count_in, weights_in, own, *rest):
-    tables, outs, rest = rest[:3], rest[3:11], rest[11:]
+    tables, outs, (nodes, count, weights, sems) = rest[:3], rest[3:11], rest[11:]
     near, source, target, scale, column, columns, far, spread = outs
-    nodes, count, weights, sems = rest
     copies = fetch([*zip(tables, (far, spread, nodes)), (count_in, count), (weights_in, weights)], sems)
     points = own.shape[1]
     pts = points // 8
@@ -354,10 +372,10 @@
     faces_of(faces_even, above, sums_for(above, left, moments, right, far), own, left, right, row)
 
 
-def side_pulls(near, left, right, early, target, sides_left, sides_right):
+def side_pulls(near, faces, early, target, scratch):
     pts = early.shape[1] // 8
     jobs = []
-    for step, side, held in ((0, left, sides_left), (1, right, sides_right)):
+    for (step, side), held in zip(faces, scratch):
         for place in range(4):
             centre = (1.5 if step else -1.5, place % 2 - 0.5, place // 2 - 0.5)
             held[lanes(place * pts, pts), :] = source_features(side, place * pts, pts, centre)
@@ -378,10 +396,14 @@
 
     @pl.when(above == 1)
     def _():
-        side_pulls(near, left, right, near, target, *sides)
-
-
-def side_kernel(left, right, early, target, near, *sides):
+        side_pulls(near, [(0, left), (1, right)], near, target, sides)
+
+    @pl.when(above == 0)
+    def _():
+        side_pulls(near, [(0, left)], near, target, sides)
+
+
+def side_kernel(right, early, target, near, held):
     _, box_z = box_place()
     odd = lax.rem(box_z, 2) == 1
 
@@ -391,7 +413,11 @@
 
     @pl.when(jnp.logical_not(odd))
     def _():
-        side_pulls(near, left, right, early, target, *sides)
+        pts = early.shape[1] // 8
+        for group in (0, 2):
+            here = lanes(2 * group * pts, 2 * pts)
+            near[:, here] = early[:, here]
+        side_pulls(near, [(1, right)], early, target, [held])
 
 
 def both_kernel(rows, faces, both):
@@ -526,7 +552,7 @@
     own, basis, moments, totals, *given = call(
         pack_kernel,
         "pack",
-        [hbm] * 5,
+        [hbm] * 6,
         [
             ((ROWS, points), half),
             ((2 * SLOT, points), half),
@@ -541,14 +567,15 @@
             pltpu.VMEM((fields, points), half),
             pltpu.VMEM((LEAVES, SLOT), half),
             pltpu.VMEM((SLOT, SLOT), half),
-            pltpu.VMEM((SLOT, 8, pts), full),
-            pltpu.SemaphoreType.DMA((5,)),
+            pltpu.VMEM((3 * SLOT, 16), half),
+            pltpu.SemaphoreType.DMA((6,)),
         ],
         leaf_count,
         positions,
         density,
         jnp.asarray(shift, half),
         jnp.asarray(heavy_table(), half),
+        jnp.asarray(power_table(), half),
     )
     from_2 = swapped(totals, "space", lambda i: i ^ 2)
     from_1 = swapped(given[0], "space", lambda i: i ^ 1)
@@ -614,10 +641,9 @@
     near, = call(
         side_kernel,
         "near_side",
-        [vmem] * 4,
+        [vmem] * 3,
         [near_shape],
-        side_scratch,
-        left,
+        side_scratch[:1],
         right,
         near,
         target,

time: 27.8 us -> 25.6 us (0.921)
  waiting for transfers between devices: 4.07 us -> 2.89 us
  Pallas kernels: 14.1 us -> 13.1 us
    ppermute x6, waiting for transfers between devices: 4.07 us -> 2.89 us  [swapped(): return lax.ppermute(block, axis, [(partner(i), i) for i in range(size)])]
    pallas_call x10, Pallas kernels: 14.1 us -> 13.1 us  [call(): pl.pallas_call(kernel, in_specs=in_specs, out_specs=[vmem] * len(outs), o...]
  transfers between devices with their start and end apart: 7 -> 7, of which waited for: 3 -> 3; matrix products, arithmetic and copies ran while one was open for 0% -> 0% of each run, Pallas kernels for 31% -> 34%
where the time goes in v21:
time: 25.6 us; the launch traced here: 25.4 us
  Pallas kernels  13.1 us (51%)
  starting transfers between devices  8.78 us (34%)
  waiting for transfers between devices  2.89 us (11%)
  between operations  0.69 us (3%)
    pallas_call x10, Pallas kernels, call(): pl.pallas_call(kernel, in_specs=in_specs, out_specs=[vmem] * len(outs), o...  13.1 us
    ppermute x6, starting transfers between devices, swapped(): return lax.ppermute(block, axis, [(partner(i), i) for i in range(size)])  8.78 us
    ppermute x6, waiting for transfers between devices, swapped(): return lax.ppermute(block, axis, [(partner(i), i) for i in range(size)])  2.89 us
  transfers between devices with their start and end apart: 7, of which 3 were waited for; matrix products, arithmetic and copies ran while one was open for 0% of the time, Pallas kernels for 34%

profile of v21, /device:TPU:0, one launch (start us, length us, event | category | flops | bytes accessed | tf_op | source)
XLA Modules:
  0.0 25.4 jit_solution(2175791681927059697)
XLA Ops:
  0.6 1.9 %pack.1 = (bf16[24,2048]{1,0:T(8,128)(2,1)S(1)}, bf16[128,2048]{1,0:T(8,128)(2,1)S(1)}, bf16[24,512]{1,0:T(8,128)(2,1)S(1)}, bf16[24,128]{1,0:T(8,128)(2,1)S(1)}...) custom-call(s32[8]{0:T(128)} %count_in.3, f32[3,2048]{1,0:T(4,128)} %positions_in.1, ...), custom_call_target="tpu_custom_call" | custom-call | tf_op jit(solution)/shard_map/pack/pallas_call | solution.py:531
  2.5 3.0 %collective-permute-start = (bf16[24,1664]{1,0:T(8,128)(2,1)S(1)}, bf16[24,1664]{1,0:T(8,128)(2,1)S(1)}, u32[]{:S(2)}, u32[]{:S(2)}) collective-permute-start(bf16[24,1664]{1,0:T(8,128)(2,1)S(1)} %get-tuple-element.28), channel_id=1, source_target_pairs={{2,0},{0,2},{6,4},{4,6},{10,8},{8,10},{14,12},{12,14},{18,16},{16,... | collective-permute-start | bytes 239624 | tf_op jit(solution)/shard_map/ppermute | solution.py:510
  5.6 1.5 %collective-permute-start.2 = (bf16[24,1664]{1,0:T(8,128)(2,1)S(1)}, bf16[24,1664]{1,0:T(8,128)(2,1)S(1)}, u32[]{:S(2)}, u32[]{:S(2)}) collective-permute-start(bf16[24,1664]{1,0:T(8,128)(2,1)S(1)} %get-tuple-element.29), channel_id=1, source_target_pairs={{6,0},{4,2},{2,4},{0,6},{14,8},{12,10},{10,12},{8,14},{22,16},{20,... | collective-permute-start | bytes 239624 | tf_op jit(solution)/shard_map/ppermute | solution.py:510
  7.0 0.1 collective-permute-start.1
  7.1 3.1 %near_own.1 = (f32[24,1536]{1,0:T(8,128)S(1)}, bf16[2048,48]{1,0:T(8,128)(2,1)S(1)}, bf16[48,2048]{1,0:T(8,128)(2,1)S(1)}, f32[1,2048]{1,0:T(1,128)S(1)}, f32[24...) custom-call(s32[8]{0:T(128)} %count_in.3, ...), custom_call_target="tpu_custom_call" | custom-call | tf_op jit(solution)/shard_map/near_own/pallas_call | solution.py:531
  10.2 1.0 %collective-permute-done.1.from_2 = bf16[24,128]{1,0:T(8,128)(2,1)S(1)} collective-permute-done((bf16[24,128]{1,0:T(8,128)(2,1)S(1)}, bf16[24,128]{1,0:T(8,128)(2,1)S(1)}, u32[]{:S(2)}, u32[]{:S(2)}) %collective-permute-start.1) | collective-permute-done | bytes 6176 | tf_op jit(solution)/shard_map/ppermute | solution.py:510
  11.2 0.0 collective-permute-done.from_1
  11.2 0.0 collective-permute-done.2.from_3
  11.2 0.5 %row.1 = (bf16[24,1536]{1,0:T(8,128)(2,1)S(1)}, bf16[24,1536]{1,0:T(8,128)(2,1)S(1)}, bf16[24,2816]{1,0:T(8,128)(2,1)S(1)}, bf16[24,256]{1,0:T(8,128)(2,1)S(1)}) custom-call(bf16[24,2048]{1,0:T(8,128)(2,1)S(1)} %get-tuple-element.25.own, bf16[24,512]{1,0:T(8,128)(2,1)S(1)} %get-tuple-element.26.moments, bf16[24,128]{1,0:T(8,128)(2,1)S(1)} %get-tuple-element.27.totals, ...), custom_call_target="tpu_custom_call" | custom-call | tf_op jit(solution)/shard_map/row/pallas_call | solution.py:531
  11.7 1.6 %collective-permute-start.3 = (bf16[24,2816]{1,0:T(8,128)(2,1)S(1)}, bf16[24,2816]{1,0:T(8,128)(2,1)S(1)}, u32[]{:S(2)}, u32[]{:S(2)}) collective-permute-start(bf16[24,2816]{1,0:T(8,128)(2,1)S(1)} %get-tuple-element.37), channel_id=1, source_target_pairs={{8,0},{10,2},{12,4},{14,6},{0,8},{2,10},{4,12},{6,14},{24,16},{26,... | collective-permute-start | bytes 405512 | tf_op jit(solution)/shard_map/ppermute | solution.py:510
  13.4 2.7 %near_middle.1 = (f32[24,2048]{1,0:T(8,128)S(1)}, bf16[24,2560]{1,0:T(8,128)(2,1)S(1)}, f32[24,512]{1,0:T(8,128)S(1)}) custom-call(bf16[24,2048]{1,0:T(8,128)(2,1)S(1)} %get-tuple-element.25.own, bf16[24,1536]{1,0:T(8,128)(2,1)S(1)} %get-tuple-element.32.left, bf16[24,1536]{1,0:T(8,128)(2,1)S(1)} %get-tuple-element.31.right, ...), custom_call_target="tpu_custom_call" | custom-call | tf_op jit(solution)/shard_map/near_middle/pallas_call | solution.py:531
  16.1 0.0 collective-permute-start.4
  16.1 0.7 %collective-permute-done.3.faces.faces_even = bf16[24,2816]{1,0:T(8,128)(2,1)S(1)} collective-permute-done((bf16[24,2816]{1,0:T(8,128)(2,1)S(1)}, bf16[24,2816]{1,0:T(8,128)(2,1)S(1)}, u32[]{:S(2)}, u32[]{:S(2)}) %collective-permute-start.3) | collective-permute-done | bytes 135200 | tf_op jit(solution)/shard_map/ppermute | solution.py:510
  16.8 2.6 %collective-permute-start.5 = (bf16[24,512]{1,0:T(8,128)(2,1)S(1)}, bf16[24,512]{1,0:T(8,128)(2,1)S(1)}, u32[]{:S(2)}, u32[]{:S(2)}) collective-permute-start(bf16[24,512]{1,0:T(8,128)(2,1)S(1)} %row_pairs.1), channel_id=1, source_target_pairs={{16,0},{18,2},{20,4},{22,6},{24,8},{26,10},{28,12},{30,14},{0,16},... | collective-permute-start | bytes 73736 | tf_op jit(solution)/shard_map/ppermute | solution.py:510
  19.4 1.2 %near_side.1.early = f32[24,2048]{1,0:T(8,128)S(1)} custom-call(bf16[24,1536]{1,0:T(8,128)(2,1)S(1)} %get-tuple-element.31.right, f32[24,2048]{1,0:T(8,128)S(1)} %get-tuple-element.36.early, bf16[48,2048]{1,0:T(8,128)(2,1)S(1)} %get-tuple-element.35.target), custom_call_target="tpu_custom_call" | custom-call | tf_op jit(solution)/shard_map/near_side/pallas_call | solution.py:531
  20.6 1.6 %near_even.1.early = f32[24,2048]{1,0:T(8,128)S(1)} custom-call(f32[24,2048]{1,0:T(8,128)S(1)} %near_side.1.early, bf16[48,2048]{1,0:T(8,128)(2,1)S(1)} %get-tuple-element.35.target, bf16[24,2816]{1,0:T(8,128)(2,1)S(1)} %collective-permute-done.3.faces.faces_even), custom_call_target="tpu_custom_call" | custom-call | tf_op jit(solution)/shard_map/near_even/pallas_call | solution.py:531
  22.2 0.0 collective-permute-done.4.faces.faces_odd
  22.2 0.0 collective-permute-done.5.rest_1_
  22.2 1.3 %evaluate.1 = (f32[17,2048]{1,0:T(8,128)}, f32[1,2176]{1,0:T(1,128)S(1)}) custom-call(f32[24,2048]{1,0:T(8,128)S(1)} %near_odd.1.near, bf16[24,2816]{1,0:T(8,128)(2,1)S(1)} %collective-permute-done.3.faces.faces_even, bf16[24,2560]{1,0:T(8,128)(2,1)S(1)} %collective-permute-done.4.faces.faces_odd, bf16[128,2048]{1,0:T(8,128)(2,1)S(1)} %get-tuple-element.39.basis, ...), custom_call_target="tpu_custom_call" | custom-call | tf_op jit(solution)/shard_map/evaluate/pallas_call | solution.py:531
  23.6 0.0 collective-permute-start.6
  23.6 1.2 %collective-permute-done.6.other = f32[1,2176]{1,0:T(1,128)S(1)} collective-permute-done((f32[1,2176]{1,0:T(1,128)S(1)}, f32[1,2176]{1,0:T(1,128)S(1)}, u32[]{:S(2)}, u32[]{:S(2)}) %collective-permute-start.6) | collective-permute-done | bytes 8736 | tf_op jit(solution)/shard_map/ppermute | solution.py:510
  24.7 0.7 %mean.1 = f32[1,2048]{1,0:T(1,128)} custom-call(f32[1,2176]{1,0:T(1,128)S(1)} %get-tuple-element.47.mine, f32[1,2176]{1,0:T(1,128)S(1)} %collective-permute-done.6.other), custom_call_target="tpu_custom_call" | custom-call | tf_op jit(solution)/shard_map/mean/pallas_call | solution.py:531
  (2 shorter events, 0.0 us)
Async XLA Ops:
  2.5 8.7 %collective-permute-start = (bf16[24,1664]{1,0:T(8,128)(2,1)S(1)}, bf16[24,1664]{1,0:T(8,128)(2,1)S(1)}, u32[]{:S(2)}, u32[]{:S(2)}) collective-permute-start(bf16[24,1664]{1,0:T(8,128)(2,1)S(1)} %get-tuple-element.28), channel_id=1, source_target_pairs={{2,0},{0,2},{6,4},{4,6},{10,8},{8,10},{14,12},{12,14},{18,16},{16,... | collective-permute-start | bytes 239624 | tf_op jit(solution)/shard_map/ppermute | solution.py:510
  5.6 5.7 %collective-permute-start.2 = (bf16[24,1664]{1,0:T(8,128)(2,1)S(1)}, bf16[24,1664]{1,0:T(8,128)(2,1)S(1)}, u32[]{:S(2)}, u32[]{:S(2)}) collective-permute-start(bf16[24,1664]{1,0:T(8,128)(2,1)S(1)} %get-tuple-element.29), channel_id=1, source_target_pairs={{6,0},{4,2},{2,4},{0,6},{14,8},{12,10},{10,12},{8,14},{22,16},{20,... | collective-permute-start | bytes 239624 | tf_op jit(solution)/shard_map/ppermute | solution.py:510
  7.0 4.2 %collective-permute-start.1 = (bf16[24,128]{1,0:T(8,128)(2,1)S(1)}, bf16[24,128]{1,0:T(8,128)(2,1)S(1)}, u32[]{:S(2)}, u32[]{:S(2)}) collective-permute-start(bf16[24,128]{1,0:T(8,128)(2,1)S(1)} %get-tuple-element.27.totals), channel_id=1, source_target_pairs={{4,0},{6,2},{0,4},{2,6},{12,8},{14,10},{8,12},{10,14},{20,16},{22,... | collective-permute-start | bytes 18440 | tf_op jit(solution)/shard_map/ppermute | solution.py:510
  11.7 5.1 %collective-permute-start.3 = (bf16[24,2816]{1,0:T(8,128)(2,1)S(1)}, bf16[24,2816]{1,0:T(8,128)(2,1)S(1)}, u32[]{:S(2)}, u32[]{:S(2)}) collective-permute-start(bf16[24,2816]{1,0:T(8,128)(2,1)S(1)} %get-tuple-element.37), channel_id=1, source_target_pairs={{8,0},{10,2},{12,4},{14,6},{0,8},{2,10},{4,12},{6,14},{24,16},{26,... | collective-permute-start | bytes 405512 | tf_op jit(solution)/shard_map/ppermute | solution.py:510
  16.1 6.1 %collective-permute-start.4 = (bf16[24,2560]{1,0:T(8,128)(2,1)S(1)}, bf16[24,2560]{1,0:T(8,128)(2,1)S(1)}, u32[]{:S(2)}, u32[]{:S(2)}) collective-permute-start(bf16[24,2560]{1,0:T(8,128)(2,1)S(1)} %get-tuple-element.38), channel_id=1, source_target_pairs={{1,0},{0,1},{3,2},{2,3},{5,4},{4,5},{7,6},{6,7},{16,8},{17,9},{18,... | collective-permute-start | bytes 368648 | tf_op jit(solution)/shard_map/ppermute | solution.py:521
  16.8 5.4 %collective-permute-start.5 = (bf16[24,512]{1,0:T(8,128)(2,1)S(1)}, bf16[24,512]{1,0:T(8,128)(2,1)S(1)}, u32[]{:S(2)}, u32[]{:S(2)}) collective-permute-start(bf16[24,512]{1,0:T(8,128)(2,1)S(1)} %row_pairs.1), channel_id=1, source_target_pairs={{16,0},{18,2},{20,4},{22,6},{24,8},{26,10},{28,12},{30,14},{0,16},... | collective-permute-start | bytes 73736 | tf_op jit(solution)/shard_map/ppermute | solution.py:510
  23.6 1.2 %collective-permute-start.6 = (f32[1,2176]{1,0:T(1,128)S(1)}, f32[1,2176]{1,0:T(1,128)S(1)}, u32[]{:S(2)}, u32[]{:S(2)}) collective-permute-start(f32[1,2176]{1,0:T(1,128)S(1)} %get-tuple-element.47.mine), channel_id=1, source_target_pairs={{1,0},{0,1},{3,2},{2,3},{5,4},{4,5},{7,6},{6,7},{9,8},{8,9},{11,10... | collective-permute-start | bytes 26120 | tf_op jit(solution)/shard_map/ppermute | solution.py:510

commit v22 on v21

--- a/solution.py
+++ b/solution.py
@@ -16,7 +16,7 @@
 ROWS = 24
 LEAVES = 8 * SLOT
 MEGA = 1024 * 1024
-FEATURES = 48
+FEATURES = 32
 EARLY = 3
 
 
@@ -121,6 +121,25 @@
     return table.reshape(3 * SLOT, 16)
 
 
+def pick_tables():
+    source = np.zeros((FEATURES, 32), np.float32)
+    target = np.zeros((FEATURES, 32), np.float32)
+    row = 0
+    for left, right in ((0, 0), (0, 8), (8, 0), (0, 16), (16, 0), (8, 8)):
+        for axis in range(3):
+            source[row, left + axis] = 1.0
+            target[row, right + axis] = -2.0
+            row += 1
+    for piece in range(3):
+        source[row, 24 + piece] = target[row, 27] = 1.0
+        source[row + 1, 27] = target[row + 1, 24 + piece] = 1.0
+        row += 2
+    join = np.zeros((FEATURES, 32), np.float32)
+    for axis in range(3):
+        join[axis, 1 + axis] = join[axis, 4 + axis] = 1.0
+    return np.concatenate([source, target, join], 0)
+
+
 def high_low(value):
     high = low_bits(value)
     return high, low_bits(value - high.astype(jnp.float32))
@@ -150,7 +169,7 @@
     return copies
 
 
-def pack_kernel(count_in, positions_in, density_in, shift_in, heavy_in, powers_in, own, basis, moments, totals, *rest):
+def pack_kernel(count_in, positions_in, density_in, shift_in, heavy_in, powers_in, picks_in, own, picks, basis, moments, totals, *rest):
     payloads, (count, positions, density, shift, heavy, powers, sems) = rest[:2], rest[2:]
     copies = fetch(
         [
@@ -160,6 +179,7 @@
             (shift_in, shift),
             (heavy_in, heavy),
             (powers_in, powers),
+            (picks_in, picks),
         ],
         sems,
     )
@@ -218,36 +238,38 @@
         payload[:, lanes(4 * pts + LEAVES, 2 * SLOT)] = total
 
 
-def features(held, start, size, centre, target):
-    value = held[16:ROWS, lanes(start, size)].astype(jnp.float32)
-    x = value[1:4] + value[4:7] + by_row(centre, (3, 1))
+def pieces_of(held, start, size, centre, target, picks):
+    join = picks[2 * FEATURES : 2 * FEATURES + 8, 0:8]
+    x = dot(join, held[16:ROWS, lanes(start, size)]) + by_row(centre, (8, 1))
     norm = jnp.sum(x * x, axis=0, keepdims=True)
     if target:
         norm = norm + SOFTENING * SOFTENING
-    parts, norms = [], []
-    for source, out in ((x, parts), (norm, norms)):
-        left = source
-        for _ in range(3):
-            high = low_bits(left).astype(jnp.float32)
-            out.append(high)
-            left = left - high
-    one = jnp.ones_like(norm)
-    zero = jnp.zeros_like(norm)
-    blank = jnp.zeros((3, norm.shape[1]), jnp.float32)
     blocks = []
-    order = (0, 1, 0, 2, 0, 1) if target else (0, 0, 1, 0, 2, 1)
-    for index, which in enumerate(order):
-        coords = -2.0 * parts[which] if target else parts[which]
-        if index < 3:
-            pair = [one, norms[index]] if target else [norms[index], one]
-        else:
-            pair = [zero, zero]
-        blocks += [coords, *pair, blank]
-    return jnp.concatenate(blocks, axis=0)
-
-
-def source_features(held, start, size, centre):
-    return low_bits(jnp.transpose(features(held, start, size, centre, False)))
+    left = x
+    for _ in range(3):
+        high = low_bits(left).astype(jnp.float32)
+        blocks.append(high)
+        left = left - high
+    row = lax.broadcasted_iota(jnp.int32, x.shape, 0)
+    norms = jnp.where(row == 3, 1.0, 0.0)
+    left = norm
+    for piece in range(3):
+        high = low_bits(left).astype(jnp.float32)
+        norms = jnp.where(row == piece, high, norms)
+        left = left - high
+    return low_bits(jnp.concatenate([*blocks, norms], axis=0))
+
+
+def target_features(held, start, size, centre, picks):
+    pieces = pieces_of(held, start, size, centre, True, picks)
+    return low_bits(dot(picks[FEATURES : 2 * FEATURES, :], pieces))
+
+
+def source_features(held, start, size, centre, picks):
+    pieces = pieces_of(held, start, size, centre, False, picks)
+    contract = (((0,), (1,)), ((), ()))
+    picked = lax.dot_general(pieces, picks[0:FEATURES, :], contract, preferred_element_type=jnp.float32)
+    return low_bits(picked)
 
 
 def pulled(near, jobs, target, size, first=None):
@@ -297,7 +319,7 @@
     return jnp.concatenate(blocks, axis=0)
 
 
-def own_kernel(depth, count_in, weights_in, own, *rest):
+def own_kernel(depth, count_in, weights_in, own, picks, *rest):
     tables, outs, (nodes, count, weights, sems) = rest[:3], rest[3:11], rest[11:]
     near, source, target, scale, column, columns, far, spread = outs
     copies = fetch([*zip(tables, (far, spread, nodes)), (count_in, count), (weights_in, weights)], sems)
@@ -305,8 +327,8 @@
     pts = points // 8
     for leaf in range(8):
         centre = [bit - 0.5 for bit in bits(leaf)]
-        source[lanes(leaf * pts, pts), :] = source_features(own, leaf * pts, pts, centre)
-        target[:, lanes(leaf_slot(leaf) * pts, pts)] = low_bits(features(own, leaf * pts, pts, centre, True))
+        source[lanes(leaf * pts, pts), :] = source_features(own, leaf * pts, pts, centre, picks)
+        target[:, lanes(leaf_slot(leaf) * pts, pts)] = target_features(own, leaf * pts, pts, centre, picks)
     own_groups(near, 0, EARLY, target, source, own)
     for copy in copies:
         copy.wait()
@@ -372,18 +394,18 @@
     faces_of(faces_even, above, sums_for(above, left, moments, right, far), own, left, right, row)
 
 
-def side_pulls(near, faces, early, target, scratch):
+def side_pulls(near, faces, early, target, picks, scratch):
     pts = early.shape[1] // 8
     jobs = []
     for (step, side), held in zip(faces, scratch):
         for place in range(4):
             centre = (1.5 if step else -1.5, place % 2 - 0.5, place // 2 - 0.5)
-            held[lanes(place * pts, pts), :] = source_features(side, place * pts, pts, centre)
+            held[lanes(place * pts, pts), :] = source_features(side, place * pts, pts, centre, picks)
         jobs += [(step, held, side, [0, 2 * pts]), (step + 2, held, side, [0, 2 * pts])]
     pulled(near, jobs, target, 2 * pts, early)
 
 
-def middle_kernel(own, left, right, moments, far, early, source, target, near, faces_odd, same, *sides):
+def middle_kernel(own, left, right, moments, far, early, source, target, picks, near, faces_odd, same, *sides):
     points = own.shape[1]
     _, box_z = box_place()
     above = lax.rem(box_z, 2)
@@ -396,14 +418,10 @@
 
     @pl.when(above == 1)
     def _():
-        side_pulls(near, [(0, left), (1, right)], near, target, sides)
-
-    @pl.when(above == 0)
-    def _():
-        side_pulls(near, [(0, left)], near, target, sides)
-
-
-def side_kernel(right, early, target, near, held):
+        side_pulls(near, [(0, left), (1, right)], near, target, picks, sides)
+
+
+def side_kernel(left, right, early, target, picks, near, *sides):
     _, box_z = box_place()
     odd = lax.rem(box_z, 2) == 1
 
@@ -413,20 +431,16 @@
 
     @pl.when(jnp.logical_not(odd))
     def _():
-        pts = early.shape[1] // 8
-        for group in (0, 2):
-            here = lanes(2 * group * pts, 2 * pts)
-            near[:, here] = early[:, here]
-        side_pulls(near, [(1, right)], early, target, [held])
-
-
-def both_kernel(rows, faces, both):
+        side_pulls(near, [(0, left), (1, right)], early, target, picks, sides)
+
+
+def both_kernel(rows, faces, near, both):
     width = rows.shape[1]
     both[:, lanes(0, width)] = rows[...]
     both[:, lanes(width, width)] = faces[:, lanes(faces.shape[1] - width, width)]
 
 
-def layer_pulls(near, early, step, inside, target, faces, sides):
+def layer_pulls(near, early, step, inside, target, picks, faces, sides):
     points = early.shape[1]
     pts = points // 8
 
@@ -435,7 +449,7 @@
         for place in range(8):
             height = jnp.where(step == 1, 1.5, -1.5)
             centre = (place // 2 - 1.5, place % 2 - 0.5, height)
-            sides[lanes(place * pts, pts), :] = source_features(faces, place * pts, pts, centre)
+            sides[lanes(place * pts, pts), :] = source_features(faces, place * pts, pts, centre, picks)
 
         jobs = [(i + 2 * step, sides, faces, [2 * (x + i) * pts for x in range(3)]) for i in range(2)]
         pulled(near, jobs, target, 2 * pts, early)
@@ -446,13 +460,13 @@
         near[:, here] = early[:, here]
 
 
-def even_kernel(early, target, faces, near, sides):
+def even_kernel(early, target, picks, faces, near, sides):
     _, box_z = box_place()
     points = early.shape[1]
     step = 1 - lax.rem(box_z, 2)
     other = lanes((1 - step) * (points // 2), points // 2)
     near[:, other] = early[:, other]
-    layer_pulls(near, early, step, box_z >= 0, target, faces, sides)
+    layer_pulls(near, early, step, box_z >= 0, target, picks, faces, sides)
 
 
 def odd_inside(depth):
@@ -461,12 +475,12 @@
     return step, (box_z + 2 * step - 1 >= 0) & (box_z + 2 * step - 1 < depth)
 
 
-def odd_kernel(depth, early, target, faces, near, sides):
+def odd_kernel(depth, early, target, picks, faces, near, sides):
     points = early.shape[1]
     step, inside = odd_inside(depth)
     other = lanes((1 - step) * (points // 2), points // 2)
     near[:, other] = early[:, other]
-    layer_pulls(near, early, step, inside, target, faces, sides)
+    layer_pulls(near, early, step, inside, target, picks, faces, sides)
 
 
 def last_kernel(depth, near, faces_even, faces_odd, basis, scale, column, columns, spread, same, *rest):
@@ -549,12 +563,13 @@
     near_shape, sums_shape = ((ROWS, points), full), ((ROWS, LEAVES), full)
     side_scratch = [pltpu.VMEM((4 * pts, FEATURES), half)] * 2
     rows_scratch = pltpu.VMEM((8 * pts, FEATURES), half)
-    own, basis, moments, totals, *given = call(
+    own, picks, basis, moments, totals, *given = call(
         pack_kernel,
         "pack",
-        [hbm] * 6,
+        [hbm] * 7,
         [
             ((ROWS, points), half),
+            ((3 * FEATURES, 32), half),
             ((2 * SLOT, points), half),
             ((ROWS, LEAVES), half),
             ((ROWS, 2 * SLOT), half),
@@ -568,7 +583,7 @@
             pltpu.VMEM((LEAVES, SLOT), half),
             pltpu.VMEM((SLOT, SLOT), half),
             pltpu.VMEM((3 * SLOT, 16), half),
-            pltpu.SemaphoreType.DMA((6,)),
+            pltpu.SemaphoreType.DMA((7,)),
         ],
         leaf_count,
         positions,
@@ -576,6 +591,7 @@
         jnp.asarray(shift, half),
         jnp.asarray(heavy_table(), half),
         jnp.asarray(power_table(), half),
+        jnp.asarray(pick_tables(), half),
     )
     from_2 = swapped(totals, "space", lambda i: i ^ 2)
     from_1 = swapped(given[0], "space", lambda i: i ^ 1)
@@ -583,7 +599,7 @@
     near, source, target, scale, column, columns, far, spread = call(
         functools.partial(own_kernel, depth),
         "near_own",
-        [hbm] * 2 + [vmem] + [hbm] * 3,
+        [hbm] * 2 + [vmem] * 2 + [hbm] * 3,
         [
             ((ROWS, EARLY * points // 4), full),
             ((points, FEATURES), half),
@@ -603,6 +619,7 @@
         leaf_count,
         sigma_weights,
         own,
+        picks,
         jnp.asarray(far_table(), half),
         jnp.asarray(shift.T.copy(), half),
         jnp.asarray(box_nodes()),
@@ -625,7 +642,7 @@
     near, faces_odd, same = call(
         middle_kernel,
         "near_middle",
-        [vmem] * 8,
+        [vmem] * 9,
         [near_shape, faces_shape, sums_shape],
         side_scratch,
         own,
@@ -636,33 +653,37 @@
         near,
         source,
         target,
+        picks,
     )
     faces_odd = swapped_odd(faces_odd)
     near, = call(
         side_kernel,
         "near_side",
-        [vmem] * 3,
+        [vmem] * 5,
         [near_shape],
-        side_scratch[:1],
+        side_scratch,
+        left,
         right,
         near,
         target,
+        picks,
     )
     if depth == 4:
-        both, = call(both_kernel, "row_pairs", [vmem] * 2, [both_shape], [], rows, faces_even)
+        both, = call(both_kernel, "row_pairs", [vmem] * 3, [both_shape], [], rows, faces_even, near)
         held = [rows, swapped(both, "space", lambda i: i ^ (2 * ACROSS))]
     else:
         groups = [[z * ACROSS + x for z in range(depth)] for x in range(ACROSS)]
         held = [lax.all_gather(rows, "space", axis_index_groups=groups)]
-    near, = call(even_kernel, "near_even", [vmem] * 3, [near_shape], [rows_scratch], near, target, faces_even)
+    near, = call(even_kernel, "near_even", [vmem] * 4, [near_shape], [rows_scratch], near, target, picks, faces_even)
     near, = call(
         functools.partial(odd_kernel, depth),
         "near_odd",
-        [vmem] * 3,
+        [vmem] * 4,
         [near_shape],
         [rows_scratch],
         near,
         target,
+        picks,
         faces_odd,
     )
     potential, sums = call(

time: 25.6 us -> 28.7 us (1.12)
  Pallas kernels: 13.1 us -> 15.7 us
  starting transfers between devices: 8.78 us -> 11 us
  waiting for transfers between devices: 2.89 us -> 1.19 us
    pallas_call x10, Pallas kernels: 13.1 us -> 15.7 us  [call(): pl.pallas_call(kernel, in_specs=in_specs, out_specs=[vmem] * len(outs), o...]
    ppermute x6, starting transfers between devices: 8.78 us -> 11 us  [swapped(): return lax.ppermute(block, axis, [(partner(i), i) for i in range(size)])]
    ppermute x6, waiting for transfers between devices: 2.89 us -> 1.18 us  [swapped(): return lax.ppermute(block, axis, [(partner(i), i) for i in range(size)])]
  transfers between devices with their start and end apart: 7 -> 7, of which waited for: 3 -> 1; matrix products, arithmetic and copies ran while one was open for 0% -> 0% of each run, Pallas kernels for 34% -> 39%
where the time goes in v22:
time: 28.7 us; the launch traced here: 28.6 us
  Pallas kernels  15.7 us (55%)
  starting transfers between devices  11 us (38%)
  waiting for transfers between devices  1.19 us (4%)
  between operations  0.72 us (3%)
    pallas_call x10, Pallas kernels, call(): pl.pallas_call(kernel, in_specs=in_specs, out_specs=[vmem] * len(outs), o...  15.7 us
    ppermute x6, starting transfers between devices, swapped(): return lax.ppermute(block, axis, [(partner(i), i) for i in range(size)])  11 us
    ppermute x6, waiting for transfers between devices, swapped(): return lax.ppermute(block, axis, [(partner(i), i) for i in range(size)])  1.18 us
  transfers between devices with their start and end apart: 7, of which 1 were waited for; matrix products, arithmetic and copies ran while one was open for 0% of the time, Pallas kernels for 39%

profile of v22, /device:TPU:0, one launch (start us, length us, event | category | flops | bytes accessed | tf_op | source)
XLA Modules:
  0.0 28.6 jit_solution(15165887237110797799)
XLA Ops:
  0.6 1.9 %pack.1 = (bf16[24,2048]{1,0:T(8,128)(2,1)S(1)}, bf16[96,32]{1,0:T(8,128)(2,1)S(1)}, bf16[128,2048]{1,0:T(8,128)(2,1)S(1)}, bf16[24,512]{1,0:T(8,128)(2,1)S(1)},...) custom-call(s32[8]{0:T(128)} %count_in.3, f32[3,2048]{1,0:T(4,128)} %positions_in.1, ...), custom_call_target="tpu_custom_call" | custom-call | tf_op jit(solution)/shard_map/pack/pallas_call | solution.py:545
  2.6 3.0 %collective-permute-start = (bf16[24,1664]{1,0:T(8,128)(2,1)S(1)}, bf16[24,1664]{1,0:T(8,128)(2,1)S(1)}, u32[]{:S(2)}, u32[]{:S(2)}) collective-permute-start(bf16[24,1664]{1,0:T(8,128)(2,1)S(1)} %get-tuple-element.29), channel_id=1, source_target_pairs={{2,0},{0,2},{6,4},{4,6},{10,8},{8,10},{14,12},{12,14},{18,16},{16,... | collective-permute-start | bytes 239624 | tf_op jit(solution)/shard_map/ppermute | solution.py:524
  5.6 1.5 %collective-permute-start.2 = (bf16[24,1664]{1,0:T(8,128)(2,1)S(1)}, bf16[24,1664]{1,0:T(8,128)(2,1)S(1)}, u32[]{:S(2)}, u32[]{:S(2)}) collective-permute-start(bf16[24,1664]{1,0:T(8,128)(2,1)S(1)} %get-tuple-element.30), channel_id=1, source_target_pairs={{6,0},{4,2},{2,4},{0,6},{14,8},{12,10},{10,12},{8,14},{22,16},{20,... | collective-permute-start | bytes 239624 | tf_op jit(solution)/shard_map/ppermute | solution.py:524
  7.0 0.1 collective-permute-start.1
  7.1 4.5 %near_own.1 = (f32[24,1536]{1,0:T(8,128)S(1)}, bf16[2048,32]{1,0:T(8,128)(2,1)S(1)}, bf16[32,2048]{1,0:T(8,128)(2,1)S(1)}, f32[1,2048]{1,0:T(1,128)S(1)}, f32[24...) custom-call(s32[8]{0:T(128)} %count_in.3, ...), custom_call_target="tpu_custom_call" | custom-call | tf_op jit(solution)/shard_map/near_own/pallas_call | solution.py:545
  11.6 0.0 collective-permute-done.1.from_2
  11.6 0.0 collective-permute-done.from_1
  11.7 0.0 collective-permute-done.2.from_3
  11.7 0.5 %row.1 = (bf16[24,1536]{1,0:T(8,128)(2,1)S(1)}, bf16[24,1536]{1,0:T(8,128)(2,1)S(1)}, bf16[24,2816]{1,0:T(8,128)(2,1)S(1)}, bf16[24,256]{1,0:T(8,128)(2,1)S(1)}) custom-call(bf16[24,2048]{1,0:T(8,128)(2,1)S(1)} %get-tuple-element.26.own, bf16[24,512]{1,0:T(8,128)(2,1)S(1)} %get-tuple-element.27.moments, bf16[24,128]{1,0:T(8,128)(2,1)S(1)} %get-tuple-element.28.totals, ...), custom_call_target="tpu_custom_call" | custom-call | tf_op jit(solution)/shard_map/row/pallas_call | solution.py:545
  12.2 2.1 %collective-permute-start.3 = (bf16[24,2816]{1,0:T(8,128)(2,1)S(1)}, bf16[24,2816]{1,0:T(8,128)(2,1)S(1)}, u32[]{:S(2)}, u32[]{:S(2)}) collective-permute-start(bf16[24,2816]{1,0:T(8,128)(2,1)S(1)} %get-tuple-element.39), channel_id=1, source_target_pairs={{8,0},{10,2},{12,4},{14,6},{0,8},{2,10},{4,12},{6,14},{24,16},{26,... | collective-permute-start | bytes 405512 | tf_op jit(solution)/shard_map/ppermute | solution.py:524
  14.3 1.5 %near_middle.1 = (f32[24,2048]{1,0:T(8,128)S(1)}, bf16[24,2560]{1,0:T(8,128)(2,1)S(1)}, f32[24,512]{1,0:T(8,128)S(1)}) custom-call(bf16[24,2048]{1,0:T(8,128)(2,1)S(1)} %get-tuple-element.26.own, bf16[24,1536]{1,0:T(8,128)(2,1)S(1)} %get-tuple-element.33.left, bf16[24,1536]{1,0:T(8,128)(2,1)S(1)} %get-tuple-element.34.right, ...), custom_call_target="tpu_custom_call" | custom-call | tf_op jit(solution)/shard_map/near_middle/pallas_call | solution.py:545
  15.8 0.0 collective-permute-start.4
  15.8 2.8 %near_side.1.early.near = f32[24,2048]{1,0:T(8,128)S(1)} custom-call(bf16[24,1536]{1,0:T(8,128)(2,1)S(1)} %get-tuple-element.33.left, bf16[24,1536]{1,0:T(8,128)(2,1)S(1)} %get-tuple-element.34.right, f32[24,2048]{1,0:T(8,128)S(1)} %get-tuple-element.38.early, bf16[32,2048]{1,0:T(8,128)(2,1)S(1)} %get-tuple-element.37.target, ...), custom_call_target="tpu_custom_call" | custom-call | tf_op jit(solution)/shard_map/near_side/pallas_call | solution.py:545
  18.6 0.0 collective-permute-done.3.faces.faces_even
  18.6 4.3 %collective-permute-start.5 = (bf16[24,512]{1,0:T(8,128)(2,1)S(1)}, bf16[24,512]{1,0:T(8,128)(2,1)S(1)}, u32[]{:S(2)}, u32[]{:S(2)}) collective-permute-start(bf16[24,512]{1,0:T(8,128)(2,1)S(1)} %row_pairs.1), channel_id=1, source_target_pairs={{16,0},{18,2},{20,4},{22,6},{24,8},{26,10},{28,12},{30,14},{0,16},... | collective-permute-start | bytes 73736 | tf_op jit(solution)/shard_map/ppermute | solution.py:524
  22.9 2.4 %near_even.1.early = f32[24,2048]{1,0:T(8,128)S(1)} custom-call(f32[24,2048]{1,0:T(8,128)S(1)} %near_side.1.early.near, bf16[32,2048]{1,0:T(8,128)(2,1)S(1)} %get-tuple-element.37.target, bf16[96,32]{1,0:T(8,128)(2,1)S(1)} %get-tuple-element.31.picks, bf16[24,2816]{1,0:T(8,128)(2,1)S(1)} %collective-permute-done.3.faces.faces_even), custom_call_target="tpu_custom_call" | custom-call | tf_op jit(solution)/shard_map/near_even/pallas_call | solution.py:545
  25.3 0.0 collective-permute-done.4.faces.faces_odd
  25.4 0.0 collective-permute-done.5.rest_1_
  25.4 1.3 %evaluate.1 = (f32[17,2048]{1,0:T(8,128)}, f32[1,2176]{1,0:T(1,128)S(1)}) custom-call(f32[24,2048]{1,0:T(8,128)S(1)} %near_odd.1.near, bf16[24,2816]{1,0:T(8,128)(2,1)S(1)} %collective-permute-done.3.faces.faces_even, bf16[24,2560]{1,0:T(8,128)(2,1)S(1)} %collective-permute-done.4.faces.faces_odd, bf16[128,2048]{1,0:T(8,128)(2,1)S(1)} %get-tuple-element.41.basis, ...), custom_call_target="tpu_custom_call" | custom-call | tf_op jit(solution)/shard_map/evaluate/pallas_call | solution.py:545
  26.7 0.0 collective-permute-start.6
  26.7 1.2 %collective-permute-done.6.other = f32[1,2176]{1,0:T(1,128)S(1)} collective-permute-done((f32[1,2176]{1,0:T(1,128)S(1)}, f32[1,2176]{1,0:T(1,128)S(1)}, u32[]{:S(2)}, u32[]{:S(2)}) %collective-permute-start.6) | collective-permute-done | bytes 8736 | tf_op jit(solution)/shard_map/ppermute | solution.py:524
  27.9 0.7 %mean.1 = f32[1,2048]{1,0:T(1,128)} custom-call(f32[1,2176]{1,0:T(1,128)S(1)} %get-tuple-element.49.mine, f32[1,2176]{1,0:T(1,128)S(1)} %collective-permute-done.6.other), custom_call_target="tpu_custom_call" | custom-call | tf_op jit(solution)/shard_map/mean/pallas_call | solution.py:545
  (2 shorter events, 0.0 us)
Async XLA Ops:
  2.6 9.1 %collective-permute-start = (bf16[24,1664]{1,0:T(8,128)(2,1)S(1)}, bf16[24,1664]{1,0:T(8,128)(2,1)S(1)}, u32[]{:S(2)}, u32[]{:S(2)}) collective-permute-start(bf16[24,1664]{1,0:T(8,128)(2,1)S(1)} %get-tuple-element.29), channel_id=1, source_target_pairs={{2,0},{0,2},{6,4},{4,6},{10,8},{8,10},{14,12},{12,14},{18,16},{16,... | collective-permute-start | bytes 239624 | tf_op jit(solution)/shard_map/ppermute | solution.py:524
  5.6 6.1 %collective-permute-start.2 = (bf16[24,1664]{1,0:T(8,128)(2,1)S(1)}, bf16[24,1664]{1,0:T(8,128)(2,1)S(1)}, u32[]{:S(2)}, u32[]{:S(2)}) collective-permute-start(bf16[24,1664]{1,0:T(8,128)(2,1)S(1)} %get-tuple-element.30), channel_id=1, source_target_pairs={{6,0},{4,2},{2,4},{0,6},{14,8},{12,10},{10,12},{8,14},{22,16},{20,... | collective-permute-start | bytes 239624 | tf_op jit(solution)/shard_map/ppermute | solution.py:524
  7.0 4.6 %collective-permute-start.1 = (bf16[24,128]{1,0:T(8,128)(2,1)S(1)}, bf16[24,128]{1,0:T(8,128)(2,1)S(1)}, u32[]{:S(2)}, u32[]{:S(2)}) collective-permute-start(bf16[24,128]{1,0:T(8,128)(2,1)S(1)} %get-tuple-element.28.totals), channel_id=1, source_target_pairs={{4,0},{6,2},{0,4},{2,6},{12,8},{14,10},{8,12},{10,14},{20,16},{22,... | collective-permute-start | bytes 18440 | tf_op jit(solution)/shard_map/ppermute | solution.py:524
  12.2 6.4 %collective-permute-start.3 = (bf16[24,2816]{1,0:T(8,128)(2,1)S(1)}, bf16[24,2816]{1,0:T(8,128)(2,1)S(1)}, u32[]{:S(2)}, u32[]{:S(2)}) collective-permute-start(bf16[24,2816]{1,0:T(8,128)(2,1)S(1)} %get-tuple-element.39), channel_id=1, source_target_pairs={{8,0},{10,2},{12,4},{14,6},{0,8},{2,10},{4,12},{6,14},{24,16},{26,... | collective-permute-start | bytes 405512 | tf_op jit(solution)/shard_map/ppermute | solution.py:524
  15.8 9.5 %collective-permute-start.4 = (bf16[24,2560]{1,0:T(8,128)(2,1)S(1)}, bf16[24,2560]{1,0:T(8,128)(2,1)S(1)}, u32[]{:S(2)}, u32[]{:S(2)}) collective-permute-start(bf16[24,2560]{1,0:T(8,128)(2,1)S(1)} %get-tuple-element.40), channel_id=1, source_target_pairs={{1,0},{0,1},{3,2},{2,3},{5,4},{4,5},{7,6},{6,7},{16,8},{17,9},{18,... | collective-permute-start | bytes 368648 | tf_op jit(solution)/shard_map/ppermute | solution.py:535
  18.6 6.8 %collective-permute-start.5 = (bf16[24,512]{1,0:T(8,128)(2,1)S(1)}, bf16[24,512]{1,0:T(8,128)(2,1)S(1)}, u32[]{:S(2)}, u32[]{:S(2)}) collective-permute-start(bf16[24,512]{1,0:T(8,128)(2,1)S(1)} %row_pairs.1), channel_id=1, source_target_pairs={{16,0},{18,2},{20,4},{22,6},{24,8},{26,10},{28,12},{30,14},{0,16},... | collective-permute-start | bytes 73736 | tf_op jit(solution)/shard_map/ppermute | solution.py:524
  26.7 1.2 %collective-permute-start.6 = (f32[1,2176]{1,0:T(1,128)S(1)}, f32[1,2176]{1,0:T(1,128)S(1)}, u32[]{:S(2)}, u32[]{:S(2)}) collective-permute-start(f32[1,2176]{1,0:T(1,128)S(1)} %get-tuple-element.49.mine), channel_id=1, source_target_pairs={{1,0},{0,1},{3,2},{2,3},{5,4},{4,5},{7,6},{6,7},{9,8},{8,9},{11,10... | collective-permute-start | bytes 26120 | tf_op jit(solution)/shard_map/ppermute | solution.py:524

commit v23 on v21

--- a/solution.py
+++ b/solution.py
@@ -398,12 +398,8 @@
     def _():
         side_pulls(near, [(0, left), (1, right)], near, target, sides)
 
-    @pl.when(above == 0)
-    def _():
-        side_pulls(near, [(0, left)], near, target, sides)
-
-
-def side_kernel(right, early, target, near, held):
+
+def side_kernel(left, right, early, target, near, *sides):
     _, box_z = box_place()
     odd = lax.rem(box_z, 2) == 1
 
@@ -413,14 +409,10 @@
 
     @pl.when(jnp.logical_not(odd))
     def _():
-        pts = early.shape[1] // 8
-        for group in (0, 2):
-            here = lanes(2 * group * pts, 2 * pts)
-            near[:, here] = early[:, here]
-        side_pulls(near, [(1, right)], early, target, [held])
-
-
-def both_kernel(rows, faces, both):
+        side_pulls(near, [(0, left), (1, right)], early, target, sides)
+
+
+def both_kernel(rows, faces, near, both):
     width = rows.shape[1]
     both[:, lanes(0, width)] = rows[...]
     both[:, lanes(width, width)] = faces[:, lanes(faces.shape[1] - width, width)]
@@ -641,15 +633,16 @@
     near, = call(
         side_kernel,
         "near_side",
-        [vmem] * 3,
+        [vmem] * 4,
         [near_shape],
-        side_scratch[:1],
+        side_scratch,
+        left,
         right,
         near,
         target,
     )
     if depth == 4:
-        both, = call(both_kernel, "row_pairs", [vmem] * 2, [both_shape], [], rows, faces_even)
+        both, = call(both_kernel, "row_pairs", [vmem] * 3, [both_shape], [], rows, faces_even, near)
         held = [rows, swapped(both, "space", lambda i: i ^ (2 * ACROSS))]
     else:
         groups = [[z * ACROSS + x for z in range(depth)] for x in range(ACROSS)]

time: 25.6 us -> 26.2 us (1.023)
  starting transfers between devices: 8.78 us -> 10.2 us
  waiting for transfers between devices: 2.89 us -> 2.34 us
  Pallas kernels: 13.1 us -> 12.7 us
    ppermute x6, starting transfers between devices: 8.78 us -> 10.2 us  [swapped(): return lax.ppermute(block, axis, [(partner(i), i) for i in range(size)])]
    ppermute x6, waiting for transfers between devices: 2.89 us -> 2.34 us  [swapped(): return lax.ppermute(block, axis, [(partner(i), i) for i in range(size)])]
    pallas_call x10, Pallas kernels: 13.1 us -> 12.7 us  [call(): pl.pallas_call(kernel, in_specs=in_specs, out_specs=[vmem] * len(outs), o...]
  transfers between devices with their start and end apart: 7 -> 7, of which waited for: 3 -> 3; matrix products, arithmetic and copies ran while one was open for 0% -> 0% of each run, Pallas kernels for 34% -> 32%
where the time goes in v23:
time: 26.2 us; the launch traced here: 26 us
  Pallas kernels  12.7 us (48%)
  starting transfers between devices  10.2 us (39%)
  waiting for transfers between devices  2.34 us (9%)
  between operations  0.69 us (3%)
    pallas_call x10, Pallas kernels, call(): pl.pallas_call(kernel, in_specs=in_specs, out_specs=[vmem] * len(outs), o...  12.7 us
    ppermute x6, starting transfers between devices, swapped(): return lax.ppermute(block, axis, [(partner(i), i) for i in range(size)])  10.2 us
    ppermute x6, waiting for transfers between devices, swapped(): return lax.ppermute(block, axis, [(partner(i), i) for i in range(size)])  2.34 us
  transfers between devices with their start and end apart: 7, of which 3 were waited for; matrix products, arithmetic and copies ran while one was open for 0% of the time, Pallas kernels for 32%

profile of v23, /device:TPU:0, one launch (start us, length us, event | category | flops | bytes accessed | tf_op | source)
XLA Modules:
  0.0 26.0 jit_solution(11248342927815229337)
XLA Ops:
  0.6 1.9 %pack.1 = (bf16[24,2048]{1,0:T(8,128)(2,1)S(1)}, bf16[128,2048]{1,0:T(8,128)(2,1)S(1)}, bf16[24,512]{1,0:T(8,128)(2,1)S(1)}, bf16[24,128]{1,0:T(8,128)(2,1)S(1)}...) custom-call(s32[8]{0:T(128)} %count_in.3, f32[3,2048]{1,0:T(4,128)} %positions_in.1, ...), custom_call_target="tpu_custom_call" | custom-call | tf_op jit(solution)/shard_map/pack/pallas_call | solution.py:523
  2.5 3.0 %collective-permute-start = (bf16[24,1664]{1,0:T(8,128)(2,1)S(1)}, bf16[24,1664]{1,0:T(8,128)(2,1)S(1)}, u32[]{:S(2)}, u32[]{:S(2)}) collective-permute-start(bf16[24,1664]{1,0:T(8,128)(2,1)S(1)} %get-tuple-element.28), channel_id=1, source_target_pairs={{2,0},{0,2},{6,4},{4,6},{10,8},{8,10},{14,12},{12,14},{18,16},{16,... | collective-permute-start | bytes 239624 | tf_op jit(solution)/shard_map/ppermute | solution.py:502
  5.6 1.5 %collective-permute-start.2 = (bf16[24,1664]{1,0:T(8,128)(2,1)S(1)}, bf16[24,1664]{1,0:T(8,128)(2,1)S(1)}, u32[]{:S(2)}, u32[]{:S(2)}) collective-permute-start(bf16[24,1664]{1,0:T(8,128)(2,1)S(1)} %get-tuple-element.29), channel_id=1, source_target_pairs={{6,0},{4,2},{2,4},{0,6},{14,8},{12,10},{10,12},{8,14},{22,16},{20,... | collective-permute-start | bytes 239624 | tf_op jit(solution)/shard_map/ppermute | solution.py:502
  7.0 0.1 collective-permute-start.1
  7.1 3.1 %near_own.1 = (f32[24,1536]{1,0:T(8,128)S(1)}, bf16[2048,48]{1,0:T(8,128)(2,1)S(1)}, bf16[48,2048]{1,0:T(8,128)(2,1)S(1)}, f32[1,2048]{1,0:T(1,128)S(1)}, f32[24...) custom-call(s32[8]{0:T(128)} %count_in.3, ...), custom_call_target="tpu_custom_call" | custom-call | tf_op jit(solution)/shard_map/near_own/pallas_call | solution.py:523
  10.2 1.0 %collective-permute-done.1.from_2 = bf16[24,128]{1,0:T(8,128)(2,1)S(1)} collective-permute-done((bf16[24,128]{1,0:T(8,128)(2,1)S(1)}, bf16[24,128]{1,0:T(8,128)(2,1)S(1)}, u32[]{:S(2)}, u32[]{:S(2)}) %collective-permute-start.1) | collective-permute-done | bytes 6176 | tf_op jit(solution)/shard_map/ppermute | solution.py:502
  11.2 0.0 collective-permute-done.from_1
  11.2 0.0 collective-permute-done.2.from_3
  11.2 0.5 %row.1 = (bf16[24,1536]{1,0:T(8,128)(2,1)S(1)}, bf16[24,1536]{1,0:T(8,128)(2,1)S(1)}, bf16[24,2816]{1,0:T(8,128)(2,1)S(1)}, bf16[24,256]{1,0:T(8,128)(2,1)S(1)}) custom-call(bf16[24,2048]{1,0:T(8,128)(2,1)S(1)} %get-tuple-element.25.own, bf16[24,512]{1,0:T(8,128)(2,1)S(1)} %get-tuple-element.26.moments, bf16[24,128]{1,0:T(8,128)(2,1)S(1)} %get-tuple-element.27.totals, ...), custom_call_target="tpu_custom_call" | custom-call | tf_op jit(solution)/shard_map/row/pallas_call | solution.py:523
  11.7 1.6 %collective-permute-start.3 = (bf16[24,2816]{1,0:T(8,128)(2,1)S(1)}, bf16[24,2816]{1,0:T(8,128)(2,1)S(1)}, u32[]{:S(2)}, u32[]{:S(2)}) collective-permute-start(bf16[24,2816]{1,0:T(8,128)(2,1)S(1)} %get-tuple-element.37), channel_id=1, source_target_pairs={{8,0},{10,2},{12,4},{14,6},{0,8},{2,10},{4,12},{6,14},{24,16},{26,... | collective-permute-start | bytes 405512 | tf_op jit(solution)/shard_map/ppermute | solution.py:502
  13.4 1.5 %near_middle.1 = (f32[24,2048]{1,0:T(8,128)S(1)}, bf16[24,2560]{1,0:T(8,128)(2,1)S(1)}, f32[24,512]{1,0:T(8,128)S(1)}) custom-call(bf16[24,2048]{1,0:T(8,128)(2,1)S(1)} %get-tuple-element.25.own, bf16[24,1536]{1,0:T(8,128)(2,1)S(1)} %get-tuple-element.31.left, bf16[24,1536]{1,0:T(8,128)(2,1)S(1)} %get-tuple-element.32.right, ...), custom_call_target="tpu_custom_call" | custom-call | tf_op jit(solution)/shard_map/near_middle/pallas_call | solution.py:523
  14.9 0.0 collective-permute-start.4
  14.9 2.0 %near_side.1.early.near = f32[24,2048]{1,0:T(8,128)S(1)} custom-call(bf16[24,1536]{1,0:T(8,128)(2,1)S(1)} %get-tuple-element.31.left, bf16[24,1536]{1,0:T(8,128)(2,1)S(1)} %get-tuple-element.32.right, f32[24,2048]{1,0:T(8,128)S(1)} %get-tuple-element.36.early, bf16[48,2048]{1,0:T(8,128)(2,1)S(1)} %get-tuple-element.35.target), custom_call_target="tpu_custom_call" | custom-call | tf_op jit(solution)/shard_map/near_side/pallas_call | solution.py:523
  16.9 0.0 collective-permute-done.3.faces.faces_even
  17.0 4.0 %collective-permute-start.5 = (bf16[24,512]{1,0:T(8,128)(2,1)S(1)}, bf16[24,512]{1,0:T(8,128)(2,1)S(1)}, u32[]{:S(2)}, u32[]{:S(2)}) collective-permute-start(bf16[24,512]{1,0:T(8,128)(2,1)S(1)} %row_pairs.1), channel_id=1, source_target_pairs={{16,0},{18,2},{20,4},{22,6},{24,8},{26,10},{28,12},{30,14},{0,16},... | collective-permute-start | bytes 73736 | tf_op jit(solution)/shard_map/ppermute | solution.py:502
  21.0 1.6 %near_even.1.early = f32[24,2048]{1,0:T(8,128)S(1)} custom-call(f32[24,2048]{1,0:T(8,128)S(1)} %near_side.1.early.near, bf16[48,2048]{1,0:T(8,128)(2,1)S(1)} %get-tuple-element.35.target, bf16[24,2816]{1,0:T(8,128)(2,1)S(1)} %collective-permute-done.3.faces.faces_even), custom_call_target="tpu_custom_call" | custom-call | tf_op jit(solution)/shard_map/near_even/pallas_call | solution.py:523
  22.6 0.0 collective-permute-done.4.faces.faces_odd
  22.6 0.2 collective-permute-done.5.rest_1_
  22.8 1.3 %evaluate.1 = (f32[17,2048]{1,0:T(8,128)}, f32[1,2176]{1,0:T(1,128)S(1)}) custom-call(f32[24,2048]{1,0:T(8,128)S(1)} %near_odd.1.near, bf16[24,2816]{1,0:T(8,128)(2,1)S(1)} %collective-permute-done.3.faces.faces_even, bf16[24,2560]{1,0:T(8,128)(2,1)S(1)} %collective-permute-done.4.faces.faces_odd, bf16[128,2048]{1,0:T(8,128)(2,1)S(1)} %get-tuple-element.39.basis, ...), custom_call_target="tpu_custom_call" | custom-call | tf_op jit(solution)/shard_map/evaluate/pallas_call | solution.py:523
  24.1 0.0 collective-permute-start.6
  24.1 1.2 %collective-permute-done.6.other = f32[1,2176]{1,0:T(1,128)S(1)} collective-permute-done((f32[1,2176]{1,0:T(1,128)S(1)}, f32[1,2176]{1,0:T(1,128)S(1)}, u32[]{:S(2)}, u32[]{:S(2)}) %collective-permute-start.6) | collective-permute-done | bytes 8736 | tf_op jit(solution)/shard_map/ppermute | solution.py:502
  25.3 0.7 %mean.1 = f32[1,2048]{1,0:T(1,128)} custom-call(f32[1,2176]{1,0:T(1,128)S(1)} %get-tuple-element.47.mine, f32[1,2176]{1,0:T(1,128)S(1)} %collective-permute-done.6.other), custom_call_target="tpu_custom_call" | custom-call | tf_op jit(solution)/shard_map/mean/pallas_call | solution.py:523
  (2 shorter events, 0.0 us)
Async XLA Ops:
  2.5 8.7 %collective-permute-start = (bf16[24,1664]{1,0:T(8,128)(2,1)S(1)}, bf16[24,1664]{1,0:T(8,128)(2,1)S(1)}, u32[]{:S(2)}, u32[]{:S(2)}) collective-permute-start(bf16[24,1664]{1,0:T(8,128)(2,1)S(1)} %get-tuple-element.28), channel_id=1, source_target_pairs={{2,0},{0,2},{6,4},{4,6},{10,8},{8,10},{14,12},{12,14},{18,16},{16,... | collective-permute-start | bytes 239624 | tf_op jit(solution)/shard_map/ppermute | solution.py:502
  5.6 5.7 %collective-permute-start.2 = (bf16[24,1664]{1,0:T(8,128)(2,1)S(1)}, bf16[24,1664]{1,0:T(8,128)(2,1)S(1)}, u32[]{:S(2)}, u32[]{:S(2)}) collective-permute-start(bf16[24,1664]{1,0:T(8,128)(2,1)S(1)} %get-tuple-element.29), channel_id=1, source_target_pairs={{6,0},{4,2},{2,4},{0,6},{14,8},{12,10},{10,12},{8,14},{22,16},{20,... | collective-permute-start | bytes 239624 | tf_op jit(solution)/shard_map/ppermute | solution.py:502
  7.0 4.2 %collective-permute-start.1 = (bf16[24,128]{1,0:T(8,128)(2,1)S(1)}, bf16[24,128]{1,0:T(8,128)(2,1)S(1)}, u32[]{:S(2)}, u32[]{:S(2)}) collective-permute-start(bf16[24,128]{1,0:T(8,128)(2,1)S(1)} %get-tuple-element.27.totals), channel_id=1, source_target_pairs={{4,0},{6,2},{0,4},{2,6},{12,8},{14,10},{8,12},{10,14},{20,16},{22,... | collective-permute-start | bytes 18440 | tf_op jit(solution)/shard_map/ppermute | solution.py:502
  11.7 5.2 %collective-permute-start.3 = (bf16[24,2816]{1,0:T(8,128)(2,1)S(1)}, bf16[24,2816]{1,0:T(8,128)(2,1)S(1)}, u32[]{:S(2)}, u32[]{:S(2)}) collective-permute-start(bf16[24,2816]{1,0:T(8,128)(2,1)S(1)} %get-tuple-element.37), channel_id=1, source_target_pairs={{8,0},{10,2},{12,4},{14,6},{0,8},{2,10},{4,12},{6,14},{24,16},{26,... | collective-permute-start | bytes 405512 | tf_op jit(solution)/shard_map/ppermute | solution.py:502
  14.9 7.7 %collective-permute-start.4 = (bf16[24,2560]{1,0:T(8,128)(2,1)S(1)}, bf16[24,2560]{1,0:T(8,128)(2,1)S(1)}, u32[]{:S(2)}, u32[]{:S(2)}) collective-permute-start(bf16[24,2560]{1,0:T(8,128)(2,1)S(1)} %get-tuple-element.38), channel_id=1, source_target_pairs={{1,0},{0,1},{3,2},{2,3},{5,4},{4,5},{7,6},{6,7},{16,8},{17,9},{18,... | collective-permute-start | bytes 368648 | tf_op jit(solution)/shard_map/ppermute | solution.py:513
  17.0 5.8 %collective-permute-start.5 = (bf16[24,512]{1,0:T(8,128)(2,1)S(1)}, bf16[24,512]{1,0:T(8,128)(2,1)S(1)}, u32[]{:S(2)}, u32[]{:S(2)}) collective-permute-start(bf16[24,512]{1,0:T(8,128)(2,1)S(1)} %row_pairs.1), channel_id=1, source_target_pairs={{16,0},{18,2},{20,4},{22,6},{24,8},{26,10},{28,12},{30,14},{0,16},... | collective-permute-start | bytes 73736 | tf_op jit(solution)/shard_map/ppermute | solution.py:502
  24.1 1.2 %collective-permute-start.6 = (f32[1,2176]{1,0:T(1,128)S(1)}, f32[1,2176]{1,0:T(1,128)S(1)}, u32[]{:S(2)}, u32[]{:S(2)}) collective-permute-start(f32[1,2176]{1,0:T(1,128)S(1)} %get-tuple-element.47.mine), channel_id=1, source_target_pairs={{1,0},{0,1},{3,2},{2,3},{5,4},{4,5},{7,6},{6,7},{9,8},{8,9},{11,10... | collective-permute-start | bytes 26120 | tf_op jit(solution)/shard_map/ppermute | solution.py:502

commit v24 on v23

--- a/solution.py
+++ b/solution.py
@@ -396,20 +396,28 @@
 
     @pl.when(above == 1)
     def _():
-        side_pulls(near, [(0, left), (1, right)], near, target, sides)
-
-
-def side_kernel(left, right, early, target, near, *sides):
+        side_pulls(near, [(0, left)], near, target, sides)
+
+
+def one_side(near, step, side, early, target, held):
+    pts = early.shape[1] // 8
+    for group in (1 - step, 3 - step):
+        here = lanes(2 * group * pts, 2 * pts)
+        near[:, here] = early[:, here]
+    side_pulls(near, [(step, side)], early, target, [held])
+
+
+def side_kernel(left, right, early, target, near, held):
     _, box_z = box_place()
     odd = lax.rem(box_z, 2) == 1
 
     @pl.when(odd)
     def _():
-        near[...] = early[...]
+        one_side(near, 1, right, early, target, held)
 
     @pl.when(jnp.logical_not(odd))
     def _():
-        side_pulls(near, [(0, left), (1, right)], early, target, sides)
+        one_side(near, 0, left, early, target, held)
 
 
 def both_kernel(rows, faces, near, both):
@@ -438,13 +446,19 @@
         near[:, here] = early[:, here]
 
 
-def even_kernel(early, target, faces, near, sides):
+def even_kernel(early, target, right, faces, near, sides, held):
     _, box_z = box_place()
-    points = early.shape[1]
     step = 1 - lax.rem(box_z, 2)
-    other = lanes((1 - step) * (points // 2), points // 2)
-    near[:, other] = early[:, other]
-    layer_pulls(near, early, step, box_z >= 0, target, faces, sides)
+
+    @pl.when(step == 0)
+    def _():
+        near[...] = early[...]
+
+    @pl.when(step == 1)
+    def _():
+        one_side(near, 1, right, early, target, held)
+
+    layer_pulls(near, near, step, box_z >= 0, target, faces, sides)
 
 
 def odd_inside(depth):
@@ -539,7 +553,7 @@
     rows_shape = ((ROWS, SLOT * ACROSS), half)
     both_shape = ((ROWS, 2 * SLOT * ACROSS), half)
     near_shape, sums_shape = ((ROWS, points), full), ((ROWS, LEAVES), full)
-    side_scratch = [pltpu.VMEM((4 * pts, FEATURES), half)] * 2
+    side_scratch = pltpu.VMEM((4 * pts, FEATURES), half)
     rows_scratch = pltpu.VMEM((8 * pts, FEATURES), half)
     own, basis, moments, totals, *given = call(
         pack_kernel,
@@ -619,7 +633,7 @@
         "near_middle",
         [vmem] * 8,
         [near_shape, faces_shape, sums_shape],
-        side_scratch,
+        [side_scratch],
         own,
         left,
         right,
@@ -635,7 +649,7 @@
         "near_side",
         [vmem] * 4,
         [near_shape],
-        side_scratch,
+        [side_scratch],
         left,
         right,
         near,
@@ -647,7 +661,17 @@
     else:
         groups = [[z * ACROSS + x for z in range(depth)] for x in range(ACROSS)]
         held = [lax.all_gather(rows, "space", axis_index_groups=groups)]
-    near, = call(even_kernel, "near_even", [vmem] * 3, [near_shape], [rows_scratch], near, target, faces_even)
+    near, = call(
+        even_kernel,
+        "near_even",
+        [vmem] * 4,
+        [near_shape],
+        [rows_scratch, side_scratch],
+        near,
+        target,
+        right,
+        faces_even,
+    )
     near, = call(
         functools.partial(odd_kernel, depth),
         "near_odd",

time: 26.2 us -> 25.6 us (0.977)
  starting transfers between devices: 10.2 us -> 8.78 us
  waiting for transfers between devices: 2.34 us -> 2.9 us
  Pallas kernels: 12.7 us -> 13 us
    ppermute x6, starting transfers between devices: 10.2 us -> 8.78 us  [swapped(): return lax.ppermute(block, axis, [(partner(i), i) for i in range(size)])]
    ppermute x6, waiting for transfers between devices: 2.34 us -> 2.89 us  [swapped(): return lax.ppermute(block, axis, [(partner(i), i) for i in range(size)])]
    pallas_call x10, Pallas kernels: 12.7 us -> 13 us  [call(): pl.pallas_call(kernel, in_specs=in_specs, out_specs=[vmem] * len(outs), o...]
  transfers between devices with their start and end apart: 7 -> 7, of which waited for: 3 -> 3; matrix products, arithmetic and copies ran while one was open for 0% -> 0% of each run, Pallas kernels for 32% -> 34%
where the time goes in v24:
time: 25.6 us; the launch traced here: 25.4 us
  Pallas kernels  13 us (51%)
  starting transfers between devices  8.78 us (34%)
  waiting for transfers between devices  2.9 us (11%)
  between operations  0.69 us (3%)
    pallas_call x10, Pallas kernels, call(): pl.pallas_call(kernel, in_specs=in_specs, out_specs=[vmem] * len(outs), o...  13 us
    ppermute x6, starting transfers between devices, swapped(): return lax.ppermute(block, axis, [(partner(i), i) for i in range(size)])  8.78 us
    ppermute x6, waiting for transfers between devices, swapped(): return lax.ppermute(block, axis, [(partner(i), i) for i in range(size)])  2.89 us
  transfers between devices with their start and end apart: 7, of which 3 were waited for; matrix products, arithmetic and copies ran while one was open for 0% of the time, Pallas kernels for 34%

profile of v24, /device:TPU:0, one launch (start us, length us, event | category | flops | bytes accessed | tf_op | source)
XLA Modules:
  0.0 25.4 jit_solution(6206377536783464025)
XLA Ops:
  0.6 1.9 %pack.1 = (bf16[24,2048]{1,0:T(8,128)(2,1)S(1)}, bf16[128,2048]{1,0:T(8,128)(2,1)S(1)}, bf16[24,512]{1,0:T(8,128)(2,1)S(1)}, bf16[24,128]{1,0:T(8,128)(2,1)S(1)}...) custom-call(s32[8]{0:T(128)} %count_in.3, f32[3,2048]{1,0:T(4,128)} %positions_in.1, ...), custom_call_target="tpu_custom_call" | custom-call | tf_op jit(solution)/shard_map/pack/pallas_call | solution.py:537
  2.5 3.0 %collective-permute-start = (bf16[24,1664]{1,0:T(8,128)(2,1)S(1)}, bf16[24,1664]{1,0:T(8,128)(2,1)S(1)}, u32[]{:S(2)}, u32[]{:S(2)}) collective-permute-start(bf16[24,1664]{1,0:T(8,128)(2,1)S(1)} %get-tuple-element.28), channel_id=1, source_target_pairs={{2,0},{0,2},{6,4},{4,6},{10,8},{8,10},{14,12},{12,14},{18,16},{16,... | collective-permute-start | bytes 239624 | tf_op jit(solution)/shard_map/ppermute | solution.py:516
  5.6 1.5 %collective-permute-start.2 = (bf16[24,1664]{1,0:T(8,128)(2,1)S(1)}, bf16[24,1664]{1,0:T(8,128)(2,1)S(1)}, u32[]{:S(2)}, u32[]{:S(2)}) collective-permute-start(bf16[24,1664]{1,0:T(8,128)(2,1)S(1)} %get-tuple-element.29), channel_id=1, source_target_pairs={{6,0},{4,2},{2,4},{0,6},{14,8},{12,10},{10,12},{8,14},{22,16},{20,... | collective-permute-start | bytes 239624 | tf_op jit(solution)/shard_map/ppermute | solution.py:516
  7.0 0.1 collective-permute-start.1
  7.1 3.1 %near_own.1 = (f32[24,1536]{1,0:T(8,128)S(1)}, bf16[2048,48]{1,0:T(8,128)(2,1)S(1)}, bf16[48,2048]{1,0:T(8,128)(2,1)S(1)}, f32[1,2048]{1,0:T(1,128)S(1)}, f32[24...) custom-call(s32[8]{0:T(128)} %count_in.3, ...), custom_call_target="tpu_custom_call" | custom-call | tf_op jit(solution)/shard_map/near_own/pallas_call | solution.py:537
  10.2 1.0 %collective-permute-done.1.from_2 = bf16[24,128]{1,0:T(8,128)(2,1)S(1)} collective-permute-done((bf16[24,128]{1,0:T(8,128)(2,1)S(1)}, bf16[24,128]{1,0:T(8,128)(2,1)S(1)}, u32[]{:S(2)}, u32[]{:S(2)}) %collective-permute-start.1) | collective-permute-done | bytes 6176 | tf_op jit(solution)/shard_map/ppermute | solution.py:516
  11.2 0.0 collective-permute-done.from_1
  11.2 0.0 collective-permute-done.2.from_3
  11.2 0.5 %row.1 = (bf16[24,1536]{1,0:T(8,128)(2,1)S(1)}, bf16[24,1536]{1,0:T(8,128)(2,1)S(1)}, bf16[24,2816]{1,0:T(8,128)(2,1)S(1)}, bf16[24,256]{1,0:T(8,128)(2,1)S(1)}) custom-call(bf16[24,2048]{1,0:T(8,128)(2,1)S(1)} %get-tuple-element.25.own, bf16[24,512]{1,0:T(8,128)(2,1)S(1)} %get-tuple-element.26.moments, bf16[24,128]{1,0:T(8,128)(2,1)S(1)} %get-tuple-element.27.totals, ...), custom_call_target="tpu_custom_call" | custom-call | tf_op jit(solution)/shard_map/row/pallas_call | solution.py:537
  11.7 1.6 %collective-permute-start.3 = (bf16[24,2816]{1,0:T(8,128)(2,1)S(1)}, bf16[24,2816]{1,0:T(8,128)(2,1)S(1)}, u32[]{:S(2)}, u32[]{:S(2)}) collective-permute-start(bf16[24,2816]{1,0:T(8,128)(2,1)S(1)} %get-tuple-element.37), channel_id=1, source_target_pairs={{8,0},{10,2},{12,4},{14,6},{0,8},{2,10},{4,12},{6,14},{24,16},{26,... | collective-permute-start | bytes 405512 | tf_op jit(solution)/shard_map/ppermute | solution.py:516
  13.4 1.5 %near_middle.1 = (f32[24,2048]{1,0:T(8,128)S(1)}, bf16[24,2560]{1,0:T(8,128)(2,1)S(1)}, f32[24,512]{1,0:T(8,128)S(1)}) custom-call(bf16[24,2048]{1,0:T(8,128)(2,1)S(1)} %get-tuple-element.25.own, bf16[24,1536]{1,0:T(8,128)(2,1)S(1)} %get-tuple-element.31.left, bf16[24,1536]{1,0:T(8,128)(2,1)S(1)} %get-tuple-element.32.right, ...), custom_call_target="tpu_custom_call" | custom-call | tf_op jit(solution)/shard_map/near_middle/pallas_call | solution.py:537
  14.9 0.0 collective-permute-start.4
  14.9 1.2 %near_side.1.early.near = f32[24,2048]{1,0:T(8,128)S(1)} custom-call(bf16[24,1536]{1,0:T(8,128)(2,1)S(1)} %get-tuple-element.31.left, bf16[24,1536]{1,0:T(8,128)(2,1)S(1)} %get-tuple-element.32.right, f32[24,2048]{1,0:T(8,128)S(1)} %get-tuple-element.36.early, bf16[48,2048]{1,0:T(8,128)(2,1)S(1)} %get-tuple-element.35.target), custom_call_target="tpu_custom_call" | custom-call | tf_op jit(solution)/shard_map/near_side/pallas_call | solution.py:537
  16.1 0.7 %collective-permute-done.3.faces.faces_even = bf16[24,2816]{1,0:T(8,128)(2,1)S(1)} collective-permute-done((bf16[24,2816]{1,0:T(8,128)(2,1)S(1)}, bf16[24,2816]{1,0:T(8,128)(2,1)S(1)}, u32[]{:S(2)}, u32[]{:S(2)}) %collective-permute-start.3) | collective-permute-done | bytes 135200 | tf_op jit(solution)/shard_map/ppermute | solution.py:516
  16.8 2.6 %collective-permute-start.5 = (bf16[24,512]{1,0:T(8,128)(2,1)S(1)}, bf16[24,512]{1,0:T(8,128)(2,1)S(1)}, u32[]{:S(2)}, u32[]{:S(2)}) collective-permute-start(bf16[24,512]{1,0:T(8,128)(2,1)S(1)} %row_pairs.1), channel_id=1, source_target_pairs={{16,0},{18,2},{20,4},{22,6},{24,8},{26,10},{28,12},{30,14},{0,16},... | collective-permute-start | bytes 73736 | tf_op jit(solution)/shard_map/ppermute | solution.py:516
  19.4 2.8 %near_even.1.early = f32[24,2048]{1,0:T(8,128)S(1)} custom-call(f32[24,2048]{1,0:T(8,128)S(1)} %near_side.1.early.near, bf16[48,2048]{1,0:T(8,128)(2,1)S(1)} %get-tuple-element.35.target, bf16[24,1536]{1,0:T(8,128)(2,1)S(1)} %get-tuple-element.32.right, bf16[24,2816]{1,0:T(8,128)(2,1)S(1)} %collective-permute-done.3.faces.faces_even), custom_call_target="tpu_custom_call" | custom-call | tf_op jit(solution)/shard_map/near_even/pallas_call | solution.py:537
  22.2 0.0 collective-permute-done.4.faces.faces_odd
  22.2 0.0 collective-permute-done.5.rest_1_
  22.2 1.3 %evaluate.1 = (f32[17,2048]{1,0:T(8,128)}, f32[1,2176]{1,0:T(1,128)S(1)}) custom-call(f32[24,2048]{1,0:T(8,128)S(1)} %near_odd.1.near, bf16[24,2816]{1,0:T(8,128)(2,1)S(1)} %collective-permute-done.3.faces.faces_even, bf16[24,2560]{1,0:T(8,128)(2,1)S(1)} %collective-permute-done.4.faces.faces_odd, bf16[128,2048]{1,0:T(8,128)(2,1)S(1)} %get-tuple-element.39.basis, ...), custom_call_target="tpu_custom_call" | custom-call | tf_op jit(solution)/shard_map/evaluate/pallas_call | solution.py:537
  23.6 0.0 collective-permute-start.6
  23.6 1.2 %collective-permute-done.6.other = f32[1,2176]{1,0:T(1,128)S(1)} collective-permute-done((f32[1,2176]{1,0:T(1,128)S(1)}, f32[1,2176]{1,0:T(1,128)S(1)}, u32[]{:S(2)}, u32[]{:S(2)}) %collective-permute-start.6) | collective-permute-done | bytes 8736 | tf_op jit(solution)/shard_map/ppermute | solution.py:516
  24.7 0.7 %mean.1 = f32[1,2048]{1,0:T(1,128)} custom-call(f32[1,2176]{1,0:T(1,128)S(1)} %get-tuple-element.47.mine, f32[1,2176]{1,0:T(1,128)S(1)} %collective-permute-done.6.other), custom_call_target="tpu_custom_call" | custom-call | tf_op jit(solution)/shard_map/mean/pallas_call | solution.py:537
  (2 shorter events, 0.0 us)
Async XLA Ops:
  2.5 8.7 %collective-permute-start = (bf16[24,1664]{1,0:T(8,128)(2,1)S(1)}, bf16[24,1664]{1,0:T(8,128)(2,1)S(1)}, u32[]{:S(2)}, u32[]{:S(2)}) collective-permute-start(bf16[24,1664]{1,0:T(8,128)(2,1)S(1)} %get-tuple-element.28), channel_id=1, source_target_pairs={{2,0},{0,2},{6,4},{4,6},{10,8},{8,10},{14,12},{12,14},{18,16},{16,... | collective-permute-start | bytes 239624 | tf_op jit(solution)/shard_map/ppermute | solution.py:516
  5.6 5.7 %collective-permute-start.2 = (bf16[24,1664]{1,0:T(8,128)(2,1)S(1)}, bf16[24,1664]{1,0:T(8,128)(2,1)S(1)}, u32[]{:S(2)}, u32[]{:S(2)}) collective-permute-start(bf16[24,1664]{1,0:T(8,128)(2,1)S(1)} %get-tuple-element.29), channel_id=1, source_target_pairs={{6,0},{4,2},{2,4},{0,6},{14,8},{12,10},{10,12},{8,14},{22,16},{20,... | collective-permute-start | bytes 239624 | tf_op jit(solution)/shard_map/ppermute | solution.py:516
  7.0 4.2 %collective-permute-start.1 = (bf16[24,128]{1,0:T(8,128)(2,1)S(1)}, bf16[24,128]{1,0:T(8,128)(2,1)S(1)}, u32[]{:S(2)}, u32[]{:S(2)}) collective-permute-start(bf16[24,128]{1,0:T(8,128)(2,1)S(1)} %get-tuple-element.27.totals), channel_id=1, source_target_pairs={{4,0},{6,2},{0,4},{2,6},{12,8},{14,10},{8,12},{10,14},{20,16},{22,... | collective-permute-start | bytes 18440 | tf_op jit(solution)/shard_map/ppermute | solution.py:516
  11.7 5.1 %collective-permute-start.3 = (bf16[24,2816]{1,0:T(8,128)(2,1)S(1)}, bf16[24,2816]{1,0:T(8,128)(2,1)S(1)}, u32[]{:S(2)}, u32[]{:S(2)}) collective-permute-start(bf16[24,2816]{1,0:T(8,128)(2,1)S(1)} %get-tuple-element.37), channel_id=1, source_target_pairs={{8,0},{10,2},{12,4},{14,6},{0,8},{2,10},{4,12},{6,14},{24,16},{26,... | collective-permute-start | bytes 405512 | tf_op jit(solution)/shard_map/ppermute | solution.py:516
  14.9 7.3 %collective-permute-start.4 = (bf16[24,2560]{1,0:T(8,128)(2,1)S(1)}, bf16[24,2560]{1,0:T(8,128)(2,1)S(1)}, u32[]{:S(2)}, u32[]{:S(2)}) collective-permute-start(bf16[24,2560]{1,0:T(8,128)(2,1)S(1)} %get-tuple-element.38), channel_id=1, source_target_pairs={{1,0},{0,1},{3,2},{2,3},{5,4},{4,5},{7,6},{6,7},{16,8},{17,9},{18,... | collective-permute-start | bytes 368648 | tf_op jit(solution)/shard_map/ppermute | solution.py:527
  16.8 5.4 %collective-permute-start.5 = (bf16[24,512]{1,0:T(8,128)(2,1)S(1)}, bf16[24,512]{1,0:T(8,128)(2,1)S(1)}, u32[]{:S(2)}, u32[]{:S(2)}) collective-permute-start(bf16[24,512]{1,0:T(8,128)(2,1)S(1)} %row_pairs.1), channel_id=1, source_target_pairs={{16,0},{18,2},{20,4},{22,6},{24,8},{26,10},{28,12},{30,14},{0,16},... | collective-permute-start | bytes 73736 | tf_op jit(solution)/shard_map/ppermute | solution.py:516
  23.6 1.2 %collective-permute-start.6 = (f32[1,2176]{1,0:T(1,128)S(1)}, f32[1,2176]{1,0:T(1,128)S(1)}, u32[]{:S(2)}, u32[]{:S(2)}) collective-permute-start(f32[1,2176]{1,0:T(1,128)S(1)} %get-tuple-element.47.mine), channel_id=1, source_target_pairs={{1,0},{0,1},{3,2},{2,3},{5,4},{4,5},{7,6},{6,7},{9,8},{8,9},{11,10... | collective-permute-start | bytes 26120 | tf_op jit(solution)/shard_map/ppermute | solution.py:516

commit v25 on v24

--- a/solution.py
+++ b/solution.py
@@ -17,7 +17,7 @@
 LEAVES = 8 * SLOT
 MEGA = 1024 * 1024
 FEATURES = 48
-EARLY = 3
+EARLY = 2
 
 
 def exponent_table(order_max):

time: 25.6 us -> 26.3 us (1.027)
  starting transfers between devices: 8.78 us -> 9.34 us
    ppermute x6, starting transfers between devices: 8.78 us -> 9.33 us  [swapped(): return lax.ppermute(block, axis, [(partner(i), i) for i in range(size)])]
  transfers between devices with their start and end apart: 7 -> 7, of which waited for: 3 -> 2; matrix products, arithmetic and copies ran while one was open for 0% -> 0% of each run, Pallas kernels for 34% -> 34%
where the time goes in v25:
time: 26.3 us; the launch traced here: 26.1 us
  Pallas kernels  13.2 us (50%)
  starting transfers between devices  9.34 us (36%)
  waiting for transfers between devices  2.91 us (11%)
  between operations  0.71 us (3%)
    pallas_call x10, Pallas kernels, call(): pl.pallas_call(kernel, in_specs=in_specs, out_specs=[vmem] * len(outs), o...  13.2 us
    ppermute x6, starting transfers between devices, swapped(): return lax.ppermute(block, axis, [(partner(i), i) for i in range(size)])  9.33 us
    ppermute x6, waiting for transfers between devices, swapped(): return lax.ppermute(block, axis, [(partner(i), i) for i in range(size)])  2.91 us
  transfers between devices with their start and end apart: 7, of which 2 were waited for; matrix products, arithmetic and copies ran while one was open for 0% of the time, Pallas kernels for 34%

profile of v25, /device:TPU:0, one launch (start us, length us, event | category | flops | bytes accessed | tf_op | source)
XLA Modules:
  0.0 26.1 jit_solution(7755646297019146149)
XLA Ops:
  0.6 1.9 %pack.1 = (bf16[24,2048]{1,0:T(8,128)(2,1)S(1)}, bf16[128,2048]{1,0:T(8,128)(2,1)S(1)}, bf16[24,512]{1,0:T(8,128)(2,1)S(1)}, bf16[24,128]{1,0:T(8,128)(2,1)S(1)}...) custom-call(s32[8]{0:T(128)} %count_in.3, f32[3,2048]{1,0:T(4,128)} %positions_in.1, ...), custom_call_target="tpu_custom_call" | custom-call | tf_op jit(solution)/shard_map/pack/pallas_call | solution.py:537
  2.5 3.0 %collective-permute-start = (bf16[24,1664]{1,0:T(8,128)(2,1)S(1)}, bf16[24,1664]{1,0:T(8,128)(2,1)S(1)}, u32[]{:S(2)}, u32[]{:S(2)}) collective-permute-start(bf16[24,1664]{1,0:T(8,128)(2,1)S(1)} %get-tuple-element.28), channel_id=1, source_target_pairs={{2,0},{0,2},{6,4},{4,6},{10,8},{8,10},{14,12},{12,14},{18,16},{16,... | collective-permute-start | bytes 239624 | tf_op jit(solution)/shard_map/ppermute | solution.py:516
  5.6 1.5 %collective-permute-start.2 = (bf16[24,1664]{1,0:T(8,128)(2,1)S(1)}, bf16[24,1664]{1,0:T(8,128)(2,1)S(1)}, u32[]{:S(2)}, u32[]{:S(2)}) collective-permute-start(bf16[24,1664]{1,0:T(8,128)(2,1)S(1)} %get-tuple-element.29), channel_id=1, source_target_pairs={{6,0},{4,2},{2,4},{0,6},{14,8},{12,10},{10,12},{8,14},{22,16},{20,... | collective-permute-start | bytes 239624 | tf_op jit(solution)/shard_map/ppermute | solution.py:516
  7.0 0.1 collective-permute-start.1
  7.1 2.4 %near_own.1 = (f32[24,1024]{1,0:T(8,128)S(1)}, bf16[2048,48]{1,0:T(8,128)(2,1)S(1)}, bf16[48,2048]{1,0:T(8,128)(2,1)S(1)}, f32[1,2048]{1,0:T(1,128)S(1)}, f32[24...) custom-call(s32[8]{0:T(128)} %count_in.3, ...), custom_call_target="tpu_custom_call" | custom-call | tf_op jit(solution)/shard_map/near_own/pallas_call | solution.py:537
  9.5 1.7 %collective-permute-done.1.from_2 = bf16[24,128]{1,0:T(8,128)(2,1)S(1)} collective-permute-done((bf16[24,128]{1,0:T(8,128)(2,1)S(1)}, bf16[24,128]{1,0:T(8,128)(2,1)S(1)}, u32[]{:S(2)}, u32[]{:S(2)}) %collective-permute-start.1) | collective-permute-done | bytes 6176 | tf_op jit(solution)/shard_map/ppermute | solution.py:516
  11.2 0.0 collective-permute-done.from_1
  11.2 0.0 collective-permute-done.2.from_3
  11.2 0.5 %row.1 = (bf16[24,1536]{1,0:T(8,128)(2,1)S(1)}, bf16[24,1536]{1,0:T(8,128)(2,1)S(1)}, bf16[24,2816]{1,0:T(8,128)(2,1)S(1)}, bf16[24,256]{1,0:T(8,128)(2,1)S(1)}) custom-call(bf16[24,2048]{1,0:T(8,128)(2,1)S(1)} %get-tuple-element.25.own, bf16[24,512]{1,0:T(8,128)(2,1)S(1)} %get-tuple-element.26.moments, bf16[24,128]{1,0:T(8,128)(2,1)S(1)} %get-tuple-element.27.totals, ...), custom_call_target="tpu_custom_call" | custom-call | tf_op jit(solution)/shard_map/row/pallas_call | solution.py:537
  11.7 1.6 %collective-permute-start.3 = (bf16[24,2816]{1,0:T(8,128)(2,1)S(1)}, bf16[24,2816]{1,0:T(8,128)(2,1)S(1)}, u32[]{:S(2)}, u32[]{:S(2)}) collective-permute-start(bf16[24,2816]{1,0:T(8,128)(2,1)S(1)} %get-tuple-element.37), channel_id=1, source_target_pairs={{8,0},{10,2},{12,4},{14,6},{0,8},{2,10},{4,12},{6,14},{24,16},{26,... | collective-permute-start | bytes 405512 | tf_op jit(solution)/shard_map/ppermute | solution.py:516
  13.4 2.4 %near_middle.1 = (f32[24,2048]{1,0:T(8,128)S(1)}, bf16[24,2560]{1,0:T(8,128)(2,1)S(1)}, f32[24,512]{1,0:T(8,128)S(1)}) custom-call(bf16[24,2048]{1,0:T(8,128)(2,1)S(1)} %get-tuple-element.25.own, bf16[24,1536]{1,0:T(8,128)(2,1)S(1)} %get-tuple-element.31.left, bf16[24,1536]{1,0:T(8,128)(2,1)S(1)} %get-tuple-element.32.right, ...), custom_call_target="tpu_custom_call" | custom-call | tf_op jit(solution)/shard_map/near_middle/pallas_call | solution.py:537
  15.7 0.0 collective-permute-start.4
  15.7 1.2 %near_side.1.early.near = f32[24,2048]{1,0:T(8,128)S(1)} custom-call(bf16[24,1536]{1,0:T(8,128)(2,1)S(1)} %get-tuple-element.31.left, bf16[24,1536]{1,0:T(8,128)(2,1)S(1)} %get-tuple-element.32.right, f32[24,2048]{1,0:T(8,128)S(1)} %get-tuple-element.36.early, bf16[48,2048]{1,0:T(8,128)(2,1)S(1)} %get-tuple-element.35.target), custom_call_target="tpu_custom_call" | custom-call | tf_op jit(solution)/shard_map/near_side/pallas_call | solution.py:537
  16.9 0.0 collective-permute-done.3.faces.faces_even
  17.0 3.1 %collective-permute-start.5 = (bf16[24,512]{1,0:T(8,128)(2,1)S(1)}, bf16[24,512]{1,0:T(8,128)(2,1)S(1)}, u32[]{:S(2)}, u32[]{:S(2)}) collective-permute-start(bf16[24,512]{1,0:T(8,128)(2,1)S(1)} %row_pairs.1), channel_id=1, source_target_pairs={{16,0},{18,2},{20,4},{22,6},{24,8},{26,10},{28,12},{30,14},{0,16},... | collective-permute-start | bytes 73736 | tf_op jit(solution)/shard_map/ppermute | solution.py:516
  20.1 2.8 %near_even.1.early = f32[24,2048]{1,0:T(8,128)S(1)} custom-call(f32[24,2048]{1,0:T(8,128)S(1)} %near_side.1.early.near, bf16[48,2048]{1,0:T(8,128)(2,1)S(1)} %get-tuple-element.35.target, bf16[24,1536]{1,0:T(8,128)(2,1)S(1)} %get-tuple-element.32.right, bf16[24,2816]{1,0:T(8,128)(2,1)S(1)} %collective-permute-done.3.faces.faces_even), custom_call_target="tpu_custom_call" | custom-call | tf_op jit(solution)/shard_map/near_even/pallas_call | solution.py:537
  22.9 0.0 collective-permute-done.4.faces.faces_odd
  22.9 0.0 collective-permute-done.5.rest_1_
  22.9 1.3 %evaluate.1 = (f32[17,2048]{1,0:T(8,128)}, f32[1,2176]{1,0:T(1,128)S(1)}) custom-call(f32[24,2048]{1,0:T(8,128)S(1)} %near_odd.1.near, bf16[24,2816]{1,0:T(8,128)(2,1)S(1)} %collective-permute-done.3.faces.faces_even, bf16[24,2560]{1,0:T(8,128)(2,1)S(1)} %collective-permute-done.4.faces.faces_odd, bf16[128,2048]{1,0:T(8,128)(2,1)S(1)} %get-tuple-element.39.basis, ...), custom_call_target="tpu_custom_call" | custom-call | tf_op jit(solution)/shard_map/evaluate/pallas_call | solution.py:537
  24.3 0.0 collective-permute-start.6
  24.3 1.2 %collective-permute-done.6.other = f32[1,2176]{1,0:T(1,128)S(1)} collective-permute-done((f32[1,2176]{1,0:T(1,128)S(1)}, f32[1,2176]{1,0:T(1,128)S(1)}, u32[]{:S(2)}, u32[]{:S(2)}) %collective-permute-start.6) | collective-permute-done | bytes 8736 | tf_op jit(solution)/shard_map/ppermute | solution.py:516
  25.4 0.7 %mean.1 = f32[1,2048]{1,0:T(1,128)} custom-call(f32[1,2176]{1,0:T(1,128)S(1)} %get-tuple-element.47.mine, f32[1,2176]{1,0:T(1,128)S(1)} %collective-permute-done.6.other), custom_call_target="tpu_custom_call" | custom-call | tf_op jit(solution)/shard_map/mean/pallas_call | solution.py:537
  (2 shorter events, 0.0 us)
Async XLA Ops:
  2.5 8.7 %collective-permute-start = (bf16[24,1664]{1,0:T(8,128)(2,1)S(1)}, bf16[24,1664]{1,0:T(8,128)(2,1)S(1)}, u32[]{:S(2)}, u32[]{:S(2)}) collective-permute-start(bf16[24,1664]{1,0:T(8,128)(2,1)S(1)} %get-tuple-element.28), channel_id=1, source_target_pairs={{2,0},{0,2},{6,4},{4,6},{10,8},{8,10},{14,12},{12,14},{18,16},{16,... | collective-permute-start | bytes 239624 | tf_op jit(solution)/shard_map/ppermute | solution.py:516
  5.6 5.7 %collective-permute-start.2 = (bf16[24,1664]{1,0:T(8,128)(2,1)S(1)}, bf16[24,1664]{1,0:T(8,128)(2,1)S(1)}, u32[]{:S(2)}, u32[]{:S(2)}) collective-permute-start(bf16[24,1664]{1,0:T(8,128)(2,1)S(1)} %get-tuple-element.29), channel_id=1, source_target_pairs={{6,0},{4,2},{2,4},{0,6},{14,8},{12,10},{10,12},{8,14},{22,16},{20,... | collective-permute-start | bytes 239624 | tf_op jit(solution)/shard_map/ppermute | solution.py:516
  7.0 4.2 %collective-permute-start.1 = (bf16[24,128]{1,0:T(8,128)(2,1)S(1)}, bf16[24,128]{1,0:T(8,128)(2,1)S(1)}, u32[]{:S(2)}, u32[]{:S(2)}) collective-permute-start(bf16[24,128]{1,0:T(8,128)(2,1)S(1)} %get-tuple-element.27.totals), channel_id=1, source_target_pairs={{4,0},{6,2},{0,4},{2,6},{12,8},{14,10},{8,12},{10,14},{20,16},{22,... | collective-permute-start | bytes 18440 | tf_op jit(solution)/shard_map/ppermute | solution.py:516
  11.7 5.2 %collective-permute-start.3 = (bf16[24,2816]{1,0:T(8,128)(2,1)S(1)}, bf16[24,2816]{1,0:T(8,128)(2,1)S(1)}, u32[]{:S(2)}, u32[]{:S(2)}) collective-permute-start(bf16[24,2816]{1,0:T(8,128)(2,1)S(1)} %get-tuple-element.37), channel_id=1, source_target_pairs={{8,0},{10,2},{12,4},{14,6},{0,8},{2,10},{4,12},{6,14},{24,16},{26,... | collective-permute-start | bytes 405512 | tf_op jit(solution)/shard_map/ppermute | solution.py:516
  15.7 7.1 %collective-permute-start.4 = (bf16[24,2560]{1,0:T(8,128)(2,1)S(1)}, bf16[24,2560]{1,0:T(8,128)(2,1)S(1)}, u32[]{:S(2)}, u32[]{:S(2)}) collective-permute-start(bf16[24,2560]{1,0:T(8,128)(2,1)S(1)} %get-tuple-element.38), channel_id=1, source_target_pairs={{1,0},{0,1},{3,2},{2,3},{5,4},{4,5},{7,6},{6,7},{16,8},{17,9},{18,... | collective-permute-start | bytes 368648 | tf_op jit(solution)/shard_map/ppermute | solution.py:527
  17.0 6.0 %collective-permute-start.5 = (bf16[24,512]{1,0:T(8,128)(2,1)S(1)}, bf16[24,512]{1,0:T(8,128)(2,1)S(1)}, u32[]{:S(2)}, u32[]{:S(2)}) collective-permute-start(bf16[24,512]{1,0:T(8,128)(2,1)S(1)} %row_pairs.1), channel_id=1, source_target_pairs={{16,0},{18,2},{20,4},{22,6},{24,8},{26,10},{28,12},{30,14},{0,16},... | collective-permute-start | bytes 73736 | tf_op jit(solution)/shard_map/ppermute | solution.py:516
  24.3 1.2 %collective-permute-start.6 = (f32[1,2176]{1,0:T(1,128)S(1)}, f32[1,2176]{1,0:T(1,128)S(1)}, u32[]{:S(2)}, u32[]{:S(2)}) collective-permute-start(f32[1,2176]{1,0:T(1,128)S(1)} %get-tuple-element.47.mine), channel_id=1, source_target_pairs={{1,0},{0,1},{3,2},{2,3},{5,4},{4,5},{7,6},{6,7},{9,8},{8,9},{11,10... | collective-permute-start | bytes 26120 | tf_op jit(solution)/shard_map/ppermute | solution.py:516

commit v26 on v24

--- a/solution.py
+++ b/solution.py
@@ -256,8 +256,9 @@
     for group, source, masses, starts in jobs:
         for piece in range(2):
             here = lanes((2 * group + piece) * width, width)
-            for turn, start in enumerate(starts):
-                tiles.append((here, source, masses, lanes(start, size), turn == 0, turn + 1 == len(starts)))
+            parts = [start + step for start in starts for step in (0, size // 2)]
+            for turn, start in enumerate(parts):
+                tiles.append((here, source, masses, lanes(start, size // 2), turn == 0, turn + 1 == len(parts)))
 
     def squares(tile):
         return dot(tile[1][tile[3], :], target[:, tile[0]])

time: 25.6 us -> 27.2 us (1.062)
  Pallas kernels: 13 us -> 15.5 us
  waiting for transfers between devices: 2.9 us -> 1.19 us
  starting transfers between devices: 8.78 us -> 9.62 us
    pallas_call x10, Pallas kernels: 13 us -> 15.5 us  [call(): pl.pallas_call(kernel, in_specs=in_specs, out_specs=[vmem] * len(outs), o...]
    ppermute x6, waiting for transfers between devices: 2.89 us -> 1.18 us  [swapped(): return lax.ppermute(block, axis, [(partner(i), i) for i in range(size)])]
    ppermute x6, starting transfers between devices: 8.78 us -> 9.62 us  [swapped(): return lax.ppermute(block, axis, [(partner(i), i) for i in range(size)])]
  transfers between devices with their start and end apart: 7 -> 7, of which waited for: 3 -> 1; matrix products, arithmetic and copies ran while one was open for 0% -> 0% of each run, Pallas kernels for 34% -> 41%
where the time goes in v26:
time: 27.2 us; the launch traced here: 27.1 us
  Pallas kernels  15.5 us (57%)
  starting transfers between devices  9.62 us (35%)
  waiting for transfers between devices  1.19 us (4%)
  between operations  0.72 us (3%)
    pallas_call x10, Pallas kernels, call(): pl.pallas_call(kernel, in_specs=in_specs, out_specs=[vmem] * len(outs), o...  15.5 us
    ppermute x6, starting transfers between devices, swapped(): return lax.ppermute(block, axis, [(partner(i), i) for i in range(size)])  9.62 us
    ppermute x6, waiting for transfers between devices, swapped(): return lax.ppermute(block, axis, [(partner(i), i) for i in range(size)])  1.18 us
  transfers between devices with their start and end apart: 7, of which 1 were waited for; matrix products, arithmetic and copies ran while one was open for 0% of the time, Pallas kernels for 41%

profile of v26, /device:TPU:0, one launch (start us, length us, event | category | flops | bytes accessed | tf_op | source)
XLA Modules:
  0.0 27.1 jit_solution(14291193735441042587)
XLA Ops:
  0.6 1.9 %pack.1 = (bf16[24,2048]{1,0:T(8,128)(2,1)S(1)}, bf16[128,2048]{1,0:T(8,128)(2,1)S(1)}, bf16[24,512]{1,0:T(8,128)(2,1)S(1)}, bf16[24,128]{1,0:T(8,128)(2,1)S(1)}...) custom-call(s32[8]{0:T(128)} %count_in.3, f32[3,2048]{1,0:T(4,128)} %positions_in.1, ...), custom_call_target="tpu_custom_call" | custom-call | tf_op jit(solution)/shard_map/pack/pallas_call | solution.py:538
  2.5 3.0 %collective-permute-start = (bf16[24,1664]{1,0:T(8,128)(2,1)S(1)}, bf16[24,1664]{1,0:T(8,128)(2,1)S(1)}, u32[]{:S(2)}, u32[]{:S(2)}) collective-permute-start(bf16[24,1664]{1,0:T(8,128)(2,1)S(1)} %get-tuple-element.28), channel_id=1, source_target_pairs={{2,0},{0,2},{6,4},{4,6},{10,8},{8,10},{14,12},{12,14},{18,16},{16,... | collective-permute-start | bytes 239624 | tf_op jit(solution)/shard_map/ppermute | solution.py:517
  5.6 1.5 %collective-permute-start.2 = (bf16[24,1664]{1,0:T(8,128)(2,1)S(1)}, bf16[24,1664]{1,0:T(8,128)(2,1)S(1)}, u32[]{:S(2)}, u32[]{:S(2)}) collective-permute-start(bf16[24,1664]{1,0:T(8,128)(2,1)S(1)} %get-tuple-element.29), channel_id=1, source_target_pairs={{6,0},{4,2},{2,4},{0,6},{14,8},{12,10},{10,12},{8,14},{22,16},{20,... | collective-permute-start | bytes 239624 | tf_op jit(solution)/shard_map/ppermute | solution.py:517
  7.0 0.1 collective-permute-start.1
  7.1 4.4 %near_own.1 = (f32[24,1536]{1,0:T(8,128)S(1)}, bf16[2048,48]{1,0:T(8,128)(2,1)S(1)}, bf16[48,2048]{1,0:T(8,128)(2,1)S(1)}, f32[1,2048]{1,0:T(1,128)S(1)}, f32[24...) custom-call(s32[8]{0:T(128)} %count_in.3, ...), custom_call_target="tpu_custom_call" | custom-call | tf_op jit(solution)/shard_map/near_own/pallas_call | solution.py:538
  11.5 0.0 collective-permute-done.1.from_2
  11.5 0.0 collective-permute-done.from_1
  11.5 0.0 collective-permute-done.2.from_3
  11.5 0.5 %row.1 = (bf16[24,1536]{1,0:T(8,128)(2,1)S(1)}, bf16[24,1536]{1,0:T(8,128)(2,1)S(1)}, bf16[24,2816]{1,0:T(8,128)(2,1)S(1)}, bf16[24,256]{1,0:T(8,128)(2,1)S(1)}) custom-call(bf16[24,2048]{1,0:T(8,128)(2,1)S(1)} %get-tuple-element.25.own, bf16[24,512]{1,0:T(8,128)(2,1)S(1)} %get-tuple-element.26.moments, bf16[24,128]{1,0:T(8,128)(2,1)S(1)} %get-tuple-element.27.totals, ...), custom_call_target="tpu_custom_call" | custom-call | tf_op jit(solution)/shard_map/row/pallas_call | solution.py:538
  12.0 2.1 %collective-permute-start.3 = (bf16[24,2816]{1,0:T(8,128)(2,1)S(1)}, bf16[24,2816]{1,0:T(8,128)(2,1)S(1)}, u32[]{:S(2)}, u32[]{:S(2)}) collective-permute-start(bf16[24,2816]{1,0:T(8,128)(2,1)S(1)} %get-tuple-element.37), channel_id=1, source_target_pairs={{8,0},{10,2},{12,4},{14,6},{0,8},{2,10},{4,12},{6,14},{24,16},{26,... | collective-permute-start | bytes 405512 | tf_op jit(solution)/shard_map/ppermute | solution.py:517
  14.1 1.8 %near_middle.1 = (f32[24,2048]{1,0:T(8,128)S(1)}, bf16[24,2560]{1,0:T(8,128)(2,1)S(1)}, f32[24,512]{1,0:T(8,128)S(1)}) custom-call(bf16[24,2048]{1,0:T(8,128)(2,1)S(1)} %get-tuple-element.25.own, bf16[24,1536]{1,0:T(8,128)(2,1)S(1)} %get-tuple-element.31.left, bf16[24,1536]{1,0:T(8,128)(2,1)S(1)} %get-tuple-element.32.right, ...), custom_call_target="tpu_custom_call" | custom-call | tf_op jit(solution)/shard_map/near_middle/pallas_call | solution.py:538
  15.9 0.0 collective-permute-start.4
  15.9 1.4 %near_side.1.early.near = f32[24,2048]{1,0:T(8,128)S(1)} custom-call(bf16[24,1536]{1,0:T(8,128)(2,1)S(1)} %get-tuple-element.31.left, bf16[24,1536]{1,0:T(8,128)(2,1)S(1)} %get-tuple-element.32.right, f32[24,2048]{1,0:T(8,128)S(1)} %get-tuple-element.36.early, bf16[48,2048]{1,0:T(8,128)(2,1)S(1)} %get-tuple-element.35.target), custom_call_target="tpu_custom_call" | custom-call | tf_op jit(solution)/shard_map/near_side/pallas_call | solution.py:538
  17.4 0.0 collective-permute-done.3.faces.faces_even
  17.4 3.0 %collective-permute-start.5 = (bf16[24,512]{1,0:T(8,128)(2,1)S(1)}, bf16[24,512]{1,0:T(8,128)(2,1)S(1)}, u32[]{:S(2)}, u32[]{:S(2)}) collective-permute-start(bf16[24,512]{1,0:T(8,128)(2,1)S(1)} %row_pairs.1), channel_id=1, source_target_pairs={{16,0},{18,2},{20,4},{22,6},{24,8},{26,10},{28,12},{30,14},{0,16},... | collective-permute-start | bytes 73736 | tf_op jit(solution)/shard_map/ppermute | solution.py:517
  20.4 3.5 %near_even.1.early = f32[24,2048]{1,0:T(8,128)S(1)} custom-call(f32[24,2048]{1,0:T(8,128)S(1)} %near_side.1.early.near, bf16[48,2048]{1,0:T(8,128)(2,1)S(1)} %get-tuple-element.35.target, bf16[24,1536]{1,0:T(8,128)(2,1)S(1)} %get-tuple-element.32.right, bf16[24,2816]{1,0:T(8,128)(2,1)S(1)} %collective-permute-done.3.faces.faces_even), custom_call_target="tpu_custom_call" | custom-call | tf_op jit(solution)/shard_map/near_even/pallas_call | solution.py:538
  23.8 0.0 collective-permute-done.4.faces.faces_odd
  23.9 0.0 collective-permute-done.5.rest_1_
  23.9 1.3 %evaluate.1 = (f32[17,2048]{1,0:T(8,128)}, f32[1,2176]{1,0:T(1,128)S(1)}) custom-call(f32[24,2048]{1,0:T(8,128)S(1)} %near_odd.1.near, bf16[24,2816]{1,0:T(8,128)(2,1)S(1)} %collective-permute-done.3.faces.faces_even, bf16[24,2560]{1,0:T(8,128)(2,1)S(1)} %collective-permute-done.4.faces.faces_odd, bf16[128,2048]{1,0:T(8,128)(2,1)S(1)} %get-tuple-element.39.basis, ...), custom_call_target="tpu_custom_call" | custom-call | tf_op jit(solution)/shard_map/evaluate/pallas_call | solution.py:538
  25.2 0.0 collective-permute-start.6
  25.2 1.2 %collective-permute-done.6.other = f32[1,2176]{1,0:T(1,128)S(1)} collective-permute-done((f32[1,2176]{1,0:T(1,128)S(1)}, f32[1,2176]{1,0:T(1,128)S(1)}, u32[]{:S(2)}, u32[]{:S(2)}) %collective-permute-start.6) | collective-permute-done | bytes 8736 | tf_op jit(solution)/shard_map/ppermute | solution.py:517
  26.4 0.7 %mean.1 = f32[1,2048]{1,0:T(1,128)} custom-call(f32[1,2176]{1,0:T(1,128)S(1)} %get-tuple-element.47.mine, f32[1,2176]{1,0:T(1,128)S(1)} %collective-permute-done.6.other), custom_call_target="tpu_custom_call" | custom-call | tf_op jit(solution)/shard_map/mean/pallas_call | solution.py:538
  (2 shorter events, 0.0 us)
Async XLA Ops:
  2.5 9.0 %collective-permute-start = (bf16[24,1664]{1,0:T(8,128)(2,1)S(1)}, bf16[24,1664]{1,0:T(8,128)(2,1)S(1)}, u32[]{:S(2)}, u32[]{:S(2)}) collective-permute-start(bf16[24,1664]{1,0:T(8,128)(2,1)S(1)} %get-tuple-element.28), channel_id=1, source_target_pairs={{2,0},{0,2},{6,4},{4,6},{10,8},{8,10},{14,12},{12,14},{18,16},{16,... | collective-permute-start | bytes 239624 | tf_op jit(solution)/shard_map/ppermute | solution.py:517
  5.6 6.0 %collective-permute-start.2 = (bf16[24,1664]{1,0:T(8,128)(2,1)S(1)}, bf16[24,1664]{1,0:T(8,128)(2,1)S(1)}, u32[]{:S(2)}, u32[]{:S(2)}) collective-permute-start(bf16[24,1664]{1,0:T(8,128)(2,1)S(1)} %get-tuple-element.29), channel_id=1, source_target_pairs={{6,0},{4,2},{2,4},{0,6},{14,8},{12,10},{10,12},{8,14},{22,16},{20,... | collective-permute-start | bytes 239624 | tf_op jit(solution)/shard_map/ppermute | solution.py:517
  7.0 4.5 %collective-permute-start.1 = (bf16[24,128]{1,0:T(8,128)(2,1)S(1)}, bf16[24,128]{1,0:T(8,128)(2,1)S(1)}, u32[]{:S(2)}, u32[]{:S(2)}) collective-permute-start(bf16[24,128]{1,0:T(8,128)(2,1)S(1)} %get-tuple-element.27.totals), channel_id=1, source_target_pairs={{4,0},{6,2},{0,4},{2,6},{12,8},{14,10},{8,12},{10,14},{20,16},{22,... | collective-permute-start | bytes 18440 | tf_op jit(solution)/shard_map/ppermute | solution.py:517
  12.0 5.3 %collective-permute-start.3 = (bf16[24,2816]{1,0:T(8,128)(2,1)S(1)}, bf16[24,2816]{1,0:T(8,128)(2,1)S(1)}, u32[]{:S(2)}, u32[]{:S(2)}) collective-permute-start(bf16[24,2816]{1,0:T(8,128)(2,1)S(1)} %get-tuple-element.37), channel_id=1, source_target_pairs={{8,0},{10,2},{12,4},{14,6},{0,8},{2,10},{4,12},{6,14},{24,16},{26,... | collective-permute-start | bytes 405512 | tf_op jit(solution)/shard_map/ppermute | solution.py:517
  15.9 7.9 %collective-permute-start.4 = (bf16[24,2560]{1,0:T(8,128)(2,1)S(1)}, bf16[24,2560]{1,0:T(8,128)(2,1)S(1)}, u32[]{:S(2)}, u32[]{:S(2)}) collective-permute-start(bf16[24,2560]{1,0:T(8,128)(2,1)S(1)} %get-tuple-element.38), channel_id=1, source_target_pairs={{1,0},{0,1},{3,2},{2,3},{5,4},{4,5},{7,6},{6,7},{16,8},{17,9},{18,... | collective-permute-start | bytes 368648 | tf_op jit(solution)/shard_map/ppermute | solution.py:528
  17.4 6.5 %collective-permute-start.5 = (bf16[24,512]{1,0:T(8,128)(2,1)S(1)}, bf16[24,512]{1,0:T(8,128)(2,1)S(1)}, u32[]{:S(2)}, u32[]{:S(2)}) collective-permute-start(bf16[24,512]{1,0:T(8,128)(2,1)S(1)} %row_pairs.1), channel_id=1, source_target_pairs={{16,0},{18,2},{20,4},{22,6},{24,8},{26,10},{28,12},{30,14},{0,16},... | collective-permute-start | bytes 73736 | tf_op jit(solution)/shard_map/ppermute | solution.py:517
  25.2 1.2 %collective-permute-start.6 = (f32[1,2176]{1,0:T(1,128)S(1)}, f32[1,2176]{1,0:T(1,128)S(1)}, u32[]{:S(2)}, u32[]{:S(2)}) collective-permute-start(f32[1,2176]{1,0:T(1,128)S(1)} %get-tuple-element.47.mine), channel_id=1, source_target_pairs={{1,0},{0,1},{3,2},{2,3},{5,4},{4,5},{7,6},{6,7},{9,8},{8,9},{11,10... | collective-permute-start | bytes 26120 | tf_op jit(solution)/shard_map/ppermute | solution.py:517

commit v27 on v24

--- a/solution.py
+++ b/solution.py
@@ -280,8 +280,8 @@
 
 def own_groups(near, first, last, target, source, own):
     pts = source.shape[0] // 8
-    starts = [2 * p * pts for p in range(4)]
-    pulled(near, [(group, source, own, starts) for group in range(first, last)], target, 2 * pts)
+    starts = [0, 4 * pts]
+    pulled(near, [(group, source, own, starts) for group in range(first, last)], target, 4 * pts)
 
 
 def box_columns(depth, box_x, box_z, nodes):
@@ -379,8 +379,8 @@
         for place in range(4):
             centre = (1.5 if step else -1.5, place % 2 - 0.5, place // 2 - 0.5)
             held[lanes(place * pts, pts), :] = source_features(side, place * pts, pts, centre)
-        jobs += [(step, held, side, [0, 2 * pts]), (step + 2, held, side, [0, 2 * pts])]
-    pulled(near, jobs, target, 2 * pts, early)
+        jobs += [(step, held, side, [0]), (step + 2, held, side, [0])]
+    pulled(near, jobs, target, 4 * pts, early)
 
 
 def middle_kernel(own, left, right, moments, far, early, source, target, near, faces_odd, same, *sides):
@@ -437,8 +437,8 @@
             centre = (place // 2 - 1.5, place % 2 - 0.5, height)
             sides[lanes(place * pts, pts), :] = source_features(faces, place * pts, pts, centre)
 
-        jobs = [(i + 2 * step, sides, faces, [2 * (x + i) * pts for x in range(3)]) for i in range(2)]
-        pulled(near, jobs, target, 2 * pts, early)
+        jobs = [(i + 2 * step, sides, faces, [(2 * i + 3 * turn) * pts for turn in range(2)]) for i in range(2)]
+        pulled(near, jobs, target, 3 * pts, early)
 
     @pl.when(jnp.logical_not(inside))
     def _():

time: 25.6 us -> 25.4 us (level)
  Pallas kernels: 13 us -> 12.5 us
    pallas_call x10, Pallas kernels: 13 us -> 12.5 us  [call(): pl.pallas_call(kernel, in_specs=in_specs, out_specs=[vmem] * len(outs), o...]
  transfers between devices with their start and end apart: 7 -> 7, of which waited for: 3 -> 3; matrix products, arithmetic and copies ran while one was open for 0% -> 0% of each run, Pallas kernels for 34% -> 32%
where the time goes in v27:
time: 25.4 us; the launch traced here: 25.2 us
  Pallas kernels  12.5 us (49%)
  starting transfers between devices  8.85 us (35%)
  waiting for transfers between devices  3.12 us (12%)
  between operations  0.7 us (3%)
    pallas_call x10, Pallas kernels, call(): pl.pallas_call(kernel, in_specs=in_specs, out_specs=[vmem] * len(outs), o...  12.5 us
    ppermute x6, starting transfers between devices, swapped(): return lax.ppermute(block, axis, [(partner(i), i) for i in range(size)])  8.78 us
    ppermute x6, waiting for transfers between devices, swapped(): return lax.ppermute(block, axis, [(partner(i), i) for i in range(size)])  3.12 us
  transfers between devices with their start and end apart: 7, of which 3 were waited for; matrix products, arithmetic and copies ran while one was open for 0% of the time, Pallas kernels for 32%

profile of v27, /device:TPU:0, one launch (start us, length us, event | category | flops | bytes accessed | tf_op | source)
XLA Modules:
  0.0 25.2 jit_solution(695915152206528185)
XLA Ops:
  0.6 1.9 %pack.1 = (bf16[24,2048]{1,0:T(8,128)(2,1)S(1)}, bf16[128,2048]{1,0:T(8,128)(2,1)S(1)}, bf16[24,512]{1,0:T(8,128)(2,1)S(1)}, bf16[24,128]{1,0:T(8,128)(2,1)S(1)}...) custom-call(s32[8]{0:T(128)} %count_in.3, f32[3,2048]{1,0:T(4,128)} %positions_in.1, ...), custom_call_target="tpu_custom_call" | custom-call | tf_op jit(solution)/shard_map/pack/pallas_call | solution.py:537
  2.5 3.0 %collective-permute-start = (bf16[24,1664]{1,0:T(8,128)(2,1)S(1)}, bf16[24,1664]{1,0:T(8,128)(2,1)S(1)}, u32[]{:S(2)}, u32[]{:S(2)}) collective-permute-start(bf16[24,1664]{1,0:T(8,128)(2,1)S(1)} %get-tuple-element.28), channel_id=1, source_target_pairs={{2,0},{0,2},{6,4},{4,6},{10,8},{8,10},{14,12},{12,14},{18,16},{16,... | collective-permute-start | bytes 239624 | tf_op jit(solution)/shard_map/ppermute | solution.py:516
  5.6 1.5 %collective-permute-start.2 = (bf16[24,1664]{1,0:T(8,128)(2,1)S(1)}, bf16[24,1664]{1,0:T(8,128)(2,1)S(1)}, u32[]{:S(2)}, u32[]{:S(2)}) collective-permute-start(bf16[24,1664]{1,0:T(8,128)(2,1)S(1)} %get-tuple-element.29), channel_id=1, source_target_pairs={{6,0},{4,2},{2,4},{0,6},{14,8},{12,10},{10,12},{8,14},{22,16},{20,... | collective-permute-start | bytes 239624 | tf_op jit(solution)/shard_map/ppermute | solution.py:516
  7.0 0.1 collective-permute-start.1
  7.1 3.1 %near_own.1 = (f32[24,1536]{1,0:T(8,128)S(1)}, bf16[2048,48]{1,0:T(8,128)(2,1)S(1)}, bf16[48,2048]{1,0:T(8,128)(2,1)S(1)}, f32[1,2048]{1,0:T(1,128)S(1)}, f32[24...) custom-call(s32[8]{0:T(128)} %count_in.3, ...), custom_call_target="tpu_custom_call" | custom-call | tf_op jit(solution)/shard_map/near_own/pallas_call | solution.py:537
  10.2 1.1 %collective-permute-done.1.from_2 = bf16[24,128]{1,0:T(8,128)(2,1)S(1)} collective-permute-done((bf16[24,128]{1,0:T(8,128)(2,1)S(1)}, bf16[24,128]{1,0:T(8,128)(2,1)S(1)}, u32[]{:S(2)}, u32[]{:S(2)}) %collective-permute-start.1) | collective-permute-done | bytes 6176 | tf_op jit(solution)/shard_map/ppermute | solution.py:516
  11.2 0.0 collective-permute-done.from_1
  11.2 0.0 collective-permute-done.2.from_3
  11.2 0.5 %row.1 = (bf16[24,1536]{1,0:T(8,128)(2,1)S(1)}, bf16[24,1536]{1,0:T(8,128)(2,1)S(1)}, bf16[24,2816]{1,0:T(8,128)(2,1)S(1)}, bf16[24,256]{1,0:T(8,128)(2,1)S(1)}) custom-call(bf16[24,2048]{1,0:T(8,128)(2,1)S(1)} %get-tuple-element.25.own, bf16[24,512]{1,0:T(8,128)(2,1)S(1)} %get-tuple-element.26.moments, bf16[24,128]{1,0:T(8,128)(2,1)S(1)} %get-tuple-element.27.totals, ...), custom_call_target="tpu_custom_call" | custom-call | tf_op jit(solution)/shard_map/row/pallas_call | solution.py:537
  11.7 1.6 %collective-permute-start.3 = (bf16[24,2816]{1,0:T(8,128)(2,1)S(1)}, bf16[24,2816]{1,0:T(8,128)(2,1)S(1)}, u32[]{:S(2)}, u32[]{:S(2)}) collective-permute-start(bf16[24,2816]{1,0:T(8,128)(2,1)S(1)} %get-tuple-element.37), channel_id=1, source_target_pairs={{8,0},{10,2},{12,4},{14,6},{0,8},{2,10},{4,12},{6,14},{24,16},{26,... | collective-permute-start | bytes 405512 | tf_op jit(solution)/shard_map/ppermute | solution.py:516
  13.4 1.4 %near_middle.1 = (f32[24,2048]{1,0:T(8,128)S(1)}, bf16[24,2560]{1,0:T(8,128)(2,1)S(1)}, f32[24,512]{1,0:T(8,128)S(1)}) custom-call(bf16[24,2048]{1,0:T(8,128)(2,1)S(1)} %get-tuple-element.25.own, bf16[24,1536]{1,0:T(8,128)(2,1)S(1)} %get-tuple-element.31.left, bf16[24,1536]{1,0:T(8,128)(2,1)S(1)} %get-tuple-element.32.right, ...), custom_call_target="tpu_custom_call" | custom-call | tf_op jit(solution)/shard_map/near_middle/pallas_call | solution.py:537
  14.8 0.1 collective-permute-start.4
  14.8 1.1 %near_side.1.early.near = f32[24,2048]{1,0:T(8,128)S(1)} custom-call(bf16[24,1536]{1,0:T(8,128)(2,1)S(1)} %get-tuple-element.31.left, bf16[24,1536]{1,0:T(8,128)(2,1)S(1)} %get-tuple-element.32.right, f32[24,2048]{1,0:T(8,128)S(1)} %get-tuple-element.36.early, bf16[48,2048]{1,0:T(8,128)(2,1)S(1)} %get-tuple-element.35.target), custom_call_target="tpu_custom_call" | custom-call | tf_op jit(solution)/shard_map/near_side/pallas_call | solution.py:537
  15.9 0.9 %collective-permute-done.3.faces.faces_even = bf16[24,2816]{1,0:T(8,128)(2,1)S(1)} collective-permute-done((bf16[24,2816]{1,0:T(8,128)(2,1)S(1)}, bf16[24,2816]{1,0:T(8,128)(2,1)S(1)}, u32[]{:S(2)}, u32[]{:S(2)}) %collective-permute-start.3) | collective-permute-done | bytes 135200 | tf_op jit(solution)/shard_map/ppermute | solution.py:516
  16.8 2.6 %collective-permute-start.5 = (bf16[24,512]{1,0:T(8,128)(2,1)S(1)}, bf16[24,512]{1,0:T(8,128)(2,1)S(1)}, u32[]{:S(2)}, u32[]{:S(2)}) collective-permute-start(bf16[24,512]{1,0:T(8,128)(2,1)S(1)} %row_pairs.1), channel_id=1, source_target_pairs={{16,0},{18,2},{20,4},{22,6},{24,8},{26,10},{28,12},{30,14},{0,16},... | collective-permute-start | bytes 73736 | tf_op jit(solution)/shard_map/ppermute | solution.py:516
  19.4 2.5 %near_even.1.early = f32[24,2048]{1,0:T(8,128)S(1)} custom-call(f32[24,2048]{1,0:T(8,128)S(1)} %near_side.1.early.near, bf16[48,2048]{1,0:T(8,128)(2,1)S(1)} %get-tuple-element.35.target, bf16[24,1536]{1,0:T(8,128)(2,1)S(1)} %get-tuple-element.32.right, bf16[24,2816]{1,0:T(8,128)(2,1)S(1)} %collective-permute-done.3.faces.faces_even), custom_call_target="tpu_custom_call" | custom-call | tf_op jit(solution)/shard_map/near_even/pallas_call | solution.py:537
  21.9 0.0 collective-permute-done.4.faces.faces_odd
  22.0 0.0 collective-permute-done.5.rest_1_
  22.0 1.3 %evaluate.1 = (f32[17,2048]{1,0:T(8,128)}, f32[1,2176]{1,0:T(1,128)S(1)}) custom-call(f32[24,2048]{1,0:T(8,128)S(1)} %near_odd.1.near, bf16[24,2816]{1,0:T(8,128)(2,1)S(1)} %collective-permute-done.3.faces.faces_even, bf16[24,2560]{1,0:T(8,128)(2,1)S(1)} %collective-permute-done.4.faces.faces_odd, bf16[128,2048]{1,0:T(8,128)(2,1)S(1)} %get-tuple-element.39.basis, ...), custom_call_target="tpu_custom_call" | custom-call | tf_op jit(solution)/shard_map/evaluate/pallas_call | solution.py:537
  23.3 0.0 collective-permute-start.6
  23.3 1.2 %collective-permute-done.6.other = f32[1,2176]{1,0:T(1,128)S(1)} collective-permute-done((f32[1,2176]{1,0:T(1,128)S(1)}, f32[1,2176]{1,0:T(1,128)S(1)}, u32[]{:S(2)}, u32[]{:S(2)}) %collective-permute-start.6) | collective-permute-done | bytes 8736 | tf_op jit(solution)/shard_map/ppermute | solution.py:516
  24.5 0.7 %mean.1 = f32[1,2048]{1,0:T(1,128)} custom-call(f32[1,2176]{1,0:T(1,128)S(1)} %get-tuple-element.47.mine, f32[1,2176]{1,0:T(1,128)S(1)} %collective-permute-done.6.other), custom_call_target="tpu_custom_call" | custom-call | tf_op jit(solution)/shard_map/mean/pallas_call | solution.py:537
  (2 shorter events, 0.0 us)
Async XLA Ops:
  2.5 8.7 %collective-permute-start = (bf16[24,1664]{1,0:T(8,128)(2,1)S(1)}, bf16[24,1664]{1,0:T(8,128)(2,1)S(1)}, u32[]{:S(2)}, u32[]{:S(2)}) collective-permute-start(bf16[24,1664]{1,0:T(8,128)(2,1)S(1)} %get-tuple-element.28), channel_id=1, source_target_pairs={{2,0},{0,2},{6,4},{4,6},{10,8},{8,10},{14,12},{12,14},{18,16},{16,... | collective-permute-start | bytes 239624 | tf_op jit(solution)/shard_map/ppermute | solution.py:516
  5.6 5.7 %collective-permute-start.2 = (bf16[24,1664]{1,0:T(8,128)(2,1)S(1)}, bf16[24,1664]{1,0:T(8,128)(2,1)S(1)}, u32[]{:S(2)}, u32[]{:S(2)}) collective-permute-start(bf16[24,1664]{1,0:T(8,128)(2,1)S(1)} %get-tuple-element.29), channel_id=1, source_target_pairs={{6,0},{4,2},{2,4},{0,6},{14,8},{12,10},{10,12},{8,14},{22,16},{20,... | collective-permute-start | bytes 239624 | tf_op jit(solution)/shard_map/ppermute | solution.py:516
  7.0 4.2 %collective-permute-start.1 = (bf16[24,128]{1,0:T(8,128)(2,1)S(1)}, bf16[24,128]{1,0:T(8,128)(2,1)S(1)}, u32[]{:S(2)}, u32[]{:S(2)}) collective-permute-start(bf16[24,128]{1,0:T(8,128)(2,1)S(1)} %get-tuple-element.27.totals), channel_id=1, source_target_pairs={{4,0},{6,2},{0,4},{2,6},{12,8},{14,10},{8,12},{10,14},{20,16},{22,... | collective-permute-start | bytes 18440 | tf_op jit(solution)/shard_map/ppermute | solution.py:516
  11.7 5.1 %collective-permute-start.3 = (bf16[24,2816]{1,0:T(8,128)(2,1)S(1)}, bf16[24,2816]{1,0:T(8,128)(2,1)S(1)}, u32[]{:S(2)}, u32[]{:S(2)}) collective-permute-start(bf16[24,2816]{1,0:T(8,128)(2,1)S(1)} %get-tuple-element.37), channel_id=1, source_target_pairs={{8,0},{10,2},{12,4},{14,6},{0,8},{2,10},{4,12},{6,14},{24,16},{26,... | collective-permute-start | bytes 405512 | tf_op jit(solution)/shard_map/ppermute | solution.py:516
  14.8 7.2 %collective-permute-start.4 = (bf16[24,2560]{1,0:T(8,128)(2,1)S(1)}, bf16[24,2560]{1,0:T(8,128)(2,1)S(1)}, u32[]{:S(2)}, u32[]{:S(2)}) collective-permute-start(bf16[24,2560]{1,0:T(8,128)(2,1)S(1)} %get-tuple-element.38), channel_id=1, source_target_pairs={{1,0},{0,1},{3,2},{2,3},{5,4},{4,5},{7,6},{6,7},{16,8},{17,9},{18,... | collective-permute-start | bytes 368648 | tf_op jit(solution)/shard_map/ppermute | solution.py:527
  16.8 5.2 %collective-permute-start.5 = (bf16[24,512]{1,0:T(8,128)(2,1)S(1)}, bf16[24,512]{1,0:T(8,128)(2,1)S(1)}, u32[]{:S(2)}, u32[]{:S(2)}) collective-permute-start(bf16[24,512]{1,0:T(8,128)(2,1)S(1)} %row_pairs.1), channel_id=1, source_target_pairs={{16,0},{18,2},{20,4},{22,6},{24,8},{26,10},{28,12},{30,14},{0,16},... | collective-permute-start | bytes 73736 | tf_op jit(solution)/shard_map/ppermute | solution.py:516
  23.3 1.2 %collective-permute-start.6 = (f32[1,2176]{1,0:T(1,128)S(1)}, f32[1,2176]{1,0:T(1,128)S(1)}, u32[]{:S(2)}, u32[]{:S(2)}) collective-permute-start(f32[1,2176]{1,0:T(1,128)S(1)} %get-tuple-element.47.mine), channel_id=1, source_target_pairs={{1,0},{0,1},{3,2},{2,3},{5,4},{4,5},{7,6},{6,7},{9,8},{8,9},{11,10... | collective-permute-start | bytes 26120 | tf_op jit(solution)/shard_map/ppermute | solution.py:516

commit v28 on v27

--- a/solution.py
+++ b/solution.py
@@ -280,8 +280,7 @@
 
 def own_groups(near, first, last, target, source, own):
     pts = source.shape[0] // 8
-    starts = [0, 4 * pts]
-    pulled(near, [(group, source, own, starts) for group in range(first, last)], target, 4 * pts)
+    pulled(near, [(group, source, own, [0]) for group in range(first, last)], target, 8 * pts)
 
 
 def box_columns(depth, box_x, box_z, nodes):
@@ -437,8 +436,8 @@
             centre = (place // 2 - 1.5, place % 2 - 0.5, height)
             sides[lanes(place * pts, pts), :] = source_features(faces, place * pts, pts, centre)
 
-        jobs = [(i + 2 * step, sides, faces, [(2 * i + 3 * turn) * pts for turn in range(2)]) for i in range(2)]
-        pulled(near, jobs, target, 3 * pts, early)
+        jobs = [(i + 2 * step, sides, faces, [2 * i * pts]) for i in range(2)]
+        pulled(near, jobs, target, 6 * pts, early)
 
     @pl.when(jnp.logical_not(inside))
     def _():

time: 25.4 us -> 25.3 us (level)
  no operation moved by 1% of the time
where the time goes in v28:
time: 25.3 us; the launch traced here: 25.2 us
  Pallas kernels  12.5 us (49%)
  starting transfers between devices  8.78 us (35%)
  waiting for transfers between devices  3.23 us (13%)
  between operations  0.69 us (3%)
    pallas_call x10, Pallas kernels, call(): pl.pallas_call(kernel, in_specs=in_specs, out_specs=[vmem] * len(outs), o...  12.5 us
    ppermute x6, starting transfers between devices, swapped(): return lax.ppermute(block, axis, [(partner(i), i) for i in range(size)])  8.78 us
    ppermute x6, waiting for transfers between devices, swapped(): return lax.ppermute(block, axis, [(partner(i), i) for i in range(size)])  3.23 us
  transfers between devices with their start and end apart: 7, of which 3 were waited for; matrix products, arithmetic and copies ran while one was open for 0% of the time, Pallas kernels for 32%

profile of v28, /device:TPU:0, one launch (start us, length us, event | category | flops | bytes accessed | tf_op | source)
XLA Modules:
  0.0 25.2 jit_solution(3185024264033376157)
XLA Ops:
  0.6 1.9 %pack.1 = (bf16[24,2048]{1,0:T(8,128)(2,1)S(1)}, bf16[128,2048]{1,0:T(8,128)(2,1)S(1)}, bf16[24,512]{1,0:T(8,128)(2,1)S(1)}, bf16[24,128]{1,0:T(8,128)(2,1)S(1)}...) custom-call(s32[8]{0:T(128)} %count_in.3, f32[3,2048]{1,0:T(4,128)} %positions_in.1, ...), custom_call_target="tpu_custom_call" | custom-call | tf_op jit(solution)/shard_map/pack/pallas_call | solution.py:536
  2.5 3.0 %collective-permute-start = (bf16[24,1664]{1,0:T(8,128)(2,1)S(1)}, bf16[24,1664]{1,0:T(8,128)(2,1)S(1)}, u32[]{:S(2)}, u32[]{:S(2)}) collective-permute-start(bf16[24,1664]{1,0:T(8,128)(2,1)S(1)} %get-tuple-element.28), channel_id=1, source_target_pairs={{2,0},{0,2},{6,4},{4,6},{10,8},{8,10},{14,12},{12,14},{18,16},{16,... | collective-permute-start | bytes 239624 | tf_op jit(solution)/shard_map/ppermute | solution.py:515
  5.6 1.5 %collective-permute-start.2 = (bf16[24,1664]{1,0:T(8,128)(2,1)S(1)}, bf16[24,1664]{1,0:T(8,128)(2,1)S(1)}, u32[]{:S(2)}, u32[]{:S(2)}) collective-permute-start(bf16[24,1664]{1,0:T(8,128)(2,1)S(1)} %get-tuple-element.29), channel_id=1, source_target_pairs={{6,0},{4,2},{2,4},{0,6},{14,8},{12,10},{10,12},{8,14},{22,16},{20,... | collective-permute-start | bytes 239624 | tf_op jit(solution)/shard_map/ppermute | solution.py:515
  7.0 0.1 collective-permute-start.1
  7.1 3.0 %near_own.1 = (f32[24,1536]{1,0:T(8,128)S(1)}, bf16[2048,48]{1,0:T(8,128)(2,1)S(1)}, bf16[48,2048]{1,0:T(8,128)(2,1)S(1)}, f32[1,2048]{1,0:T(1,128)S(1)}, f32[24...) custom-call(s32[8]{0:T(128)} %count_in.3, ...), custom_call_target="tpu_custom_call" | custom-call | tf_op jit(solution)/shard_map/near_own/pallas_call | solution.py:536
  10.1 1.1 %collective-permute-done.1.from_2 = bf16[24,128]{1,0:T(8,128)(2,1)S(1)} collective-permute-done((bf16[24,128]{1,0:T(8,128)(2,1)S(1)}, bf16[24,128]{1,0:T(8,128)(2,1)S(1)}, u32[]{:S(2)}, u32[]{:S(2)}) %collective-permute-start.1) | collective-permute-done | bytes 6176 | tf_op jit(solution)/shard_map/ppermute | solution.py:515
  11.2 0.0 collective-permute-done.from_1
  11.2 0.0 collective-permute-done.2.from_3
  11.2 0.5 %row.1 = (bf16[24,1536]{1,0:T(8,128)(2,1)S(1)}, bf16[24,1536]{1,0:T(8,128)(2,1)S(1)}, bf16[24,2816]{1,0:T(8,128)(2,1)S(1)}, bf16[24,256]{1,0:T(8,128)(2,1)S(1)}) custom-call(bf16[24,2048]{1,0:T(8,128)(2,1)S(1)} %get-tuple-element.25.own, bf16[24,512]{1,0:T(8,128)(2,1)S(1)} %get-tuple-element.26.moments, bf16[24,128]{1,0:T(8,128)(2,1)S(1)} %get-tuple-element.27.totals, ...), custom_call_target="tpu_custom_call" | custom-call | tf_op jit(solution)/shard_map/row/pallas_call | solution.py:536
  11.7 1.6 %collective-permute-start.3 = (bf16[24,2816]{1,0:T(8,128)(2,1)S(1)}, bf16[24,2816]{1,0:T(8,128)(2,1)S(1)}, u32[]{:S(2)}, u32[]{:S(2)}) collective-permute-start(bf16[24,2816]{1,0:T(8,128)(2,1)S(1)} %get-tuple-element.37), channel_id=1, source_target_pairs={{8,0},{10,2},{12,4},{14,6},{0,8},{2,10},{4,12},{6,14},{24,16},{26,... | collective-permute-start | bytes 405512 | tf_op jit(solution)/shard_map/ppermute | solution.py:515
  13.4 1.4 %near_middle.1 = (f32[24,2048]{1,0:T(8,128)S(1)}, bf16[24,2560]{1,0:T(8,128)(2,1)S(1)}, f32[24,512]{1,0:T(8,128)S(1)}) custom-call(bf16[24,2048]{1,0:T(8,128)(2,1)S(1)} %get-tuple-element.25.own, bf16[24,1536]{1,0:T(8,128)(2,1)S(1)} %get-tuple-element.31.left, bf16[24,1536]{1,0:T(8,128)(2,1)S(1)} %get-tuple-element.32.right, ...), custom_call_target="tpu_custom_call" | custom-call | tf_op jit(solution)/shard_map/near_middle/pallas_call | solution.py:536
  14.8 0.0 collective-permute-start.4
  14.8 1.1 %near_side.1.early.near = f32[24,2048]{1,0:T(8,128)S(1)} custom-call(bf16[24,1536]{1,0:T(8,128)(2,1)S(1)} %get-tuple-element.31.left, bf16[24,1536]{1,0:T(8,128)(2,1)S(1)} %get-tuple-element.32.right, f32[24,2048]{1,0:T(8,128)S(1)} %get-tuple-element.36.early, bf16[48,2048]{1,0:T(8,128)(2,1)S(1)} %get-tuple-element.35.target), custom_call_target="tpu_custom_call" | custom-call | tf_op jit(solution)/shard_map/near_side/pallas_call | solution.py:536
  15.9 0.9 %collective-permute-done.3.faces.faces_even = bf16[24,2816]{1,0:T(8,128)(2,1)S(1)} collective-permute-done((bf16[24,2816]{1,0:T(8,128)(2,1)S(1)}, bf16[24,2816]{1,0:T(8,128)(2,1)S(1)}, u32[]{:S(2)}, u32[]{:S(2)}) %collective-permute-start.3) | collective-permute-done | bytes 135200 | tf_op jit(solution)/shard_map/ppermute | solution.py:515
  16.8 2.6 %collective-permute-start.5 = (bf16[24,512]{1,0:T(8,128)(2,1)S(1)}, bf16[24,512]{1,0:T(8,128)(2,1)S(1)}, u32[]{:S(2)}, u32[]{:S(2)}) collective-permute-start(bf16[24,512]{1,0:T(8,128)(2,1)S(1)} %row_pairs.1), channel_id=1, source_target_pairs={{16,0},{18,2},{20,4},{22,6},{24,8},{26,10},{28,12},{30,14},{0,16},... | collective-permute-start | bytes 73736 | tf_op jit(solution)/shard_map/ppermute | solution.py:515
  19.4 2.5 %near_even.1.early = f32[24,2048]{1,0:T(8,128)S(1)} custom-call(f32[24,2048]{1,0:T(8,128)S(1)} %near_side.1.early.near, bf16[48,2048]{1,0:T(8,128)(2,1)S(1)} %get-tuple-element.35.target, bf16[24,1536]{1,0:T(8,128)(2,1)S(1)} %get-tuple-element.32.right, bf16[24,2816]{1,0:T(8,128)(2,1)S(1)} %collective-permute-done.3.faces.faces_even), custom_call_target="tpu_custom_call" | custom-call | tf_op jit(solution)/shard_map/near_even/pallas_call | solution.py:536
  21.9 0.0 collective-permute-done.4.faces.faces_odd
  22.0 0.0 collective-permute-done.5.rest_1_
  22.0 1.3 %evaluate.1 = (f32[17,2048]{1,0:T(8,128)}, f32[1,2176]{1,0:T(1,128)S(1)}) custom-call(f32[24,2048]{1,0:T(8,128)S(1)} %near_odd.1.near, bf16[24,2816]{1,0:T(8,128)(2,1)S(1)} %collective-permute-done.3.faces.faces_even, bf16[24,2560]{1,0:T(8,128)(2,1)S(1)} %collective-permute-done.4.faces.faces_odd, bf16[128,2048]{1,0:T(8,128)(2,1)S(1)} %get-tuple-element.39.basis, ...), custom_call_target="tpu_custom_call" | custom-call | tf_op jit(solution)/shard_map/evaluate/pallas_call | solution.py:536
  23.3 0.0 collective-permute-start.6
  23.3 1.2 %collective-permute-done.6.other = f32[1,2176]{1,0:T(1,128)S(1)} collective-permute-done((f32[1,2176]{1,0:T(1,128)S(1)}, f32[1,2176]{1,0:T(1,128)S(1)}, u32[]{:S(2)}, u32[]{:S(2)}) %collective-permute-start.6) | collective-permute-done | bytes 8736 | tf_op jit(solution)/shard_map/ppermute | solution.py:515
  24.5 0.7 %mean.1 = f32[1,2048]{1,0:T(1,128)} custom-call(f32[1,2176]{1,0:T(1,128)S(1)} %get-tuple-element.47.mine, f32[1,2176]{1,0:T(1,128)S(1)} %collective-permute-done.6.other), custom_call_target="tpu_custom_call" | custom-call | tf_op jit(solution)/shard_map/mean/pallas_call | solution.py:536
  (2 shorter events, 0.0 us)
Async XLA Ops:
  2.5 8.7 %collective-permute-start = (bf16[24,1664]{1,0:T(8,128)(2,1)S(1)}, bf16[24,1664]{1,0:T(8,128)(2,1)S(1)}, u32[]{:S(2)}, u32[]{:S(2)}) collective-permute-start(bf16[24,1664]{1,0:T(8,128)(2,1)S(1)} %get-tuple-element.28), channel_id=1, source_target_pairs={{2,0},{0,2},{6,4},{4,6},{10,8},{8,10},{14,12},{12,14},{18,16},{16,... | collective-permute-start | bytes 239624 | tf_op jit(solution)/shard_map/ppermute | solution.py:515
  5.6 5.7 %collective-permute-start.2 = (bf16[24,1664]{1,0:T(8,128)(2,1)S(1)}, bf16[24,1664]{1,0:T(8,128)(2,1)S(1)}, u32[]{:S(2)}, u32[]{:S(2)}) collective-permute-start(bf16[24,1664]{1,0:T(8,128)(2,1)S(1)} %get-tuple-element.29), channel_id=1, source_target_pairs={{6,0},{4,2},{2,4},{0,6},{14,8},{12,10},{10,12},{8,14},{22,16},{20,... | collective-permute-start | bytes 239624 | tf_op jit(solution)/shard_map/ppermute | solution.py:515
  7.0 4.2 %collective-permute-start.1 = (bf16[24,128]{1,0:T(8,128)(2,1)S(1)}, bf16[24,128]{1,0:T(8,128)(2,1)S(1)}, u32[]{:S(2)}, u32[]{:S(2)}) collective-permute-start(bf16[24,128]{1,0:T(8,128)(2,1)S(1)} %get-tuple-element.27.totals), channel_id=1, source_target_pairs={{4,0},{6,2},{0,4},{2,6},{12,8},{14,10},{8,12},{10,14},{20,16},{22,... | collective-permute-start | bytes 18440 | tf_op jit(solution)/shard_map/ppermute | solution.py:515
  11.7 5.1 %collective-permute-start.3 = (bf16[24,2816]{1,0:T(8,128)(2,1)S(1)}, bf16[24,2816]{1,0:T(8,128)(2,1)S(1)}, u32[]{:S(2)}, u32[]{:S(2)}) collective-permute-start(bf16[24,2816]{1,0:T(8,128)(2,1)S(1)} %get-tuple-element.37), channel_id=1, source_target_pairs={{8,0},{10,2},{12,4},{14,6},{0,8},{2,10},{4,12},{6,14},{24,16},{26,... | collective-permute-start | bytes 405512 | tf_op jit(solution)/shard_map/ppermute | solution.py:515
  14.8 7.1 %collective-permute-start.4 = (bf16[24,2560]{1,0:T(8,128)(2,1)S(1)}, bf16[24,2560]{1,0:T(8,128)(2,1)S(1)}, u32[]{:S(2)}, u32[]{:S(2)}) collective-permute-start(bf16[24,2560]{1,0:T(8,128)(2,1)S(1)} %get-tuple-element.38), channel_id=1, source_target_pairs={{1,0},{0,1},{3,2},{2,3},{5,4},{4,5},{7,6},{6,7},{16,8},{17,9},{18,... | collective-permute-start | bytes 368648 | tf_op jit(solution)/shard_map/ppermute | solution.py:526
  16.8 5.2 %collective-permute-start.5 = (bf16[24,512]{1,0:T(8,128)(2,1)S(1)}, bf16[24,512]{1,0:T(8,128)(2,1)S(1)}, u32[]{:S(2)}, u32[]{:S(2)}) collective-permute-start(bf16[24,512]{1,0:T(8,128)(2,1)S(1)} %row_pairs.1), channel_id=1, source_target_pairs={{16,0},{18,2},{20,4},{22,6},{24,8},{26,10},{28,12},{30,14},{0,16},... | collective-permute-start | bytes 73736 | tf_op jit(solution)/shard_map/ppermute | solution.py:515
  23.3 1.2 %collective-permute-start.6 = (f32[1,2176]{1,0:T(1,128)S(1)}, f32[1,2176]{1,0:T(1,128)S(1)}, u32[]{:S(2)}, u32[]{:S(2)}) collective-permute-start(f32[1,2176]{1,0:T(1,128)S(1)} %get-tuple-element.47.mine), channel_id=1, source_target_pairs={{1,0},{0,1},{3,2},{2,3},{5,4},{4,5},{7,6},{6,7},{9,8},{8,9},{11,10... | collective-permute-start | bytes 26120 | tf_op jit(solution)/shard_map/ppermute | solution.py:515
